TPU v7x, 32 devices: a whole 2x2x4 slice. The times are simulated.
32 devices in a mesh: dp: 8 (over z, x), tensor: 4 (over y, core).
Axes of the slice: x: 2, y: 2, z: 4, core: 2. Of those that a mesh axis runs over, the one named last changes fastest.
Arguments:
- tokens: bfloat16 [8192, 2048], P('dp', 'tensor'), may hold values from -6 to 6
- cotangent: bfloat16 [8192, 2048], P('dp', 'tensor'), may hold values from -6 to 6
- doc_lengths: int32 [8, 4], P('dp'), may hold values from 0 to 1024, as said below
- norm_gain: float32 [2048], replicated, may hold values from 0.5 to 1.5
- w_inner: bfloat16 [2048, 2, 4096], P(None, None, 'tensor'), may hold values from -0.125 to 0.125
- w_step: bfloat16 [2048, 64], P(None, 'tensor'), may hold values from -0.125 to 0.125
- w_state: bfloat16 [2048, 256], replicated, may hold values from -0.125 to 0.125
- conv_inner: float32 [5, 4096], P(None, 'tensor'), may hold values from -3 to 3
- conv_state: float32 [5, 256], replicated, may hold values from -3 to 3
- step_bias: float32 [64], P('tensor'), may hold values from -4 to -1
- log_rate: float32 [64], P('tensor'), may hold values from 0 to 2.5
- skip_gain: float32 [64], P('tensor'), may hold values from 0.5 to 1.5
- gate_gain: float32 [4096], P('tensor'), may hold values from 0.5 to 1.5
- w_out: bfloat16 [4096, 2048], P('tensor'), may hold values from -0.09375 to 0.09375
Outputs:
- mixed_out: bfloat16 [8192, 2048], P('dp', 'tensor')
- grad_tokens: bfloat16 [8192, 2048], P('dp', 'tensor')
- grad_norm_gain: float32 [2048], P('tensor')
- grad_w_inner: float32 [2048, 2, 4096], P('dp', None, 'tensor')
- grad_w_step: float32 [2048, 64], P('dp', 'tensor')
- grad_w_state: float32 [2048, 256], P(('dp', 'tensor'))
- grad_conv_inner: float32 [5, 4096], P(None, 'tensor')
- grad_conv_state: float32 [5, 256], replicated
- grad_step_bias: float32 [64], P('tensor')
- grad_log_rate: float32 [64], P('tensor')
- grad_skip_gain: float32 [64], P('tensor')
- grad_gate_gain: float32 [4096], P('tensor')
- grad_w_out: float32 [4096, 2048], P('tensor', 'dp')
Inputs may be any that keep to these rules, and one draw needn't show every extreme that they name: `doc_lengths`: row s lists the lengths of up to 4 documents packed from the start of slot s, followed by padding; zero is an empty document; a row's sum lies between 513 and 1024; some row is one document of 1024 tokens.
All inputs are finite; a program needn't handle non-finite values.
Results may differ from a plain program's by a relative error of at most 0.0091.
Values may be sent and summed in bfloat16 or wider, within the bound.
No kernel may reach another device: no remote copies, remote signals or barrier semaphores. Data moves between devices by JAX's collectives and lax.ppermute only.
A program may use at most 192 MiB of HBM per device.

v0:
```python
import jax
import jax.numpy as jnp
from jax import lax
from jax.sharding import PartitionSpec as P

BLOCK = 256


epsilon = 1e-05
highest = lax.Precision.HIGHEST


def segment_ids(lengths, length_all):
    doc_ends = jnp.cumsum(lengths)
    places = jnp.arange(length_all, dtype=jnp.int32)
    segment = jnp.sum((places[:, None] >= doc_ends[None, :]).astype(jnp.int32), axis=1)
    present = (places < doc_ends[-1]).astype(jnp.float32)
    return (segment, present)


def causal_conv(values, filters, segment):
    taps_count = filters.shape[0] - 1
    result = filters[taps_count] + filters[0] * values
    for offset in range(1, taps_count):
        shifted = jnp.concatenate(
            [jnp.zeros((offset, values.shape[1]), values.dtype), values[:-offset]], axis=0
        )
        earlier = jnp.concatenate([jnp.full((offset,), -1, jnp.int32), segment[:-offset]])
        result = (
            result + filters[offset] * shifted * (earlier == segment).astype(values.dtype)[:, None]
        )
    return jax.nn.silu(result)


def scan_block(carried, block_data):
    memory, last_doc = carried
    inputs, decay_rate, keys_in, queries, segment = block_data
    blocksize = segment.shape[0]
    rising = jnp.cumsum(decay_rate, axis=0)
    places = jnp.arange(blocksize)
    linked = (places[:, None] >= places[None, :]) & (segment[:, None] == segment[None, :])
    linked_cube = linked[:, :, None]
    spread = rising[:, None, :] - rising[None, :, :]
    weights = jnp.where(linked_cube, jnp.exp(jnp.where(linked_cube, spread, 0.0)), 0.0)
    intersection = jnp.dot(queries, keys_in.T, precision=highest)
    outputs = jnp.einsum(
        "ijh,jhp->ihp", weights * intersection[:, :, None], inputs, precision=highest
    )
    entering = jnp.exp(rising) * (segment == last_doc).astype(jnp.float32)[:, None]
    outputs = outputs + entering[:, :, None] * jnp.einsum(
        "is,hps->ihp", queries, memory, precision=highest
    )
    final_doc = segment[-1]
    leaving = jnp.where((segment == final_doc)[:, None], jnp.exp(rising[-1][None, :] - rising), 0.0)
    carry_scale = jnp.exp(rising[-1]) * (final_doc == last_doc).astype(jnp.float32)
    fresh = jnp.einsum("jhp,js->hps", leaving[:, :, None] * inputs, keys_in, precision=highest)
    memory = memory * carry_scale[:, None, None] + fresh
    return ((memory, final_doc), outputs)


def state_scan(shaped, step_size, decay_rate, keys_in, queries, segment):
    length_all, heads_all, headsize = shaped.shape
    blocks_all = length_all // BLOCK
    states = keys_in.shape[1]
    pieces = (
        (shaped * step_size[:, :, None]).reshape(blocks_all, BLOCK, heads_all, headsize),
        decay_rate.reshape(blocks_all, BLOCK, heads_all),
        keys_in.reshape(blocks_all, BLOCK, states),
        queries.reshape(blocks_all, BLOCK, states),
        segment.reshape(blocks_all, BLOCK),
    )
    initial = (
        jnp.zeros((heads_all, headsize, states), jnp.float32),
        jnp.array(-1, dtype=jnp.int32),
    )
    _, outputs = lax.scan(jax.checkpoint(scan_block), initial, pieces)
    return outputs.reshape(length_all, heads_all, headsize)


def mixer(
    proj_inner,
    proj_step,
    proj_state,
    conv_inner,
    conv_state,
    step_bias,
    log_rate,
    skip_gain,
    segment,
):
    channels = proj_inner.shape[1] // 2
    gate_part = proj_inner[:, :channels]
    value_part = proj_inner[:, channels:]
    convolved = causal_conv(value_part, conv_inner, segment)
    state_conv = causal_conv(proj_state, conv_state, segment)
    step_size = jax.nn.softplus(proj_step + step_bias)
    decay_rate = -jnp.exp(log_rate) * step_size
    heads_all = step_size.shape[1]
    length_all = convolved.shape[0]
    shaped = convolved.reshape(length_all, heads_all, channels // heads_all)
    states = state_conv.shape[1] // 2
    mixed_heads = state_scan(
        shaped, step_size, decay_rate, state_conv[:, :states], state_conv[:, states:], segment
    )
    mixed_heads = mixed_heads + skip_gain[None, :, None] * shaped
    return mixed_heads.reshape(length_all, channels) * jax.nn.silu(gate_part)


def contract_rows(left, right):
    return lax.dot_general(
        left, right, (((0,), (0,)), ((), ())), preferred_element_type=jnp.float32
    )


def contract_cols(left, right):
    return lax.dot_general(
        left, right, (((1,), (1,)), ((), ())), preferred_element_type=jnp.float32
    )


def shards(
    tokens,
    cotangent,
    doc_lengths,
    norm_gain,
    w_inner,
    w_step,
    w_state,
    conv_inner,
    conv_state,
    step_bias,
    log_rate,
    skip_gain,
    gate_gain,
    w_out,
):
    parts = lax.axis_size("tensor")
    groups = lax.axis_size("dp")
    rank = lax.axis_index("tensor")
    full_tokens, full_grad = (
        lax.all_gather(tokens, "tensor", axis=1, tiled=True),
        lax.all_gather(cotangent, "tensor", axis=1, tiled=True),
    )
    length_all, model_width = full_tokens.shape
    quarter = model_width // parts
    channels = w_inner.shape[2]
    segment, present = segment_ids(doc_lengths[0], length_all)
    wide_tokens = full_tokens.astype(jnp.float32)
    scale_in = lax.rsqrt(jnp.mean(wide_tokens * wide_tokens, axis=1, keepdims=True) + epsilon)
    normed = (wide_tokens * scale_in * norm_gain).astype(jnp.bfloat16)
    inner_flat = w_inner.reshape(model_width, 2 * channels)
    proj_inner = jnp.dot(normed, inner_flat, preferred_element_type=jnp.float32)
    proj_step = jnp.dot(normed, w_step, preferred_element_type=jnp.float32)
    proj_state = jnp.dot(normed, w_state, preferred_element_type=jnp.float32)

    def local_mixer(
        inner_now, step_now, state_now, conv_now, conv_shared, bias_now, rate_now, skip_now
    ):
        return mixer(
            inner_now,
            step_now,
            state_now,
            conv_now,
            conv_shared,
            bias_now,
            rate_now,
            skip_now,
            segment,
        )

    gated, mixer_back = jax.vjp(
        local_mixer,
        proj_inner,
        proj_step,
        proj_state,
        conv_inner,
        conv_state,
        step_bias,
        log_rate,
        skip_gain,
    )
    squares = lax.psum(jnp.sum(gated * gated, axis=1), "tensor")
    scale_out = lax.rsqrt(squares / (channels * parts) + epsilon)[:, None]
    factor = scale_out * gate_gain * present[:, None]
    mixed = (gated * factor).astype(jnp.bfloat16)
    branch = lax.psum_scatter(
        jnp.dot(mixed, w_out, preferred_element_type=jnp.float32),
        "tensor",
        scatter_dimension=1,
        tiled=True,
    )
    own_tokens = tokens.astype(jnp.float32)
    output = (own_tokens + branch).astype(jnp.bfloat16)
    grad_mixed = contract_cols(full_grad, w_out)
    grad_w_out = contract_rows(mixed, full_grad)
    weighted = grad_mixed * gated * present[:, None]
    row_inner = lax.psum(jnp.sum(weighted * gate_gain, axis=1), "tensor")
    grad_gated = grad_mixed * factor - gated * (
        scale_out**3 * row_inner[:, None] / (channels * parts)
    )
    grad_gate_gain = jnp.sum(weighted * scale_out, axis=0)
    (
        grad_inner,
        grad_step,
        grad_state,
        grad_conv_inner,
        grad_conv_state,
        grad_step_bias,
        grad_log_rate,
        grad_skip,
    ) = mixer_back(grad_gated)
    grad_state, grad_conv_state = lax.psum((grad_state, grad_conv_state), "tensor")
    low_inner = grad_inner.astype(jnp.bfloat16)
    low_step = grad_step.astype(jnp.bfloat16)
    low_state = grad_state.astype(jnp.bfloat16)
    partial_in = contract_cols(low_inner, inner_flat) + contract_cols(low_step, w_step)
    grad_normed = lax.psum_scatter(partial_in, "tensor", scatter_dimension=1, tiled=True)
    own_state = lax.dynamic_slice_in_dim(w_state, rank * quarter, quarter, 0)
    grad_normed = grad_normed + contract_cols(low_state, own_state)
    own_gain = lax.dynamic_slice_in_dim(norm_gain, rank * quarter, quarter, 0)
    row_norm = lax.psum(jnp.sum(own_tokens * own_gain * grad_normed, axis=1), "tensor")
    grad_tokens = (
        cotangent.astype(jnp.float32)
        + scale_in * own_gain * grad_normed
        - own_tokens * scale_in**3 * row_norm[:, None] / model_width
    )
    grad_norm_gain = jnp.sum(grad_normed * own_tokens * scale_in, axis=0)
    grad_w_inner = contract_rows(normed, low_inner)
    grad_w_step = contract_rows(normed, low_step)
    picked = lax.dynamic_index_in_dim(
        normed.reshape(length_all, groups, parts, model_width // (groups * parts)),
        rank,
        axis=2,
        keepdims=False,
    )
    grad_w_state = contract_rows(picked.reshape(length_all, model_width // parts), low_state)
    sum_inner, sum_step, sum_out, sum_state = (
        lax.psum_scatter(grad_w_inner, "dp", scatter_dimension=0, tiled=True),
        lax.psum_scatter(grad_w_step, "dp", scatter_dimension=0, tiled=True),
        lax.psum_scatter(grad_w_out, "dp", scatter_dimension=1, tiled=True),
        lax.psum_scatter(grad_w_state, "dp", scatter_dimension=0, tiled=True),
    )
    small_sums = lax.psum(
        (
            grad_norm_gain,
            grad_conv_inner,
            grad_conv_state,
            grad_step_bias,
            grad_log_rate,
            grad_skip,
            grad_gate_gain,
        ),
        "dp",
    )
    return (
        output,
        grad_tokens.astype(jnp.bfloat16),
        small_sums[0],
        sum_inner.reshape(sum_inner.shape[0], 2, channels),
        sum_step,
        sum_state,
        small_sums[1],
        small_sums[2],
        small_sums[3],
        small_sums[4],
        small_sums[5],
        small_sums[6],
        sum_out,
    )


def solution(mesh):
    placed = (
        P("dp", "tensor"),
        P("dp", "tensor"),
        P("dp", None),
        P(),
        P(None, None, "tensor"),
        P(None, "tensor"),
        P(),
        P(None, "tensor"),
        P(),
        P("tensor"),
        P("tensor"),
        P("tensor"),
        P("tensor"),
        P("tensor", None),
    )
    return jax.shard_map(
        shards,
        mesh=mesh,
        in_specs=placed,
        out_specs=(
            P("dp", "tensor"),
            P("dp", "tensor"),
            P("tensor"),
            P("dp", None, "tensor"),
            P("dp", "tensor"),
            P(("dp", "tensor"), None),
            P(None, "tensor"),
            P(),
            P("tensor"),
            P("tensor"),
            P("tensor"),
            P("tensor"),
            P("tensor", "dp"),
        ),
        check_vma=False,
    )
```

profile of v0, /device:TPU:0, one launch (start us, length us, event | category | flops | bytes accessed | tf_op | source)
XLA Modules:
  0.0 1278.9 jit_solution(34237540312225990)
XLA Ops:
  11.4 10.9 copy.180
  24.0 23.4 %all-gather.3.cloned.1.call-done = bf16[1024,2048]{0,1:T(8,128)(2,1)} async-done(((bf16[1024,512]{0,1:T(8,128)(2,1)}), bf16[1024,2048]{0,1:T(8,128)(2,1)}) %all-gather.3.cloned.1.call-update) | async-done | bytes 4194320 | tf_op jit(solution)/shard_map/all_gather | solution.py:141
  56.3 9.1 fusion.149
  71.3 6.5 fusion.101
  77.8 5.4 copy.102
  83.2 5.7 reshape.474
  106.9 94.2 %while.44 = (s32[]{:T(128)}, f32[16,64,128]{2,1,0:T(8,128)S(1)}, s32[]{:T(128)}, f32[4,256,16,64]{1,3,2,0:T(8,128)}, f32[4,16,64,128]{3,2,1,0:T(8,128)}, /*index...) while((s32[]{:T(128)}, f32[16,64,128]{2,1,0:T(8,128)S(1)}, ...), condition=%wide.region_6.7_spmd.clone, body=%wide.region_3.6_spmd.clone.sunk | while | flops 1717650176 | bytes 9269931 | solution.py:76
  121.7 6.1 fusion.232
  142.5 6.1 fusion.232
  163.3 6.1 fusion.232
  184.0 6.1 fusion.232
  201.0 8.1 copy.117
  209.1 7.6 reshape.511
  216.8 7.2 multiply_reduce_fusion.10
  223.9 5.9 psum.84
  229.9 11.9 multiply_reduce_fusion.2
  241.8 5.6 psum.85
  247.4 11.7 multiply_reduce_fusion.3
  259.2 7.2 reshape.512
  266.4 7.7 copy.110
  278.8 182.8 %while.45 = (s32[]{:T(128)}, f32[16,64,128]{2,1,0:T(8,128)}, f32[4,256,16,64]{1,3,2,0:T(8,128)}, f32[4,256,16]{1,0,2:T(4,128)}, f32[4,256,128]{2,1,0:T(8,128)}, ...) while((s32[]{:T(128)}, f32[16,64,128]{2,1,0:T(8,128)}, ...), condition=%wide.region_24.25_spmd.clone, body=%wide.region_12.24_spmd.clone.sunk | while | flops 3945923328 | bytes 31917148 | solution.py:76
  298.1 7.3 fusion.255
  316.5 5.8 fusion.258
  343.9 7.3 fusion.255
  362.3 5.8 fusion.258
  389.7 7.3 fusion.255
  408.1 5.8 fusion.258
  435.5 7.3 fusion.255
  453.9 5.8 fusion.258
  461.6 8.1 copy.120
  469.7 7.6 reshape.513
  479.8 5.4 copy.113
  485.2 10.7 multiply_reduce_fusion.7
  511.2 4.0 multiply_reduce_fusion.4
  515.3 15.9 %fusion.117 = f32[1024,2048]{1,0:T(8,128)} fusion(bf16[2048,2048]{1,0:T(8,128)(2,1)} %bitcast.410, f32[1024,1024]{1,0:T(8,128)} %get-tuple-element.752, f32[1024,1024]{1,0:T(8,128)} %get-tuple-element.753), kind=kOutput, calls=%fused_computation.207 | convolution fusion | flops 8594128896 | bytes 25165824 | tf_op jit(solution)/shard_map/dot_general | solution.py:116
  531.4 7.9 convolution_add_fusion.4
  539.9 13.0 %fusion.138 = f32[1024,2048]{1,0:T(8,128)} fusion(bf16[1024,2048]{1,0:T(8,128)(2,1)} %param.31, f32[1024,1024]{1,0:T(8,128)} %get-tuple-element.730, f32[1024]{0:T(1024)S(1)} %copy-done.56, f32[1024]{0:T(1024)S(1)} %copy-done.71, f32[1024]{0:T(1024)S(1)} %copy-done.58), kind=kOutput, calls=%fused_computation.252 | convolution fusion | flops 4299161600 | bytes 16789504 | tf_op jit(solution)/shard_map/dot_general | solution.py:187
  553.0 17.3 %fusion.116 = f32[2048,2048]{1,0:T(8,128)} fusion(bf16[1024,2048]{0,1:T(8,128)(2,1)} %copy-done.5, f32[1024,1024]{1,0:T(8,128)} %get-tuple-element.752, f32[1024,1024]{1,0:T(8,128)} %get-tuple-element.753), kind=kOutput, calls=%fused_computation.206 | convolution fusion | flops 8594128896 | bytes 29360128 | tf_op jit(solution)/shard_map/dot_general | solution.py:110
  579.9 41.9 %all-reduce.33 = bf16[1024,256]{1,0:T(8,128)(2,1)S(1)} all-reduce(f32[1024,256]{1,0:T(8,128)S(1)} %copy-done.20), channel_id=1, replica_groups=mesh['dp'=8,'tensor'=4] {'tensor'}, use_global_device_ids=true, to_apply=%region_27.28 | all-reduce | flops 262144 | bytes 1572864 | tf_op jit(solution)/shard_map/psum | solution.py:212
  624.4 11.5 fusion.137
  640.9 11.0 all-reduce.31
  652.0 38.1 %all-reduce.30 = (f32[512]{0:T(512)}, f32[5,1024]{1,0:T(8,128)}, f32[5,256]{1,0:T(8,128)}, f32[16]{0:T(128)}, f32[16]{0:T(128)}, /*index=5*/f32[16]{0:T(128)}, f32[1024]{0:T(1024)}) all-reduce(f32[512]{0:T(512)S(1)} %get-tuple-element.648, f32[5,1024]{1,0:T(8,128)S(1)} %pad_add_fusion, ...), channel_id=1, replica_groups=mesh['dp'=8,'tensor'=4] {'dp'}, use_global_device_ids=true, to_apply=%region_31.32 | all-reduce | flops 7984 | bytes 63872 | tf_op jit(solution)/shard_map/psum | solution.py:243
  690.1 13.5 %reduce-scatter.7.cloned.1.call-done = f32[1024,512]{1,0:T(8,128)} async-done(((f32[1024,2048]{1,0:T(8,128)}), f32[1024,512]{1,0:T(8,128)}) %reduce-scatter.7.cloned.1.call-update) | async-done | bytes 2097168 | tf_op jit(solution)/shard_map/reduce_scatter | solution.py:186
  707.4 281.8 %reduce-scatter.11.cloned.1.call-done = f32[256,2048]{1,0:T(8,128)} async-done(((f32[2048,2048]{1,0:T(8,128)}), f32[256,2048]{1,0:T(8,128)}) %reduce-scatter.11.cloned.1.call-update) | async-done | bytes 2097168 | tf_op jit(solution)/shard_map/reduce_scatter | solution.py:238
  989.2 4.0 reshape.485
  993.2 60.4 %reduce-scatter.13.cloned.1.call-done = f32[256,16]{0,1:T(8,128)} async-done(((f32[2048,16]{0,1:T(8,128)}), f32[256,16]{0,1:T(8,128)}) %reduce-scatter.13.cloned.1.call-update) | async-done | bytes 16400 | tf_op jit(solution)/shard_map/reduce_scatter | solution.py:239
  1053.7 65.2 %reduce-scatter.15.cloned.1.call-done = f32[64,256]{1,0:T(8,128)} async-done(((f32[512,256]{1,0:T(8,128)}), f32[64,256]{1,0:T(8,128)}) %reduce-scatter.15.cloned.1.call-update) | async-done | bytes 65552 | tf_op jit(solution)/shard_map/reduce_scatter | solution.py:241
  1118.9 152.7 %reduce-scatter.17.cloned.1.call-done = f32[1024,256]{1,0:T(8,128)} async-done(((f32[1024,2048]{1,0:T(8,128)}), f32[1024,256]{1,0:T(8,128)}) %reduce-scatter.17.cloned.1.call-update) | async-done | bytes 1048592 | tf_op jit(solution)/shard_map/reduce_scatter | solution.py:240
  (532 shorter events, 259.7 us)
Async XLA Ops:
  7.2 91.3 %copy-start = (bf16[2048,256]{1,0:T(8,128)(2,1)S(1)}, bf16[2048,256]{1,0:T(8,128)(2,1)}, u32[]{:S(2)}) copy-start(bf16[2048,256]{1,0:T(8,128)(2,1)} %param.24) | copy-start | bytes 3145732
  7.2 40.2 %all-gather.3.cloned.1.call-start = ((), (), s32[]{:S(2)}) async-start(), calls=%async_computation.6 | async-start | bytes 5242880 | tf_op jit(solution)/shard_map/all_gather | solution.py:141
  9.6 220.3 %all-gather.5.cloned.1.call-start = ((), (), s32[]{:S(2)}) async-start(), calls=%async_computation.8 | async-start | bytes 5242880 | tf_op jit(solution)/shard_map/all_gather | solution.py:142
  10.4 626.7 %reduce-scatter.9.cloned.1.call-start = ((), (), s32[]{:S(2)}) async-start(), calls=%async_computation.9 | async-start | bytes 10485760 | tf_op jit(solution)/shard_map/reduce_scatter | solution.py:217
  11.4 11.7 copy-start.76
  22.3 29.0 %copy-start.59 = (f32[2048]{0:T(1024)S(1)}, f32[2048]{0:T(1024)}, u32[]{:S(2)}) copy-start(f32[2048]{0:T(1024)} %param.21) | copy-start | bytes 24580
  22.3 44.9 %copy-start.45 = (f32[1,1024]{1,0:T(1,128)}, f32[1,1024]{1,0:T(1,128)S(1)}, u32[]{:S(2)}) copy-start(f32[1,1024]{1,0:T(1,128)S(1)} %get-tuple-element.768) | copy-start | bytes 12292
  22.3 44.9 %copy-start.47 = (f32[1,1024]{1,0:T(1,128)}, f32[1,1024]{1,0:T(1,128)S(1)}, u32[]{:S(2)}) copy-start(f32[1,1024]{1,0:T(1,128)S(1)} %get-tuple-element.769) | copy-start | bytes 12292
  22.4 44.9 %copy-start.49 = (f32[1,1024]{1,0:T(1,128)}, f32[1,1024]{1,0:T(1,128)S(1)}, u32[]{:S(2)}) copy-start(f32[1,1024]{1,0:T(1,128)S(1)} %get-tuple-element.767) | copy-start | bytes 12292
  22.4 44.9 %copy-start.51 = (f32[1,1024]{1,0:T(1,128)}, f32[1,1024]{1,0:T(1,128)S(1)}, u32[]{:S(2)}) copy-start(f32[1,1024]{1,0:T(1,128)S(1)} %get-tuple-element.770) | copy-start | bytes 12292
  22.4 66.5 %copy-start.73 = (f32[16]{0:T(128)}, f32[16]{0:T(128)S(1)}, u32[]{:S(2)}) copy-start(f32[16]{0:T(128)S(1)} %exponential_negate_fusion) | copy-start | bytes 196
  22.4 78.0 %copy-start.61 = (f32[1,256]{1,0:T(1,128)}, f32[1,256]{1,0:T(1,128)S(1)}, u32[]{:S(2)}) copy-start(f32[1,256]{1,0:T(1,128)S(1)} %get-tuple-element.773) | copy-start | bytes 3076
  22.4 78.0 %copy-start.63 = (f32[1,256]{1,0:T(1,128)}, f32[1,256]{1,0:T(1,128)S(1)}, u32[]{:S(2)}) copy-start(f32[1,256]{1,0:T(1,128)S(1)} %get-tuple-element.774) | copy-start | bytes 3076
  22.4 78.0 %copy-start.65 = (f32[1,256]{1,0:T(1,128)}, f32[1,256]{1,0:T(1,128)S(1)}, u32[]{:S(2)}) copy-start(f32[1,256]{1,0:T(1,128)S(1)} %get-tuple-element.772) | copy-start | bytes 3076
  22.4 78.0 %copy-start.67 = (f32[1,256]{1,0:T(1,128)}, f32[1,256]{1,0:T(1,128)S(1)}, u32[]{:S(2)}) copy-start(f32[1,256]{1,0:T(1,128)S(1)} %get-tuple-element.775) | copy-start | bytes 3076
  23.2 224.2 %copy-start.43 = (f32[1024]{0:T(1024)}, f32[1024]{0:T(1024)S(1)}, u32[]{:S(2)}) copy-start(f32[1024]{0:T(1024)S(1)} %mul.903) | copy-start | bytes 12292
  23.9 223.5 %copy-start.55 = (f32[1024]{0:T(1024)}, f32[1024]{0:T(1024)S(1)}, u32[]{:S(2)}) copy-start(f32[1024]{0:T(1024)S(1)} %fusion.132) | copy-start | bytes 12292
  24.0 76.5 %copy-start.35 = (f32[1024]{0:T(1024)}, f32[1024]{0:T(1024)S(1)}, u32[]{:S(2)}) copy-start(f32[1024]{0:T(1024)S(1)} %get-tuple-element.778) | copy-start | bytes 12292
  24.0 76.5 %copy-start.37 = (f32[1024]{0:T(1024)}, f32[1024]{0:T(1024)S(1)}, u32[]{:S(2)}) copy-start(f32[1024]{0:T(1024)S(1)} %get-tuple-element.780) | copy-start | bytes 12292
  24.0 76.5 %copy-start.39 = (f32[1024]{0:T(1024)}, f32[1024]{0:T(1024)S(1)}, u32[]{:S(2)}) copy-start(f32[1024]{0:T(1024)S(1)} %get-tuple-element.779) | copy-start | bytes 12292
  52.6 12.8 %copy-start.5 = (bf16[1024,2048]{0,1:T(8,128)(2,1)}, bf16[1024,2048]{0,1:T(8,128)(2,1)S(1)}, u32[]{:S(2)}) copy-start(bf16[1024,2048]{0,1:T(8,128)(2,1)S(1)} %fusion.95) | copy-start | bytes 12582916
  216.8 13.1 %copy-start.70 = (f32[1024]{0:T(1024)S(1)}, f32[1024]{0:T(1024)}, u32[]{:S(2)}) copy-start(f32[1024]{0:T(1024)} %param.30) | copy-start | bytes 12292
  229.9 17.6 %copy-start.57 = (f32[1024]{0:T(1024)}, f32[1024]{0:T(1024)S(1)}, u32[]{:S(2)}) copy-start(f32[1024]{0:T(1024)S(1)} %add_rsqrt_fusion) | copy-start | bytes 12292
  289.2 16.3 %copy-start.33 = (pred[256]{0:T(512)(128)(4,1)}, pred[256]{0:T(512)(128)(4,1)S(1)}, u32[]{:S(2)}) copy-start(pred[256]{0:T(512)(128)(4,1)S(1)} %get-tuple-element.989) | copy-start | bytes 772 | tf_op jit(solution)/shard_map/transpose(jvp())/while
  291.5 13.9 %copy-start.26 = (f32[16,2]{0,1:T(2,128)}, f32[16,2]{0,1:T(2,128)S(1)}, u32[]{:S(2)}) copy-start(f32[16,2]{0,1:T(2,128)S(1)} %slice.251) | copy-start | bytes 388 | tf_op jit(solution)/shard_map/transpose(jvp())/while
  292.4 13.0 %copy-start.31 = (f32[16]{0:T(128)}, f32[16]{0:T(128)S(1)}, u32[]{:S(2)}) copy-start(f32[16]{0:T(128)S(1)} %get-tuple-element.988) | copy-start | bytes 196 | tf_op jit(solution)/shard_map/transpose(jvp())/while
  298.1 11.1 copy-start.1
  335.0 16.2 %copy-start.33 = (pred[256]{0:T(512)(128)(4,1)}, pred[256]{0:T(512)(128)(4,1)S(1)}, u32[]{:S(2)}) copy-start(pred[256]{0:T(512)(128)(4,1)S(1)} %get-tuple-element.989) | copy-start | bytes 772 | tf_op jit(solution)/shard_map/transpose(jvp())/while
  337.4 13.9 %copy-start.26 = (f32[16,2]{0,1:T(2,128)}, f32[16,2]{0,1:T(2,128)S(1)}, u32[]{:S(2)}) copy-start(f32[16,2]{0,1:T(2,128)S(1)} %slice.251) | copy-start | bytes 388 | tf_op jit(solution)/shard_map/transpose(jvp())/while
  338.2 13.0 %copy-start.31 = (f32[16]{0:T(128)}, f32[16]{0:T(128)S(1)}, u32[]{:S(2)}) copy-start(f32[16]{0:T(128)S(1)} %get-tuple-element.988) | copy-start | bytes 196 | tf_op jit(solution)/shard_map/transpose(jvp())/while
  343.9 11.1 copy-start.1
  380.8 16.3 %copy-start.33 = (pred[256]{0:T(512)(128)(4,1)}, pred[256]{0:T(512)(128)(4,1)S(1)}, u32[]{:S(2)}) copy-start(pred[256]{0:T(512)(128)(4,1)S(1)} %get-tuple-element.989) | copy-start | bytes 772 | tf_op jit(solution)/shard_map/transpose(jvp())/while
  383.2 13.9 %copy-start.26 = (f32[16,2]{0,1:T(2,128)}, f32[16,2]{0,1:T(2,128)S(1)}, u32[]{:S(2)}) copy-start(f32[16,2]{0,1:T(2,128)S(1)} %slice.251) | copy-start | bytes 388 | tf_op jit(solution)/shard_map/transpose(jvp())/while
  384.1 13.0 %copy-start.31 = (f32[16]{0:T(128)}, f32[16]{0:T(128)S(1)}, u32[]{:S(2)}) copy-start(f32[16]{0:T(128)S(1)} %get-tuple-element.988) | copy-start | bytes 196 | tf_op jit(solution)/shard_map/transpose(jvp())/while
  389.7 11.1 copy-start.1
  426.6 16.3 %copy-start.33 = (pred[256]{0:T(512)(128)(4,1)}, pred[256]{0:T(512)(128)(4,1)S(1)}, u32[]{:S(2)}) copy-start(pred[256]{0:T(512)(128)(4,1)S(1)} %get-tuple-element.989) | copy-start | bytes 772 | tf_op jit(solution)/shard_map/transpose(jvp())/while
  429.0 13.9 %copy-start.26 = (f32[16,2]{0,1:T(2,128)}, f32[16,2]{0,1:T(2,128)S(1)}, u32[]{:S(2)}) copy-start(f32[16,2]{0,1:T(2,128)S(1)} %slice.251) | copy-start | bytes 388 | tf_op jit(solution)/shard_map/transpose(jvp())/while
  429.9 13.0 %copy-start.31 = (f32[16]{0:T(128)}, f32[16]{0:T(128)S(1)}, u32[]{:S(2)}) copy-start(f32[16]{0:T(128)S(1)} %get-tuple-element.988) | copy-start | bytes 196 | tf_op jit(solution)/shard_map/transpose(jvp())/while
  515.3 15.9 %copy-start.29 = (f32[1024,16]{0,1:T(8,128)S(1)}, f32[1024,16]{0,1:T(8,128)}, u32[]{:S(2)}) copy-start(f32[1024,16]{0,1:T(8,128)} %get-tuple-element.781) | copy-start | bytes 196612
  515.3 15.9 %copy-start.74 = (f32[16]{0:T(128)S(1)}, f32[16]{0:T(128)}, u32[]{:S(2)}) copy-start(f32[16]{0:T(128)} %copy-done.73) | copy-start | bytes 196
  515.3 16.1 %copy-start.28 = (bf16[2048,16]{0,1:T(8,128)(2,1)S(1)}, bf16[2048,16]{0,1:T(8,128)(2,1)}, u32[]{:S(2)}) copy-start(bf16[2048,16]{0,1:T(8,128)(2,1)} %param.23) | copy-start | bytes 196612
  539.2 164.3 %reduce-scatter.7.cloned.1.call-start = ((), (), s32[]{:S(2)}) async-start(), calls=%async_computation.7 | async-start | bytes 10485760 | tf_op jit(solution)/shard_map/reduce_scatter | solution.py:186
  553.0 436.3 %reduce-scatter.11.cloned.1.call-start = ((), (), s32[]{:S(2)}) async-start(), calls=%async_computation.10 | async-start | bytes 18874368 | tf_op jit(solution)/shard_map/reduce_scatter | solution.py:238
  570.3 483.3 %reduce-scatter.13.cloned.1.call-start = ((), (), s32[]{:S(2)}) async-start(), calls=%async_computation.11 | async-start | bytes 147456 | tf_op jit(solution)/shard_map/reduce_scatter | solution.py:239
  621.8 497.1 %reduce-scatter.15.cloned.1.call-start = ((), (), s32[]{:S(2)}) async-start(), calls=%async_computation.12 | async-start | bytes 589824 | tf_op jit(solution)/shard_map/reduce_scatter | solution.py:241
  624.3 647.2 %reduce-scatter.17.cloned.1.call-start = ((), (), s32[]{:S(2)}) async-start(), calls=%async_computation.13 | async-start | bytes 9437184 | tf_op jit(solution)/shard_map/reduce_scatter | solution.py:240
  635.9 16.0 %copy-start.69 = (f32[1024]{0:T(1024)S(1)}, f32[1024]{0:T(1024)}, u32[]{:S(2)}) copy-start(f32[1024]{0:T(1024)} %get-tuple-element.644) | copy-start | bytes 12292
  635.9 67.6 %copy-start.53 = (f32[1024]{0:T(1024)S(1)}, f32[1024]{0:T(1024)}, u32[]{:S(2)}) copy-start(f32[1024]{0:T(1024)} %get-tuple-element.776) | copy-start | bytes 12292
  (69 other events, 364.4 us)
Sparse Core Ops, SparseCore 0:
  10.2 37.1 all-gather.2
  48.9 34.4 all-gather.4
  539.4 89.7 reduce-scatter.8
  631.8 71.6 reduce-scatter.6
  707.2 282.0 reduce-scatter.10
  993.3 60.2 reduce-scatter.12
  1057.9 60.8 reduce-scatter.14
  1123.1 148.4 reduce-scatter.16
where the time goes:
time: 1290 us; the launch traced here: 1280 us
  waiting for transfers between devices  598 us (46%)
  matrix products  252 us (20%)
  local copies, waits for them, and re-layouts  178 us (14%)
  other arithmetic  110 us (9%)
  blocking collectives  103 us (8%)
  loops' own time  23.1 us (2%)
  between operations  15.4 us (1%)
    reduce_scatter x1, waiting for transfers between devices, shards(): lax.psum_scatter(grad_w_inner, 'dp', scatter_dimension=0, tiled=True)  282 us
    reduce_scatter x1, waiting for transfers between devices, shards(): lax.psum_scatter(grad_w_out, 'dp', scatter_dimension=1, tiled=True)  153 us
    dot_general x12, matrix products, scan_block(): jnp.einsum('ijh,jhp->ihp', weights * intersection[:, :, None], inputs, pr...  76.6 us
    reduce_scatter x1, waiting for transfers between devices, shards(): lax.psum_scatter(grad_w_state, 'dp', scatter_dimension=0, tiled=True)  65.2 us
    reduce_scatter x1, waiting for transfers between devices, shards(): lax.psum_scatter(grad_w_step, 'dp', scatter_dimension=0, tiled=True)  60.4 us
    psum x1, blocking collectives, shards(): lax.psum((grad_state, grad_conv_state), 'tensor')  41.9 us
    unnamed x151, local copies, waits for them, and re-layouts  39.7 us
    dot_general x4, matrix products, contract_cols(): lax.dot_general(left, right, (((1,), (1,)), ((), ())), preferred_element_...  39.3 us
  transfers between devices with their start and end apart: 8, of which 6 were waited for; matrix products, arithmetic and copies ran while one was open for 18% of the time, Pallas kernels for 0%

commit v1 on v0

v1 whole, which is shorter than its diff:
```python
import functools
import math

import jax
import jax.numpy as jnp
from jax import lax
from jax.experimental import pallas as pl
from jax.experimental.pallas import tpu as pltpu
from jax.sharding import PartitionSpec as P

F32 = jnp.float32
BF16 = jnp.bfloat16
HIGHEST = lax.Precision.HIGHEST
EPSILON = 1e-05
LOG2E = math.log2(math.e)
LANES = 128
SPAN = 128
GROUP = 256
VMEM_LIMIT = 56 * 1024 * 1024

NN = (((1,), (0,)), ((), ()))
NT = (((1,), (1,)), ((), ()))
TN = (((0,), (0,)), ((), ()))


def dot(left, right, dims=NN, precision=None):
    return lax.dot_general(left, right, dims, precision=precision, preferred_element_type=F32)


def sigmoid(a):
    return 0.5 * jnp.tanh(0.5 * a) + 0.5


def iota(shape, dim):
    return lax.broadcasted_iota(jnp.int32, shape, dim)


def tri(upper):
    rows, cols = iota((SPAN, SPAN), 0), iota((SPAN, SPAN), 1)
    return ((rows <= cols) if upper else (rows >= cols)).astype(F32)


def call(body, grid, in_specs, out_specs, out_shape, scratch=(), prefetch=0, flops=0, moved=0, name=None):
    return pl.pallas_call(
        body,
        grid_spec=pltpu.PrefetchScalarGridSpec(
            num_scalar_prefetch=prefetch,
            grid=grid,
            in_specs=in_specs,
            out_specs=out_specs,
            scratch_shapes=list(scratch),
        ),
        out_shape=out_shape,
        compiler_params=pltpu.CompilerParams(
            vmem_limit_bytes=VMEM_LIMIT, dimension_semantics=("arbitrary",) * len(grid)
        ),
        cost_estimate=pl.CostEstimate(flops=int(flops), bytes_accessed=int(moved), transcendentals=0),
        name=name,
    )


def held(shape):
    zeros = (0,) * len(shape)
    return pl.BlockSpec(shape, lambda *_: zeros, pipeline_mode=pl.Buffered(1))


def shape_of(*dims, dtype=F32):
    return jax.ShapeDtypeStruct(dims, dtype)


def conv_taps(wide, marks, filters):
    rows = wide.shape[0] - 8
    now = wide[8:]
    total = filters[4:5] + filters[0:1] * now
    shifted = [now]
    for k in range(1, 4):
        moved = wide[8 - k : 8 - k + rows] * marks[:, k - 1 : k]
        shifted.append(moved)
        total = total + filters[k : k + 1] * moved
    return total, shifted


def conv_back(later, marks, filters):
    rows = later.shape[0] - 8
    total = filters[0:1] * later[:rows]
    for k in range(1, 4):
        total = total + filters[k : k + 1] * (later[k : k + rows] * marks[k : k + rows, k - 1 : k])
    return total


def prep_kernel(
    parts, heads, groups_all, rank,
    *refs,
):
    pieces, refs = refs[:parts], refs[parts:]
    (gain, w_state, w_step, conv, bias, rate, marks, seg_row,
     normed, pre_state, maps, maps_t, per_head, rows_out, cross, cross_t, halo) = refs
    step = pl.program_id(0)
    width = w_state.shape[0]
    quarter = width // parts
    wide = [piece[...].astype(F32) for piece in pieces]
    squares = wide[0] * wide[0]
    for other in wide[1:]:
        squares = squares + other * other
    scale = lax.rsqrt(jnp.sum(squares, axis=1, keepdims=True) / width + EPSILON)
    proj = jnp.zeros((SPAN, w_state.shape[1]), F32)
    pre = jnp.zeros((SPAN, LANES), F32)
    for k in range(parts):
        at = pl.multiple_of((rank[0] ^ k) * quarter, quarter)
        low = (wide[k] * scale * gain[:, pl.ds(at, quarter)]).astype(BF16)
        normed[:, pl.ds(at, quarter)] = low
        proj = proj + dot(low, w_state[pl.ds(at, quarter), :])
        pre = pre + dot(low, w_step[pl.ds(at, quarter), :])
    pre = pre + bias[...]
    pre_state[...] = proj

    @pl.when(step == 0)
    def _():
        halo[...] = jnp.zeros_like(halo)

    mark = marks[...]
    total, _ = conv_taps(jnp.concatenate([halo[...], proj], axis=0), mark, conv[...])
    halo[...] = proj[SPAN - 8 :]
    both = total * sigmoid(total)
    maps[...] = both.astype(BF16)
    states = both.shape[1] // 2
    keys, queries = both[:, :states], both[:, states:]
    maps_t[:states] = keys.T.astype(BF16)
    maps_t[states:] = queries.T.astype(BF16)

    size = jnp.maximum(pre, 0.0) + jnp.log1p(jnp.exp(-jnp.abs(pre)))
    rising = dot(tri(False), -rate[...] * size, precision=HIGHEST)
    entering = jnp.exp(rising) * mark[:, 3:4]
    leaving = jnp.exp(rising[SPAN - 1 :] - rising) * mark[:, 4:5]
    rising = rising * LOG2E
    section = iota((SPAN, LANES), 1) // heads
    packed = jnp.where(section == 0, rising, entering)
    packed = jnp.where(section == 2, leaving, packed)
    packed = jnp.where(section == 3, size, packed)
    packed = jnp.where(section == 4, pre, packed)
    packed = jnp.where(section == 5, scale, packed)
    per_head[...] = packed
    turned = rising.T
    for g in range(groups_all):
        rows_out[g] = turned[g * heads // groups_all : g * heads // groups_all + 8]

    low_keys, low_queries = keys.astype(BF16), queries.astype(BF16)
    same = mark[:, 6:7] == seg_row[0:1, :]
    rows, cols = iota((SPAN, SPAN), 0), iota((SPAN, SPAN), 1)
    cross[...] = jnp.where(same & (rows >= cols), dot(low_queries, low_keys, NT), 0.0)
    cross_t[...] = jnp.where(same & (rows <= cols), dot(low_keys, low_queries, NT), 0.0)


def spread(table, section, heads, count):
    lane = iota((table.shape[0], LANES), 1)
    tiles = []
    for pair in range(count // 2):
        at = section * heads + 2 * pair
        tiles.append(jnp.where(lane < LANES // 2, table[:, at : at + 1], table[:, at + 1 : at + 2]))
    return jnp.concatenate(tiles, axis=1)


def forward_kernel(
    heads, normed, w_gate, w_value, conv, skip, per_head, marks, rows_in, maps, maps_t, cross,
    value, gate, mixed, memory, squares, state,
):
    g = pl.program_id(0)
    length = normed.shape[0]
    states = maps.shape[1] // 2
    count = GROUP // 64
    lane = iota((SPAN, LANES), 1)
    value[0:8] = jnp.zeros((8, GROUP), F32)

    def project(i, _):
        at = pl.multiple_of(i * 256, 256)
        rows = normed[pl.ds(at, 256), :]
        value[pl.ds(at + 8, 256), :] = dot(rows, w_value[...])
        gate[pl.ds(at, 256), :] = dot(rows, w_gate[...])
        return 0

    lax.fori_loop(0, length // 256, project, 0)
    state[...] = jnp.zeros_like(state)
    turn = lax.rem(LANES - count * g, LANES)

    def block(b, _):
        at = pl.multiple_of(b * SPAN, SPAN)
        total, _ = conv_taps(value[pl.ds(at, SPAN + 8), :], marks[pl.ds(at, SPAN), :], conv[...])
        inputs = total * sigmoid(total)
        table = pltpu.roll(per_head[pl.ds(at, SPAN), :], turn, 1)
        entering, leaving, size = (spread(table, s, heads, count) for s in (1, 2, 3))
        scaled = inputs * size
        keys_t = maps_t[0:states, pl.ds(at, SPAN)]
        queries = maps[pl.ds(at, SPAN), states:]
        low_state = state[...].astype(BF16)
        memory[b] = low_state
        out = entering * dot(queries, low_state) + skip[...] * inputs
        rising_rows = rows_in[0, pl.ds(pl.multiple_of(b * 8, 8), 8), :]
        crossed = cross[pl.ds(at, SPAN), :]
        parts = []
        for pair in range(count // 2):
            weights = []
            for j in (2 * pair, 2 * pair + 1):
                gap = jnp.minimum(table[:, j : j + 1] - rising_rows[j : j + 1, :], 0.0)
                weights.append((jnp.exp2(gap) * crossed).astype(BF16))
            tile = scaled[:, pair * LANES : (pair + 1) * LANES]
            stacked = jnp.concatenate(
                [
                    jnp.where(lane < LANES // 2, tile, 0.0).astype(BF16),
                    jnp.where(lane < LANES // 2, 0.0, tile).astype(BF16),
                ],
                axis=0,
            )
            parts.append(dot(jnp.concatenate(weights, axis=1), stacked))
        out = out + jnp.concatenate(parts, axis=1)
        fresh = dot(keys_t, (leaving * scaled).astype(BF16))
        state[...] = state[...] * entering[SPAN - 1 :] + fresh
        mixed[pl.ds(at, SPAN), :] = out
        opened = gate[pl.ds(at, SPAN), :]
        gated = out * (opened * sigmoid(opened))
        power = gated * gated
        folded = power[:, :LANES]
        for tile in range(1, GROUP // LANES):
            folded = folded + power[:, tile * LANES : (tile + 1) * LANES]

        @pl.when(g == 0)
        def _():
            squares[pl.ds(at, SPAN), :] = folded

        @pl.when(g > 0)
        def _():
            squares[pl.ds(at, SPAN), :] += folded

        return 0

    lax.fori_loop(0, length // SPAN, block, 0)


def cotangent_kernel(cotangent, w_out, gate, mixed, gain, grad, sums):
    g = pl.program_id(0)

    def chunk(i, _):
        at = pl.multiple_of(i * 256, 256)
        now = dot(cotangent[pl.ds(at, 256), :], w_out[...], NT)
        grad[pl.ds(at, 256), :] = now
        opened = gate[pl.ds(at, 256), :]
        power = now * mixed[pl.ds(at, 256), :] * (opened * sigmoid(opened)) * gain[...]
        folded = power[:, :LANES]
        for tile in range(1, GROUP // LANES):
            folded = folded + power[:, tile * LANES : (tile + 1) * LANES]

        @pl.when(g == 0)
        def _():
            sums[pl.ds(at, 256), :] = folded

        @pl.when(g > 0)
        def _():
            sums[pl.ds(at, 256), :] += folded

        return 0

    lax.fori_loop(0, cotangent.shape[0] // 256, chunk, 0)


def gate_kernel(
    run, place, cotangent, grad, gate, mixed, gain, factors,
    low_mixed, grad_mixer, grad_gate, grad_gain, w_send, w_own,
):
    length = cotangent.shape[0]
    grad_gain[...] = jnp.zeros_like(grad_gain)

    def chunk(i, _):
        at = pl.ds(pl.multiple_of(i * SPAN, SPAN), SPAN)
        factor, pull = factors[at, 0:1], factors[at, 1:2]
        opened, out, now = gate[at, :], mixed[at, :], grad[at, :]
        chance = sigmoid(opened)
        swish = opened * chance
        gated = out * swish
        scaled = gated * factor
        low_mixed[at, :] = (scaled * gain[...]).astype(BF16)
        grad_gain[...] += jnp.sum(now * scaled, axis=0, keepdims=True)
        grad_gated = now * (factor * gain[...]) - gated * pull
        grad_mixer[at, :] = (grad_gated * swish).astype(BF16)
        grad_gate[at, :] = (grad_gated * out * chance * (1.0 + opened * (1.0 - chance))).astype(BF16)
        return 0

    lax.fori_loop(0, length // SPAN, chunk, 0)
    for half, target in ((1, w_send), (0, w_own)):
        for z in range(cotangent.shape[1] // (2 * run)):
            at = pl.multiple_of((2 * z + (place[0] ^ half)) * run, run)
            target[:, z * run : (z + 1) * run] = dot(
                low_mixed[...], cotangent[:, pl.ds(at, run)], TN
            ).astype(BF16)


def weight_kernel(place, left_send, left_own, right, send, own):
    send[...] = dot(left_send[...], right[...], TN).astype(BF16)
    own[...] = dot(left_own[...], right[...], TN).astype(BF16)


def backward_kernel(
    heads, groups_all, value, grad_out, mixed, memory, conv, skip, per_head, marks, rows_in, maps, maps_t,
    cross, cross_t, seg_row, pre_state, conv_state, rate,
    grad_value, grad_conv, grad_skip, grad_state, grad_step, grad_conv_state, grad_heads,
    later, grad_memory, grad_cross, folded, grad_maps, later_state,
):
    g = pl.program_id(0)
    length = grad_out.shape[0]
    blocks = length // SPAN
    states = maps.shape[1] // 2
    count = GROUP // 64
    lane = iota((SPAN, LANES), 1)
    row = iota((SPAN, GROUP), 0)
    turn = lax.rem(LANES - count * g, LANES)
    channel, target = iota((GROUP, LANES), 0), iota((GROUP, LANES), 1)
    pick_rise = (target == count * g + channel // 64).astype(BF16)
    pick_size = (target == heads + count * g + channel // 64).astype(BF16)
    later[...] = jnp.zeros_like(later)
    grad_memory[...] = jnp.zeros_like(grad_memory)
    grad_conv[...] = jnp.zeros_like(grad_conv)
    grad_skip[...] = jnp.zeros_like(grad_skip)

    @pl.when(g == 0)
    def _():
        grad_cross[...] = jnp.zeros_like(grad_cross)
        folded[...] = jnp.zeros_like(folded)
        grad_maps[...] = jnp.zeros_like(grad_maps)

    def block(i, _):
        b = blocks - 1 - i
        start = pl.multiple_of(b * SPAN, SPAN)
        at = pl.ds(start, SPAN)
        filters = conv[...]
        total, shifted = conv_taps(value[pl.ds(start, SPAN + 8), :], marks[at, :], filters)
        chance = sigmoid(total)
        inputs = total * chance
        table = pltpu.roll(per_head[at, :], turn, 1)
        entering, leaving, size = (spread(table, s, heads, count) for s in (1, 2, 3))
        scaled = inputs * size
        low_scaled = scaled.astype(BF16)
        pulled = grad_out[at, :].astype(F32)
        keys, queries_t = maps[at, 0:states], maps_t[states:, pl.ds(start, SPAN)]
        memory_now = memory[b]
        grad_next = grad_memory[...]
        low_next = grad_next.astype(BF16)
        entered = (entering * pulled).astype(BF16)
        left = (leaving * scaled).astype(BF16)
        grad_maps[at, 0:states] += dot(left, low_next, NT)
        grad_maps[at, states:] += dot(entered, memory_now, NT)
        rising_rows = rows_in[0, pl.ds(pl.multiple_of(b * 8, 8), 8), :]
        crossed_t = cross_t[at, :]
        cross_sum = jnp.zeros((SPAN, SPAN), F32)
        parts = []
        for pair in range(count // 2):
            tile = pulled[:, pair * LANES : (pair + 1) * LANES]
            one = jnp.where(lane < LANES // 2, tile, 0.0).astype(BF16)
            two = jnp.where(lane < LANES // 2, 0.0, tile).astype(BF16)
            low_tile = low_scaled[:, pair * LANES : (pair + 1) * LANES]
            weights = []
            for j, masked in ((2 * pair, one), (2 * pair + 1, two)):
                gap = table[:, j : j + 1] - rising_rows[j : j + 1, :]
                cross_sum = cross_sum + jnp.exp2(jnp.minimum(gap, 0.0)) * dot(masked, low_tile, NT)
                weights.append((jnp.exp2(jnp.minimum(-gap, 0.0)) * crossed_t).astype(BF16))
            parts.append(dot(jnp.concatenate(weights, axis=1), jnp.concatenate([one, two], axis=0)))
        grad_cross[at, :] += cross_sum
        grad_within = jnp.concatenate(parts, axis=1)
        grad_left = dot(keys, low_next)
        grad_scaled = grad_within + leaving * grad_left
        scanned = mixed[at, :] - skip[...] * inputs
        kept = left.astype(F32) * grad_left
        rise = pulled * scanned - low_scaled.astype(F32) * grad_within - kept
        carried = entering[SPAN - 1 :] * jnp.sum(low_next.astype(F32) * memory_now.astype(F32), axis=0, keepdims=True)
        rise = rise + jnp.where(row == SPAN - 1, carried + jnp.sum(kept, axis=0, keepdims=True), 0.0)
        grown = grad_scaled * inputs
        summed = folded[at, :]
        for product, pick in ((rise, pick_rise), (grown, pick_size)):
            high = product.astype(BF16)
            rest = (product - high.astype(F32)).astype(BF16)
            summed = summed + dot(high, pick) + dot(rest, pick)
        folded[at, :] = summed
        grad_skip[...] += jnp.sum(pulled * inputs, axis=0, keepdims=True)
        grad_inputs = size * grad_scaled + skip[...] * pulled
        grad_total = grad_inputs * (chance * (1.0 + total * (1.0 - chance)))
        for k in range(4):
            grad_conv[k : k + 1] += jnp.sum(grad_total * shifted[k], axis=0, keepdims=True)
        grad_conv[4:5] += jnp.sum(grad_total, axis=0, keepdims=True)
        wide = pl.ds(start, SPAN + 8)
        longer = jnp.concatenate([grad_total, later[...]], axis=0)
        later[...] = grad_total[:8]
        grad_value[at, :] = conv_back(longer, marks[wide, :], filters).astype(BF16)
        grad_memory[...] = entering[SPAN - 1 :] * grad_next + dot(queries_t, entered)
        return 0

    lax.fori_loop(0, blocks, block, 0)

    @pl.when(g == groups_all - 1)
    def _():
        later_state[...] = jnp.zeros_like(later_state)
        grad_conv_state[...] = jnp.zeros_like(grad_conv_state)
        grad_heads[...] = jnp.zeros_like(grad_heads)

        def finish(i, _):
            start = pl.multiple_of((blocks - 1 - i) * SPAN, SPAN)
            at = pl.ds(start, SPAN)
            mark = marks[at, :]
            rows, cols = iota((SPAN, SPAN), 0), iota((SPAN, SPAN), 1)
            linked = (rows >= cols) & (mark[:, 6:7] == seg_row[0:1, pl.ds(start, SPAN)])
            crossed = jnp.where(linked, grad_cross[at, :], 0.0)
            keys, queries = maps[at, 0:states], maps[at, states:]
            grad_keys = grad_maps[at, 0:states] + dot(crossed.T.astype(BF16), queries)
            grad_queries = grad_maps[at, states:] + dot(crossed.astype(BF16), keys)
            filters = conv_state[...]
            total, shifted = conv_taps(pre_state[pl.ds(start, SPAN + 8), :], mark, filters)
            chance = sigmoid(total)
            grad_total = jnp.concatenate([grad_keys, grad_queries], axis=1) * (
                chance * (1.0 + total * (1.0 - chance))
            )
            for k in range(4):
                grad_conv_state[k : k + 1] += jnp.sum(grad_total * shifted[k], axis=0, keepdims=True)
            grad_conv_state[4:5] += jnp.sum(grad_total, axis=0, keepdims=True)
            wide = pl.ds(start, SPAN + 8)
            longer = jnp.concatenate([grad_total, later_state[...]], axis=0)
            later_state[...] = grad_total[:8]
            grad_state[at, :] = conv_back(longer, marks[wide, :], filters).astype(BF16)

            summed = folded[at, :]
            table = per_head[at, :]
            grad_decay = dot(tri(True), summed, precision=HIGHEST)
            size = pltpu.roll(table, LANES - 3 * heads, 1)
            pre = pltpu.roll(table, LANES - 4 * heads, 1)
            grad_size = pltpu.roll(summed, LANES - heads, 1) - rate[...] * grad_decay
            valid = iota((SPAN, LANES), 1) < heads
            grad_pre = jnp.where(valid, grad_size * sigmoid(pre), 0.0)
            grad_step[at, :] = grad_pre.astype(BF16)
            grad_heads[0:1] += jnp.sum(grad_pre, axis=0, keepdims=True)
            grad_heads[1:2] += jnp.sum(-rate[...] * size * grad_decay, axis=0, keepdims=True)
            return 0

        lax.fori_loop(0, blocks, finish, 0)


def output_kernel(ks, rank, mixed, w_out, out):
    out[0] = dot(mixed[...], w_out[...]).astype(BF16)


def normed_kernel(ks, rank, grad_gate, grad_value, grad_state, grad_step, w_gate, w_value, w_state, w_step, out):
    total = dot(grad_gate[...], w_gate[...], NT) + dot(grad_value[...], w_value[...], NT)
    total = total + dot(grad_state[...], w_state[...], NT) + dot(grad_step[...], w_step[...], NT)
    out[0] = total.astype(BF16)


def swap(array, axis, mask):
    count = lax.axis_size(axis)
    return lax.ppermute(array, axis, [(i, i ^ mask) for i in range(count)])


def gather_pieces(own, parts):
    pieces = {0: own}
    bit = parts // 2
    while bit >= 1:
        pieces.update({k | bit: swap(piece, "tensor", bit) for k, piece in list(pieces.items())})
        bit //= 2
    return [pieces[k] for k in range(parts)]


def after(first, then):
    return lax.optimization_barrier((first, then))[1]


def sum_all(array, axis):
    bit = 1
    while bit < lax.axis_size(axis):
        array = array + swap(array, axis, bit)
        bit *= 2
    return array


def scatter_rest(own, received, dim, low_bits):
    count = lax.axis_size("dp")
    index = lax.axis_index("dp")
    left = count // 2
    place = ((index >> (low_bits + 1)) << low_bits) | (index & ((1 << low_bits) - 1))

    def original(mask):
        return ((mask >> low_bits) << (low_bits + 1)) | (mask & ((1 << low_bits) - 1))

    def cut(array, at, pieces):
        size = array.shape[dim] // pieces
        return lax.dynamic_slice_in_dim(array, at * size, size, dim)

    terms = [own] if received is None else [own, received]

    def total(at, pieces):
        return functools.reduce(jnp.add, [cut(term, at, pieces).astype(F32) for term in terms])

    while left > 4:
        half = left // 2
        top = (place // half) % 2
        sent = swap(total(1 - top, 2).astype(BF16), "dp", original(half))
        terms = [total(top, 2).astype(BF16), sent]
        left = half
    mine = place % left
    arrived = [swap(total(mine ^ k, left).astype(BF16), "dp", original(k)) for k in range(1, left)]
    result = total(mine, left)
    for piece in arrived:
        result = result + piece.astype(F32)
    return result


def shards(
    tokens,
    cotangent,
    doc_lengths,
    norm_gain,
    w_inner,
    w_step,
    w_state,
    conv_inner,
    conv_state,
    step_bias,
    log_rate,
    skip_gain,
    gate_gain,
    w_out,
):
    parts = lax.axis_size("tensor")
    groups = lax.axis_size("dp")
    rank = lax.axis_index("tensor").astype(jnp.int32)
    ranks = rank.reshape(1)
    length, quarter = tokens.shape
    width = quarter * parts
    channels = w_inner.shape[2]
    heads = w_step.shape[1]
    states2 = w_state.shape[1]
    states = states2 // 2
    blocks = length // SPAN
    steps = channels // GROUP
    repeat = LANES // heads
    piece_rows = width // groups
    low_bits = 0
    while (piece_rows << low_bits) < LANES:
        low_bits += 1
    run = piece_rows << low_bits
    half_width = width // 2
    place = ((lax.axis_index("dp") >> low_bits) & 1).astype(jnp.int32).reshape(1)

    token_pieces = gather_pieces(tokens, parts)
    grad_pieces = gather_pieces(after(token_pieces[parts // 2], cotangent), parts)
    full_grad = jnp.zeros((length, width), BF16)
    for k in range(parts):
        full_grad = lax.dynamic_update_slice(full_grad, grad_pieces[k], (0, (rank ^ k) * quarter))

    flat = w_inner.reshape(width, 2 * channels)
    step8 = jnp.tile(w_step, (1, repeat))
    step_pad = jnp.pad(w_step, ((0, 0), (0, LANES - heads)))
    bias8 = jnp.tile(step_bias, repeat)[None, :]
    rate8 = jnp.exp(jnp.tile(log_rate, repeat))[None, :]
    skip_row = jnp.repeat(skip_gain, channels // heads)[None, :]
    gain_row = gate_gain[None, :]
    conv_pad = jnp.pad(conv_inner, ((0, 3), (0, 0)))
    conv_state_pad = jnp.pad(conv_state, ((0, 3), (0, 0)))

    doc_ends = jnp.cumsum(doc_lengths[0])
    positions = jnp.arange(length, dtype=jnp.int32)
    segment = jnp.sum((positions[:, None] >= doc_ends[None, :]).astype(jnp.int32), axis=1)
    present = positions < doc_ends[-1]
    by_block = segment.reshape(blocks, SPAN)
    final = by_block[:, -1:]
    before = jnp.concatenate([jnp.full((1, 1), -1, jnp.int32), final[:-1]], axis=0)
    marks = [
        jnp.concatenate([jnp.full((k,), -1, jnp.int32), segment[:-k]]) == segment for k in (1, 2, 3)
    ]
    marks += [(by_block == before).reshape(-1), (by_block == final).reshape(-1), present]
    marks = [mark.astype(F32) for mark in marks] + [segment.astype(F32)]
    marks = jnp.pad(jnp.stack(marks, axis=1), ((0, 8), (0, LANES - len(marks))))
    seg_row = jnp.broadcast_to(segment.astype(F32)[None, :], (8, length))

    by_span = lambda cols: pl.BlockSpec((SPAN, cols), lambda b, *_: (b, 0))
    (normed, pre_state, maps, maps_t, per_head, rising_rows, cross, cross_t) = call(
        functools.partial(prep_kernel, parts, heads, steps),
        (blocks,),
        [by_span(quarter)] * parts
        + [
            held((1, width)), held((width, states2)), held((width, LANES)), held((8, states2)),
            held((1, LANES)), held((1, LANES)), by_span(LANES), pl.BlockSpec((8, SPAN), lambda b, *_: (0, b)),
        ],
        [
            by_span(width), by_span(states2), by_span(states2),
            pl.BlockSpec((states2, SPAN), lambda b, *_: (0, b)), by_span(LANES),
            pl.BlockSpec((steps, 8, SPAN), lambda b, *_: (0, b, 0)), by_span(SPAN), by_span(SPAN),
        ],
        [
            shape_of(length, width, dtype=BF16), shape_of(length, states2), shape_of(length, states2, dtype=BF16),
            shape_of(states2, length, dtype=BF16), shape_of(length, LANES), shape_of(steps, blocks * 8, SPAN),
            shape_of(length, SPAN), shape_of(length, SPAN),
        ],
        [pltpu.VMEM((8, states2), F32)],
        prefetch=1,
        flops=2 * length * width * (states2 + LANES),
        moved=length * width * 4 + width * (states2 + LANES) * 2 + length * 4000,
        name="prep",
    )(
        ranks, *token_pieces, norm_gain[None, :], w_state, step8, conv_state_pad, bias8, rate8, marks[:length], seg_row
    )
    pre_state = jnp.pad(pre_state, ((8, 0), (0, 0)))

    by_group = lambda rows: pl.BlockSpec((rows, GROUP), lambda g, *_: (0, g))
    w_rows = pl.BlockSpec((width, GROUP), lambda g, *_: (0, g))
    w_rows_value = pl.BlockSpec((width, GROUP), lambda g, *_: (0, steps + g))
    rows_spec = pl.BlockSpec((1, blocks * 8, SPAN), lambda g, *_: (g, 0, 0))
    memory_spec = pl.BlockSpec((blocks, states, GROUP), lambda g, *_: (0, 0, g))
    value, gate, mixer_out, memory, squares = call(
        functools.partial(forward_kernel, heads),
        (steps,),
        [
            held((length, width)), w_rows, w_rows_value, by_group(8), by_group(1), held((length, LANES)),
            held((length + 8, LANES)), rows_spec, held((length, states2)), held((states2, length)),
            held((length, SPAN)),
        ],
        [by_group(length + 8), by_group(length), by_group(length), memory_spec, held((length, LANES))],
        [
            shape_of(length + 8, channels), shape_of(length, channels), shape_of(length, channels),
            shape_of(blocks, states, channels, dtype=BF16), shape_of(length, LANES),
        ],
        [pltpu.VMEM((states, GROUP), F32)],
        flops=8 * length * width * channels,
        moved=length * width * 2 + width * channels * 4 + length * channels * 12,
        name="forward",
    )(
        normed, flat, flat, conv_pad, skip_row, per_head, marks, rising_rows, maps, maps_t, cross
    )

    grad_mixed, weighted = call(
        cotangent_kernel,
        (steps,),
        [
            held((length, width)), pl.BlockSpec((GROUP, width), lambda g, *_: (g, 0)),
            by_group(length), by_group(length), by_group(1),
        ],
        [by_group(length), held((length, LANES))],
        [shape_of(length, channels), shape_of(length, LANES)],
        flops=2 * length * width * channels,
        moved=length * width * 2 + width * channels * 2 + length * channels * 12,
        name="cotangent",
    )(full_grad, w_out, gate, mixer_out, gain_row)

    keep = marks[:length, 5]
    sums = jnp.stack([jnp.sum(squares, axis=1), jnp.sum(weighted, axis=1)])
    sums = sum_all(sums, "tensor")
    total_channels = channels * parts
    scale_out = lax.rsqrt(sums[0] / total_channels + EPSILON)
    factor = scale_out * keep
    pull = scale_out**3 * (sums[1] * keep) / total_channels
    factors = jnp.pad(jnp.stack([factor, pull], axis=1), ((0, 0), (0, LANES - 2)))

    by_channel = pl.BlockSpec((GROUP, half_width), lambda g, *_: (g, 0))
    low_mixed, grad_mixer, grad_gate, grad_gate_gain, out_send, out_own = call(
        functools.partial(gate_kernel, run),
        (steps,),
        [
            held((length, width)), by_group(length), by_group(length), by_group(length), by_group(1),
            held((length, LANES)),
        ],
        [by_group(length), by_group(length), by_group(length), by_group(1), by_channel, by_channel],
        [
            shape_of(length, channels, dtype=BF16), shape_of(length, channels, dtype=BF16),
            shape_of(length, channels, dtype=BF16), shape_of(1, channels),
            shape_of(channels, half_width, dtype=BF16), shape_of(channels, half_width, dtype=BF16),
        ],
        prefetch=1,
        flops=2 * length * width * channels,
        moved=length * width * 2 + length * channels * 18 + width * channels * 2,
        name="gate",
    )(place, full_grad, grad_mixed, gate, mixer_out, gain_row, factors)
    out_received = swap(out_send, "dp", 1 << low_bits)

    def weight_grads(right):
        runs = half_width // run
        columns = right.shape[1]
        out = pl.BlockSpec((run, columns), lambda j, p: (j, 0))
        shape = shape_of(half_width, columns, dtype=BF16)
        return call(
            weight_kernel,
            (runs,),
            [
                pl.BlockSpec((length, run), lambda j, p: (0, 2 * j + (p[0] ^ 1))),
                pl.BlockSpec((length, run), lambda j, p: (0, 2 * j + p[0])),
                held((length, columns)),
            ],
            [out, out],
            [shape, shape],
            prefetch=1,
            flops=2 * length * width * columns,
            moved=length * width * 2 + length * columns * 2 + width * columns * 2,
            name="weights",
        )(place, normed, normed, right)

    gate_send, gate_own = weight_grads(grad_gate)
    gate_received = swap(after(out_received, gate_send), "dp", 1 << low_bits)

    def output_part(ks):
        return call(
            functools.partial(output_kernel, ks),
            (len(ks), quarter // 256),
            [
                held((length, channels)),
                pl.BlockSpec(
                    (channels, 256),
                    lambda i, j, r: (0, (r[0] ^ (ks[0] + i * (ks[-1] - ks[0]))) * (quarter // 256) + j),
                ),
            ],
            pl.BlockSpec((1, length, 256), lambda i, j, r: (i, 0, j)),
            shape_of(len(ks), length, quarter, dtype=BF16),
            prefetch=1,
            flops=2 * length * channels * quarter * len(ks),
            moved=length * channels * 2 + channels * quarter * 2 * len(ks) + length * quarter * 2 * len(ks),
            name="output",
        )(ranks, low_mixed, w_out)

    out_far = swap(output_part((1, 3)), "tensor", 1)
    out_near = output_part((2, 0))
    out_y = swap((out_near[0].astype(F32) + out_far[1].astype(F32)).astype(BF16), "tensor", 2)
    branch = out_near[1].astype(F32) + out_far[0].astype(F32) + out_y.astype(F32)
    own_tokens = tokens.astype(F32)
    output = (own_tokens + branch).astype(BF16)

    all_lanes = held((length, LANES))
    (grad_value, grad_conv, grad_skip, grad_state, grad_step, grad_conv_state, grad_heads) = call(
        functools.partial(backward_kernel, heads, steps),
        (steps,),
        [
            by_group(length + 8), by_group(length), by_group(length), memory_spec, by_group(8), by_group(1),
            all_lanes, held((length + 8, LANES)), rows_spec, held((length, states2)), held((states2, length)),
            held((length, SPAN)), held((length, SPAN)), held((8, length)), held((length + 8, states2)),
            held((8, states2)), held((1, LANES)),
        ],
        [
            by_group(length), by_group(8), by_group(1), held((length, states2)), all_lanes,
            held((8, states2)), held((8, LANES)),
        ],
        [
            shape_of(length, channels, dtype=BF16), shape_of(8, channels), shape_of(1, channels),
            shape_of(length, states2, dtype=BF16), shape_of(length, LANES, dtype=BF16),
            shape_of(8, states2), shape_of(8, LANES),
        ],
        [
            pltpu.VMEM((8, GROUP), F32), pltpu.VMEM((states, GROUP), F32),
            pltpu.VMEM((length, SPAN), F32), pltpu.VMEM((length, LANES), F32),
            pltpu.VMEM((length, states2), F32), pltpu.VMEM((8, states2), F32),
        ],
        flops=40e9,
        moved=length * channels * 14,
        name="backward",
    )(
        value, grad_mixer, mixer_out, memory, conv_pad, skip_row, per_head, marks, rising_rows, maps, maps_t,
        cross, cross_t, seg_row, pre_state, conv_state_pad, rate8,
    )

    value_send, value_own = weight_grads(grad_value)
    value_received = swap(after(gate_received, value_send), "dp", 1 << low_bits)

    def normed_part(ks):
        def row(i, j, r):
            return (r[0] ^ (ks[0] + i * (ks[-1] - ks[0]))) * (quarter // 256) + j

        return call(
            functools.partial(normed_kernel, ks),
            (len(ks), quarter // 256),
            [
                held((length, channels)), held((length, channels)), held((length, states2)), held((length, LANES)),
                pl.BlockSpec((256, channels), lambda i, j, r: (row(i, j, r), 0)),
                pl.BlockSpec((256, channels), lambda i, j, r: (row(i, j, r), 1)),
                pl.BlockSpec((256, states2), lambda i, j, r: (row(i, j, r), 0)),
                pl.BlockSpec((256, LANES), lambda i, j, r: (row(i, j, r), 0)),
            ],
            pl.BlockSpec((1, length, 256), lambda i, j, r: (i, 0, j)),
            shape_of(len(ks), length, quarter, dtype=BF16),
            prefetch=1,
            flops=2 * length * (2 * channels + states2 + LANES) * quarter * len(ks),
            moved=length * channels * 4 + channels * quarter * 4 * len(ks) + length * quarter * 2 * len(ks),
            name="normed_grad",
        )(ranks, grad_gate, grad_value, grad_state, grad_step, flat, flat, w_state, step_pad)

    near_far = swap(normed_part((1, 3)), "tensor", 1)
    near = normed_part((2, 0))
    over_y = swap((near[0].astype(F32) + near_far[1].astype(F32)).astype(BF16), "tensor", 2)
    grad_normed = near[1].astype(F32) + near_far[0].astype(F32) + over_y.astype(F32)

    own_gain = lax.dynamic_slice_in_dim(norm_gain, rank * quarter, quarter, 0)
    scale_in = per_head[:, 5 * heads : 5 * heads + 1]
    row_norm = sum_all(jnp.sum(own_tokens * own_gain * grad_normed, axis=1), "tensor")
    grad_tokens = (
        cotangent.astype(F32)
        + scale_in * own_gain * grad_normed
        - own_tokens * scale_in**3 * row_norm[:, None] / width
    ).astype(BF16)
    grad_norm_gain = jnp.sum(grad_normed * own_tokens * scale_in, axis=0)

    state_all = grad_state
    for bit in (1, 2):
        state_all = (state_all.astype(F32) + swap(state_all, "tensor", bit).astype(F32)).astype(BF16)
    grad_w_state = dot(normed, state_all, TN).astype(BF16)
    own_rows = piece_rows // parts
    grad_w_state = lax.dynamic_slice_in_dim(
        grad_w_state.reshape(groups, parts, own_rows, states2), rank, 1, axis=1
    )
    grad_w_step = dot(grad_step[:, :heads], normed, TN).astype(BF16)
    grad_w_step = grad_w_step.reshape(heads, groups, piece_rows).transpose(1, 0, 2)
    small = jnp.concatenate(
        [grad_w_state.reshape(groups, own_rows * states2), grad_w_step.reshape(groups, heads * piece_rows)], axis=1
    ).reshape(groups // (2 << low_bits), 2, 1 << low_bits, -1)
    small_own = lax.dynamic_slice_in_dim(small, place[0], 1, 1).reshape(groups // 2, -1)
    small_send = lax.dynamic_slice_in_dim(small, 1 - place[0], 1, 1).reshape(groups // 2, -1)
    small_sum = scatter_rest(small_own, swap(small_send, "dp", 1 << low_bits), 0, low_bits)[0]
    sum_state = small_sum[: own_rows * states2].reshape(own_rows, states2)
    sum_step = small_sum[own_rows * states2 :].reshape(heads, piece_rows).T

    sum_out = scatter_rest(out_own, out_received, 1, low_bits)
    sum_gate = scatter_rest(gate_own, gate_received, 0, low_bits)
    sum_value = scatter_rest(value_own, value_received, 0, low_bits)
    sum_inner = jnp.stack([sum_gate, sum_value], axis=1)

    grad_conv_state = sum_all(grad_conv_state[:5], "tensor")
    skip_sums = jnp.sum(grad_skip.reshape(heads, channels // heads), axis=1)
    pack = [
        grad_norm_gain, grad_conv[:5].reshape(-1), grad_conv_state.reshape(-1),
        grad_heads[0, :heads], grad_heads[1, :heads], skip_sums, grad_gate_gain[0],
    ]
    sums_all = sum_all(jnp.concatenate(pack), "dp")
    split = []
    at = 0
    for piece in pack:
        split.append(sums_all[at : at + piece.shape[0]])
        at += piece.shape[0]
    return (
        output,
        grad_tokens,
        split[0],
        sum_inner,
        sum_step,
        sum_state,
        split[1].reshape(5, channels),
        split[2].reshape(5, states2),
        split[3],
        split[4],
        split[5],
        split[6],
        sum_out,
    )


def solution(mesh):
    placed = (
        P("dp", "tensor"),
        P("dp", "tensor"),
        P("dp", None),
        P(),
        P(None, None, "tensor"),
        P(None, "tensor"),
        P(),
        P(None, "tensor"),
        P(),
        P("tensor"),
        P("tensor"),
        P("tensor"),
        P("tensor"),
        P("tensor", None),
    )
    return jax.shard_map(
        shards,
        mesh=mesh,
        in_specs=placed,
        out_specs=(
            P("dp", "tensor"),
            P("dp", "tensor"),
            P("tensor"),
            P("dp", None, "tensor"),
            P("dp", "tensor"),
            P(("dp", "tensor"), None),
            P(None, "tensor"),
            P(),
            P("tensor"),
            P("tensor"),
            P("tensor"),
            P("tensor"),
            P("tensor", "dp"),
        ),
        check_vma=False,
    )
```

time: 1290 us -> 470 us (0.36)
  waiting for transfers between devices: 598 us -> 163 us
  matrix products: 252 us -> 5.16 us
  Pallas kernels: 0 us -> 174 us
  local copies, waits for them, and re-layouts: 178 us -> 43.9 us
  blocking collectives: 103 us -> 0 us
  other arithmetic: 110 us -> 35 us
  starting transfers between devices: 0.58 us -> 38.8 us
  loops' own time: 23.1 us -> 0 us
  between operations: 15.4 us -> 1.14 us
    reduce_scatter x6 -> x0, waiting for transfers between devices: 574 us -> none  [the longest x1 282 us: shards(): lax.psum_scatter(grad_w_inner, 'dp', scatter_dimension=0, tiled=True)]
    dot_general x68 -> x2, matrix products: 252 us -> 5.16 us  [dot(): lax.dot_general(left, right, dims, precision=precision, preferred_element...]
    pallas_call x0 -> x11, Pallas kernels: none -> 174 us  [the longest x1 45.9 us: shards(): call(functools.partial(backward_kernel, heads, steps), (steps,), [by_grou...]
    ppermute x0 -> x37, waiting for transfers between devices: none -> 163 us  [swap(): return lax.ppermute(array, axis, [(i, i ^ mask) for i in range(count)])]
    psum x5 -> x0, blocking collectives: 103 us -> none  [the longest x1 41.9 us: shards(): lax.psum((grad_state, grad_conv_state), 'tensor')]
    reshape x14 -> x8, local copies, waits for them, and re-layouts: 55.1 us -> 2.56 us  [the longest x1 0.65 us: shards(): sum_state = small_sum[:own_rows * states2].reshape(own_rows, states2)]
    reduce_sum x21 -> x5, other arithmetic: 48.5 us -> 5.12 us  [the longest x2 2.61 us: shards(): sums = jnp.stack([jnp.sum(squares, axis=1), jnp.sum(weighted, axis=1)])]
    ppermute x0 -> x37, starting transfers between devices: none -> 38.8 us  [swap(): return lax.ppermute(array, axis, [(i, i ^ mask) for i in range(count)])]
  transfers between devices with their start and end apart: 8 -> 37, of which waited for: 6 -> 12; matrix products, arithmetic and copies ran while one was open for 18% -> 16% of each run, Pallas kernels for 0% -> 32%
where the time goes in v1:
time: 470 us; the launch traced here: 461 us
  Pallas kernels  174 us (37%)
  waiting for transfers between devices  163 us (35%)
  local copies, waits for them, and re-layouts  43.9 us (9%)
  starting transfers between devices  38.8 us (8%)
  other arithmetic  35 us (7%)
  matrix products  5.16 us (1%)
    ppermute x37, waiting for transfers between devices, swap(): return lax.ppermute(array, axis, [(i, i ^ mask) for i in range(count)])  163 us
    pallas_call x1, Pallas kernels, shards(): call(functools.partial(backward_kernel, heads, steps), (steps,), [by_grou...  45.9 us
    pallas_call x1, Pallas kernels, shards(): call(functools.partial(forward_kernel, heads), (steps,), [held((length, w...  40.3 us
    ppermute x37, starting transfers between devices, swap(): return lax.ppermute(array, axis, [(i, i ^ mask) for i in range(count)])  38.8 us
    pallas_call x2, Pallas kernels, normed_part(): call(functools.partial(normed_kernel, ks), (len(ks), quarter // 256), [he...  20.8 us
    pallas_call x2, Pallas kernels, weight_grads(): call(weight_kernel, (runs,), [pl.BlockSpec((length, run), lambda j, p: (0...  16.2 us
    unnamed x56, local copies, waits for them, and re-layouts  14.8 us
    pallas_call x1, Pallas kernels, shards(): call(functools.partial(gate_kernel, run), (steps,), [held((length, width)...  14.6 us
  transfers between devices with their start and end apart: 37, of which 12 were waited for; matrix products, arithmetic and copies ran while one was open for 16% of the time, Pallas kernels for 32%

profile of v1, /device:TPU:0, one launch (start us, length us, event | category | flops | bytes accessed | tf_op | source)
XLA Modules:
  0.0 461.2 jit_solution(16142264325682504074)
XLA Ops:
  0.7 3.0 collective-permute-start
  5.1 22.1 %collective-permute-done.refs_2_ = bf16[1024,512]{1,0:T(8,128)(2,1)} collective-permute-done((bf16[1024,512]{1,0:T(8,128)(2,1)}, bf16[1024,512]{1,0:T(8,128)(2,1)}, u32[]{:S(2)}, u32[]{:S(2)}) %collective-permute-start) | collective-permute-done | bytes 1048608 | tf_op jit(solution)/shard_map/ppermute | solution.py:453
  27.2 1.7 collective-permute-start.2
  35.9 10.3 %copy.88 = bf16[256,8,2,1024]{3,1,2,0:T(8,128)(2,1)} copy(bf16[256,8,2,1024]{3,2,1,0:T(2,128)(2,1)} %bitcast.103) | data formatting | bytes 16777216
  48.9 2.5 broadcast_in_dim.10
  53.1 11.1 %prep.1 = (bf16[1024,2048]{1,0:T(8,128)(2,1)}, f32[1024,256]{1,0:T(8,128)}, bf16[1024,256]{1,0:T(8,128)(2,1)}, bf16[256,1024]{1,0:T(8,128)(2,1)}, f32[1024,128]{...) custom-call(s32[1]{0:T(128)} %bitcast.rank, bf16[1024,512]{1,0:T(8,128)(2,1)} %refs_0_.1, ...), custom_call_target="tpu_custom_call" | custom-call | flops 1610612736 | bytes 14057472 | tf_op jit(solution)/shard_map/prep/pallas_call | solution.py:578
  64.3 40.3 %forward.1 = (f32[1032,1024]{1,0:T(8,128)}, f32[1024,1024]{1,0:T(8,128)}, f32[1024,1024]{1,0:T(8,128)}, bf16[8,128,1024]{2,1,0:T(8,128)(2,1)}, f32[1024,128]{1,0:T(8,128)}) custom-call(bf16[1024,2048]{1,0:T(8,128)(2,1)} %get-tuple-element.49.normed.left_send.left_own, bf16[2048,2048]{1,0:T(8,128)(2,1)} %bitcast.97, bf16[2048,2048]{1,0:T(8,128)(2,1)} %bitcast.98, ...), custom_call_target="tpu_custom_call" | custom-call | flops 17179869184 | bytes 25165824 | tf_op jit(solution)/shard_map/forward/pallas_call | solution.py:611
  105.9 2.4 constant_dynamic-update-slice_fusion.2
  109.4 2.4 constant_dynamic-update-slice_fusion.cotangent
  111.8 13.2 %cotangent.1 = (f32[1024,1024]{1,0:T(8,128)}, f32[1024,128]{1,0:T(8,128)}) custom-call(bf16[1024,2048]{1,0:T(8,128)(2,1)} %constant_dynamic-update-slice_fusion.cotangent, bf16[1024,2048]{1,0:T(8,128)(2,1)} %w_out.5, f32[1024,1024]{1,0:T(8,128)} %get-tuple-element.55.gate, f32[1024,1024]{1,0:T(8,128)} %get-tuple-element.56.mixed, f32[1,1024]{1,0:T(1,128)} %bitcast.128), custom_call_target="tpu_custom_call" | custom-call | flops 4294967296 | bytes 20971520 | tf_op jit(solution)/shard_map/cotangent/pallas_call | solution.py:632
  134.4 14.6 %gate.1 = (bf16[1024,1024]{1,0:T(8,128)(2,1)}, bf16[1024,1024]{1,0:T(8,128)(2,1)}, bf16[1024,1024]{1,0:T(8,128)(2,1)}, f32[1,1024]{1,0:T(1,128)}, bf16[1024,1024...) custom-call(s32[1]{0:T(128)} %bitcast.1.place, bf16[1024,2048]{1,0:T(8,128)(2,1)} %constant_dynamic-update-slice_fusion.cotangent, ...), custom_call_target="tpu_custom_call" | custom-call | flops 4294967296 | bytes 27262976 | tf_op jit(solution)/shard_map/gate/pallas_call | solution.py:656
  149.0 1.6 collective-permute-start.19
  150.5 45.9 %backward.1 = (bf16[1024,1024]{1,0:T(8,128)(2,1)}, f32[8,1024]{1,0:T(8,128)}, f32[1,1024]{1,0:T(1,128)}, bf16[1024,256]{1,0:T(8,128)(2,1)}, bf16[1024,128]{1,0:T...) custom-call(f32[1032,1024]{1,0:T(8,128)} %get-tuple-element.62.value, bf16[1024,1024]{1,0:T(8,128)(2,1)} %get-tuple-element.63.grad_out, ...), custom_call_target="tpu_custom_call" | custom-call | flops 40000000000 | bytes 14680064 | tf_op jit(solution)/shard_map/backward/pallas_call | solution.py:727
  196.6 1.6 convolution_convert_fusion.1
  198.2 8.1 %weights.2 = (bf16[1024,1024]{1,0:T(8,128)(2,1)}, bf16[1024,1024]{1,0:T(8,128)(2,1)}) custom-call(s32[1]{0:T(128)} %bitcast.1.place, bf16[1024,2048]{1,0:T(8,128)(2,1)} %get-tuple-element.49.normed.left_send.left_own, bf16[1024,2048]{1,0:T(8,128)(2,1)} %get-tuple-element.49.normed.left_send.left_own, bf16[1024,1024]{1,0:T(8,128)(2,1)} %get-tuple-element.61.grad_gate.right), custom_call_target="tpu_custom_call" | custom-call | flops 4294967296 | bytes 10485760 | tf_op jit(solution)/shard_map/weights/pallas_call | solution.py:681
  206.3 8.1 %weights.3 = (bf16[1024,1024]{1,0:T(8,128)(2,1)}, bf16[1024,1024]{1,0:T(8,128)(2,1)}) custom-call(s32[1]{0:T(128)} %bitcast.1.place, bf16[1024,2048]{1,0:T(8,128)(2,1)} %get-tuple-element.49.normed.left_send.left_own, bf16[1024,2048]{1,0:T(8,128)(2,1)} %get-tuple-element.49.normed.left_send.left_own, bf16[1024,1024]{1,0:T(8,128)(2,1)} %get-tuple-element.67.grad_value.right), custom_call_target="tpu_custom_call" | custom-call | flops 4294967296 | bytes 10485760 | tf_op jit(solution)/shard_map/weights/pallas_call | solution.py:681
  214.9 10.2 %normed_grad.2 = bf16[2,1024,512]{2,1,0:T(8,128)(2,1)} custom-call(s32[1]{0:T(128)} %bitcast.rank, bf16[1024,1024]{1,0:T(8,128)(2,1)} %get-tuple-element.61.grad_gate.right, bf16[1024,1024]{1,0:T(8,128)(2,1)} %get-tuple-element.67.grad_value.right, bf16[1024,256]{1,0:T(8,128)(2,1)} %get-tuple-element.68.grad_state, ...), custom_call_target="tpu_custom_call" | custom-call | flops 5100273664 | bytes 10485760 | tf_op jit(solution)/shard_map/normed_grad/pallas_call | solution.py:765
  225.1 10.6 %normed_grad.3 = bf16[2,1024,512]{2,1,0:T(8,128)(2,1)} custom-call(s32[1]{0:T(128)} %bitcast.rank, bf16[1024,1024]{1,0:T(8,128)(2,1)} %get-tuple-element.61.grad_gate.right, bf16[1024,1024]{1,0:T(8,128)(2,1)} %get-tuple-element.67.grad_value.right, bf16[1024,256]{1,0:T(8,128)(2,1)} %get-tuple-element.68.grad_state, ...), custom_call_target="tpu_custom_call" | custom-call | flops 5100273664 | bytes 10485760 | tf_op jit(solution)/shard_map/normed_grad/pallas_call | solution.py:765
  237.3 6.1 %output.3 = bf16[2,1024,512]{2,1,0:T(8,128)(2,1)} custom-call(s32[1]{0:T(128)} %bitcast.rank, bf16[1024,1024]{1,0:T(8,128)(2,1)} %get-tuple-element.60.mixed, bf16[1024,2048]{1,0:T(8,128)(2,1)} %w_out.5), custom_call_target="tpu_custom_call" | custom-call | flops 2147483648 | bytes 6291456 | tf_op jit(solution)/shard_map/output/pallas_call | solution.py:701
  244.9 4.9 %collective-permute-done.29 = bf16[1024,256]{1,0:T(8,128)(2,1)S(1)} collective-permute-done((bf16[1024,256]{1,0:T(8,128)(2,1)S(1)}, bf16[1024,256]{1,0:T(8,128)(2,1)S(1)}, u32[]{:S(2)}, u32[]{:S(2)}) %collective-permute-start.29) | collective-permute-done | bytes 524320 | tf_op jit(solution)/shard_map/ppermute | solution.py:453
  249.9 3.5 convolution_convert_fusion
  255.0 6.1 %output.2 = bf16[2,1024,512]{2,1,0:T(8,128)(2,1)} custom-call(s32[1]{0:T(128)} %bitcast.rank, bf16[1024,1024]{1,0:T(8,128)(2,1)} %get-tuple-element.60.mixed, bf16[1024,2048]{1,0:T(8,128)(2,1)} %w_out.5), custom_call_target="tpu_custom_call" | custom-call | flops 2147483648 | bytes 6291456 | tf_op jit(solution)/shard_map/output/pallas_call | solution.py:701
  263.0 1.5 collective-permute-start.20
  265.1 1.6 collective-permute-start.31
  266.7 2.6 collective-permute-start.32
  271.1 39.8 %collective-permute-done.20 = bf16[1024,1024]{1,0:T(8,128)(2,1)S(1)} collective-permute-done((bf16[1024,1024]{1,0:T(8,128)(2,1)}, bf16[1024,1024]{1,0:T(8,128)(2,1)S(1)}, u32[]{:S(2)}, u32[]{:S(2)}) %collective-permute-start.20) | collective-permute-done | bytes 2097184 | tf_op jit(solution)/shard_map/ppermute | solution.py:453
  313.2 3.1 add_convert_fusion.4
  316.3 1.6 collective-permute-start.34
  317.9 2.6 collective-permute-start.35
  320.7 2.5 fusion.9
  323.2 12.0 %collective-permute-done.11 = bf16[1024,512]{1,0:T(8,128)(2,1)S(1)} collective-permute-done((bf16[1024,512]{1,0:T(8,128)(2,1)S(1)}, bf16[1024,512]{1,0:T(8,128)(2,1)S(1)}, u32[]{:S(2)}, u32[]{:S(2)}) %collective-permute-start.11) | collective-permute-done | bytes 1048608 | tf_op jit(solution)/shard_map/ppermute | solution.py:453
  335.7 2.3 fusion.8
  341.7 3.5 add_convert_fusion.12
  345.2 13.6 %collective-permute-done.16 = f32[7984]{0:T(1024)S(1)} collective-permute-done((f32[7984]{0:T(1024)S(1)}, f32[7984]{0:T(1024)S(1)}, u32[]{:S(2)}, u32[]{:S(2)}) %collective-permute-start.16) | collective-permute-done | bytes 31968 | tf_op jit(solution)/shard_map/ppermute | solution.py:453
  358.8 1.6 collective-permute-start.21
  362.6 3.0 collective-permute-start.17
  365.6 3.0 convert_add_fusion.1
  368.5 3.1 collective-permute-done.17
  371.6 2.8 collective-permute-start.18
  374.6 3.6 collective-permute-start.23
  378.2 3.1 add_convert_fusion.9
  381.3 15.5 %collective-permute-done.18 = f32[7984]{0:T(1024)S(1)} collective-permute-done((f32[7984]{0:T(1024)S(1)}, f32[7984]{0:T(1024)S(1)}, u32[]{:S(2)}, u32[]{:S(2)}) %collective-permute-start.18) | collective-permute-done | bytes 31968 | tf_op jit(solution)/shard_map/ppermute | solution.py:453
  396.9 4.3 fusion.4
  404.2 29.2 %collective-permute-done.22 = bf16[256,1024]{1,0:T(8,128)(2,1)} collective-permute-done((bf16[256,1024]{1,0:T(8,128)(2,1)}, bf16[256,1024]{1,0:T(8,128)(2,1)}, u32[]{:S(2)}, u32[]{:S(2)}) %collective-permute-start.22) | collective-permute-done | bytes 524320 | tf_op jit(solution)/shard_map/ppermute | solution.py:453
  433.4 2.1 add_bitcast_fusion.1
  435.6 20.3 %collective-permute-done.26 = bf16[256,1024]{1,0:T(8,128)(2,1)} collective-permute-done((bf16[256,1024]{1,0:T(8,128)(2,1)}, bf16[256,1024]{1,0:T(8,128)(2,1)}, u32[]{:S(2)}, u32[]{:S(2)}) %collective-permute-start.26) | collective-permute-done | bytes 524320 | tf_op jit(solution)/shard_map/ppermute | solution.py:453
  455.9 2.1 add_bitcast_fusion
  458.3 2.9 copy.84
  (187 shorter events, 46.3 us)
Async XLA Ops:
  0.6 33.2 %copy-start.23 = (f32[16]{0:T(128)S(1)}, f32[16]{0:T(128)}, u32[]{:S(2)}) copy-start(f32[16]{0:T(128)} %param.23) | copy-start | bytes 196
  0.7 33.8 %copy-start.20 = (f32[5,256]{1,0:T(8,128)S(1)}, f32[5,256]{1,0:T(8,128)}, u32[]{:S(2)}) copy-start(f32[5,256]{1,0:T(8,128)} %param.22) | copy-start | bytes 15364
  0.7 26.5 %collective-permute-start = (bf16[1024,512]{1,0:T(8,128)(2,1)}, bf16[1024,512]{1,0:T(8,128)(2,1)}, u32[]{:S(2)}, u32[]{:S(2)}) collective-permute-start(bf16[1024,512]{1,0:T(8,128)(2,1)} %refs_0_.1), channel_id=1, source_target_pairs={{0,2},{1,3},{2,0},{3,1},{4,6},{5,7},{6,4},{7,5},{8,10},{9,11},{10,... | collective-permute-start | bytes 3145736 | tf_op jit(solution)/shard_map/ppermute | solution.py:453
  3.7 48.8 %collective-permute-start.4 = (bf16[1024,512]{1,0:T(8,128)(2,1)}, bf16[1024,512]{1,0:T(8,128)(2,1)}, u32[]{:S(2)}, u32[]{:S(2)}) collective-permute-start(bf16[1024,512]{1,0:T(8,128)(2,1)} %refs_0_.1), channel_id=1, source_target_pairs={{0,1},{1,0},{2,3},{3,2},{4,5},{5,4},{6,7},{7,6},{8,9},{9,8},{10,11... | collective-permute-start | bytes 3145736 | tf_op jit(solution)/shard_map/ppermute | solution.py:453
  27.2 25.3 %collective-permute-start.2 = (bf16[1024,512]{1,0:T(8,128)(2,1)}, bf16[1024,512]{1,0:T(8,128)(2,1)S(1)}, u32[]{:S(2)}, u32[]{:S(2)}) collective-permute-start(bf16[1024,512]{1,0:T(8,128)(2,1)} %param.15), channel_id=1, source_target_pairs={{0,2},{1,3},{2,0},{3,1},{4,6},{5,7},{6,4},{7,5},{8,10},{9,11},{10,... | collective-permute-start | bytes 3145736 | tf_op jit(solution)/shard_map/ppermute | solution.py:453
  28.9 23.6 %collective-permute-start.5 = (bf16[1024,512]{1,0:T(8,128)(2,1)}, bf16[1024,512]{1,0:T(8,128)(2,1)}, u32[]{:S(2)}, u32[]{:S(2)}) collective-permute-start(bf16[1024,512]{1,0:T(8,128)(2,1)} %collective-permute-done.refs_2_), channel_id=1, source_target_pairs={{0,1},{1,0},{2,3},{3,2},{4,5},{5,4},{6,7},{7,6},{8,9},{9,8},{10,11... | collective-permute-start | bytes 3145736 | tf_op jit(solution)/shard_map/ppermute | solution.py:453
  48.4 57.5 %collective-permute-start.1 = (bf16[1024,512]{1,0:T(8,128)(2,1)S(1)}, bf16[1024,512]{1,0:T(8,128)(2,1)}, u32[]{:S(2)}, u32[]{:S(2)}) collective-permute-start(bf16[1024,512]{1,0:T(8,128)(2,1)S(1)} %copy-done.7), channel_id=1, source_target_pairs={{0,1},{1,0},{2,3},{3,2},{4,5},{5,4},{6,7},{7,6},{8,9},{9,8},{10,11... | collective-permute-start | bytes 3145736 | tf_op jit(solution)/shard_map/ppermute | solution.py:453
  52.5 56.9 %collective-permute-start.3 = (bf16[1024,512]{1,0:T(8,128)(2,1)S(1)}, bf16[1024,512]{1,0:T(8,128)(2,1)}, u32[]{:S(2)}, u32[]{:S(2)}) collective-permute-start(bf16[1024,512]{1,0:T(8,128)(2,1)S(1)} %collective-permute-done.2), channel_id=1, source_target_pairs={{0,1},{1,0},{2,3},{3,2},{4,5},{5,4},{6,7},{7,6},{8,9},{9,8},{10,11... | collective-permute-start | bytes 3145736 | tf_op jit(solution)/shard_map/ppermute | solution.py:453
  111.8 15.1 %copy-start.16 = (bf16[2048,16]{0,1:T(8,128)(2,1)S(1)}, bf16[2048,16]{0,1:T(8,128)(2,1)}, u32[]{:S(2)}) copy-start(bf16[2048,16]{0,1:T(8,128)(2,1)} %param.19) | copy-start | bytes 196612
  126.4 2.5 collective-permute-start.6
  128.9 3.7 collective-permute-start.7
  149.0 114.0 %collective-permute-start.19 = (bf16[1024,1024]{1,0:T(8,128)(2,1)}, bf16[1024,1024]{1,0:T(8,128)(2,1)}, u32[]{:S(2)}, u32[]{:S(2)}) collective-permute-start(bf16[1024,1024]{1,0:T(8,128)(2,1)} %get-tuple-element.76), channel_id=1, source_target_pairs={{0,4},{4,0},{8,12},{12,8},{16,20},{20,16},{24,28},{28,24},{1,5},{5... | collective-permute-start | bytes 6291464 | tf_op jit(solution)/shard_map/ppermute | solution.py:453
  150.5 46.0 %copy-start.9 = (bf16[1024,2048]{1,0:T(8,128)(2,1)S(1)}, bf16[1024,2048]{1,0:T(8,128)(2,1)}, u32[]{:S(2)}) copy-start(bf16[1024,2048]{1,0:T(8,128)(2,1)} %get-tuple-element.49.normed.left_send.left_own) | copy-start | bytes 12582916
  196.5 39.2 %collective-permute-start.28 = (bf16[1024,256]{1,0:T(8,128)(2,1)}, bf16[1024,256]{1,0:T(8,128)(2,1)S(1)}, u32[]{:S(2)}, u32[]{:S(2)}) collective-permute-start(bf16[1024,256]{1,0:T(8,128)(2,1)} %get-tuple-element.68.grad_state), channel_id=1, source_target_pairs={{0,1},{1,0},{2,3},{3,2},{4,5},{5,4},{6,7},{7,6},{8,9},{9,8},{10,11... | collective-permute-start | bytes 1572872 | tf_op jit(solution)/shard_map/ppermute | solution.py:453
  214.4 29.0 %collective-permute-start.14 = (f32[5,256]{1,0:T(8,128)S(1)}, f32[5,256]{1,0:T(8,128)S(1)}, u32[]{:S(2)}, u32[]{:S(2)}) collective-permute-start(f32[5,256]{1,0:T(8,128)S(1)} %bitcast.131), channel_id=1, source_target_pairs={{0,1},{1,0},{2,3},{3,2},{4,5},{5,4},{6,7},{7,6},{8,9},{9,8},{10,11... | collective-permute-start | bytes 15368 | tf_op jit(solution)/shard_map/ppermute | solution.py:453
  235.9 14.0 %collective-permute-start.29 = (bf16[1024,256]{1,0:T(8,128)(2,1)S(1)}, bf16[1024,256]{1,0:T(8,128)(2,1)S(1)}, u32[]{:S(2)}, u32[]{:S(2)}) collective-permute-start(bf16[1024,256]{1,0:T(8,128)(2,1)S(1)} %add_convert_fusion.6), channel_id=1, source_target_pairs={{0,2},{1,3},{2,0},{3,1},{4,6},{5,7},{6,4},{7,5},{8,10},{9,11},{10,... | collective-permute-start | bytes 1572872 | tf_op jit(solution)/shard_map/ppermute | solution.py:453
  243.5 19.5 %collective-permute-start.15 = (f32[5,256]{1,0:T(8,128)S(1)}, f32[5,256]{1,0:T(8,128)S(1)}, u32[]{:S(2)}, u32[]{:S(2)}) collective-permute-start(f32[5,256]{1,0:T(8,128)S(1)} %slice_add_fusion), channel_id=1, source_target_pairs={{0,2},{1,3},{2,0},{3,1},{4,6},{5,7},{6,4},{7,5},{8,10},{9,11},{10,... | collective-permute-start | bytes 15368 | tf_op jit(solution)/shard_map/ppermute | solution.py:453
  254.4 15.2 %copy-start = (bf16[2,1024,512]{2,1,0:T(8,128)(2,1)S(1)}, bf16[2,1024,512]{2,1,0:T(8,128)(2,1)}, u32[]{:S(2)}) copy-start(bf16[2,1024,512]{2,1,0:T(8,128)(2,1)} %normed_grad.2) | copy-start | bytes 6291460
  254.4 10.2 %collective-permute-start.30 = (bf16[4,20480]{1,0:T(4,128)(2,1)S(1)}, bf16[4,20480]{1,0:T(4,128)(2,1)S(1)}, u32[]{:S(2)}, u32[]{:S(2)}) collective-permute-start(bf16[4,20480]{1,0:T(4,128)(2,1)S(1)} %bitcast.114), channel_id=1, source_target_pairs={{0,4},{4,0},{8,12},{12,8},{16,20},{20,16},{24,28},{28,24},{1,5},{5... | collective-permute-start | bytes 491528 | tf_op jit(solution)/shard_map/ppermute | solution.py:453
  261.0 8.3 %collective-permute-start.10 = (bf16[2,1024,512]{2,1,0:T(8,128)(2,1)}, bf16[2,1024,512]{2,1,0:T(8,128)(2,1)}, u32[]{:S(2)}, u32[]{:S(2)}) collective-permute-start(bf16[2,1024,512]{2,1,0:T(8,128)(2,1)} %normed_grad.3), channel_id=1, source_target_pairs={{0,1},{1,0},{2,3},{3,2},{4,5},{5,4},{6,7},{7,6},{8,9},{9,8},{10,11... | collective-permute-start | bytes 6291464 | tf_op jit(solution)/shard_map/ppermute | solution.py:453
  262.4 58.1 %collective-permute-start.8 = (bf16[2,1024,512]{2,1,0:T(8,128)(2,1)}, bf16[2,1024,512]{2,1,0:T(8,128)(2,1)}, u32[]{:S(2)}, u32[]{:S(2)}) collective-permute-start(bf16[2,1024,512]{2,1,0:T(8,128)(2,1)} %output.3), channel_id=1, source_target_pairs={{0,1},{1,0},{2,3},{3,2},{4,5},{5,4},{6,7},{7,6},{8,9},{9,8},{10,11... | collective-permute-start | bytes 6291464 | tf_op jit(solution)/shard_map/ppermute | solution.py:453
  263.0 50.2 %copy-start.11 = (bf16[1024,1024]{1,0:T(8,128)(2,1)S(1)}, bf16[1024,1024]{1,0:T(8,128)(2,1)}, u32[]{:S(2)}) copy-start(bf16[1024,1024]{1,0:T(8,128)(2,1)} %get-tuple-element.82) | copy-start | bytes 6291460
  263.0 47.8 %collective-permute-start.20 = (bf16[1024,1024]{1,0:T(8,128)(2,1)}, bf16[1024,1024]{1,0:T(8,128)(2,1)S(1)}, u32[]{:S(2)}, u32[]{:S(2)}) collective-permute-start(bf16[1024,1024]{1,0:T(8,128)(2,1)} %get-tuple-element.78), channel_id=1, source_target_pairs={{0,4},{4,0},{8,12},{12,8},{16,20},{20,16},{24,28},{28,24},{1,5},{5... | collective-permute-start | bytes 6291464 | tf_op jit(solution)/shard_map/ppermute | solution.py:453
  265.1 46.4 %collective-permute-start.31 = (bf16[1,20480]{1,0:T(2,128)(2,1)S(1)}, bf16[1,20480]{1,0:T(2,128)(2,1)S(1)}, u32[]{:S(2)}, u32[]{:S(2)}) collective-permute-start(bf16[1,20480]{1,0:T(2,128)(2,1)S(1)} %get-tuple-element.163), channel_id=1, source_target_pairs={{0,8},{4,12},{8,0},{12,4},{16,24},{20,28},{24,16},{28,20},{1,9},{5... | collective-permute-start | bytes 122888 | tf_op jit(solution)/shard_map/ppermute | solution.py:453
  266.7 46.2 %collective-permute-start.32 = (bf16[1,20480]{1,0:T(2,128)(2,1)S(1)}, bf16[1,20480]{1,0:T(2,128)(2,1)S(1)}, u32[]{:S(2)}, u32[]{:S(2)}) collective-permute-start(bf16[1,20480]{1,0:T(2,128)(2,1)S(1)} %get-tuple-element.165), channel_id=1, source_target_pairs={{0,16},{4,20},{8,24},{12,28},{16,0},{20,4},{24,8},{28,12},{1,17},{... | collective-permute-start | bytes 122888 | tf_op jit(solution)/shard_map/ppermute | solution.py:453
  269.3 43.6 %collective-permute-start.33 = (bf16[1,20480]{1,0:T(2,128)(2,1)S(1)}, bf16[1,20480]{1,0:T(2,128)(2,1)S(1)}, u32[]{:S(2)}, u32[]{:S(2)}) collective-permute-start(bf16[1,20480]{1,0:T(2,128)(2,1)S(1)} %get-tuple-element.164), channel_id=1, source_target_pairs={{0,24},{4,28},{8,16},{12,20},{16,8},{20,12},{24,0},{28,4},{1,25},{... | collective-permute-start | bytes 122888 | tf_op jit(solution)/shard_map/ppermute | solution.py:453
  310.9 24.3 %collective-permute-start.11 = (bf16[1024,512]{1,0:T(8,128)(2,1)S(1)}, bf16[1024,512]{1,0:T(8,128)(2,1)S(1)}, u32[]{:S(2)}, u32[]{:S(2)}) collective-permute-start(bf16[1024,512]{1,0:T(8,128)(2,1)S(1)} %fusion.10), channel_id=1, source_target_pairs={{0,2},{1,3},{2,0},{3,1},{4,6},{5,7},{6,4},{7,5},{8,10},{9,11},{10,... | collective-permute-start | bytes 3145736 | tf_op jit(solution)/shard_map/ppermute | solution.py:453
  311.4 63.1 %collective-permute-start.24 = (bf16[1024,1024]{1,0:T(8,128)(2,1)}, bf16[1024,1024]{1,0:T(8,128)(2,1)}, u32[]{:S(2)}, u32[]{:S(2)}) collective-permute-start(bf16[1024,1024]{1,0:T(8,128)(2,1)} %get-tuple-element.81), channel_id=1, source_target_pairs={{0,4},{4,0},{8,12},{12,8},{16,20},{20,16},{24,28},{28,24},{1,5},{5... | collective-permute-start | bytes 6291464 | tf_op jit(solution)/shard_map/ppermute | solution.py:453
  316.3 19.4 %copy-start.1 = (bf16[1024,512]{1,0:T(8,128)(2,1)S(1)}, bf16[1024,512]{1,0:T(8,128)(2,1)}, u32[]{:S(2)}) copy-start(bf16[1024,512]{1,0:T(8,128)(2,1)} %refs_0_.1) | copy-start | bytes 3145732
  316.3 22.2 %collective-permute-start.34 = (bf16[1024,256]{1,0:T(8,128)(2,1)S(1)}, bf16[1024,256]{1,0:T(8,128)(2,1)S(1)}, u32[]{:S(2)}, u32[]{:S(2)}) collective-permute-start(bf16[1024,256]{1,0:T(8,128)(2,1)S(1)} %get-tuple-element.152), channel_id=1, source_target_pairs={{0,8},{4,12},{8,0},{12,4},{16,24},{20,28},{24,16},{28,20},{1,9},{5... | collective-permute-start | bytes 1572872 | tf_op jit(solution)/shard_map/ppermute | solution.py:453
  317.9 43.2 %collective-permute-start.35 = (bf16[1024,256]{1,0:T(8,128)(2,1)}, bf16[1024,256]{1,0:T(8,128)(2,1)}, u32[]{:S(2)}, u32[]{:S(2)}) collective-permute-start(bf16[1024,256]{1,0:T(8,128)(2,1)} %get-tuple-element.154), channel_id=1, source_target_pairs={{0,16},{4,20},{8,24},{12,28},{16,0},{20,4},{24,8},{28,12},{1,17},{... | collective-permute-start | bytes 1572872 | tf_op jit(solution)/shard_map/ppermute | solution.py:453
  320.5 42.1 %collective-permute-start.36 = (bf16[1024,256]{1,0:T(8,128)(2,1)}, bf16[1024,256]{1,0:T(8,128)(2,1)}, u32[]{:S(2)}, u32[]{:S(2)}) collective-permute-start(bf16[1024,256]{1,0:T(8,128)(2,1)} %get-tuple-element.153), channel_id=1, source_target_pairs={{0,24},{4,28},{8,16},{12,20},{16,8},{20,12},{24,0},{28,4},{1,25},{... | collective-permute-start | bytes 1572872 | tf_op jit(solution)/shard_map/ppermute | solution.py:453
  335.1 46.2 %collective-permute-start.9 = (bf16[1024,512]{1,0:T(8,128)(2,1)}, bf16[1024,512]{1,0:T(8,128)(2,1)}, u32[]{:S(2)}, u32[]{:S(2)}) collective-permute-start(bf16[1024,512]{1,0:T(8,128)(2,1)} %fusion.9), channel_id=1, source_target_pairs={{0,2},{1,3},{2,0},{3,1},{4,6},{5,7},{6,4},{7,5},{8,10},{9,11},{10,... | collective-permute-start | bytes 3145736 | tf_op jit(solution)/shard_map/ppermute | solution.py:453
  339.3 1.2 collective-permute-start.12
  340.5 18.3 %collective-permute-start.16 = (f32[7984]{0:T(1024)S(1)}, f32[7984]{0:T(1024)S(1)}, u32[]{:S(2)}, u32[]{:S(2)}) collective-permute-start(f32[7984]{0:T(1024)S(1)} %concatenate.37), channel_id=1, source_target_pairs={{0,4},{4,0},{8,12},{12,8},{16,20},{20,16},{24,28},{28,24},{1,5},{5... | collective-permute-start | bytes 95816 | tf_op jit(solution)/shard_map/ppermute | solution.py:453
  358.8 38.0 %collective-permute-start.21 = (bf16[256,1024]{1,0:T(8,128)(2,1)}, bf16[256,1024]{1,0:T(8,128)(2,1)}, u32[]{:S(2)}, u32[]{:S(2)}) collective-permute-start(bf16[256,1024]{1,0:T(8,128)(2,1)} %get-tuple-element.155), channel_id=1, source_target_pairs={{0,8},{4,12},{8,0},{12,4},{16,24},{20,28},{24,16},{28,20},{1,9},{5... | collective-permute-start | bytes 1572872 | tf_op jit(solution)/shard_map/ppermute | solution.py:453
  361.0 17.1 %copy-start.10 = (bf16[1024,1024]{1,0:T(8,128)(2,1)S(1)}, bf16[1024,1024]{1,0:T(8,128)(2,1)}, u32[]{:S(2)}) copy-start(bf16[1024,1024]{1,0:T(8,128)(2,1)} %get-tuple-element.79) | copy-start | bytes 6291460
  361.1 7.5 %collective-permute-start.13 = (f32[1024]{0:T(1024)S(1)}, f32[1024]{0:T(1024)S(1)}, u32[]{:S(2)}, u32[]{:S(2)}) collective-permute-start(f32[1024]{0:T(1024)S(1)} %add.295), channel_id=1, source_target_pairs={{0,2},{1,3},{2,0},{3,1},{4,6},{5,7},{6,4},{7,5},{8,10},{9,11},{10,... | collective-permute-start | bytes 12296 | tf_op jit(solution)/shard_map/ppermute | solution.py:453
  362.6 9.0 %collective-permute-start.17 = (f32[7984]{0:T(1024)S(1)}, f32[7984]{0:T(1024)S(1)}, u32[]{:S(2)}, u32[]{:S(2)}) collective-permute-start(f32[7984]{0:T(1024)S(1)} %add.299), channel_id=1, source_target_pairs={{0,8},{4,12},{8,0},{12,4},{16,24},{20,28},{24,16},{28,20},{1,9},{5... | collective-permute-start | bytes 95816 | tf_op jit(solution)/shard_map/ppermute | solution.py:453
  371.6 25.2 %collective-permute-start.18 = (f32[7984]{0:T(1024)S(1)}, f32[7984]{0:T(1024)S(1)}, u32[]{:S(2)}, u32[]{:S(2)}) collective-permute-start(f32[7984]{0:T(1024)S(1)} %add.300), channel_id=1, source_target_pairs={{0,16},{4,20},{8,24},{12,28},{16,0},{20,4},{24,8},{28,12},{1,17},{... | collective-permute-start | bytes 95816 | tf_op jit(solution)/shard_map/ppermute | solution.py:453
  374.4 59.0 %collective-permute-start.22 = (bf16[256,1024]{1,0:T(8,128)(2,1)}, bf16[256,1024]{1,0:T(8,128)(2,1)}, u32[]{:S(2)}, u32[]{:S(2)}) collective-permute-start(bf16[256,1024]{1,0:T(8,128)(2,1)} %get-tuple-element.157), channel_id=1, source_target_pairs={{0,16},{4,20},{8,24},{12,28},{16,0},{20,4},{24,8},{28,12},{1,17},{... | collective-permute-start | bytes 1572872 | tf_op jit(solution)/shard_map/ppermute | solution.py:453
  374.6 58.9 %collective-permute-start.23 = (bf16[256,1024]{1,0:T(8,128)(2,1)}, bf16[256,1024]{1,0:T(8,128)(2,1)}, u32[]{:S(2)}, u32[]{:S(2)}) collective-permute-start(bf16[256,1024]{1,0:T(8,128)(2,1)} %get-tuple-element.156), channel_id=1, source_target_pairs={{0,24},{4,28},{8,16},{12,20},{16,8},{20,12},{24,0},{28,4},{1,25},{... | collective-permute-start | bytes 1572872 | tf_op jit(solution)/shard_map/ppermute | solution.py:453
  378.2 18.7 %copy-start.3 = (bf16[2,1024,512]{2,1,0:T(8,128)(2,1)S(1)}, bf16[2,1024,512]{2,1,0:T(8,128)(2,1)}, u32[]{:S(2)}) copy-start(bf16[2,1024,512]{2,1,0:T(8,128)(2,1)} %output.2) | copy-start | bytes 6291460
  378.2 18.7 %copy-start.6 = (bf16[1024,512]{1,0:T(8,128)(2,1)S(1)}, bf16[1024,512]{1,0:T(8,128)(2,1)}, u32[]{:S(2)}) copy-start(bf16[1024,512]{1,0:T(8,128)(2,1)} %copy-done.5) | copy-start | bytes 3145732
  378.2 18.7 %copy-start.8 = (bf16[1024,512]{1,0:T(8,128)(2,1)S(1)}, bf16[1024,512]{1,0:T(8,128)(2,1)}, u32[]{:S(2)}) copy-start(bf16[1024,512]{1,0:T(8,128)(2,1)} %param.15) | copy-start | bytes 3145732
  381.3 54.2 %collective-permute-start.25 = (bf16[256,1024]{1,0:T(8,128)(2,1)}, bf16[256,1024]{1,0:T(8,128)(2,1)}, u32[]{:S(2)}, u32[]{:S(2)}) collective-permute-start(bf16[256,1024]{1,0:T(8,128)(2,1)} %get-tuple-element.158), channel_id=1, source_target_pairs={{0,8},{4,12},{8,0},{12,4},{16,24},{20,28},{24,16},{28,20},{1,9},{5... | collective-permute-start | bytes 1572872 | tf_op jit(solution)/shard_map/ppermute | solution.py:453
  396.8 59.1 %collective-permute-start.26 = (bf16[256,1024]{1,0:T(8,128)(2,1)}, bf16[256,1024]{1,0:T(8,128)(2,1)}, u32[]{:S(2)}, u32[]{:S(2)}) collective-permute-start(bf16[256,1024]{1,0:T(8,128)(2,1)} %get-tuple-element.160), channel_id=1, source_target_pairs={{0,16},{4,20},{8,24},{12,28},{16,0},{20,4},{24,8},{28,12},{1,17},{... | collective-permute-start | bytes 1572872 | tf_op jit(solution)/shard_map/ppermute | solution.py:453
  396.8 59.1 %collective-permute-start.27 = (bf16[256,1024]{1,0:T(8,128)(2,1)}, bf16[256,1024]{1,0:T(8,128)(2,1)}, u32[]{:S(2)}, u32[]{:S(2)}) collective-permute-start(bf16[256,1024]{1,0:T(8,128)(2,1)} %get-tuple-element.159), channel_id=1, source_target_pairs={{0,24},{4,28},{8,16},{12,20},{16,8},{20,12},{24,0},{28,4},{1,25},{... | collective-permute-start | bytes 1572872 | tf_op jit(solution)/shard_map/ppermute | solution.py:453
  (14 other events, 94.0 us)

commit v2 on v1

v2 whole, which is shorter than its diff:
```python
import functools
import math

import jax
import jax.numpy as jnp
from jax import lax
from jax.experimental import pallas as pl
from jax.experimental.pallas import tpu as pltpu
from jax.sharding import PartitionSpec as P

F32 = jnp.float32
BF16 = jnp.bfloat16
HIGHEST = lax.Precision.HIGHEST
EPSILON = 1e-05
LOG2E = math.log2(math.e)
LANES = 128
SPAN = 128
GROUP = 256
UNROLL = 8
HINT = 0.02
ROWS = 512
CHUNKS = 2

NN = (((1,), (0,)), ((), ()))
NT = (((1,), (1,)), ((), ()))
TN = (((0,), (0,)), ((), ()))


def dot(left, right, dims=NN, precision=None):
    return lax.dot_general(left, right, dims, precision=precision, preferred_element_type=F32)


def sigmoid(a):
    return 0.5 * jnp.tanh(0.5 * a) + 0.5


def iota(shape, dim):
    return lax.broadcasted_iota(jnp.int32, shape, dim)


def tri(upper):
    rows, cols = iota((SPAN, SPAN), 0), iota((SPAN, SPAN), 1)
    return ((rows <= cols) if upper else (rows >= cols)).astype(F32)


def call(body, grid, in_specs, out_specs, out_shape, scratch=(), prefetch=0, flops=0, moved=0, name=None, vmem=56):
    return pl.pallas_call(
        body,
        grid_spec=pltpu.PrefetchScalarGridSpec(
            num_scalar_prefetch=prefetch,
            grid=grid,
            in_specs=in_specs,
            out_specs=out_specs,
            scratch_shapes=list(scratch),
        ),
        out_shape=out_shape,
        compiler_params=pltpu.CompilerParams(
            vmem_limit_bytes=vmem * 1024 * 1024, dimension_semantics=("arbitrary",) * len(grid)
        ),
        cost_estimate=pl.CostEstimate(
            flops=int(flops * HINT), bytes_accessed=int(moved * HINT), transcendentals=0
        ),
        name=name,
    )


def held(shape):
    zeros = (0,) * len(shape)
    return pl.BlockSpec(shape, lambda *_: zeros, pipeline_mode=pl.Buffered(1))


def shape_of(*dims, dtype=F32):
    return jax.ShapeDtypeStruct(dims, dtype)


def conv_taps(before, now, marks, filters):
    rows = now.shape[0]
    wide = jnp.concatenate([before, now], axis=0)
    total = filters[4:5] + filters[0:1] * now
    shifted = [now]
    for k in range(1, 4):
        moved = wide[8 - k : 8 - k + rows] * marks[:, k - 1 : k]
        shifted.append(moved)
        total = total + filters[k : k + 1] * moved
    return total, shifted


def rows_before(array, start):
    return array[pl.ds(pl.multiple_of(jnp.maximum(start - 8, 0), 8), 8), :]


def conv_back(later, marks, filters):
    rows = later.shape[0] - 8
    total = filters[0:1] * later[:rows]
    for k in range(1, 4):
        total = total + filters[k : k + 1] * (later[k : k + rows] * marks[k : k + rows, k - 1 : k])
    return total


def fold_lanes(power):
    folded = power[:, :LANES]
    for tile in range(1, power.shape[1] // LANES):
        folded = folded + power[:, tile * LANES : (tile + 1) * LANES]
    return folded


def spread(table, section, heads, count):
    lane = iota((table.shape[0], LANES), 1)
    tiles = []
    for pair in range(count // 2):
        at = section * heads + 2 * pair
        tiles.append(jnp.where(lane < LANES // 2, table[:, at : at + 1], table[:, at + 1 : at + 2]))
    return jnp.concatenate(tiles, axis=1)


def front_kernel(
    parts, heads, rank, *refs,
):
    pieces, refs = refs[:parts], refs[parts:]
    (gain, w_maps, conv_maps, bias, rate, seg_row, w_gate, w_value, conv, skip, marks,
     normed, pre_state, maps, maps_t, per_head, rows_out, cross_t, value, gate, mixed, low_gated, memory, squares,
     proj, cross, state) = refs
    g = pl.program_id(0)
    length, quarter = pieces[0].shape
    width = quarter * parts
    blocks = length // SPAN
    states = maps.shape[1] // 2
    count = GROUP // 64
    lane = iota((SPAN, LANES), 1)

    @pl.when(g == 0)
    def _():
        squares[...] = jnp.zeros_like(squares)

        def normalise(b, _):
            at = pl.ds(pl.multiple_of(b * SPAN, SPAN), SPAN)
            wide = [piece[at, :].astype(F32) for piece in pieces]
            total = functools.reduce(jnp.add, [array * array for array in wide])
            scale = lax.rsqrt(jnp.sum(total, axis=1, keepdims=True) / width + EPSILON)
            per_head[at, :] = jnp.broadcast_to(scale, (SPAN, LANES))
            for k in range(parts):
                to = pl.multiple_of((rank[0] ^ k) * quarter, quarter)
                normed[at, pl.ds(to, quarter)] = (wide[k] * scale * gain[:, pl.ds(to, quarter)]).astype(BF16)
            return 0

        lax.fori_loop(0, blocks, normalise, 0, unroll=2)
        proj[...] = dot(normed[...], w_maps[...])

        def tables(b, _):
            start = pl.multiple_of(b * SPAN, SPAN)
            at = pl.ds(start, SPAN)
            mark = marks[at, :]
            now = proj[at, : 2 * states]
            pre_state[at, :] = now
            total, _ = conv_taps(rows_before(proj, start)[:, : 2 * states], now, mark, conv_maps[...])
            both = total * sigmoid(total)
            keys, queries = both[:, :states], both[:, states:]
            low_keys, low_queries = keys.astype(BF16), queries.astype(BF16)
            maps[at, :states] = low_keys
            maps[at, states:] = low_queries
            maps_t[:states, pl.ds(start, SPAN)] = keys.T.astype(BF16)
            maps_t[states:, pl.ds(start, SPAN)] = queries.T.astype(BF16)

            pre = proj[at, 2 * states :] + bias[...]
            size = jnp.maximum(pre, 0.0) + jnp.log1p(jnp.exp(-jnp.abs(pre)))
            rising = dot(tri(False), -rate[...] * size, precision=HIGHEST)
            entering = jnp.exp(rising) * mark[:, 3:4]
            leaving = jnp.exp(rising[SPAN - 1 :] - rising) * mark[:, 4:5]
            rising = rising * LOG2E
            section = lane // heads
            packed = jnp.where(section == 0, rising, entering)
            packed = jnp.where(section == 2, leaving, packed)
            packed = jnp.where(section == 3, size, packed)
            packed = jnp.where(section == 4, pre, packed)
            packed = jnp.where(section == 5, per_head[at, :], packed)
            per_head[at, :] = packed
            turned = rising.T
            for group in range(rows_out.shape[0]):
                rows_out[group, pl.ds(pl.multiple_of(b * 8, 8), 8), :] = turned[group * count : group * count + 8]
            same = mark[:, 6:7] == seg_row[0:1, pl.ds(start, SPAN)]
            rows, cols = iota((SPAN, SPAN), 0), iota((SPAN, SPAN), 1)
            cross[at, :] = jnp.where(same & (rows >= cols), dot(low_queries, low_keys, NT), 0.0)
            cross_t[at, :] = jnp.where(same & (rows <= cols), dot(low_keys, low_queries, NT), 0.0)
            return 0

        lax.fori_loop(0, blocks, tables, 0, unroll=2)

    both = dot(normed[...], jnp.concatenate([w_gate[...], w_value[...]], axis=1))
    gate[...] = both[:, :GROUP].astype(BF16)
    value[...] = both[:, GROUP:]
    state[...] = jnp.zeros_like(state)
    turn = lax.rem(LANES - count * g, LANES)

    def block(b, _):
        start = pl.multiple_of(b * SPAN, SPAN)
        at = pl.ds(start, SPAN)
        total, _ = conv_taps(rows_before(value, start), value[at, :], marks[at, :], conv[...])
        inputs = total * sigmoid(total)
        table = pltpu.roll(per_head[at, :], turn, 1)
        entering, leaving, size = (spread(table, s, heads, count) for s in (1, 2, 3))
        scaled = inputs * size
        keys_t = maps_t[0:states, pl.ds(start, SPAN)]
        queries = maps[at, states:]
        low_state = state[...].astype(BF16)
        memory[b] = low_state
        out = entering * dot(queries, low_state) + skip[...] * inputs
        rising_rows = rows_out[g, pl.ds(pl.multiple_of(b * 8, 8), 8), :]
        crossed = cross[at, :]
        parts_out = []
        for pair in range(count // 2):
            weights = []
            for j in (2 * pair, 2 * pair + 1):
                gap = jnp.minimum(table[:, j : j + 1] - rising_rows[j : j + 1, :], 0.0)
                weights.append((jnp.exp2(gap) * crossed).astype(BF16))
            tile = scaled[:, pair * LANES : (pair + 1) * LANES]
            stacked = jnp.concatenate(
                [
                    jnp.where(lane < LANES // 2, tile, 0.0).astype(BF16),
                    jnp.where(lane < LANES // 2, 0.0, tile).astype(BF16),
                ],
                axis=0,
            )
            parts_out.append(dot(jnp.concatenate(weights, axis=1), stacked))
        out = out + jnp.concatenate(parts_out, axis=1)
        fresh = dot(keys_t, (leaving * scaled).astype(BF16))
        state[...] = state[...] * entering[SPAN - 1 :] + fresh
        mixed[at, :] = out
        opened = gate[at, :].astype(F32)
        gated = out * (opened * sigmoid(opened))
        low_gated[at, :] = gated.astype(BF16)
        squares[at, :] += fold_lanes(gated * gated)
        return 0

    lax.fori_loop(0, blocks, block, 0, unroll=UNROLL)


def assemble(pieces, target, sems, where):
    copies = [
        pltpu.make_async_copy(pieces[k].at[:, pl.ds(at, size)], target.at[:, pl.ds(to, size)], sems.at[i])
        for i, (k, at, to, size) in enumerate(where)
    ]
    for copy in copies:
        copy.start()
    for copy in copies:
        copy.wait()


def cotangent_kernel(parts, rank, *refs):
    pieces, (w_out, gated, gain, squares, grad, stats, sums, full, sems) = refs[:parts], refs[parts:]
    g = pl.program_id(0)
    length, quarter = pieces[0].shape

    @pl.when(g == 0)
    def _():
        sums[...] = jnp.zeros_like(sums)
        places = [pl.multiple_of((rank[0] ^ k) * quarter, quarter) for k in range(parts)]
        assemble(pieces, full, sems, [(k, 0, places[k], quarter) for k in range(parts)])

    grad[...] = dot(full[...], w_out[...], NT).astype(BF16)

    def chunk(i, _):
        at = pl.ds(pl.multiple_of(i * SPAN, SPAN), SPAN)
        sums[at, :] += fold_lanes(grad[at, :].astype(F32) * gated[at, :].astype(F32) * gain[...])
        return 0

    lax.fori_loop(0, length // SPAN, chunk, 0, unroll=2)

    @pl.when(g == pl.num_programs(0) - 1)
    def _():
        row = iota((8, LANES), 0)
        stats[...] = dot((row == 0).astype(F32), squares[...], NT, HIGHEST) + dot(
            (row == 1).astype(F32), sums[...], NT, HIGHEST
        )


def gate_kernel(
    parts, run, channels_all, place, rank, *refs,
):
    pieces, refs = refs[:parts], refs[parts:]
    (grad, gate, mixed, gain, stats, marks,
     low_mixed, grad_mixer, grad_gate, grad_gain, w_send, w_own, sent, kept, sems) = refs
    length, quarter = pieces[0].shape
    grad_gain[...] = jnp.zeros_like(grad_gain)
    pick = (iota((8, LANES), 0) == iota((8, LANES), 1)).astype(F32)
    pairs = quarter // (2 * run)
    bits = (parts * pairs - 1).bit_length()

    @pl.when(pl.program_id(0) == 0)
    def _():
        for half, target in ((1, sent), (0, kept)):
            where = []
            for k in range(parts):
                for j in range(pairs):
                    at = pl.multiple_of((2 * j + (place[0] ^ half)) * run, run)
                    to = turned((rank[0] ^ k) * pairs + j, bits) * run
                    where.append((k, at, pl.multiple_of(to, run), run))
            assemble(pieces, target, sems, where)

    def chunk(i, _):
        start = pl.multiple_of(i * SPAN, SPAN)
        at = pl.ds(start, SPAN)
        columns = dot(stats[:, pl.ds(start, SPAN)], pick, TN, HIGHEST)
        keep = marks[at, 5:6]
        scale = lax.rsqrt(columns[:, 0:1] / channels_all + EPSILON)
        factor = scale * keep
        pull = scale * scale * factor * columns[:, 1:2] / channels_all
        opened, out, now = gate[at, :].astype(F32), mixed[at, :], grad[at, :].astype(F32)
        chance = sigmoid(opened)
        swish = opened * chance
        gated = out * swish
        scaled = gated * factor
        low_mixed[at, :] = (scaled * gain[...]).astype(BF16)
        grad_gain[...] += jnp.sum(now * scaled, axis=0, keepdims=True)
        grad_gated = now * (factor * gain[...]) - gated * pull
        grad_mixer[at, :] = (grad_gated * swish).astype(BF16)
        grad_gate[at, :] = (grad_gated * out * chance * (1.0 + opened * (1.0 - chance))).astype(BF16)
        return 0

    lax.fori_loop(0, length // SPAN, chunk, 0, unroll=2)
    w_send[...] = dot(low_mixed[...], sent[...], TN).astype(BF16)
    w_own[...] = dot(low_mixed[...], kept[...], TN).astype(BF16)


def weight_kernel(place, left_send, left_own, *refs):
    parts = len(refs) // 3
    right = refs[:parts]
    for left, targets in ((left_send, refs[parts : 2 * parts]), (left_own, refs[2 * parts :])):
        for part, target in zip(right, targets):
            target[...] = dot(left[...], part[...], TN).astype(BF16)


def backward_kernel(
    heads, first, value, grad_out, mixed, memory, conv, skip, per_head, marks, rows_in, maps, maps_t, cross_t,
    grad_value, grad_conv, grad_skip, grad_cross, folded, grad_maps,
    later, grad_memory,
):
    g = pl.program_id(0) + first
    length = grad_out.shape[0]
    blocks = length // SPAN
    states = maps.shape[1] // 2
    count = GROUP // 64
    lane = iota((SPAN, LANES), 1)
    row = iota((SPAN, GROUP), 0)
    turn = lax.rem(LANES - count * g, LANES)
    channel, target = iota((GROUP, LANES), 0), iota((GROUP, LANES), 1)
    pick_rise = (target == count * g + channel // 64).astype(BF16)
    pick_size = (target == heads + count * g + channel // 64).astype(BF16)
    later[...] = jnp.zeros_like(later)
    grad_memory[...] = jnp.zeros_like(grad_memory)
    grad_conv[...] = jnp.zeros_like(grad_conv)
    grad_skip[...] = jnp.zeros_like(grad_skip)

    @pl.when(g == first)
    def _():
        grad_cross[...] = jnp.zeros_like(grad_cross)
        folded[...] = jnp.zeros_like(folded)
        grad_maps[...] = jnp.zeros_like(grad_maps)

    def block(i, _):
        b = blocks - 1 - i
        start = pl.multiple_of(b * SPAN, SPAN)
        at = pl.ds(start, SPAN)
        filters = conv[...]
        total, shifted = conv_taps(rows_before(value, start), value[at, :], marks[at, :], filters)
        chance = sigmoid(total)
        inputs = total * chance
        table = pltpu.roll(per_head[at, :], turn, 1)
        entering, leaving, size = (spread(table, s, heads, count) for s in (1, 2, 3))
        scaled = inputs * size
        low_scaled = scaled.astype(BF16)
        pulled = grad_out[at, :].astype(F32)
        keys, queries_t = maps[at, 0:states], maps_t[states:, pl.ds(start, SPAN)]
        memory_now = memory[b]
        grad_next = grad_memory[...]
        low_next = grad_next.astype(BF16)
        entered = (entering * pulled).astype(BF16)
        left = (leaving * scaled).astype(BF16)
        grad_maps[at, 0:states] += dot(left, low_next, NT)
        grad_maps[at, states:] += dot(entered, memory_now, NT)
        rising_rows = rows_in[0, pl.ds(pl.multiple_of(b * 8, 8), 8), :]
        crossed_t = cross_t[at, :]
        cross_sum = jnp.zeros((SPAN, SPAN), F32)
        parts = []
        for pair in range(count // 2):
            tile = pulled[:, pair * LANES : (pair + 1) * LANES]
            one = jnp.where(lane < LANES // 2, tile, 0.0).astype(BF16)
            two = jnp.where(lane < LANES // 2, 0.0, tile).astype(BF16)
            low_tile = low_scaled[:, pair * LANES : (pair + 1) * LANES]
            weights = []
            for j, masked in ((2 * pair, one), (2 * pair + 1, two)):
                gap = table[:, j : j + 1] - rising_rows[j : j + 1, :]
                cross_sum = cross_sum + jnp.exp2(jnp.minimum(gap, 0.0)) * dot(masked, low_tile, NT)
                weights.append((jnp.exp2(jnp.minimum(-gap, 0.0)) * crossed_t).astype(BF16))
            parts.append(dot(jnp.concatenate(weights, axis=1), jnp.concatenate([one, two], axis=0)))
        grad_cross[at, :] += cross_sum
        grad_within = jnp.concatenate(parts, axis=1)
        grad_left = dot(keys, low_next)
        grad_scaled = grad_within + leaving * grad_left
        scanned = mixed[at, :] - skip[...] * inputs
        kept = left.astype(F32) * grad_left
        rise = pulled * scanned - low_scaled.astype(F32) * grad_within - kept
        carried = entering[SPAN - 1 :] * jnp.sum(low_next.astype(F32) * memory_now.astype(F32), axis=0, keepdims=True)
        rise = rise + jnp.where(row == SPAN - 1, carried + jnp.sum(kept, axis=0, keepdims=True), 0.0)
        grown = grad_scaled * inputs
        summed = folded[at, :]
        for product, pick in ((rise, pick_rise), (grown, pick_size)):
            high = product.astype(BF16)
            rest = (product - high.astype(F32)).astype(BF16)
            summed = summed + dot(high, pick) + dot(rest, pick)
        folded[at, :] = summed
        grad_skip[...] += jnp.sum(pulled * inputs, axis=0, keepdims=True)
        grad_inputs = size * grad_scaled + skip[...] * pulled
        grad_total = grad_inputs * (chance * (1.0 + total * (1.0 - chance)))
        for k in range(4):
            grad_conv[k : k + 1] += jnp.sum(grad_total * shifted[k], axis=0, keepdims=True)
        grad_conv[4:5] += jnp.sum(grad_total, axis=0, keepdims=True)
        longer = jnp.concatenate([grad_total, later[...]], axis=0)
        later[...] = grad_total[:8]
        grad_value[at, :] = conv_back(longer, marks[pl.ds(start, SPAN + 8), :], filters).astype(BF16)
        grad_memory[...] = entering[SPAN - 1 :] * grad_next + dot(queries_t, entered)
        return 0

    lax.fori_loop(0, blocks, block, 0, unroll=UNROLL)


def finish_kernel(
    heads, calls, *refs,
):
    summed_parts, refs = refs[: 3 * calls], refs[3 * calls :]
    (per_head, marks, maps, seg_row, pre_state, conv_state, rate,
     grad_state, grad_step, grad_conv_state, grad_heads, later) = refs
    length = maps.shape[0]
    blocks = length // SPAN
    states = maps.shape[1] // 2
    later[...] = jnp.zeros_like(later)
    grad_conv_state[...] = jnp.zeros_like(grad_conv_state)
    grad_heads[...] = jnp.zeros_like(grad_heads)

    def block(i, _):
        start = pl.multiple_of((blocks - 1 - i) * SPAN, SPAN)
        at = pl.ds(start, SPAN)
        mark = marks[at, :]
        rows, cols = iota((SPAN, SPAN), 0), iota((SPAN, SPAN), 1)
        linked = (rows >= cols) & (mark[:, 6:7] == seg_row[0:1, pl.ds(start, SPAN)])
        grad_cross, summed, grad_maps = (
            functools.reduce(jnp.add, [ref[at, :] for ref in summed_parts[j::3]]) for j in range(3)
        )
        crossed = jnp.where(linked, grad_cross, 0.0)
        keys, queries = maps[at, 0:states], maps[at, states:]
        grad_keys = grad_maps[:, :states] + dot(crossed.T.astype(BF16), queries)
        grad_queries = grad_maps[:, states:] + dot(crossed.astype(BF16), keys)
        filters = conv_state[...]
        total, shifted = conv_taps(rows_before(pre_state, start), pre_state[at, :], mark, filters)
        chance = sigmoid(total)
        grad_total = jnp.concatenate([grad_keys, grad_queries], axis=1) * (chance * (1.0 + total * (1.0 - chance)))
        for k in range(4):
            grad_conv_state[k : k + 1] += jnp.sum(grad_total * shifted[k], axis=0, keepdims=True)
        grad_conv_state[4:5] += jnp.sum(grad_total, axis=0, keepdims=True)
        longer = jnp.concatenate([grad_total, later[...]], axis=0)
        later[...] = grad_total[:8]
        grad_state[at, :] = conv_back(longer, marks[pl.ds(start, SPAN + 8), :], filters).astype(BF16)

        table = per_head[at, :]
        grad_decay = dot(tri(True), summed, precision=HIGHEST)
        size = pltpu.roll(table, LANES - 3 * heads, 1)
        pre = pltpu.roll(table, LANES - 4 * heads, 1)
        grad_size = pltpu.roll(summed, LANES - heads, 1) - rate[...] * grad_decay
        valid = iota((SPAN, LANES), 1) < heads
        grad_pre = jnp.where(valid, grad_size * sigmoid(pre), 0.0)
        grad_step[at, :] = grad_pre.astype(BF16)
        grad_heads[0:1] += jnp.sum(grad_pre, axis=0, keepdims=True)
        grad_heads[1:2] += jnp.sum(-rate[...] * size * grad_decay, axis=0, keepdims=True)
        return 0

    lax.fori_loop(0, blocks, block, 0, unroll=UNROLL)


def output_kernel(chunks, rank, *refs):
    mixed, w_out, out = refs[:chunks], refs[chunks], refs[chunks + 1]
    size = mixed[0].shape[1]
    total = dot(mixed[0][...], w_out[:size])
    for c in range(1, chunks):
        total = total + dot(mixed[c][...], w_out[c * size : (c + 1) * size])
    out[0] = total.astype(BF16)


def normed_kernel(chunks, rank, *refs):
    grads, (grad_state, grad_step, w_inner, w_state, w_step, out) = refs[: 2 * chunks], refs[2 * chunks :]
    total = dot(grad_state[...], w_state[...], NT) + dot(grad_step[...], w_step[...], NT)
    at = 0
    for part in grads:
        size = part.shape[1]
        total = total + dot(part[...], w_inner[:, at : at + size], NT)
        at += size
    out[0] = total.astype(BF16)


def swap(array, axis, mask):
    count = lax.axis_size(axis)
    return lax.ppermute(array, axis, [(i, i ^ mask) for i in range(count)])


def gather_pieces(own, parts):
    pieces = {0: own}
    bit = parts // 2
    while bit >= 1:
        pieces.update({k | bit: swap(piece, "tensor", bit) for k, piece in list(pieces.items())})
        bit //= 2
    return [pieces[k] for k in range(parts)]


def tie(array, *first):
    return lax.optimization_barrier((array, *first))[0]


def meet(sums, *arrays):
    arrays = lax.optimization_barrier((*arrays, *(part.got for part in sums)))
    for part, got in zip(sums, arrays[len(arrays) - len(sums) :]):
        part.got = got
    return arrays[: len(arrays) - len(sums)]


def sum_all(array, axis):
    bit = 1
    while bit < lax.axis_size(axis):
        array = array + swap(array, axis, bit)
        bit *= 2
    return array


def rest_masks(low_bits):
    bits = (lax.axis_size("dp") - 1).bit_length()
    return [1 << bit for bit in (*range(low_bits + 1, bits), *range(low_bits - 1, -1, -1))]


def turned(index, bits):
    result = index * 0
    for bit in range(bits):
        result = result | (((index >> bit) & 1) << (bits - 1 - bit))
    return result


class Sum:
    def __init__(self, own, got, dim, low_bits):
        self.terms, self.got, self.dim, self.masks = [own], got, dim, rest_masks(low_bits)

    def advance(self):
        self.terms.append(self.got)
        mask = self.masks.pop(0)
        top = (lax.axis_index("dp") & mask) // mask
        size = self.terms[0].shape[self.dim] // 2

        def cut(half):
            return [lax.dynamic_slice_in_dim(term, half * size, size, self.dim) for term in self.terms]

        sent = functools.reduce(jnp.add, [term.astype(F32) for term in cut(1 - top)]).astype(BF16)
        self.terms, self.got = cut(top), swap(sent, "dp", mask)
        return sent

    def result(self):
        while self.masks:
            self.advance()
        return functools.reduce(jnp.add, [term.astype(F32) for term in (*self.terms, self.got)])


def add_low(left, right):
    return (left.astype(F32) + right.astype(F32)).astype(BF16)


def shards(
    tokens,
    cotangent,
    doc_lengths,
    norm_gain,
    w_inner,
    w_step,
    w_state,
    conv_inner,
    conv_state,
    step_bias,
    log_rate,
    skip_gain,
    gate_gain,
    w_out,
):
    parts = lax.axis_size("tensor")
    groups = lax.axis_size("dp")
    rank = lax.axis_index("tensor").astype(jnp.int32)
    ranks = rank.reshape(1)
    length, quarter = tokens.shape
    width = quarter * parts
    channels = w_inner.shape[2]
    heads = w_step.shape[1]
    states2 = w_state.shape[1]
    states = states2 // 2
    blocks = length // SPAN
    steps = channels // GROUP
    repeat = LANES // heads
    piece_rows = width // groups
    low_bits = 0
    while (piece_rows << low_bits) < LANES:
        low_bits += 1
    run = piece_rows << low_bits
    half_width = width // 2
    high_bits = (groups - 1).bit_length() - 1 - low_bits
    place = ((lax.axis_index("dp") >> low_bits) & 1).astype(jnp.int32).reshape(1)

    token_y = swap(tokens, "tensor", 2)
    grad_y = swap(tie(cotangent, token_y), "tensor", 2)
    flat = w_inner.reshape(width, 2 * channels)
    w_maps = jnp.concatenate([w_state, jnp.tile(w_step, (1, repeat))], axis=1)
    step_pad = jnp.pad(w_step, ((0, 0), (0, LANES - heads)))
    bias8 = jnp.tile(step_bias, repeat)[None, :]
    rate8 = jnp.exp(jnp.tile(log_rate, repeat))[None, :]
    skip_row = jnp.repeat(skip_gain, channels // heads)[None, :]
    gain_row = gate_gain[None, :]
    conv_pad = jnp.pad(conv_inner, ((0, 3), (0, 0)))
    conv_state_pad = jnp.pad(conv_state, ((0, 3), (0, 0)))

    doc_ends = jnp.cumsum(doc_lengths[0])
    positions = jnp.arange(length, dtype=jnp.int32)
    segment = jnp.sum((positions[:, None] >= doc_ends[None, :]).astype(jnp.int32), axis=1)
    present = positions < doc_ends[-1]
    by_block = segment.reshape(blocks, SPAN)
    final = by_block[:, -1:]
    before = jnp.concatenate([jnp.full((1, 1), -1, jnp.int32), final[:-1]], axis=0)
    marks = [
        jnp.concatenate([jnp.full((k,), -1, jnp.int32), segment[:-k]]) == segment for k in (1, 2, 3)
    ]
    marks += [(by_block == before).reshape(-1), (by_block == final).reshape(-1), present]
    marks = [mark.astype(F32) for mark in marks] + [segment.astype(F32)]
    marks = jnp.pad(jnp.stack(marks, axis=1), ((0, 8), (0, LANES - len(marks))))
    seg_row = jnp.broadcast_to(segment.astype(F32)[None, :], (8, length))

    token_y, flat, w_maps, step_pad, marks, seg_row, skip_row, conv_pad = lax.optimization_barrier(
        (token_y, flat, w_maps, step_pad, marks, seg_row, skip_row, conv_pad)
    )
    token_pieces = [tokens, swap(tokens, "tensor", 1), token_y, swap(token_y, "tensor", 1)]

    by_group = lambda rows: pl.BlockSpec((rows, GROUP), lambda g, *_: (0, g))
    (normed, pre_state, maps, maps_t, per_head, rising_rows, cross_t, value, gate, mixer_out, low_gated, memory, squares) = call(
        functools.partial(front_kernel, parts, heads),
        (steps,),
        [held((length, quarter))] * parts
        + [
            held((1, width)), held((width, states2 + LANES)), held((8, states2)),
            held((1, LANES)), held((1, LANES)), held((8, length)),
            pl.BlockSpec((width, GROUP), lambda g, *_: (0, g)), pl.BlockSpec((width, GROUP), lambda g, *_: (0, steps + g)),
            by_group(8), by_group(1), held((length + 8, LANES)),
        ],
        [
            held((length, width)), held((length, states2)), held((length, states2)), held((states2, length)),
            held((length, LANES)), held((steps, blocks * 8, SPAN)), held((length, SPAN)),
            by_group(length), by_group(length), by_group(length), by_group(length),
            pl.BlockSpec((blocks, states, GROUP), lambda g, *_: (0, 0, g)), held((length, LANES)),
        ],
        [
            shape_of(length, width, dtype=BF16), shape_of(length, states2), shape_of(length, states2, dtype=BF16),
            shape_of(states2, length, dtype=BF16), shape_of(length, LANES), shape_of(steps, blocks * 8, SPAN),
            shape_of(length, SPAN), shape_of(length, channels), shape_of(length, channels, dtype=BF16),
            shape_of(length, channels), shape_of(length, channels, dtype=BF16),
            shape_of(blocks, states, channels, dtype=BF16), shape_of(length, LANES),
        ],
        [
            pltpu.VMEM((length, states2 + LANES), F32), pltpu.VMEM((length, SPAN), F32),
            pltpu.VMEM((states, GROUP), F32),
        ],
        prefetch=1,
        flops=8 * length * width * channels,
        moved=length * width * 4 + width * channels * 4 + length * channels * 14,
        name="front",
        vmem=56,
    )(
        ranks, *token_pieces, norm_gain[None, :], w_maps, conv_state_pad, bias8, rate8, seg_row, flat, flat, conv_pad,
        skip_row, marks,
    )

    grad_y = tie(grad_y, squares)
    grad_pieces = [cotangent, swap(cotangent, "tensor", 1), grad_y, swap(grad_y, "tensor", 1)]
    pieces_any = [pl.BlockSpec(memory_space=pl.ANY)] * parts
    double = 2 * GROUP
    by_double = lambda rows: pl.BlockSpec((rows, double), lambda g, *_: (0, g))
    grad_mixed, stats = call(
        functools.partial(cotangent_kernel, parts),
        (channels // double,),
        pieces_any
        + [
            pl.BlockSpec((double, width), lambda g, *_: (g, 0)),
            by_double(length), by_double(1), held((length, LANES)),
        ],
        [by_double(length), held((8, length))],
        [shape_of(length, channels, dtype=BF16), shape_of(8, length)],
        [pltpu.VMEM((length, LANES), F32), pltpu.VMEM((length, width), BF16), pltpu.SemaphoreType.DMA((parts,))],
        prefetch=1,
        flops=2 * length * width * channels,
        moved=length * width * 2 + width * channels * 2 + length * channels * 12,
        name="cotangent",
        vmem=56,
    )(ranks, *grad_pieces, w_out, low_gated, gain_row, squares)
    stats = sum_all(stats, "tensor")

    spans = steps // CHUNKS

    def chunk_spec(rows, c):
        return pl.BlockSpec((rows, GROUP), lambda g, *_: (0, c * spans + g))

    def gate_part(c, stats):
        size = spans * GROUP
        by_channel = pl.BlockSpec((GROUP, half_width), lambda g, *_: (g, 0))
        return call(
            functools.partial(gate_kernel, parts, run, channels * parts),
            (spans,),
            pieces_any
            + [
                chunk_spec(length, c), chunk_spec(length, c), chunk_spec(length, c), chunk_spec(1, c),
                held((8, length)), held((length + 8, LANES)),
            ],
            [by_group(length), by_group(length), by_group(length), by_group(1), by_channel, by_channel],
            [
                shape_of(length, size, dtype=BF16), shape_of(length, size, dtype=BF16),
                shape_of(length, size, dtype=BF16), shape_of(1, size),
                shape_of(size, half_width, dtype=BF16), shape_of(size, half_width, dtype=BF16),
            ],
            [
                pltpu.VMEM((length, half_width), BF16), pltpu.VMEM((length, half_width), BF16),
                pltpu.SemaphoreType.DMA((half_width // run,)),
            ],
            prefetch=2,
            flops=2 * length * width * size,
            moved=length * width * 2 + length * size * 18 + width * size * 2,
            name="gate",
            vmem=56,
        )(place, ranks, *grad_pieces, grad_mixed, gate, mixer_out, gain_row, stats, marks)

    def weight_part(*right):
        runs = half_width // run
        columns = [part.shape[1] for part in right]
        outs = [pl.BlockSpec((run, size), lambda j, p: (turned(j, (runs - 1).bit_length()), 0)) for size in columns]
        shapes = [shape_of(half_width, size, dtype=BF16) for size in columns]
        result = call(
            weight_kernel,
            (runs,),
            [
                pl.BlockSpec((length, run), lambda j, p: (0, 2 * j + (p[0] ^ 1))),
                pl.BlockSpec((length, run), lambda j, p: (0, 2 * j + p[0])),
            ]
            + [held((length, size)) for size in columns],
            outs + outs,
            shapes + shapes,
            prefetch=1,
            flops=2 * length * width * sum(columns),
            moved=length * width * 2 + length * sum(columns) * 2 + width * sum(columns) * 2,
            name="weights",
        )(place, normed, normed, *right)
        return result[: len(columns)], result[len(columns) :]

    all_lanes = held((length, LANES))

    def backward_part(c, grad_out):
        size = spans * GROUP
        return call(
            functools.partial(backward_kernel, heads, c * spans),
            (spans,),
            [
                chunk_spec(length, c), by_group(length), chunk_spec(length, c),
                pl.BlockSpec((blocks, states, GROUP), lambda g, *_: (0, 0, c * spans + g)),
                chunk_spec(8, c), chunk_spec(1, c), all_lanes, held((length + 8, LANES)),
                pl.BlockSpec((1, blocks * 8, SPAN), lambda g, *_: (c * spans + g, 0, 0)),
                held((length, states2)), held((states2, length)), held((length, SPAN)),
            ],
            [by_group(length), by_group(8), by_group(1), held((length, SPAN)), all_lanes, held((length, states2))],
            [
                shape_of(length, size, dtype=BF16), shape_of(8, size), shape_of(1, size),
                shape_of(length, SPAN), shape_of(length, LANES), shape_of(length, states2),
            ],
            [pltpu.VMEM((8, GROUP), F32), pltpu.VMEM((states, GROUP), F32)],
            flops=40e9 / CHUNKS,
            moved=length * size * 14,
            name="backward",
            vmem=56,
        )(
            value, grad_out, mixer_out, memory, conv_pad, skip_row, per_head, marks, rising_rows, maps, maps_t,
            cross_t,
        )

    def output_part(ks, mixed):
        return call(
            functools.partial(output_kernel, len(mixed)),
            (len(ks), quarter // 256),
            [held((length, mixed[0].shape[1]))] * len(mixed)
            + [
                pl.BlockSpec(
                    (channels, 256),
                    lambda i, j, r: (0, (r[0] ^ (ks[0] + i * (ks[-1] - ks[0]))) * (quarter // 256) + j),
                ),
            ],
            pl.BlockSpec((1, length, 256), lambda i, j, r: (i, 0, j)),
            shape_of(len(ks), length, quarter, dtype=BF16),
            prefetch=1,
            flops=2 * length * channels * quarter * len(ks),
            moved=length * channels * 2 + channels * quarter * 2 * len(ks) + length * quarter * 2 * len(ks),
            name="output",
        )(ranks, *mixed, w_out)

    def normed_part(ks, grad_gate, grad_value):
        def row(i, j, r):
            return (r[0] ^ (ks[0] + i * (ks[-1] - ks[0]))) * (quarter // 256) + j

        return call(
            functools.partial(normed_kernel, len(grad_gate)),
            (len(ks), quarter // 256),
            [held((length, part.shape[1])) for part in (*grad_gate, *grad_value)]
            + [
                held((length, states2)), held((length, LANES)),
                pl.BlockSpec((256, 2 * channels), lambda i, j, r: (row(i, j, r), 0)),
                pl.BlockSpec((256, states2), lambda i, j, r: (row(i, j, r), 0)),
                pl.BlockSpec((256, LANES), lambda i, j, r: (row(i, j, r), 0)),
            ],
            pl.BlockSpec((1, length, 256), lambda i, j, r: (i, 0, j)),
            shape_of(len(ks), length, quarter, dtype=BF16),
            prefetch=1,
            flops=2 * length * (2 * channels + states2 + LANES) * quarter * len(ks),
            moved=length * channels * 4 + channels * quarter * 4 * len(ks) + length * quarter * 2 * len(ks),
            name="normed_grad",
        )(ranks, *grad_gate, *grad_value, grad_state, grad_step, flat, w_state, step_pad)

    def over_x(send):
        return swap(send, "dp", 1 << low_bits)

    chunks = range(CHUNKS)
    gates, sum_out = [], []
    last = stats
    for c in chunks:
        gates.append(gate_part(c, tie(stats, last)))
        sum_out.append(Sum(gates[c][5], over_x(gates[c][4]), 1, low_bits))
        last = gates[c][5]
    low_mixed, grad_mixer, grad_gate, grad_gain, _, _ = zip(*gates)
    gate_send, gate_own = weight_part(tie(grad_gate[0], last), *grad_gate[1:])
    out_far = output_part((1, 3), [tie(low_mixed[0], gate_send[0]), *low_mixed[1:]])

    out_far, send = meet(sum_out[:1], out_far, gate_send[0])
    sum_gate = [Sum(gate_own[0], over_x(send), 0, low_bits)]
    out_far_got = swap(out_far, "tensor", 1)
    moved = [sum_out[0].advance(), out_far, send]
    out_near = output_part((2, 0), [tie(low_mixed[0], *moved), *low_mixed[1:]])
    back = backward_part(0, tie(grad_mixer[0], out_near))
    (value_send,), (value_own,) = weight_part(back[0])

    value_own, out_far_got, send = meet(sum_out, value_own, out_far_got, gate_send[1])
    sum_gate.append(Sum(gate_own[1], over_x(send), 0, low_bits))
    out_sum = add_low(out_near[0], out_far_got[1])
    out_y = swap(out_sum, "tensor", 2)
    moved = [sum_out[0].advance(), sum_out[1].advance(), out_sum, send, value_own]
    backs = [back, backward_part(1, tie(grad_mixer[1], *moved))]
    (value_send2,), (value_own2,) = weight_part(backs[1][0])

    value_own2, out_y, value_send = meet([*sum_out, sum_gate[0]], value_own2, out_y, value_send)
    sum_value = [Sum(value_own, over_x(value_send), 0, low_bits)]
    moved = [sum_gate[0].advance(), sum_out[1].advance(), value_send, value_own2]
    grad_value, grad_conv, grad_skip, cross_parts, folded_parts, maps_parts = zip(*backs)
    (grad_state, grad_step, grad_conv_state, grad_heads) = call(
        functools.partial(finish_kernel, heads, CHUNKS),
        (1,),
        [held((length, SPAN)), all_lanes, held((length, states2))] * CHUNKS
        + [
            all_lanes, held((length + 8, LANES)), held((length, states2)), held((8, length)),
            held((length, states2)), held((8, states2)), held((1, LANES)),
        ],
        [held((length, states2)), all_lanes, held((8, states2)), held((8, LANES))],
        [
            shape_of(length, states2, dtype=BF16), shape_of(length, LANES, dtype=BF16),
            shape_of(8, states2), shape_of(8, LANES),
        ],
        [pltpu.VMEM((8, states2), F32)],
        flops=4e9,
        moved=length * 2048 * CHUNKS + length * 5000,
        name="finish",
        vmem=56,
    )(
        tie(cross_parts[0], *moved), folded_parts[0], maps_parts[0],
        *[part for three in zip(cross_parts[1:], folded_parts[1:], maps_parts[1:]) for part in three],
        per_head, marks, maps, seg_row, pre_state, conv_state_pad, rate8,
    )


    grad_state, value_send2 = meet(sum_gate, grad_state, value_send2)
    sum_value.append(Sum(value_own2, over_x(value_send2), 0, low_bits))
    state_got = swap(grad_state, "tensor", 1)
    total_out = [sum_out[0].result()]
    moved = [sum_gate[0].advance(), sum_gate[1].advance(), total_out[0], value_send2]
    near_far = normed_part((1, 3), [tie(grad_gate[0], *moved), *grad_gate[1:]], grad_value)

    near_far, state_got = meet(sum_out[1:], near_far, state_got)
    state_sum = add_low(grad_state, state_got)
    state_got = swap(state_sum, "tensor", 2)
    near_far_got = swap(near_far, "tensor", 1)
    total_out.append(sum_out[1].result())
    near = normed_part((2, 0), [tie(grad_gate[0], near_far, state_sum, total_out[1]), *grad_gate[1:]], grad_value)

    near, near_far_got, state_got = meet(sum_gate, near, near_far_got, state_got)
    near_sum = add_low(near[0], near_far_got[1])
    over_y = swap(near_sum, "tensor", 2)
    total_gate = [sum_gate[0].result()]
    moved = [sum_gate[1].advance()]
    state_all = tie(add_low(state_sum, state_got), near_sum, *total_gate, *moved)
    grad_step, norm_gain, grad_conv_state, grad_heads, normed = lax.optimization_barrier(
        (grad_step, norm_gain, grad_conv_state, grad_heads, normed, state_all)
    )[:-1]

    branch = out_near[1].astype(F32) + out_far_got[0].astype(F32) + out_y.astype(F32)
    own_tokens = tokens.astype(F32)
    output = (own_tokens + branch).astype(BF16)

    grad_w_state = dot(normed, state_all, TN).astype(BF16)
    own_rows = piece_rows // parts
    grad_w_state = lax.dynamic_slice_in_dim(
        grad_w_state.reshape(groups, parts, own_rows, states2), rank, 1, axis=1
    )
    grad_w_step = dot(grad_step[:, :heads], normed, TN).astype(BF16)
    grad_w_step = grad_w_step.reshape(heads, groups, piece_rows).transpose(1, 0, 2)
    small = jnp.concatenate(
        [grad_w_state.reshape(groups, own_rows * states2), grad_w_step.reshape(groups, heads * piece_rows)], axis=1
    ).reshape(groups // (2 << low_bits), 2, 1 << low_bits, -1)
    small = jnp.stack([small[turned(j, high_bits)] for j in range(small.shape[0])])
    small_own = lax.dynamic_slice_in_dim(small, place[0], 1, 1).reshape(groups // 2, -1)
    small_send = lax.dynamic_slice_in_dim(small, 1 - place[0], 1, 1).reshape(groups // 2, -1)
    small_sum = Sum(small_own, over_x(small_send), 0, low_bits)
    (small_send,) = meet([*sum_value[:1], *sum_gate[1:]], small_send)
    total_gate.append(sum_gate[1].result())
    moved = [sum_value[0].advance(), total_gate[1], small_send]
    over_y, *_ = meet([*sum_value, small_sum], over_y, *moved)
    moved = [sum_value[1].advance(), sum_value[0].advance(), small_sum.advance()]
    grad_normed = near[1].astype(F32) + near_far_got[0].astype(F32) + over_y.astype(F32)
    own_gain = lax.dynamic_slice_in_dim(norm_gain, rank * quarter, quarter, 0)
    scale_in = per_head[:, 5 * heads : 5 * heads + 1]
    row_norm = sum_all(jnp.sum(own_tokens * own_gain * grad_normed, axis=1), "tensor")
    grad_tokens = (
        cotangent.astype(F32)
        + scale_in * own_gain * grad_normed
        - own_tokens * scale_in**3 * row_norm[:, None] / width
    ).astype(BF16)
    grad_norm_gain = jnp.sum(grad_normed * own_tokens * scale_in, axis=0)

    moved = meet([sum_value[1], small_sum], grad_tokens, *moved)
    grad_tokens = moved[0]
    moved = [sum_value[1].advance(), small_sum.advance()]
    small_sum = small_sum.result()[0]
    sum_state = small_sum[: own_rows * states2].reshape(own_rows, states2)
    sum_step = small_sum[own_rows * states2 :].reshape(heads, piece_rows).T

    total_value = [part.result() for part in sum_value]
    sum_out = jnp.concatenate(total_out, axis=0)
    sum_gate = jnp.concatenate(total_gate, axis=1)
    sum_value = jnp.concatenate(total_value, axis=1)
    sum_inner = jnp.stack([sum_gate, sum_value], axis=1)

    grad_conv, grad_skip, grad_gate_gain = (
        jnp.concatenate(array, axis=1) for array in (grad_conv, grad_skip, grad_gain)
    )
    grad_conv_state = sum_all(grad_conv_state[:5], "tensor")
    skip_sums = jnp.sum(grad_skip.reshape(heads, channels // heads), axis=1)
    pack = [
        grad_norm_gain, grad_conv[:5].reshape(-1), grad_conv_state.reshape(-1),
        grad_heads[0, :heads], grad_heads[1, :heads], skip_sums, grad_gate_gain[0],
    ]
    sums_all = sum_all(jnp.concatenate(pack), "dp")
    split = []
    at = 0
    for piece in pack:
        split.append(sums_all[at : at + piece.shape[0]])
        at += piece.shape[0]
    return (
        output,
        grad_tokens,
        split[0],
        sum_inner,
        sum_step,
        sum_state,
        split[1].reshape(5, channels),
        split[2].reshape(5, states2),
        split[3],
        split[4],
        split[5],
        split[6],
        sum_out,
    )


def solution(mesh):
    placed = (
        P("dp", "tensor"),
        P("dp", "tensor"),
        P("dp", None),
        P(),
        P(None, None, "tensor"),
        P(None, "tensor"),
        P(),
        P(None, "tensor"),
        P(),
        P("tensor"),
        P("tensor"),
        P("tensor"),
        P("tensor"),
        P("tensor", None),
    )
    return jax.shard_map(
        shards,
        mesh=mesh,
        in_specs=placed,
        out_specs=(
            P("dp", "tensor"),
            P("dp", "tensor"),
            P("tensor"),
            P("dp", None, "tensor"),
            P("dp", "tensor"),
            P(("dp", "tensor"), None),
            P(None, "tensor"),
            P(),
            P("tensor"),
            P("tensor"),
            P("tensor"),
            P("tensor"),
            P("tensor", "dp"),
        ),
        check_vma=False,
    )
```

time: 470 us -> 362 us (0.77)
  waiting for transfers between devices: 163 us -> 48.1 us
  other arithmetic: 35 us -> 57.9 us
  local copies, waits for them, and re-layouts: 43.9 us -> 36 us
    ppermute x37 -> x42, waiting for transfers between devices: 163 us -> 48.1 us  [swap(): return lax.ppermute(array, axis, [(i, i ^ mask) for i in range(count)])]
    convert_element_type x7 -> x19, other arithmetic: 14.3 us -> 27.2 us  [the longest x14 22.3 us: advance(): functools.reduce(jnp.add, [term.astype(F32) for term in cut(1 - top)])]
    add x2 -> x7, other arithmetic: 3.22 us -> 10.3 us  [result(): functools.reduce(jnp.add, [term.astype(F32) for term in (*self.terms, sel...]
    dynamic_update_slice x4 -> x0, local copies, waits for them, and re-layouts: 7.02 us -> none  [shards(): lax.dynamic_update_slice(full_grad, grad_pieces[k], (0, (rank ^ k) * quar...]
    pallas_call x11 -> x14, Pallas kernels: 174 us -> 170 us  [the longest x1 36.1 us: shards(): call(functools.partial(front_kernel, parts, heads), (steps,), [held((leng...]
    unnamed x56 -> x103, local copies, waits for them, and re-layouts: 14.8 us -> 18.5 us
    ppermute x37 -> x42, starting transfers between devices: 38.8 us -> 40.2 us  [swap(): return lax.ppermute(array, axis, [(i, i ^ mask) for i in range(count)])]
  transfers between devices with their start and end apart: 37 -> 42, of which waited for: 12 -> 11; matrix products, arithmetic and copies ran while one was open for 16% -> 23% of each run, Pallas kernels for 32% -> 40%
where the time goes in v2:
time: 362 us; the launch traced here: 357 us
  Pallas kernels  170 us (47%)
  other arithmetic  57.9 us (16%)
  waiting for transfers between devices  48.1 us (13%)
  starting transfers between devices  40.2 us (11%)
  local copies, waits for them, and re-layouts  36 us (10%)
    ppermute x42, waiting for transfers between devices, swap(): return lax.ppermute(array, axis, [(i, i ^ mask) for i in range(count)])  48.1 us
    ppermute x42, starting transfers between devices, swap(): return lax.ppermute(array, axis, [(i, i ^ mask) for i in range(count)])  40.2 us
    pallas_call x1, Pallas kernels, shards(): call(functools.partial(front_kernel, parts, heads), (steps,), [held((leng...  36.1 us
    pallas_call x2, Pallas kernels, backward_part(): call(functools.partial(backward_kernel, heads, c * spans), (spans,), [chu...  33.8 us
    pallas_call x2, Pallas kernels, gate_part(): call(functools.partial(gate_kernel, parts, run, channels * parts), (spans...  27.3 us
    convert_element_type x14, other arithmetic, advance(): functools.reduce(jnp.add, [term.astype(F32) for term in cut(1 - top)])  22.3 us
    pallas_call x3, Pallas kernels, weight_part(): call(weight_kernel, (runs,), [pl.BlockSpec((length, run), lambda j, p: (0...  20.3 us
    pallas_call x2, Pallas kernels, normed_part(): call(functools.partial(normed_kernel, len(grad_gate)), (len(ks), quarter...  20.3 us
  transfers between devices with their start and end apart: 42, of which 11 were waited for; matrix products, arithmetic and copies ran while one was open for 23% of the time, Pallas kernels for 40%

profile of v2, /device:TPU:0, one launch (start us, length us, event | category | flops | bytes accessed | tf_op | source)
XLA Modules:
  0.0 356.5 jit_solution(15828137216411035381)
XLA Ops:
  0.6 3.0 collective-permute-start.1
  6.9 10.3 %copy.70 = bf16[256,8,2,1024]{3,1,2,0:T(8,128)(2,1)} copy(bf16[256,8,2,1024]{3,2,1,0:T(2,128)(2,1)} %bitcast.88) | data formatting | bytes 16777216
  22.3 4.9 %collective-permute-done.1.refs_2_ = bf16[1024,512]{1,0:T(8,128)(2,1)} collective-permute-done((bf16[1024,512]{1,0:T(8,128)(2,1)}, bf16[1024,512]{1,0:T(8,128)(2,1)}, u32[]{:S(2)}, u32[]{:S(2)}) %collective-permute-start.1) | collective-permute-done | bytes 1048608 | tf_op jit(solution)/shard_map/ppermute | solution.py:500
  27.8 1.7 collective-permute-start.2
  31.6 36.1 %front.1 = (bf16[1024,2048]{1,0:T(8,128)(2,1)}, f32[1024,256]{1,0:T(8,128)}, bf16[1024,256]{1,0:T(8,128)(2,1)}, bf16[256,1024]{1,0:T(8,128)(2,1)}, f32[1024,128]...) custom-call(s32[1]{0:T(128)} %bitcast.rank, ...), custom_call_target="tpu_custom_call" | custom-call | flops 343597376 | bytes 629145 | tf_op jit(solution)/shard_map/front/pallas_call | solution.py:641
  68.0 2.4 collective-permute-done.5.refs_3_
  71.4 12.7 %cotangent.1 = (bf16[1024,1024]{1,0:T(8,128)(2,1)}, f32[8,1024]{1,0:T(8,128)}) custom-call(s32[1]{0:T(128)} %bitcast.rank, bf16[1024,512]{1,0:T(8,128)(2,1)} %refs_0_.7, bf16[1024,512]{1,0:T(8,128)(2,1)} %copy-done.8, bf16[1024,512]{1,0:T(8,128)(2,1)} %copy-done.7, bf16[1024,512]{1,0:T(8,128)(2,1)} %copy-done.9, bf16[1024,2048]{1,0:T(8,128)(2,1)} %refs_2_.3, ...), custom_call_target="tpu_custom_call" | custom-call | flops 85899344 | bytes 419430 | tf_op jit(solution)/shard_map/cotangent/pallas_call | solution.py:683
  87.3 3.0 collective-permute-done.7
  90.9 13.9 %gate.2 = (bf16[1024,512]{1,0:T(8,128)(2,1)}, bf16[1024,512]{1,0:T(8,128)(2,1)}, bf16[1024,512]{1,0:T(8,128)(2,1)}, f32[1,512]{1,0:T(1,128)}, bf16[512,1024]{1,0:T(8,128)(2,1)}, /*index=5*/bf16[512,1024]{1,0:T(8,128)(2,1)}) custom-call(s32[1]{0:T(128)} %bitcast.1.place, s32[1]{0:T(128)} %bitcast.rank, bf16[1024,512]{1,0:T(8,128)(2,1)} %refs_0_.7, ...), custom_call_target="tpu_custom_call" | custom-call | flops 42949672 | bytes 314572 | tf_op jit(solution)/shard_map/gate/pallas_call | solution.py:710
  104.8 1.6 collective-permute-start.8
  106.4 13.4 %gate.3 = (bf16[1024,512]{1,0:T(8,128)(2,1)}, bf16[1024,512]{1,0:T(8,128)(2,1)}, bf16[1024,512]{1,0:T(8,128)(2,1)}, f32[1,512]{1,0:T(1,128)}, bf16[512,1024]{1,0:T(8,128)(2,1)}, /*index=5*/bf16[512,1024]{1,0:T(8,128)(2,1)}) custom-call(s32[1]{0:T(128)} %bitcast.1.place, s32[1]{0:T(128)} %bitcast.rank, bf16[1024,512]{1,0:T(8,128)(2,1)} %refs_0_.7, ...), custom_call_target="tpu_custom_call" | custom-call | flops 42949672 | bytes 314572 | tf_op jit(solution)/shard_map/gate/pallas_call | solution.py:710
  119.8 7.9 %weights.3 = (bf16[1024,512]{1,0:T(8,128)(2,1)}, bf16[1024,512]{1,0:T(8,128)(2,1)}, bf16[1024,512]{1,0:T(8,128)(2,1)}, bf16[1024,512]{1,0:T(8,128)(2,1)}) custom-call(s32[1]{0:T(128)} %bitcast.1.place, bf16[1024,2048]{1,0:T(8,128)(2,1)} %get-tuple-element.218.left_send.left_own, bf16[1024,2048]{1,0:T(8,128)(2,1)} %get-tuple-element.218.left_send.left_own, ...), custom_call_target="tpu_custom_call" | custom-call | flops 85899344 | bytes 209715 | tf_op jit(solution)/shard_map/weights/pallas_call | solution.py:740
  127.7 6.0 %output.2 = bf16[2,1024,512]{2,1,0:T(8,128)(2,1)} custom-call(s32[1]{0:T(128)} %bitcast.rank, bf16[1024,512]{1,0:T(8,128)(2,1)} %get-tuple-element.156.refs_0_, bf16[1024,512]{1,0:T(8,128)(2,1)} %get-tuple-element.151.refs_1_, bf16[1024,2048]{1,0:T(8,128)(2,1)} %refs_2_.3), custom_call_target="tpu_custom_call" | custom-call | flops 42949672 | bytes 125829 | tf_op jit(solution)/shard_map/output/pallas_call | solution.py:787
  136.6 1.6 collective-permute-start.10
  139.7 6.0 %output.3 = bf16[2,1024,512]{2,1,0:T(8,128)(2,1)} custom-call(s32[1]{0:T(128)} %bitcast.rank, bf16[1024,512]{1,0:T(8,128)(2,1)} %get-tuple-element.156.refs_0_, bf16[1024,512]{1,0:T(8,128)(2,1)} %get-tuple-element.151.refs_1_, bf16[1024,2048]{1,0:T(8,128)(2,1)} %refs_2_.3), custom_call_target="tpu_custom_call" | custom-call | flops 42949672 | bytes 125829 | tf_op jit(solution)/shard_map/output/pallas_call | solution.py:787
  145.7 16.9 %backward.2 = (bf16[1024,512]{1,0:T(8,128)(2,1)}, f32[8,512]{1,0:T(8,128)}, f32[1,512]{1,0:T(1,128)}, f32[1024,128]{1,0:T(8,128)}, f32[1024,128]{1,0:T(8,128)}, /*index=5*/f32[1024,256]{1,0:T(8,128)}) custom-call(f32[1024,1024]{1,0:T(8,128)} %get-tuple-element.157.value, bf16[1024,512]{1,0:T(8,128)(2,1)} %get-tuple-element.159.grad_out, ...), custom_call_target="tpu_custom_call" | custom-call | flops 400000000 | bytes 146800 | tf_op jit(solution)/shard_map/backward/pallas_call | solution.py:761
  162.7 6.2 %weights.4 = (bf16[1024,512]{1,0:T(8,128)(2,1)}, bf16[1024,512]{1,0:T(8,128)(2,1)}) custom-call(s32[1]{0:T(128)} %bitcast.1.place, bf16[1024,2048]{1,0:T(8,128)(2,1)} %get-tuple-element.218.left_send.left_own, bf16[1024,2048]{1,0:T(8,128)(2,1)} %get-tuple-element.218.left_send.left_own, bf16[1024,512]{1,0:T(8,128)(2,1)} %get-tuple-element.166.refs_0_.refs_2_), custom_call_target="tpu_custom_call" | custom-call | flops 42949672 | bytes 146800 | tf_op jit(solution)/shard_map/weights/pallas_call | solution.py:740
  172.1 2.0 add_convert_fusion.8
  176.6 2.7 collective-permute-start.13
  179.3 16.8 %backward.3 = (bf16[1024,512]{1,0:T(8,128)(2,1)}, f32[8,512]{1,0:T(8,128)}, f32[1,512]{1,0:T(1,128)}, f32[1024,128]{1,0:T(8,128)}, f32[1024,128]{1,0:T(8,128)}, /*index=5*/f32[1024,256]{1,0:T(8,128)}) custom-call(f32[1024,1024]{1,0:T(8,128)} %get-tuple-element.157.value, bf16[1024,512]{1,0:T(8,128)(2,1)} %get-tuple-element.176.grad_out, ...), custom_call_target="tpu_custom_call" | custom-call | flops 400000000 | bytes 146800 | tf_op jit(solution)/shard_map/backward/pallas_call | solution.py:761
  196.1 6.2 %weights.5 = (bf16[1024,512]{1,0:T(8,128)(2,1)}, bf16[1024,512]{1,0:T(8,128)(2,1)}) custom-call(s32[1]{0:T(128)} %bitcast.1.place, bf16[1024,2048]{1,0:T(8,128)(2,1)} %get-tuple-element.218.left_send.left_own, bf16[1024,2048]{1,0:T(8,128)(2,1)} %get-tuple-element.218.left_send.left_own, bf16[1024,512]{1,0:T(8,128)(2,1)} %get-tuple-element.177.refs_0_.refs_3_), custom_call_target="tpu_custom_call" | custom-call | flops 42949672 | bytes 146800 | tf_op jit(solution)/shard_map/weights/pallas_call | solution.py:740
  202.4 1.6 add_convert_fusion.7
  204.0 1.7 collective-permute-start.16
  205.6 2.2 add_convert_fusion.14
  207.8 7.9 %finish.1 = (bf16[1024,256]{1,0:T(8,128)(2,1)}, bf16[1024,128]{1,0:T(8,128)(2,1)}, f32[8,256]{1,0:T(8,128)}, f32[8,128]{1,0:T(8,128)}) custom-call(f32[1024,128]{1,0:T(8,128)} %get-tuple-element.187.refs_0_, f32[1024,128]{1,0:T(8,128)} %get-tuple-element.188.refs_1_, f32[1024,256]{1,0:T(8,128)} %get-tuple-element.189.refs_2_, ...), custom_call_target="tpu_custom_call" | custom-call | flops 80000000 | bytes 186286 | tf_op jit(solution)/shard_map/finish/pallas_call | solution.py:861
  219.5 2.0 add_convert_fusion.6
  221.5 10.0 %normed_grad.2 = bf16[2,1024,512]{2,1,0:T(8,128)(2,1)} custom-call(s32[1]{0:T(128)} %bitcast.rank, bf16[1024,512]{1,0:T(8,128)(2,1)} %get-tuple-element.210.refs_0_, bf16[1024,512]{1,0:T(8,128)(2,1)} %get-tuple-element.148.refs_1_, bf16[1024,512]{1,0:T(8,128)(2,1)} %get-tuple-element.166.refs_0_.refs_2_, ...), custom_call_target="tpu_custom_call" | custom-call | flops 102005472 | bytes 209715 | tf_op jit(solution)/shard_map/normed_grad/pallas_call | solution.py:809
  239.1 2.5 collective-permute-start.22
  241.6 1.5 convert_add_fusion.5
  243.2 10.2 %normed_grad.3 = bf16[2,1024,512]{2,1,0:T(8,128)(2,1)} custom-call(s32[1]{0:T(128)} %bitcast.rank, bf16[1024,512]{1,0:T(8,128)(2,1)} %get-tuple-element.210.refs_0_, bf16[1024,512]{1,0:T(8,128)(2,1)} %get-tuple-element.148.refs_1_, bf16[1024,512]{1,0:T(8,128)(2,1)} %get-tuple-element.166.refs_0_.refs_2_, ...), custom_call_target="tpu_custom_call" | custom-call | flops 102005472 | bytes 209715 | tf_op jit(solution)/shard_map/normed_grad/pallas_call | solution.py:809
  256.4 2.0 convert_add_fusion.4
  258.6 1.7 collective-permute-start.26
  260.3 2.5 fusion.10
  275.9 11.3 %collective-permute-done.35 = f32[5,256]{1,0:T(8,128)S(1)} collective-permute-done((f32[5,256]{1,0:T(8,128)S(1)}, f32[5,256]{1,0:T(8,128)S(1)}, u32[]{:S(2)}, u32[]{:S(2)}) %collective-permute-start.35) | collective-permute-done | bytes 5152 | tf_op jit(solution)/shard_map/ppermute | solution.py:500
  289.2 2.1 maximum_bitcast_fusion
  291.3 1.7 fusion.13
  293.8 3.2 fusion.8
  297.1 1.5 concatenate.58
  300.1 2.2 add_convert_fusion.2
  305.3 1.6 collective-permute-start.37
  306.9 2.0 add_convert_fusion.11
  308.8 1.6 collective-permute-start.39
  310.4 12.4 %collective-permute-done.37 = f32[7984]{0:T(1024)S(1)} collective-permute-done((f32[7984]{0:T(1024)S(1)}, f32[7984]{0:T(1024)S(1)}, u32[]{:S(2)}, u32[]{:S(2)}) %collective-permute-start.37) | collective-permute-done | bytes 31968 | tf_op jit(solution)/shard_map/ppermute | solution.py:500
  322.9 4.6 %fusion.4 = (bf16[1024,512]{1,0:T(8,128)(2,1)}, bf16[1024,512]{1,0:T(8,128)(2,1)}) fusion(bf16[1024,512]{1,0:T(8,128)(2,1)S(1)} %copy-done.6, bf16[1024,512]{1,0:T(8,128)(2,1)S(1)} %copy-done.2, f32[1024]{0:T(1024)S(1)} %add.420, f32[1024]{0:T(1024)S(1)} %copy-done.36, f32[512]{0:T(512)S(1)} %copy-done.35, f32[1024]{0:T(1024)S(1)} %copy-done.32, ...), kind=kLoop, calls=%fused_computation.10 | loop fusion | flops 11534336 | bytes 10500096 | tf_op jit(solution)/shard_map/convert_element_type | solution.py:941
  333.3 2.8 collective-permute-start.41
  337.6 8.5 %collective-permute-done.41 = bf16[1,20480]{1,0:T(2,128)(2,1)S(1)} collective-permute-done((bf16[1,20480]{1,0:T(2,128)(2,1)S(1)}, bf16[1,20480]{1,0:T(2,128)(2,1)S(1)}, u32[]{:S(2)}, u32[]{:S(2)}) %collective-permute-start.41) | collective-permute-done | bytes 40992 | tf_op jit(solution)/shard_map/ppermute | solution.py:500
  348.8 2.7 collective-permute-done.40
  353.1 2.9 copy.67
  (251 shorter events, 72.5 us)
Async XLA Ops:
  0.6 26.5 %collective-permute-start.1 = (bf16[1024,512]{1,0:T(8,128)(2,1)}, bf16[1024,512]{1,0:T(8,128)(2,1)}, u32[]{:S(2)}, u32[]{:S(2)}) collective-permute-start(bf16[1024,512]{1,0:T(8,128)(2,1)} %refs_0_.4), channel_id=1, source_target_pairs={{0,2},{1,3},{2,0},{3,1},{4,6},{5,7},{6,4},{7,5},{8,10},{9,11},{10,... | collective-permute-start | bytes 3145736 | tf_op jit(solution)/shard_map/ppermute | solution.py:500
  3.7 27.9 %collective-permute-start.3 = (bf16[1024,512]{1,0:T(8,128)(2,1)}, bf16[1024,512]{1,0:T(8,128)(2,1)}, u32[]{:S(2)}, u32[]{:S(2)}) collective-permute-start(bf16[1024,512]{1,0:T(8,128)(2,1)} %refs_0_.4), channel_id=1, source_target_pairs={{0,1},{1,0},{2,3},{3,2},{4,5},{5,4},{6,7},{7,6},{8,9},{9,8},{10,11... | collective-permute-start | bytes 3145736 | tf_op jit(solution)/shard_map/ppermute | solution.py:500
  27.8 3.8 %collective-permute-start.4 = (bf16[1024,512]{1,0:T(8,128)(2,1)}, bf16[1024,512]{1,0:T(8,128)(2,1)}, u32[]{:S(2)}, u32[]{:S(2)}) collective-permute-start(bf16[1024,512]{1,0:T(8,128)(2,1)} %collective-permute-done.1.refs_2_), channel_id=1, source_target_pairs={{0,1},{1,0},{2,3},{3,2},{4,5},{5,4},{6,7},{7,6},{8,9},{9,8},{10,11... | collective-permute-start | bytes 3145736 | tf_op jit(solution)/shard_map/ppermute | solution.py:500
  27.8 39.9 %collective-permute-start.2 = (bf16[1024,512]{1,0:T(8,128)(2,1)S(1)}, bf16[1024,512]{1,0:T(8,128)(2,1)S(1)}, u32[]{:S(2)}, u32[]{:S(2)}) collective-permute-start(bf16[1024,512]{1,0:T(8,128)(2,1)S(1)} %copy-done.1), channel_id=1, source_target_pairs={{0,2},{1,3},{2,0},{3,1},{4,6},{5,7},{6,4},{7,5},{8,10},{9,11},{10,... | collective-permute-start | bytes 3145736 | tf_op jit(solution)/shard_map/ppermute | solution.py:500
  29.5 38.5 %collective-permute-start = (bf16[1024,512]{1,0:T(8,128)(2,1)S(1)}, bf16[1024,512]{1,0:T(8,128)(2,1)S(1)}, u32[]{:S(2)}, u32[]{:S(2)}) collective-permute-start(bf16[1024,512]{1,0:T(8,128)(2,1)S(1)} %copy-done.1), channel_id=1, source_target_pairs={{0,1},{1,0},{2,3},{3,2},{4,5},{5,4},{6,7},{7,6},{8,9},{9,8},{10,11... | collective-permute-start | bytes 3145736 | tf_op jit(solution)/shard_map/ppermute | solution.py:500
  67.7 2.7 collective-permute-start.5
  84.1 1.5 collective-permute-start.6
  86.4 3.9 %collective-permute-start.7 = (f32[8,1024]{1,0:T(8,128)S(1)}, f32[8,1024]{1,0:T(8,128)S(1)}, u32[]{:S(2)}, u32[]{:S(2)}) collective-permute-start(f32[8,1024]{1,0:T(8,128)S(1)} %add.373), channel_id=1, source_target_pairs={{0,2},{1,3},{2,0},{3,1},{4,6},{5,7},{6,4},{7,5},{8,10},{9,11},{10,... | collective-permute-start | bytes 98312 | tf_op jit(solution)/shard_map/ppermute | solution.py:500
  104.8 28.8 %collective-permute-start.8 = (bf16[512,1024]{1,0:T(8,128)(2,1)}, bf16[512,1024]{1,0:T(8,128)(2,1)S(1)}, u32[]{:S(2)}, u32[]{:S(2)}) collective-permute-start(bf16[512,1024]{1,0:T(8,128)(2,1)} %get-tuple-element.152), channel_id=1, source_target_pairs={{0,4},{4,0},{8,12},{12,8},{16,20},{20,16},{24,28},{28,24},{1,5},{5... | collective-permute-start | bytes 3145736 | tf_op jit(solution)/shard_map/ppermute | solution.py:500
  133.7 35.3 %collective-permute-start.9 = (bf16[2,1024,512]{2,1,0:T(8,128)(2,1)}, bf16[2,1024,512]{2,1,0:T(8,128)(2,1)S(1)}, u32[]{:S(2)}, u32[]{:S(2)}) collective-permute-start(bf16[2,1024,512]{2,1,0:T(8,128)(2,1)} %output.2), channel_id=1, source_target_pairs={{0,1},{1,0},{2,3},{3,2},{4,5},{5,4},{6,7},{7,6},{8,9},{9,8},{10,11... | collective-permute-start | bytes 6291464 | tf_op jit(solution)/shard_map/ppermute | solution.py:500
  134.7 34.2 %collective-permute-start.11 = (bf16[512,1024]{1,0:T(8,128)(2,1)}, bf16[512,1024]{1,0:T(8,128)(2,1)S(1)}, u32[]{:S(2)}, u32[]{:S(2)}) collective-permute-start(bf16[512,1024]{1,0:T(8,128)(2,1)} %get-tuple-element.169), channel_id=1, source_target_pairs={{0,4},{4,0},{8,12},{12,8},{16,20},{20,16},{24,28},{28,24},{1,5},{5... | collective-permute-start | bytes 3145736 | tf_op jit(solution)/shard_map/ppermute | solution.py:500
  136.6 32.4 %collective-permute-start.10 = (bf16[512,512]{1,0:T(8,128)(2,1)S(1)}, bf16[512,512]{1,0:T(8,128)(2,1)S(1)}, u32[]{:S(2)}, u32[]{:S(2)}) collective-permute-start(bf16[512,512]{1,0:T(8,128)(2,1)S(1)} %add_convert_fusion.9), channel_id=1, source_target_pairs={{0,8},{4,12},{8,0},{12,4},{16,24},{20,28},{24,16},{28,20},{1,9},{5... | collective-permute-start | bytes 1572872 | tf_op jit(solution)/shard_map/ppermute | solution.py:500
  138.2 64.2 %collective-permute-start.15 = (bf16[1024,512]{1,0:T(8,128)(2,1)}, bf16[1024,512]{1,0:T(8,128)(2,1)}, u32[]{:S(2)}, u32[]{:S(2)}) collective-permute-start(bf16[1024,512]{1,0:T(8,128)(2,1)} %get-tuple-element.155), channel_id=1, source_target_pairs={{0,4},{4,0},{8,12},{12,8},{16,20},{20,16},{24,28},{28,24},{1,5},{5... | collective-permute-start | bytes 3145736 | tf_op jit(solution)/shard_map/ppermute | solution.py:500
  171.2 31.2 %collective-permute-start.12 = (bf16[1024,512]{1,0:T(8,128)(2,1)}, bf16[1024,512]{1,0:T(8,128)(2,1)S(1)}, u32[]{:S(2)}, u32[]{:S(2)}) collective-permute-start(bf16[1024,512]{1,0:T(8,128)(2,1)} %fusion.9), channel_id=1, source_target_pairs={{0,2},{1,3},{2,0},{3,1},{4,6},{5,7},{6,4},{7,5},{8,10},{9,11},{10,... | collective-permute-start | bytes 3145736 | tf_op jit(solution)/shard_map/ppermute | solution.py:500
  174.2 28.2 %collective-permute-start.14 = (bf16[512,512]{1,0:T(8,128)(2,1)}, bf16[512,512]{1,0:T(8,128)(2,1)}, u32[]{:S(2)}, u32[]{:S(2)}) collective-permute-start(bf16[512,512]{1,0:T(8,128)(2,1)} %add_convert_fusion.8), channel_id=1, source_target_pairs={{0,8},{4,12},{8,0},{12,4},{16,24},{20,28},{24,16},{28,20},{1,9},{5... | collective-permute-start | bytes 1572872 | tf_op jit(solution)/shard_map/ppermute | solution.py:500
  174.6 41.1 %collective-permute-start.17 = (bf16[1024,512]{1,0:T(8,128)(2,1)}, bf16[1024,512]{1,0:T(8,128)(2,1)}, u32[]{:S(2)}, u32[]{:S(2)}) collective-permute-start(bf16[1024,512]{1,0:T(8,128)(2,1)} %get-tuple-element.174), channel_id=1, source_target_pairs={{0,4},{4,0},{8,12},{12,8},{16,20},{20,16},{24,28},{28,24},{1,5},{5... | collective-permute-start | bytes 3145736 | tf_op jit(solution)/shard_map/ppermute | solution.py:500
  176.6 25.8 %collective-permute-start.13 = (bf16[512,256]{1,0:T(8,128)(2,1)S(1)}, bf16[512,256]{1,0:T(8,128)(2,1)S(1)}, u32[]{:S(2)}, u32[]{:S(2)}) collective-permute-start(bf16[512,256]{1,0:T(8,128)(2,1)S(1)} %add_convert_fusion.15), channel_id=1, source_target_pairs={{0,16},{4,20},{8,24},{12,28},{16,0},{20,4},{24,8},{28,12},{1,17},{... | collective-permute-start | bytes 786440 | tf_op jit(solution)/shard_map/ppermute | solution.py:500
  204.0 11.7 %collective-permute-start.16 = (bf16[512,512]{1,0:T(8,128)(2,1)S(1)}, bf16[512,512]{1,0:T(8,128)(2,1)S(1)}, u32[]{:S(2)}, u32[]{:S(2)}) collective-permute-start(bf16[512,512]{1,0:T(8,128)(2,1)S(1)} %add_convert_fusion.7), channel_id=1, source_target_pairs={{0,8},{4,12},{8,0},{12,4},{16,24},{20,28},{24,16},{28,20},{1,9},{5... | collective-permute-start | bytes 1572872 | tf_op jit(solution)/shard_map/ppermute | solution.py:500
  216.5 15.5 %collective-permute-start.18 = (bf16[1024,256]{1,0:T(8,128)(2,1)}, bf16[1024,256]{1,0:T(8,128)(2,1)S(1)}, u32[]{:S(2)}, u32[]{:S(2)}) collective-permute-start(bf16[1024,256]{1,0:T(8,128)(2,1)} %get-tuple-element.199.refs_4_), channel_id=1, source_target_pairs={{0,1},{1,0},{2,3},{3,2},{4,5},{5,4},{6,7},{7,6},{8,9},{9,8},{10,11... | collective-permute-start | bytes 1572872 | tf_op jit(solution)/shard_map/ppermute | solution.py:500
  216.5 15.4 %collective-permute-start.19 = (bf16[512,256]{1,0:T(8,128)(2,1)}, bf16[512,256]{1,0:T(8,128)(2,1)S(1)}, u32[]{:S(2)}, u32[]{:S(2)}) collective-permute-start(bf16[512,256]{1,0:T(8,128)(2,1)} %add_convert_fusion.14), channel_id=1, source_target_pairs={{0,16},{4,20},{8,24},{12,28},{16,0},{20,4},{24,8},{28,12},{1,17},{... | collective-permute-start | bytes 786440 | tf_op jit(solution)/shard_map/ppermute | solution.py:500
  232.0 23.1 %collective-permute-start.20 = (bf16[2,1024,512]{2,1,0:T(8,128)(2,1)}, bf16[2,1024,512]{2,1,0:T(8,128)(2,1)}, u32[]{:S(2)}, u32[]{:S(2)}) collective-permute-start(bf16[2,1024,512]{2,1,0:T(8,128)(2,1)} %normed_grad.2), channel_id=1, source_target_pairs={{0,1},{1,0},{2,3},{3,2},{4,5},{5,4},{6,7},{7,6},{8,9},{9,8},{10,11... | collective-permute-start | bytes 6291464 | tf_op jit(solution)/shard_map/ppermute | solution.py:500
  233.1 21.9 %collective-permute-start.23 = (bf16[512,512]{1,0:T(8,128)(2,1)}, bf16[512,512]{1,0:T(8,128)(2,1)}, u32[]{:S(2)}, u32[]{:S(2)}) collective-permute-start(bf16[512,512]{1,0:T(8,128)(2,1)} %add_convert_fusion.6), channel_id=1, source_target_pairs={{0,8},{4,12},{8,0},{12,4},{16,24},{20,28},{24,16},{28,20},{1,9},{5... | collective-permute-start | bytes 1572872 | tf_op jit(solution)/shard_map/ppermute | solution.py:500
  234.6 20.5 %collective-permute-start.21 = (bf16[1024,256]{1,0:T(8,128)(2,1)S(1)}, bf16[1024,256]{1,0:T(8,128)(2,1)S(1)}, u32[]{:S(2)}, u32[]{:S(2)}) collective-permute-start(bf16[1024,256]{1,0:T(8,128)(2,1)S(1)} %add_convert_fusion.5), channel_id=1, source_target_pairs={{0,2},{1,3},{2,0},{3,1},{4,6},{5,7},{6,4},{7,5},{8,10},{9,11},{10,... | collective-permute-start | bytes 1572872 | tf_op jit(solution)/shard_map/ppermute | solution.py:500
  237.6 32.2 %collective-permute-start.25 = (bf16[1024,512]{1,0:T(8,128)(2,1)}, bf16[1024,512]{1,0:T(8,128)(2,1)S(1)}, u32[]{:S(2)}, u32[]{:S(2)}) collective-permute-start(bf16[1024,512]{1,0:T(8,128)(2,1)} %get-tuple-element.185), channel_id=1, source_target_pairs={{0,4},{4,0},{8,12},{12,8},{16,20},{20,16},{24,28},{28,24},{1,5},{5... | collective-permute-start | bytes 3145736 | tf_op jit(solution)/shard_map/ppermute | solution.py:500
  239.1 15.3 %collective-permute-start.22 = (bf16[256,512]{1,0:T(8,128)(2,1)S(1)}, bf16[256,512]{1,0:T(8,128)(2,1)S(1)}, u32[]{:S(2)}, u32[]{:S(2)}) collective-permute-start(bf16[256,512]{1,0:T(8,128)(2,1)S(1)} %add_convert_fusion.13), channel_id=1, source_target_pairs={{0,16},{4,20},{8,24},{12,28},{16,0},{20,4},{24,8},{28,12},{1,17},{... | collective-permute-start | bytes 786440 | tf_op jit(solution)/shard_map/ppermute | solution.py:500
  254.5 36.8 %collective-permute-start.28 = (bf16[1024,512]{1,0:T(8,128)(2,1)}, bf16[1024,512]{1,0:T(8,128)(2,1)}, u32[]{:S(2)}, u32[]{:S(2)}) collective-permute-start(bf16[1024,512]{1,0:T(8,128)(2,1)} %get-tuple-element.204), channel_id=1, source_target_pairs={{0,4},{4,0},{8,12},{12,8},{16,20},{20,16},{24,28},{28,24},{1,5},{5... | collective-permute-start | bytes 3145736 | tf_op jit(solution)/shard_map/ppermute | solution.py:500
  258.6 13.8 %collective-permute-start.26 = (bf16[256,512]{1,0:T(8,128)(2,1)S(1)}, bf16[256,512]{1,0:T(8,128)(2,1)S(1)}, u32[]{:S(2)}, u32[]{:S(2)}) collective-permute-start(bf16[256,512]{1,0:T(8,128)(2,1)S(1)} %add_convert_fusion.12), channel_id=1, source_target_pairs={{0,16},{4,20},{8,24},{12,28},{16,0},{20,4},{24,8},{28,12},{1,17},{... | collective-permute-start | bytes 786440 | tf_op jit(solution)/shard_map/ppermute | solution.py:500
  262.8 28.5 %collective-permute-start.24 = (bf16[1024,512]{1,0:T(8,128)(2,1)}, bf16[1024,512]{1,0:T(8,128)(2,1)}, u32[]{:S(2)}, u32[]{:S(2)}) collective-permute-start(bf16[1024,512]{1,0:T(8,128)(2,1)} %fusion.10), channel_id=1, source_target_pairs={{0,2},{1,3},{2,0},{3,1},{4,6},{5,7},{6,4},{7,5},{8,10},{9,11},{10,... | collective-permute-start | bytes 3145736 | tf_op jit(solution)/shard_map/ppermute | solution.py:500
  266.2 3.0 collective-permute-start.34
  269.2 22.1 %collective-permute-start.29 = (bf16[4,20480]{1,0:T(4,128)(2,1)}, bf16[4,20480]{1,0:T(4,128)(2,1)}, u32[]{:S(2)}, u32[]{:S(2)}) collective-permute-start(bf16[4,20480]{1,0:T(4,128)(2,1)} %bitcast.79), channel_id=1, source_target_pairs={{0,4},{4,0},{8,12},{12,8},{16,20},{20,16},{24,28},{28,24},{1,5},{5... | collective-permute-start | bytes 491528 | tf_op jit(solution)/shard_map/ppermute | solution.py:500
  269.9 17.3 %collective-permute-start.35 = (f32[5,256]{1,0:T(8,128)S(1)}, f32[5,256]{1,0:T(8,128)S(1)}, u32[]{:S(2)}, u32[]{:S(2)}) collective-permute-start(f32[5,256]{1,0:T(8,128)S(1)} %slice_add_fusion), channel_id=1, source_target_pairs={{0,2},{1,3},{2,0},{3,1},{4,6},{5,7},{6,4},{7,5},{8,10},{9,11},{10,... | collective-permute-start | bytes 15368 | tf_op jit(solution)/shard_map/ppermute | solution.py:500
  273.3 20.6 %copy-start.5 = (bf16[1024,512]{1,0:T(8,128)(2,1)S(1)}, bf16[1024,512]{1,0:T(8,128)(2,1)}, u32[]{:S(2)}) copy-start(bf16[1024,512]{1,0:T(8,128)(2,1)} %refs_0_.4) | copy-start | bytes 3145732
  273.3 18.0 %collective-permute-start.27 = (bf16[512,512]{1,0:T(8,128)(2,1)}, bf16[512,512]{1,0:T(8,128)(2,1)}, u32[]{:S(2)}, u32[]{:S(2)}) collective-permute-start(bf16[512,512]{1,0:T(8,128)(2,1)} %add_convert_fusion.3), channel_id=1, source_target_pairs={{0,8},{4,12},{8,0},{12,4},{16,24},{20,28},{24,16},{28,20},{1,9},{5... | collective-permute-start | bytes 1572872 | tf_op jit(solution)/shard_map/ppermute | solution.py:500
  293.1 39.0 %collective-permute-start.33 = (bf16[2,20480]{1,0:T(2,128)(2,1)}, bf16[2,20480]{1,0:T(2,128)(2,1)S(1)}, u32[]{:S(2)}, u32[]{:S(2)}) collective-permute-start(bf16[2,20480]{1,0:T(2,128)(2,1)} %fusion.13), channel_id=1, source_target_pairs={{0,8},{4,12},{8,0},{12,4},{16,24},{20,28},{24,16},{28,20},{1,9},{5... | collective-permute-start | bytes 245768 | tf_op jit(solution)/shard_map/ppermute | solution.py:500
  297.1 25.7 %copy-start.2 = (bf16[1024,512]{1,0:T(8,128)(2,1)S(1)}, bf16[1024,512]{1,0:T(8,128)(2,1)}, u32[]{:S(2)}) copy-start(bf16[1024,512]{1,0:T(8,128)(2,1)} %refs_0_.7) | copy-start | bytes 3145732
  297.1 5.8 %collective-permute-start.30 = (f32[1024]{0:T(1024)}, f32[1024]{0:T(1024)}, u32[]{:S(2)}, u32[]{:S(2)}) collective-permute-start(f32[1024]{0:T(1024)} %get-tuple-element.303), channel_id=1, source_target_pairs={{0,1},{1,0},{2,3},{3,2},{4,5},{5,4},{6,7},{7,6},{8,9},{9,8},{10,11... | collective-permute-start | bytes 12296 | tf_op jit(solution)/shard_map/ppermute | solution.py:500
  298.6 24.2 %copy-start.6 = (bf16[1024,512]{1,0:T(8,128)(2,1)S(1)}, bf16[1024,512]{1,0:T(8,128)(2,1)}, u32[]{:S(2)}) copy-start(bf16[1024,512]{1,0:T(8,128)(2,1)} %refs_0_.4) | copy-start | bytes 3145732
  298.6 24.2 %copy-start.32 = (f32[1024]{0:T(1024)S(1)}, f32[1024]{0:T(1024)}, u32[]{:S(2)}) copy-start(f32[1024]{0:T(1024)} %get-tuple-element.304) | copy-start | bytes 12292
  298.6 24.2 %copy-start.35 = (f32[512]{0:T(512)S(1)}, f32[512]{0:T(512)}, u32[]{:S(2)}) copy-start(f32[512]{0:T(512)} %dynamic_slice.257) | copy-start | bytes 6148
  298.6 24.2 %copy-start.36 = (f32[1024]{0:T(1024)S(1)}, f32[1024]{0:T(1024)}, u32[]{:S(2)}) copy-start(f32[1024]{0:T(1024)} %get-tuple-element.305) | copy-start | bytes 12292
  298.6 5.9 %collective-permute-start.36 = (f32[7984]{0:T(1024)}, f32[7984]{0:T(1024)S(1)}, u32[]{:S(2)}, u32[]{:S(2)}) collective-permute-start(f32[7984]{0:T(1024)} %concatenate.58), channel_id=1, source_target_pairs={{0,4},{4,0},{8,12},{12,8},{16,20},{20,16},{24,28},{28,24},{1,5},{5... | collective-permute-start | bytes 95816 | tf_op jit(solution)/shard_map/ppermute | solution.py:500
  302.3 29.8 %collective-permute-start.32 = (bf16[512,512]{1,0:T(8,128)(2,1)}, bf16[512,512]{1,0:T(8,128)(2,1)}, u32[]{:S(2)}, u32[]{:S(2)}) collective-permute-start(bf16[512,512]{1,0:T(8,128)(2,1)} %add_convert_fusion.2), channel_id=1, source_target_pairs={{0,8},{4,12},{8,0},{12,4},{16,24},{20,28},{24,16},{28,20},{1,9},{5... | collective-permute-start | bytes 1572872 | tf_op jit(solution)/shard_map/ppermute | solution.py:500
  303.6 6.8 %collective-permute-start.31 = (f32[1024]{0:T(1024)S(1)}, f32[1024]{0:T(1024)S(1)}, u32[]{:S(2)}, u32[]{:S(2)}) collective-permute-start(f32[1024]{0:T(1024)S(1)} %add.419), channel_id=1, source_target_pairs={{0,2},{1,3},{2,0},{3,1},{4,6},{5,7},{6,4},{7,5},{8,10},{9,11},{10,... | collective-permute-start | bytes 12296 | tf_op jit(solution)/shard_map/ppermute | solution.py:500
  305.3 17.5 %collective-permute-start.37 = (f32[7984]{0:T(1024)S(1)}, f32[7984]{0:T(1024)S(1)}, u32[]{:S(2)}, u32[]{:S(2)}) collective-permute-start(f32[7984]{0:T(1024)S(1)} %add.429), channel_id=1, source_target_pairs={{0,8},{4,12},{8,0},{12,4},{16,24},{20,28},{24,16},{28,20},{1,9},{5... | collective-permute-start | bytes 95816 | tf_op jit(solution)/shard_map/ppermute | solution.py:500
  308.8 21.9 %collective-permute-start.39 = (bf16[256,512]{1,0:T(8,128)(2,1)}, bf16[256,512]{1,0:T(8,128)(2,1)}, u32[]{:S(2)}, u32[]{:S(2)}) collective-permute-start(bf16[256,512]{1,0:T(8,128)(2,1)} %add_convert_fusion.11), channel_id=1, source_target_pairs={{0,16},{4,20},{8,24},{12,28},{16,0},{20,4},{24,8},{28,12},{1,17},{... | collective-permute-start | bytes 786440 | tf_op jit(solution)/shard_map/ppermute | solution.py:500
  322.8 4.8 %collective-permute-start.38 = (f32[7984]{0:T(1024)S(1)}, f32[7984]{0:T(1024)S(1)}, u32[]{:S(2)}, u32[]{:S(2)}) collective-permute-start(f32[7984]{0:T(1024)S(1)} %add.430), channel_id=1, source_target_pairs={{0,16},{4,20},{8,24},{12,28},{16,0},{20,4},{24,8},{28,12},{1,17},{... | collective-permute-start | bytes 95816 | tf_op jit(solution)/shard_map/ppermute | solution.py:500
  333.3 12.8 %collective-permute-start.41 = (bf16[1,20480]{1,0:T(2,128)(2,1)S(1)}, bf16[1,20480]{1,0:T(2,128)(2,1)S(1)}, u32[]{:S(2)}, u32[]{:S(2)}) collective-permute-start(bf16[1,20480]{1,0:T(2,128)(2,1)S(1)} %fusion.19), channel_id=1, source_target_pairs={{0,16},{4,20},{8,24},{12,28},{16,0},{20,4},{24,8},{28,12},{1,17},{... | collective-permute-start | bytes 122888 | tf_op jit(solution)/shard_map/ppermute | solution.py:500
  337.3 14.1 %collective-permute-start.40 = (bf16[256,512]{1,0:T(8,128)(2,1)S(1)}, bf16[256,512]{1,0:T(8,128)(2,1)}, u32[]{:S(2)}, u32[]{:S(2)}) collective-permute-start(bf16[256,512]{1,0:T(8,128)(2,1)S(1)} %add_convert_fusion.10), channel_id=1, source_target_pairs={{0,16},{4,20},{8,24},{12,28},{16,0},{20,4},{24,8},{28,12},{1,17},{... | collective-permute-start | bytes 786440 | tf_op jit(solution)/shard_map/ppermute | solution.py:500
  (42 other events, 214.3 us)

commit v3 on v2

--- a/solution.py
+++ b/solution.py
@@ -117,7 +117,7 @@
     parts, heads, rank, *refs,
 ):
     pieces, refs = refs[:parts], refs[parts:]
-    (gain, w_maps, conv_maps, bias, rate, seg_row, w_gate, w_value, conv, skip, marks,
+    (gain, w_maps, conv_maps, bias, rate, seg_row, w_gate, w_value, conv, skip, gate_gain, marks,
      normed, pre_state, maps, maps_t, per_head, rows_out, cross_t, value, gate, mixed, low_gated, memory, squares,
      proj, cross, state) = refs
     g = pl.program_id(0)
@@ -227,7 +227,7 @@
         mixed[at, :] = out
         opened = gate[at, :].astype(F32)
         gated = out * (opened * sigmoid(opened))
-        low_gated[at, :] = gated.astype(BF16)
+        low_gated[at, :] = (gated * gate_gain[...]).astype(BF16)
         squares[at, :] += fold_lanes(gated * gated)
         return 0
 
@@ -246,7 +246,7 @@
 
 
 def cotangent_kernel(parts, rank, *refs):
-    pieces, (w_out, gated, gain, squares, grad, stats, sums, full, sems) = refs[:parts], refs[parts:]
+    pieces, (w_out, gated, squares, grad, stats, sums, full, sems) = refs[:parts], refs[parts:]
     g = pl.program_id(0)
     length, quarter = pieces[0].shape
 
@@ -260,7 +260,7 @@
 
     def chunk(i, _):
         at = pl.ds(pl.multiple_of(i * SPAN, SPAN), SPAN)
-        sums[at, :] += fold_lanes(grad[at, :].astype(F32) * gated[at, :].astype(F32) * gain[...])
+        sums[at, :] += fold_lanes(grad[at, :].astype(F32) * gated[at, :].astype(F32))
         return 0
 
     lax.fori_loop(0, length // SPAN, chunk, 0, unroll=2)
@@ -273,33 +273,35 @@
         )
 
 
-def gate_kernel(
-    parts, run, channels_all, place, rank, *refs,
-):
+def gate_kernel(parts, run, channels_all, stacked, place, rank, *refs):
     pieces, refs = refs[:parts], refs[parts:]
-    (grad, gate, mixed, gain, stats, marks,
-     low_mixed, grad_mixer, grad_gate, grad_gain, w_send, w_own, sent, kept, sems) = refs
+    (grad, gate, mixed, gain, stats, marks, low_mixed, grad_mixer, grad_gate, grad_gain), refs = refs[:10], refs[10:]
+    targets, (sent, kept, sems) = refs[:-3], refs[-3:]
     length, quarter = pieces[0].shape
     grad_gain[...] = jnp.zeros_like(grad_gain)
-    pick = (iota((8, LANES), 0) == iota((8, LANES), 1)).astype(F32)
     pairs = quarter // (2 * run)
     bits = (parts * pairs - 1).bit_length()
+    copies = []
+    for half, target in ((1, sent), (0, kept)):
+        for k in range(parts):
+            for j in range(pairs):
+                at = pl.multiple_of((2 * j + (place[0] ^ half)) * run, run)
+                to = pl.multiple_of(turned((rank[0] ^ k) * pairs + j, bits) * run, run)
+                copies.append(
+                    pltpu.make_async_copy(
+                        pieces[k].at[:, pl.ds(at, run)], target.at[:, pl.ds(to, run)], sems.at[len(copies)]
+                    )
+                )
 
     @pl.when(pl.program_id(0) == 0)
     def _():
-        for half, target in ((1, sent), (0, kept)):
-            where = []
-            for k in range(parts):
-                for j in range(pairs):
-                    at = pl.multiple_of((2 * j + (place[0] ^ half)) * run, run)
-                    to = turned((rank[0] ^ k) * pairs + j, bits) * run
-                    where.append((k, at, pl.multiple_of(to, run), run))
-            assemble(pieces, target, sems, where)
+        for copy in copies:
+            copy.start()
 
     def chunk(i, _):
         start = pl.multiple_of(i * SPAN, SPAN)
         at = pl.ds(start, SPAN)
-        columns = dot(stats[:, pl.ds(start, SPAN)], pick, TN, HIGHEST)
+        columns = jnp.concatenate([stats[:, pl.ds(start, SPAN)]] * (SPAN // 8), axis=0).T
         keep = marks[at, 5:6]
         scale = lax.rsqrt(columns[:, 0:1] / channels_all + EPSILON)
         factor = scale * keep
@@ -316,17 +318,29 @@
         grad_gate[at, :] = (grad_gated * out * chance * (1.0 + opened * (1.0 - chance))).astype(BF16)
         return 0
 
-    lax.fori_loop(0, length // SPAN, chunk, 0, unroll=2)
-    w_send[...] = dot(low_mixed[...], sent[...], TN).astype(BF16)
-    w_own[...] = dot(low_mixed[...], kept[...], TN).astype(BF16)
+    lax.fori_loop(0, length // SPAN, chunk, 0, unroll=4)
+
+    @pl.when(pl.program_id(0) == 0)
+    def _():
+        for copy in copies:
+            copy.wait()
+
+    for half, source in enumerate((sent, kept)):
+        now = dot(low_mixed[...], source[...], TN).astype(BF16)
+        if stacked:
+            targets[0][half] = now
+        else:
+            targets[half][...] = now
 
 
 def weight_kernel(place, left_send, left_own, *refs):
-    parts = len(refs) // 3
-    right = refs[:parts]
-    for left, targets in ((left_send, refs[parts : 2 * parts]), (left_own, refs[2 * parts :])):
-        for part, target in zip(right, targets):
-            target[...] = dot(left[...], part[...], TN).astype(BF16)
+    right, targets = refs[:-2], refs[-2:]
+    for left, target in zip((left_send, left_own), targets):
+        at = 0
+        for part in right:
+            size = part.shape[1]
+            target[:, at : at + size] = dot(left[...], part[...], TN).astype(BF16)
+            at += size
 
 
 def backward_kernel(
@@ -475,24 +489,36 @@
     lax.fori_loop(0, blocks, block, 0, unroll=UNROLL)
 
 
-def output_kernel(chunks, rank, *refs):
-    mixed, w_out, out = refs[:chunks], refs[chunks], refs[chunks + 1]
-    size = mixed[0].shape[1]
-    total = dot(mixed[0][...], w_out[:size])
-    for c in range(1, chunks):
-        total = total + dot(mixed[c][...], w_out[c * size : (c + 1) * size])
-    out[0] = total.astype(BF16)
+def put(far, near, total):
+    step = pl.program_id(0)
+
+    @pl.when(step < 2)
+    def _():
+        far[0] = total.astype(BF16)
+
+    @pl.when(step >= 2)
+    def _():
+        near[0] = total.astype(BF16)
+
+
+def output_kernel(rank, gated, w_out, far, near):
+    put(far, near, dot(gated[...], w_out[...]))
 
 
 def normed_kernel(chunks, rank, *refs):
-    grads, (grad_state, grad_step, w_inner, w_state, w_step, out) = refs[: 2 * chunks], refs[2 * chunks :]
-    total = dot(grad_state[...], w_state[...], NT) + dot(grad_step[...], w_step[...], NT)
-    at = 0
-    for part in grads:
-        size = part.shape[1]
-        total = total + dot(part[...], w_inner[:, at : at + size], NT)
-        at += size
-    out[0] = total.astype(BF16)
+    grads, (grad_state, grad_step, w_inner, w_maps), refs = refs[: 2 * chunks], refs[2 * chunks : 2 * chunks + 4], refs[2 * chunks + 4 :]
+    outs, (joined, joined_maps) = refs[:-2], refs[-2:]
+
+    @pl.when(pl.program_id(0) == 0)
+    def _():
+        for target, parts in ((joined, grads), (joined_maps, (grad_state, grad_step))):
+            at = 0
+            for part in parts:
+                target[:, at : at + part.shape[1]] = part[...]
+                at += part.shape[1]
+
+    total = dot(joined[...], w_inner[...], NT) + dot(joined_maps[...], w_maps[...], NT)
+    put(*outs, total)
 
 
 def swap(array, axis, mask):
@@ -543,9 +569,14 @@
 class Sum:
     def __init__(self, own, got, dim, low_bits):
         self.terms, self.got, self.dim, self.masks = [own], got, dim, rest_masks(low_bits)
+        if got is None:
+            self.send()
 
     def advance(self):
         self.terms.append(self.got)
+        return self.send()
+
+    def send(self):
         mask = self.masks.pop(0)
         top = (lax.axis_index("dp") & mask) // mask
         size = self.terms[0].shape[self.dim] // 2
@@ -554,7 +585,7 @@
             return [lax.dynamic_slice_in_dim(term, half * size, size, self.dim) for term in self.terms]
 
         sent = functools.reduce(jnp.add, [term.astype(F32) for term in cut(1 - top)]).astype(BF16)
-        self.terms, self.got = cut(top), swap(sent, "dp", mask)
+        self.terms, self.got, self.sent = cut(top), swap(sent, "dp", mask), sent
         return sent
 
     def result(self):
@@ -646,7 +677,7 @@
             held((1, width)), held((width, states2 + LANES)), held((8, states2)),
             held((1, LANES)), held((1, LANES)), held((8, length)),
             pl.BlockSpec((width, GROUP), lambda g, *_: (0, g)), pl.BlockSpec((width, GROUP), lambda g, *_: (0, steps + g)),
-            by_group(8), by_group(1), held((length + 8, LANES)),
+            by_group(8), by_group(1), by_group(1), held((length + 8, LANES)),
         ],
         [
             held((length, width)), held((length, states2)), held((length, states2)), held((states2, length)),
@@ -672,7 +703,7 @@
         vmem=56,
     )(
         ranks, *token_pieces, norm_gain[None, :], w_maps, conv_state_pad, bias8, rate8, seg_row, flat, flat, conv_pad,
-        skip_row, marks,
+        skip_row, gain_row, marks,
     )
 
     grad_y = tie(grad_y, squares)
@@ -686,7 +717,7 @@
         pieces_any
         + [
             pl.BlockSpec((double, width), lambda g, *_: (g, 0)),
-            by_double(length), by_double(1), held((length, LANES)),
+            by_double(length), held((length, LANES)),
         ],
         [by_double(length), held((8, length))],
         [shape_of(length, channels, dtype=BF16), shape_of(8, length)],
@@ -696,48 +727,49 @@
         moved=length * width * 2 + width * channels * 2 + length * channels * 12,
         name="cotangent",
         vmem=56,
-    )(ranks, *grad_pieces, w_out, low_gated, gain_row, squares)
-    stats = sum_all(stats, "tensor")
-
+    )(ranks, *grad_pieces, w_out, low_gated, squares)
     spans = steps // CHUNKS
 
     def chunk_spec(rows, c):
         return pl.BlockSpec((rows, GROUP), lambda g, *_: (0, c * spans + g))
 
-    def gate_part(c, stats):
+    def gate_part(c, stats, stacked):
         size = spans * GROUP
-        by_channel = pl.BlockSpec((GROUP, half_width), lambda g, *_: (g, 0))
+        if stacked:
+            outs = [pl.BlockSpec((2, GROUP, half_width), lambda g, *_: (0, g, 0))]
+            shapes = [shape_of(2, size, half_width, dtype=BF16)]
+        else:
+            outs = [pl.BlockSpec((GROUP, half_width), lambda g, *_: (g, 0))] * 2
+            shapes = [shape_of(size, half_width, dtype=BF16)] * 2
         return call(
-            functools.partial(gate_kernel, parts, run, channels * parts),
+            functools.partial(gate_kernel, parts, run, channels * parts, stacked),
             (spans,),
             pieces_any
             + [
                 chunk_spec(length, c), chunk_spec(length, c), chunk_spec(length, c), chunk_spec(1, c),
                 held((8, length)), held((length + 8, LANES)),
             ],
-            [by_group(length), by_group(length), by_group(length), by_group(1), by_channel, by_channel],
+            [by_group(length), by_group(length), by_group(length), by_group(1), *outs],
             [
                 shape_of(length, size, dtype=BF16), shape_of(length, size, dtype=BF16),
-                shape_of(length, size, dtype=BF16), shape_of(1, size),
-                shape_of(size, half_width, dtype=BF16), shape_of(size, half_width, dtype=BF16),
+                shape_of(length, size, dtype=BF16), shape_of(1, size), *shapes,
             ],
             [
                 pltpu.VMEM((length, half_width), BF16), pltpu.VMEM((length, half_width), BF16),
-                pltpu.SemaphoreType.DMA((half_width // run,)),
+                pltpu.SemaphoreType.DMA((width // run,)),
             ],
             prefetch=2,
             flops=2 * length * width * size,
             moved=length * width * 2 + length * size * 18 + width * size * 2,
             name="gate",
-            vmem=56,
         )(place, ranks, *grad_pieces, grad_mixed, gate, mixer_out, gain_row, stats, marks)
 
     def weight_part(*right):
         runs = half_width // run
         columns = [part.shape[1] for part in right]
-        outs = [pl.BlockSpec((run, size), lambda j, p: (turned(j, (runs - 1).bit_length()), 0)) for size in columns]
-        shapes = [shape_of(half_width, size, dtype=BF16) for size in columns]
-        result = call(
+        out = pl.BlockSpec((run, sum(columns)), lambda j, p: (turned(j, (runs - 1).bit_length()), 0))
+        shape = shape_of(half_width, sum(columns), dtype=BF16)
+        return call(
             weight_kernel,
             (runs,),
             [
@@ -745,14 +777,13 @@
                 pl.BlockSpec((length, run), lambda j, p: (0, 2 * j + p[0])),
             ]
             + [held((length, size)) for size in columns],
-            outs + outs,
-            shapes + shapes,
+            [out, out],
+            [shape, shape],
             prefetch=1,
             flops=2 * length * width * sum(columns),
             moved=length * width * 2 + length * sum(columns) * 2 + width * sum(columns) * 2,
             name="weights",
         )(place, normed, normed, *right)
-        return result[: len(columns)], result[len(columns) :]
 
     all_lanes = held((length, LANES))
 
@@ -783,80 +814,80 @@
             cross_t,
         )
 
-    def output_part(ks, mixed):
+    def piece_of(i, r):
+        return r[0] ^ jnp.where(i == 0, 1, jnp.where(i == 1, 3, jnp.where(i == 2, 2, 0)))
+
+    def far_near(count):
+        specs = [
+            pl.BlockSpec((1, length, quarter), lambda i, r: (jnp.minimum(i, 1), 0, 0)),
+            pl.BlockSpec((1, length, quarter), lambda i, r: (jnp.maximum(i, 2) - 2, 0, 0)),
+        ]
+        return specs, [shape_of(2, length, quarter, dtype=BF16), shape_of(count, length, quarter, dtype=BF16)]
+
+    def output_part(low_gated):
         return call(
-            functools.partial(output_kernel, len(mixed)),
-            (len(ks), quarter // 256),
-            [held((length, mixed[0].shape[1]))] * len(mixed)
-            + [
-                pl.BlockSpec(
-                    (channels, 256),
-                    lambda i, j, r: (0, (r[0] ^ (ks[0] + i * (ks[-1] - ks[0]))) * (quarter // 256) + j),
-                ),
-            ],
-            pl.BlockSpec((1, length, 256), lambda i, j, r: (i, 0, j)),
-            shape_of(len(ks), length, quarter, dtype=BF16),
+            output_kernel,
+            (4,),
+            [held((length, channels)), pl.BlockSpec((channels, quarter), lambda i, r: (0, piece_of(i, r)))],
+            *far_near(2),
             prefetch=1,
-            flops=2 * length * channels * quarter * len(ks),
-            moved=length * channels * 2 + channels * quarter * 2 * len(ks) + length * quarter * 2 * len(ks),
+            flops=2 * length * channels * width,
+            moved=length * channels * 2 + channels * width * 2 + length * width * 2,
             name="output",
-        )(ranks, *mixed, w_out)
-
-    def normed_part(ks, grad_gate, grad_value):
-        def row(i, j, r):
-            return (r[0] ^ (ks[0] + i * (ks[-1] - ks[0]))) * (quarter // 256) + j
-
+        )(ranks, low_gated, w_out)
+
+    def normed_part(grad_gate):
+        grads = (*grad_gate, *grad_value)
         return call(
             functools.partial(normed_kernel, len(grad_gate)),
-            (len(ks), quarter // 256),
-            [held((length, part.shape[1])) for part in (*grad_gate, *grad_value)]
+            (4,),
+            [held((length, part.shape[1])) for part in grads]
             + [
                 held((length, states2)), held((length, LANES)),
-                pl.BlockSpec((256, 2 * channels), lambda i, j, r: (row(i, j, r), 0)),
-                pl.BlockSpec((256, states2), lambda i, j, r: (row(i, j, r), 0)),
-                pl.BlockSpec((256, LANES), lambda i, j, r: (row(i, j, r), 0)),
+                pl.BlockSpec((quarter, 2 * channels), lambda i, r: (piece_of(i, r), 0)),
+                pl.BlockSpec((quarter, states2 + LANES), lambda i, r: (piece_of(i, r), 0)),
             ],
-            pl.BlockSpec((1, length, 256), lambda i, j, r: (i, 0, j)),
-            shape_of(len(ks), length, quarter, dtype=BF16),
+            *far_near(2),
+            [pltpu.VMEM((length, 2 * channels), BF16), pltpu.VMEM((length, states2 + LANES), BF16)],
             prefetch=1,
-            flops=2 * length * (2 * channels + states2 + LANES) * quarter * len(ks),
-            moved=length * channels * 4 + channels * quarter * 4 * len(ks) + length * quarter * 2 * len(ks),
+            flops=2 * length * (2 * channels + states2 + LANES) * width,
+            moved=length * channels * 4 + channels * width * 4 + length * width * 2,
             name="normed_grad",
-        )(ranks, *grad_gate, *grad_value, grad_state, grad_step, flat, w_state, step_pad)
+        )(ranks, *grads, grad_state, grad_step, flat, w_maps)
 
     def over_x(send):
         return swap(send, "dp", 1 << low_bits)
 
-    chunks = range(CHUNKS)
-    gates, sum_out = [], []
-    last = stats
-    for c in chunks:
-        gates.append(gate_part(c, tie(stats, last)))
-        sum_out.append(Sum(gates[c][5], over_x(gates[c][4]), 1, low_bits))
-        last = gates[c][5]
-    low_mixed, grad_mixer, grad_gate, grad_gain, _, _ = zip(*gates)
-    gate_send, gate_own = weight_part(tie(grad_gate[0], last), *grad_gate[1:])
-    out_far = output_part((1, 3), [tie(low_mixed[0], gate_send[0]), *low_mixed[1:]])
-
-    out_far, send = meet(sum_out[:1], out_far, gate_send[0])
-    sum_gate = [Sum(gate_own[0], over_x(send), 0, low_bits)]
+    stats = sum_all(stats, "tensor")
+
+    first = gate_part(0, stats, False)
+    sum_out = [Sum(first[5], over_x(first[4]), 1, low_bits)]
+    other = gate_part(1, tie(stats, first[5]), True)
+    low_mixed, grad_mixer, grad_gate, grad_gain = zip(first[:4], other[:4])
+    gate_send, gate_own = weight_part(tie(grad_gate[0], other[4]), *grad_gate[1:])
+    sum_gate = Sum(gate_own, over_x(gate_send), 0, low_bits)
+    out_far, out_near = output_part(tie(low_gated, gate_own))
+
+    out_far, out_near, stack = meet(sum_out, out_far, out_near, other[4])
+    moved = [sum_out[0].advance(), out_far]
     out_far_got = swap(out_far, "tensor", 1)
-    moved = [sum_out[0].advance(), out_far, send]
-    out_near = output_part((2, 0), [tie(low_mixed[0], *moved), *low_mixed[1:]])
-    back = backward_part(0, tie(grad_mixer[0], out_near))
-    (value_send,), (value_own,) = weight_part(back[0])
-
-    value_own, out_far_got, send = meet(sum_out, value_own, out_far_got, gate_send[1])
-    sum_gate.append(Sum(gate_own[1], over_x(send), 0, low_bits))
+    sum_out.append(Sum(stack, None, 2, low_bits))
+    back = backward_part(0, tie(grad_mixer[0], *moved, sum_out[1].sent))
+
+    grad_value, out_far_got = meet(sum_out[:1], back[0], out_far_got)
+    moved = [sum_out[0].advance()]
     out_sum = add_low(out_near[0], out_far_got[1])
     out_y = swap(out_sum, "tensor", 2)
-    moved = [sum_out[0].advance(), sum_out[1].advance(), out_sum, send, value_own]
-    backs = [back, backward_part(1, tie(grad_mixer[1], *moved))]
-    (value_send2,), (value_own2,) = weight_part(backs[1][0])
-
-    value_own2, out_y, value_send = meet([*sum_out, sum_gate[0]], value_own2, out_y, value_send)
+    value_send, value_own = weight_part(tie(grad_value, *moved, out_sum))
     sum_value = [Sum(value_own, over_x(value_send), 0, low_bits)]
-    moved = [sum_gate[0].advance(), sum_out[1].advance(), value_send, value_own2]
+    backs = [back, backward_part(1, tie(grad_mixer[1], value_own))]
+
+    grad_value2, out_y = meet([sum_gate, *sum_out], backs[1][0], out_y)
+    total_out = [sum_out[0].result()]
+    moved = [sum_gate.advance(), sum_out[1].advance(), total_out[0]]
+    value_send2, value_own2 = weight_part(tie(grad_value2, *moved))
+    sum_value.append(Sum(value_own2, over_x(value_send2), 0, low_bits))
+    moved = [value_own2]
     grad_value, grad_conv, grad_skip, cross_parts, folded_parts, maps_parts = zip(*backs)
     (grad_state, grad_step, grad_conv_state, grad_heads) = call(
         functools.partial(finish_kernel, heads, CHUNKS),
@@ -882,37 +913,37 @@
         per_head, marks, maps, seg_row, pre_state, conv_state_pad, rate8,
     )
 
-
-    grad_state, value_send2 = meet(sum_gate, grad_state, value_send2)
-    sum_value.append(Sum(value_own2, over_x(value_send2), 0, low_bits))
+    (grad_state,) = meet(sum_value[:1], grad_state)
     state_got = swap(grad_state, "tensor", 1)
-    total_out = [sum_out[0].result()]
-    moved = [sum_gate[0].advance(), sum_gate[1].advance(), total_out[0], value_send2]
-    near_far = normed_part((1, 3), [tie(grad_gate[0], *moved), *grad_gate[1:]], grad_value)
-
-    near_far, state_got = meet(sum_out[1:], near_far, state_got)
+    moved = [sum_value[0].advance(), grad_state]
+    near_far, near = normed_part([tie(grad_gate[0], *moved), *grad_gate[1:]])
+
+    near_far, near, state_got = meet([*sum_value, sum_gate, sum_out[1]], near_far, near, state_got)
+    near_far_got = swap(near_far, "tensor", 1)
     state_sum = add_low(grad_state, state_got)
     state_got = swap(state_sum, "tensor", 2)
-    near_far_got = swap(near_far, "tensor", 1)
-    total_out.append(sum_out[1].result())
-    near = normed_part((2, 0), [tie(grad_gate[0], near_far, state_sum, total_out[1]), *grad_gate[1:]], grad_value)
-
-    near, near_far_got, state_got = meet(sum_gate, near, near_far_got, state_got)
+    moved = [sum_value[1].advance(), sum_gate.advance(), state_sum]
+    near, near_far_got, *_ = lax.optimization_barrier((near, near_far_got, *moved))
     near_sum = add_low(near[0], near_far_got[1])
     over_y = swap(near_sum, "tensor", 2)
-    total_gate = [sum_gate[0].result()]
-    moved = [sum_gate[1].advance()]
-    state_all = tie(add_low(state_sum, state_got), near_sum, *total_gate, *moved)
-    grad_step, norm_gain, grad_conv_state, grad_heads, normed = lax.optimization_barrier(
-        (grad_step, norm_gain, grad_conv_state, grad_heads, normed, state_all)
-    )[:-1]
-
-    branch = out_near[1].astype(F32) + out_far_got[0].astype(F32) + out_y.astype(F32)
-    own_tokens = tokens.astype(F32)
-    output = (own_tokens + branch).astype(BF16)
-
+    sum_value[0].got = tie(sum_value[0].got, near_sum)
+    moved = [sum_value[0].advance()]
+    sum_out[1].got = tie(sum_out[1].got, *moved)
+    out_x = sum_out[1].result()
+    out_x_low = out_x[0].astype(BF16)
+    near_sum = tie(near_sum, out_x_low)
+    late = (
+        out_x_low, grad_step, norm_gain, grad_conv_state, grad_heads, normed, state_got,
+        grad_conv, grad_skip, grad_gain, stats, marks, per_head,
+    )
+    (
+        out_x_low, grad_step, norm_gain, grad_conv_state, grad_heads, normed, state_got,
+        grad_conv, grad_skip, grad_gain, stats, marks, per_head,
+    ) = lax.optimization_barrier((late, near_sum))[0]
+    out_x_got = over_x(out_x_low)
+    state_all = add_low(state_sum, state_got)
+    own_rows = piece_rows // parts
     grad_w_state = dot(normed, state_all, TN).astype(BF16)
-    own_rows = piece_rows // parts
     grad_w_state = lax.dynamic_slice_in_dim(
         grad_w_state.reshape(groups, parts, own_rows, states2), rank, 1, axis=1
     )
@@ -925,15 +956,23 @@
     small_own = lax.dynamic_slice_in_dim(small, place[0], 1, 1).reshape(groups // 2, -1)
     small_send = lax.dynamic_slice_in_dim(small, 1 - place[0], 1, 1).reshape(groups // 2, -1)
     small_sum = Sum(small_own, over_x(small_send), 0, low_bits)
-    (small_send,) = meet([*sum_value[:1], *sum_gate[1:]], small_send)
-    total_gate.append(sum_gate[1].result())
-    moved = [sum_value[0].advance(), total_gate[1], small_send]
-    over_y, *_ = meet([*sum_value, small_sum], over_y, *moved)
-    moved = [sum_value[1].advance(), sum_value[0].advance(), small_sum.advance()]
+    (small_send,) = meet([sum_value[1], sum_gate], small_send)
+    total_gate = sum_gate.result()
+    moved = [sum_value[1].advance(), total_gate]
+    over_y, *_ = lax.optimization_barrier((over_y, *moved))
+    scale_out = lax.rsqrt(stats[0] / (channels * parts) + EPSILON)
+    factor = scale_out * marks[:length, 5]
+    branch = out_near[1].astype(F32) + out_far_got[0].astype(F32) + out_y.astype(F32)
+    own_tokens = tokens.astype(F32)
+    output = (own_tokens + factor[:, None] * branch).astype(BF16)
     grad_normed = near[1].astype(F32) + near_far_got[0].astype(F32) + over_y.astype(F32)
     own_gain = lax.dynamic_slice_in_dim(norm_gain, rank * quarter, quarter, 0)
     scale_in = per_head[:, 5 * heads : 5 * heads + 1]
     row_norm = sum_all(jnp.sum(own_tokens * own_gain * grad_normed, axis=1), "tensor")
+    row_norm, out_x_got = meet([*sum_value, small_sum], row_norm, out_x_got)
+    moved = [small_sum.advance()]
+    total_value = [part.result() for part in sum_value]
+    total_out.append(out_x[1] + out_x_got.astype(F32))
     grad_tokens = (
         cotangent.astype(F32)
         + scale_in * own_gain * grad_normed
@@ -941,16 +980,13 @@
     ).astype(BF16)
     grad_norm_gain = jnp.sum(grad_normed * own_tokens * scale_in, axis=0)
 
-    moved = meet([sum_value[1], small_sum], grad_tokens, *moved)
-    grad_tokens = moved[0]
-    moved = [sum_value[1].advance(), small_sum.advance()]
+    (total_value[0],) = meet([small_sum], tie(total_value[0], *moved))
     small_sum = small_sum.result()[0]
     sum_state = small_sum[: own_rows * states2].reshape(own_rows, states2)
     sum_step = small_sum[own_rows * states2 :].reshape(heads, piece_rows).T
 
-    total_value = [part.result() for part in sum_value]
     sum_out = jnp.concatenate(total_out, axis=0)
-    sum_gate = jnp.concatenate(total_gate, axis=1)
+    sum_gate = total_gate
     sum_value = jnp.concatenate(total_value, axis=1)
     sum_inner = jnp.stack([sum_gate, sum_value], axis=1)
 

time: 362 us -> 336 us (0.928)
  Pallas kernels: 170 us -> 157 us
  other arithmetic: 57.9 us -> 49.2 us
  starting transfers between devices: 40.2 us -> 34.7 us
    pallas_call x6 -> x4, Pallas kernels: 59.6 us -> 45.5 us  [the longest x2 19.1 us: gate_part(): call(functools.partial(gate_kernel, parts, run, channels * parts, stacked...]
    convert_element_type x15 -> x12, other arithmetic: 23.2 us -> 14.7 us  [the longest x11 13.9 us: send(): functools.reduce(jnp.add, [term.astype(F32) for term in cut(1 - top)])]
    ppermute x42 -> x39, starting transfers between devices: 40.2 us -> 34.7 us  [swap(): return lax.ppermute(array, axis, [(i, i ^ mask) for i in range(count)])]
    unnamed x103 -> x122, local copies, waits for them, and re-layouts: 18.5 us -> 20.2 us
    add x7 -> x6, other arithmetic: 10.3 us -> 10.6 us  [result(): functools.reduce(jnp.add, [term.astype(F32) for term in (*self.terms, sel...]
    ppermute x42 -> x39, waiting for transfers between devices: 48.1 us -> 48.2 us  [swap(): return lax.ppermute(array, axis, [(i, i ^ mask) for i in range(count)])]
  transfers between devices with their start and end apart: 42 -> 39, of which waited for: 11 -> 12; matrix products, arithmetic and copies ran while one was open for 23% -> 24% of each run, Pallas kernels for 40% -> 41%
where the time goes in v3:
time: 336 us; the launch traced here: 331 us
  Pallas kernels  157 us (47%)
  other arithmetic  49.2 us (15%)
  waiting for transfers between devices  48.2 us (14%)
  local copies, waits for them, and re-layouts  38 us (11%)
  starting transfers between devices  34.7 us (10%)
    ppermute x39, waiting for transfers between devices, swap(): return lax.ppermute(array, axis, [(i, i ^ mask) for i in range(count)])  48.2 us
    pallas_call x1, Pallas kernels, shards(): call(functools.partial(front_kernel, parts, heads), (steps,), [held((leng...  37.1 us
    pallas_call x2, Pallas kernels, backward_part(): call(functools.partial(backward_kernel, heads, c * spans), (spans,), [chu...  34.7 us
    ppermute x39, starting transfers between devices, swap(): return lax.ppermute(array, axis, [(i, i ^ mask) for i in range(count)])  34.7 us
    unnamed x122, local copies, waits for them, and re-layouts  20.2 us
    pallas_call x3, Pallas kernels, weight_part(): call(weight_kernel, (runs,), [pl.BlockSpec((length, run), lambda j, p: (0...  20 us
    pallas_call x2, Pallas kernels, gate_part(): call(functools.partial(gate_kernel, parts, run, channels * parts, stacked...  19.1 us
    pallas_call x1, Pallas kernels, normed_part(): call(functools.partial(normed_kernel, len(grad_gate)), (4,), [held((lengt...  17.3 us
  transfers between devices with their start and end apart: 39, of which 12 were waited for; matrix products, arithmetic and copies ran while one was open for 24% of the time, Pallas kernels for 41%

profile of v3, /device:TPU:0, one launch (start us, length us, event | category | flops | bytes accessed | tf_op | source)
XLA Modules:
  0.0 331.1 jit_solution(9443345977717921307)
XLA Ops:
  0.6 3.0 collective-permute-start.1
  6.9 10.3 %copy.69 = bf16[256,8,2,1024]{3,1,2,0:T(8,128)(2,1)} copy(bf16[256,8,2,1024]{3,2,1,0:T(2,128)(2,1)} %bitcast.95) | data formatting | bytes 16777216
  21.1 6.1 %collective-permute-done.1.refs_2_ = bf16[1024,512]{1,0:T(8,128)(2,1)} collective-permute-done((bf16[1024,512]{1,0:T(8,128)(2,1)}, bf16[1024,512]{1,0:T(8,128)(2,1)}, u32[]{:S(2)}, u32[]{:S(2)}) %collective-permute-start.1) | collective-permute-done | bytes 1048608 | tf_op jit(solution)/shard_map/ppermute | solution.py:526
  27.8 1.7 collective-permute-start.4
  32.5 37.1 %front.1 = (bf16[1024,2048]{1,0:T(8,128)(2,1)}, f32[1024,256]{1,0:T(8,128)}, bf16[1024,256]{1,0:T(8,128)(2,1)}, bf16[256,1024]{1,0:T(8,128)(2,1)}, f32[1024,128]...) custom-call(s32[1]{0:T(128)} %bitcast.rank, ...), custom_call_target="tpu_custom_call" | custom-call | flops 343597376 | bytes 629145 | tf_op jit(solution)/shard_map/front/pallas_call | solution.py:672
  70.1 2.4 collective-permute-done.5.refs_3_
  73.4 11.8 %cotangent.1 = (bf16[1024,1024]{1,0:T(8,128)(2,1)}, f32[8,1024]{1,0:T(8,128)}) custom-call(s32[1]{0:T(128)} %bitcast.rank, bf16[1024,512]{1,0:T(8,128)(2,1)} %refs_0_.7, bf16[1024,512]{1,0:T(8,128)(2,1)} %collective-permute-done.3.refs_1_, bf16[1024,512]{1,0:T(8,128)(2,1)} %copy-done.5, bf16[1024,512]{1,0:T(8,128)(2,1)} %copy-done.6, ...), custom_call_target="tpu_custom_call" | custom-call | flops 85899344 | bytes 419430 | tf_op jit(solution)/shard_map/cotangent/pallas_call | solution.py:714
  88.3 3.1 collective-permute-done.7
  92.0 9.6 %gate.2 = (bf16[1024,512]{1,0:T(8,128)(2,1)}, bf16[1024,512]{1,0:T(8,128)(2,1)}, bf16[1024,512]{1,0:T(8,128)(2,1)}, f32[1,512]{1,0:T(1,128)}, bf16[512,1024]{1,0:T(8,128)(2,1)}, /*index=5*/bf16[512,1024]{1,0:T(8,128)(2,1)}) custom-call(s32[1]{0:T(128)} %bitcast.15.place, s32[1]{0:T(128)} %bitcast.rank, bf16[1024,512]{1,0:T(8,128)(2,1)} %refs_0_.7, ...), custom_call_target="tpu_custom_call" | custom-call | flops 42949672 | bytes 314572 | tf_op jit(solution)/shard_map/gate/pallas_call | solution.py:744
  101.6 1.6 collective-permute-start.8
  103.2 9.5 %gate.3 = (bf16[1024,512]{1,0:T(8,128)(2,1)}, bf16[1024,512]{1,0:T(8,128)(2,1)}, bf16[1024,512]{1,0:T(8,128)(2,1)}, f32[1,512]{1,0:T(1,128)}, bf16[2,512,1024]{2,1,0:T(8,128)(2,1)}) custom-call(s32[1]{0:T(128)} %bitcast.15.place, s32[1]{0:T(128)} %bitcast.rank, bf16[1024,512]{1,0:T(8,128)(2,1)} %refs_0_.7, bf16[1024,512]{1,0:T(8,128)(2,1)} %collective-permute-done.3.refs_1_, ...), custom_call_target="tpu_custom_call" | custom-call | flops 42949672 | bytes 314572 | tf_op jit(solution)/shard_map/gate/pallas_call | solution.py:744
  112.7 8.0 %weights.3 = (bf16[1024,1024]{1,0:T(8,128)(2,1)}, bf16[1024,1024]{1,0:T(8,128)(2,1)}) custom-call(s32[1]{0:T(128)} %bitcast.15.place, bf16[1024,2048]{1,0:T(8,128)(2,1)} %get-tuple-element.230.left_send.left_own, bf16[1024,2048]{1,0:T(8,128)(2,1)} %get-tuple-element.230.left_send.left_own, bf16[1024,512]{1,0:T(8,128)(2,1)} %get-tuple-element.201.refs_0_, ...), custom_call_target="tpu_custom_call" | custom-call | flops 85899344 | bytes 209715 | tf_op jit(solution)/shard_map/weights/pallas_call | solution.py:772
  120.7 9.1 %output.1 = (bf16[2,1024,512]{2,1,0:T(8,128)(2,1)}, bf16[2,1024,512]{2,1,0:T(8,128)(2,1)}) custom-call(s32[1]{0:T(128)} %bitcast.rank, bf16[1024,1024]{1,0:T(8,128)(2,1)} %get-tuple-element.156.refs_5_.gated, bf16[1024,2048]{1,0:T(8,128)(2,1)} %w_out.1), custom_call_target="tpu_custom_call" | custom-call | flops 85899344 | bytes 209715 | tf_op jit(solution)/shard_map/output/pallas_call | solution.py:828
  132.5 1.6 collective-permute-start.10
  134.2 2.3 constant_dynamic-slice_fusion.1
  136.9 17.3 %backward.2 = (bf16[1024,512]{1,0:T(8,128)(2,1)}, f32[8,512]{1,0:T(8,128)}, f32[1,512]{1,0:T(1,128)}, f32[1024,128]{1,0:T(8,128)}, f32[1024,128]{1,0:T(8,128)}, /*index=5*/f32[1024,256]{1,0:T(8,128)}) custom-call(f32[1024,1024]{1,0:T(8,128)} %get-tuple-element.161.value, bf16[1024,512]{1,0:T(8,128)(2,1)} %get-tuple-element.166.grad_out, ...), custom_call_target="tpu_custom_call" | custom-call | flops 400000000 | bytes 146800 | tf_op jit(solution)/shard_map/backward/pallas_call | solution.py:792
  154.3 1.6 fusion.10
  156.7 1.5 add_convert_fusion.13
  158.2 2.7 collective-permute-start.13
  160.8 5.9 %weights.4 = (bf16[1024,512]{1,0:T(8,128)(2,1)}, bf16[1024,512]{1,0:T(8,128)(2,1)}) custom-call(s32[1]{0:T(128)} %bitcast.15.place, bf16[1024,2048]{1,0:T(8,128)(2,1)} %get-tuple-element.230.left_send.left_own, bf16[1024,2048]{1,0:T(8,128)(2,1)} %get-tuple-element.230.left_send.left_own, bf16[1024,512]{1,0:T(8,128)(2,1)} %get-tuple-element.178.refs_0_.refs_2_), custom_call_target="tpu_custom_call" | custom-call | flops 42949672 | bytes 146800 | tf_op jit(solution)/shard_map/weights/pallas_call | solution.py:772
  166.7 1.5 collective-permute-start.15
  168.2 17.4 %backward.3 = (bf16[1024,512]{1,0:T(8,128)(2,1)}, f32[8,512]{1,0:T(8,128)}, f32[1,512]{1,0:T(1,128)}, f32[1024,128]{1,0:T(8,128)}, f32[1024,128]{1,0:T(8,128)}, /*index=5*/f32[1024,256]{1,0:T(8,128)}) custom-call(f32[1024,1024]{1,0:T(8,128)} %get-tuple-element.161.value, bf16[1024,512]{1,0:T(8,128)(2,1)} %get-tuple-element.180.grad_out, ...), custom_call_target="tpu_custom_call" | custom-call | flops 400000000 | bytes 146800 | tf_op jit(solution)/shard_map/backward/pallas_call | solution.py:792
  185.7 2.0 add_convert_fusion.8
  187.7 1.6 add_convert_fusion.1
  189.4 2.3 convert_add_fusion.5
  191.6 6.0 %weights.5 = (bf16[1024,512]{1,0:T(8,128)(2,1)}, bf16[1024,512]{1,0:T(8,128)(2,1)}) custom-call(s32[1]{0:T(128)} %bitcast.15.place, bf16[1024,2048]{1,0:T(8,128)(2,1)} %get-tuple-element.230.left_send.left_own, bf16[1024,2048]{1,0:T(8,128)(2,1)} %get-tuple-element.230.left_send.left_own, bf16[1024,512]{1,0:T(8,128)(2,1)} %get-tuple-element.188.refs_0_.refs_3_), custom_call_target="tpu_custom_call" | custom-call | flops 42949672 | bytes 146800 | tf_op jit(solution)/shard_map/weights/pallas_call | solution.py:772
  198.3 1.5 collective-permute-start.19
  199.8 7.9 %finish.1 = (bf16[1024,256]{1,0:T(8,128)(2,1)}, bf16[1024,128]{1,0:T(8,128)(2,1)}, f32[8,256]{1,0:T(8,128)}, f32[8,128]{1,0:T(8,128)}) custom-call(f32[1024,128]{1,0:T(8,128)} %get-tuple-element.190.refs_0_, f32[1024,128]{1,0:T(8,128)} %get-tuple-element.191.refs_1_, f32[1024,256]{1,0:T(8,128)} %get-tuple-element.192.refs_2_, ...), custom_call_target="tpu_custom_call" | custom-call | flops 80000000 | bytes 186286 | tf_op jit(solution)/shard_map/finish/pallas_call | solution.py:892
  208.8 17.3 %normed_grad.1 = (bf16[2,1024,512]{2,1,0:T(8,128)(2,1)}, bf16[2,1024,512]{2,1,0:T(8,128)(2,1)}) custom-call(s32[1]{0:T(128)} %bitcast.rank, bf16[1024,512]{1,0:T(8,128)(2,1)} %get-tuple-element.201.refs_0_, bf16[1024,512]{1,0:T(8,128)(2,1)} %get-tuple-element.154.refs_1_, bf16[1024,512]{1,0:T(8,128)(2,1)} %get-tuple-element.178.refs_0_.refs_2_, ...), custom_call_target="tpu_custom_call" | custom-call | flops 204010944 | bytes 335544 | tf_op jit(solution)/shard_map/normed_grad/pallas_call | solution.py:841
  226.1 18.2 %collective-permute-done.17 = bf16[512,512]{1,0:T(8,128)(2,1)S(1)} collective-permute-done((bf16[512,512]{1,0:T(8,128)(2,1)S(1)}, bf16[512,512]{1,0:T(8,128)(2,1)S(1)}, u32[]{:S(2)}, u32[]{:S(2)}) %collective-permute-start.17) | collective-permute-done | bytes 524320 | tf_op jit(solution)/shard_map/ppermute | solution.py:526
  248.8 1.7 add_convert_fusion.5
  250.5 2.1 collective-permute-start.25
  255.0 2.3 add_convert_fusion.12
  258.2 1.6 convert_add_fusion.2
  262.3 1.4 convolution_convert_fusion
  266.7 1.5 collective-permute-start.31
  268.3 8.8 %collective-permute-done.25 = bf16[256,1024]{1,0:T(8,128)(2,1)S(1)} collective-permute-done((bf16[256,1024]{1,0:T(8,128)(2,1)S(1)}, bf16[256,1024]{1,0:T(8,128)(2,1)S(1)}, u32[]{:S(2)}, u32[]{:S(2)}) %collective-permute-start.25) | collective-permute-done | bytes 524320 | tf_op jit(solution)/shard_map/ppermute | solution.py:526
  278.8 1.5 collective-permute-start.28
  286.2 2.9 convert_add_fusion.1
  289.3 2.3 fusion.8
  293.8 2.8 collective-permute-done.33
  298.3 1.4 concatenate.55
  303.9 1.7 collective-permute-start.37
  305.6 1.4 convert_add_fusion.4
  307.0 4.5 %fusion.4 = (bf16[1024,512]{1,0:T(8,128)(2,1)}, bf16[1024,512]{1,0:T(8,128)(2,1)}) fusion(bf16[1024,512]{1,0:T(8,128)(2,1)S(1)} %copy-done.4, bf16[1024,512]{1,0:T(8,128)(2,1)S(1)} %copy-done.3, f32[1024]{0:T(1024)S(1)} %add.382, f32[1024]{0:T(1024)} %get-tuple-element.321, f32[512]{0:T(512)S(1)} %copy-done.46, f32[1024]{0:T(1024)S(1)} %copy-done.43, ...), kind=kLoop, calls=%fused_computation.10 | loop fusion | flops 12058624 | bytes 10504192 | tf_op jit(solution)/shard_map/convert_element_type | solution.py:980
  315.1 2.5 collective-permute-done.35
  317.6 2.1 collective-permute-start.36
  322.1 2.9 copy.66
  (261 shorter events, 61.9 us)
Async XLA Ops:
  0.6 26.5 %collective-permute-start.1 = (bf16[1024,512]{1,0:T(8,128)(2,1)}, bf16[1024,512]{1,0:T(8,128)(2,1)}, u32[]{:S(2)}, u32[]{:S(2)}) collective-permute-start(bf16[1024,512]{1,0:T(8,128)(2,1)} %refs_0_.4), channel_id=1, source_target_pairs={{0,2},{1,3},{2,0},{3,1},{4,6},{5,7},{6,4},{7,5},{8,10},{9,11},{10,... | collective-permute-start | bytes 3145736 | tf_op jit(solution)/shard_map/ppermute | solution.py:526
  3.7 27.9 %collective-permute-start = (bf16[1024,512]{1,0:T(8,128)(2,1)}, bf16[1024,512]{1,0:T(8,128)(2,1)}, u32[]{:S(2)}, u32[]{:S(2)}) collective-permute-start(bf16[1024,512]{1,0:T(8,128)(2,1)} %refs_0_.4), channel_id=1, source_target_pairs={{0,1},{1,0},{2,3},{3,2},{4,5},{5,4},{6,7},{7,6},{8,9},{9,8},{10,11... | collective-permute-start | bytes 3145736 | tf_op jit(solution)/shard_map/ppermute | solution.py:526
  17.5 12.3 %copy-start.50 = (f32[5,256]{1,0:T(8,128)S(1)}, f32[5,256]{1,0:T(8,128)}, u32[]{:S(2)}) copy-start(f32[5,256]{1,0:T(8,128)} %param.22) | copy-start | bytes 15364
  17.5 12.8 %copy-start.57 = (f32[16]{0:T(128)S(1)}, f32[16]{0:T(128)}, u32[]{:S(2)}) copy-start(f32[16]{0:T(128)} %param.24) | copy-start | bytes 196
  17.5 13.4 %copy-start.56 = (f32[16]{0:T(128)S(1)}, f32[16]{0:T(128)}, u32[]{:S(2)}) copy-start(f32[16]{0:T(128)} %param.23) | copy-start | bytes 196
  27.8 3.8 %collective-permute-start.2 = (bf16[1024,512]{1,0:T(8,128)(2,1)}, bf16[1024,512]{1,0:T(8,128)(2,1)S(1)}, u32[]{:S(2)}, u32[]{:S(2)}) collective-permute-start(bf16[1024,512]{1,0:T(8,128)(2,1)} %collective-permute-done.1.refs_2_), channel_id=1, source_target_pairs={{0,1},{1,0},{2,3},{3,2},{4,5},{5,4},{6,7},{7,6},{8,9},{9,8},{10,11... | collective-permute-start | bytes 3145736 | tf_op jit(solution)/shard_map/ppermute | solution.py:526
  27.8 41.9 %collective-permute-start.4 = (bf16[1024,512]{1,0:T(8,128)(2,1)S(1)}, bf16[1024,512]{1,0:T(8,128)(2,1)S(1)}, u32[]{:S(2)}, u32[]{:S(2)}) collective-permute-start(bf16[1024,512]{1,0:T(8,128)(2,1)S(1)} %copy-done.2), channel_id=1, source_target_pairs={{0,2},{1,3},{2,0},{3,1},{4,6},{5,7},{6,4},{7,5},{8,10},{9,11},{10,... | collective-permute-start | bytes 3145736 | tf_op jit(solution)/shard_map/ppermute | solution.py:526
  29.5 40.5 %collective-permute-start.3 = (bf16[1024,512]{1,0:T(8,128)(2,1)S(1)}, bf16[1024,512]{1,0:T(8,128)(2,1)}, u32[]{:S(2)}, u32[]{:S(2)}) collective-permute-start(bf16[1024,512]{1,0:T(8,128)(2,1)S(1)} %copy-done.2), channel_id=1, source_target_pairs={{0,1},{1,0},{2,3},{3,2},{4,5},{5,4},{6,7},{7,6},{8,9},{9,8},{10,11... | collective-permute-start | bytes 3145736 | tf_op jit(solution)/shard_map/ppermute | solution.py:526
  69.7 2.7 collective-permute-start.5
  85.2 1.5 collective-permute-start.6
  87.5 3.9 %collective-permute-start.7 = (f32[8,1024]{1,0:T(8,128)S(1)}, f32[8,1024]{1,0:T(8,128)S(1)}, u32[]{:S(2)}, u32[]{:S(2)}) collective-permute-start(f32[8,1024]{1,0:T(8,128)S(1)} %add.337), channel_id=1, source_target_pairs={{0,2},{1,3},{2,0},{3,1},{4,6},{5,7},{6,4},{7,5},{8,10},{9,11},{10,... | collective-permute-start | bytes 98312 | tf_op jit(solution)/shard_map/ppermute | solution.py:526
  101.6 28.2 %collective-permute-start.8 = (bf16[512,1024]{1,0:T(8,128)(2,1)}, bf16[512,1024]{1,0:T(8,128)(2,1)S(1)}, u32[]{:S(2)}, u32[]{:S(2)}) collective-permute-start(bf16[512,1024]{1,0:T(8,128)(2,1)} %get-tuple-element.159), channel_id=1, source_target_pairs={{0,4},{4,0},{8,12},{12,8},{16,20},{20,16},{24,28},{28,24},{1,5},{5... | collective-permute-start | bytes 3145736 | tf_op jit(solution)/shard_map/ppermute | solution.py:526
  130.8 23.4 %collective-permute-start.9 = (bf16[2,1024,512]{2,1,0:T(8,128)(2,1)}, bf16[2,1024,512]{2,1,0:T(8,128)(2,1)S(1)}, u32[]{:S(2)}, u32[]{:S(2)}) collective-permute-start(bf16[2,1024,512]{2,1,0:T(8,128)(2,1)} %get-tuple-element.165), channel_id=1, source_target_pairs={{0,1},{1,0},{2,3},{3,2},{4,5},{5,4},{6,7},{7,6},{8,9},{9,8},{10,11... | collective-permute-start | bytes 6291464 | tf_op jit(solution)/shard_map/ppermute | solution.py:526
  130.8 54.9 %collective-permute-start.12 = (bf16[1024,1024]{1,0:T(8,128)(2,1)}, bf16[1024,1024]{1,0:T(8,128)(2,1)}, u32[]{:S(2)}, u32[]{:S(2)}) collective-permute-start(bf16[1024,1024]{1,0:T(8,128)(2,1)} %get-tuple-element.182), channel_id=1, source_target_pairs={{0,4},{4,0},{8,12},{12,8},{16,20},{20,16},{24,28},{28,24},{1,5},{5... | collective-permute-start | bytes 6291464 | tf_op jit(solution)/shard_map/ppermute | solution.py:526
  132.5 21.7 %collective-permute-start.10 = (bf16[512,512]{1,0:T(8,128)(2,1)S(1)}, bf16[512,512]{1,0:T(8,128)(2,1)S(1)}, u32[]{:S(2)}, u32[]{:S(2)}) collective-permute-start(bf16[512,512]{1,0:T(8,128)(2,1)S(1)} %add_convert_fusion.9), channel_id=1, source_target_pairs={{0,8},{4,12},{8,0},{12,4},{16,24},{20,28},{24,16},{28,20},{1,9},{5... | collective-permute-start | bytes 1572872 | tf_op jit(solution)/shard_map/ppermute | solution.py:526
  136.4 49.2 %collective-permute-start.14 = (bf16[2,512,512]{2,1,0:T(8,128)(2,1)}, bf16[2,512,512]{2,1,0:T(8,128)(2,1)}, u32[]{:S(2)}, u32[]{:S(2)}) collective-permute-start(bf16[2,512,512]{2,1,0:T(8,128)(2,1)} %constant_dynamic-slice_fusion.1), channel_id=1, source_target_pairs={{0,8},{4,12},{8,0},{12,4},{16,24},{20,28},{24,16},{28,20},{1,9},{5... | collective-permute-start | bytes 3145736 | tf_op jit(solution)/shard_map/ppermute | solution.py:526
  136.9 17.4 %copy-start.14 = (bf16[2,1024,512]{2,1,0:T(8,128)(2,1)S(1)}, bf16[2,1024,512]{2,1,0:T(8,128)(2,1)}, u32[]{:S(2)}) copy-start(bf16[2,1024,512]{2,1,0:T(8,128)(2,1)} %get-tuple-element.176) | copy-start | bytes 6291460
  155.9 29.8 %collective-permute-start.11 = (bf16[1024,512]{1,0:T(8,128)(2,1)}, bf16[1024,512]{1,0:T(8,128)(2,1)S(1)}, u32[]{:S(2)}, u32[]{:S(2)}) collective-permute-start(bf16[1024,512]{1,0:T(8,128)(2,1)} %fusion.10), channel_id=1, source_target_pairs={{0,2},{1,3},{2,0},{3,1},{4,6},{5,7},{6,4},{7,5},{8,10},{9,11},{10,... | collective-permute-start | bytes 3145736 | tf_op jit(solution)/shard_map/ppermute | solution.py:526
  158.2 27.5 %collective-permute-start.13 = (bf16[512,256]{1,0:T(8,128)(2,1)S(1)}, bf16[512,256]{1,0:T(8,128)(2,1)}, u32[]{:S(2)}, u32[]{:S(2)}) collective-permute-start(bf16[512,256]{1,0:T(8,128)(2,1)S(1)} %add_convert_fusion.13), channel_id=1, source_target_pairs={{0,16},{4,20},{8,24},{12,28},{16,0},{20,4},{24,8},{28,12},{1,17},{... | collective-permute-start | bytes 786440 | tf_op jit(solution)/shard_map/ppermute | solution.py:526
  166.7 40.9 %collective-permute-start.15 = (bf16[1024,512]{1,0:T(8,128)(2,1)}, bf16[1024,512]{1,0:T(8,128)(2,1)S(1)}, u32[]{:S(2)}, u32[]{:S(2)}) collective-permute-start(bf16[1024,512]{1,0:T(8,128)(2,1)} %get-tuple-element.198), channel_id=1, source_target_pairs={{0,4},{4,0},{8,12},{12,8},{16,20},{20,16},{24,28},{28,24},{1,5},{5... | collective-permute-start | bytes 3145736 | tf_op jit(solution)/shard_map/ppermute | solution.py:526
  168.2 19.5 %copy-start.17 = (bf16[1024,1024]{1,0:T(8,128)(2,1)S(1)}, bf16[1024,1024]{1,0:T(8,128)(2,1)}, u32[]{:S(2)}) copy-start(bf16[1024,1024]{1,0:T(8,128)(2,1)} %get-tuple-element.155) | copy-start | bytes 6291460
  197.7 46.7 %collective-permute-start.18 = (bf16[1024,512]{1,0:T(8,128)(2,1)}, bf16[1024,512]{1,0:T(8,128)(2,1)S(1)}, u32[]{:S(2)}, u32[]{:S(2)}) collective-permute-start(bf16[1024,512]{1,0:T(8,128)(2,1)} %get-tuple-element.205), channel_id=1, source_target_pairs={{0,4},{4,0},{8,12},{12,8},{16,20},{20,16},{24,28},{28,24},{1,5},{5... | collective-permute-start | bytes 3145736 | tf_op jit(solution)/shard_map/ppermute | solution.py:526
  198.3 46.1 %collective-permute-start.19 = (bf16[512,1024]{1,0:T(8,128)(2,1)S(1)}, bf16[512,1024]{1,0:T(8,128)(2,1)S(1)}, u32[]{:S(2)}, u32[]{:S(2)}) collective-permute-start(bf16[512,1024]{1,0:T(8,128)(2,1)S(1)} %add_convert_fusion.1), channel_id=1, source_target_pairs={{0,8},{4,12},{8,0},{12,4},{16,24},{20,28},{24,16},{28,20},{1,9},{5... | collective-permute-start | bytes 3145736 | tf_op jit(solution)/shard_map/ppermute | solution.py:526
  207.8 36.5 %collective-permute-start.17 = (bf16[512,512]{1,0:T(8,128)(2,1)S(1)}, bf16[512,512]{1,0:T(8,128)(2,1)S(1)}, u32[]{:S(2)}, u32[]{:S(2)}) collective-permute-start(bf16[512,512]{1,0:T(8,128)(2,1)S(1)} %add_convert_fusion.7), channel_id=1, source_target_pairs={{0,8},{4,12},{8,0},{12,4},{16,24},{20,28},{24,16},{28,20},{1,9},{5... | collective-permute-start | bytes 1572872 | tf_op jit(solution)/shard_map/ppermute | solution.py:526
  208.5 35.9 %collective-permute-start.16 = (bf16[1024,256]{1,0:T(8,128)(2,1)}, bf16[1024,256]{1,0:T(8,128)(2,1)S(1)}, u32[]{:S(2)}, u32[]{:S(2)}) collective-permute-start(bf16[1024,256]{1,0:T(8,128)(2,1)} %get-tuple-element.200.refs_4_), channel_id=1, source_target_pairs={{0,1},{1,0},{2,3},{3,2},{4,5},{5,4},{6,7},{7,6},{8,9},{9,8},{10,11... | collective-permute-start | bytes 1572872 | tf_op jit(solution)/shard_map/ppermute | solution.py:526
  208.5 35.9 %collective-permute-start.20 = (bf16[2,512,256]{2,1,0:T(8,128)(2,1)S(1)}, bf16[2,512,256]{2,1,0:T(8,128)(2,1)S(1)}, u32[]{:S(2)}, u32[]{:S(2)}) collective-permute-start(bf16[2,512,256]{2,1,0:T(8,128)(2,1)S(1)} %add_convert_fusion.8), channel_id=1, source_target_pairs={{0,16},{4,20},{8,24},{12,28},{16,0},{20,4},{24,8},{28,12},{1,17},{... | collective-permute-start | bytes 1572872 | tf_op jit(solution)/shard_map/ppermute | solution.py:526
  208.8 37.4 %copy-start.16 = (bf16[1024,256]{1,0:T(8,128)(2,1)S(1)}, bf16[1024,256]{1,0:T(8,128)(2,1)}, u32[]{:S(2)}) copy-start(bf16[1024,256]{1,0:T(8,128)(2,1)} %get-tuple-element.200.refs_4_) | copy-start | bytes 1572868
  246.2 6.7 %collective-permute-start.21 = (bf16[2,1024,512]{2,1,0:T(8,128)(2,1)}, bf16[2,1024,512]{2,1,0:T(8,128)(2,1)S(1)}, u32[]{:S(2)}, u32[]{:S(2)}) collective-permute-start(bf16[2,1024,512]{2,1,0:T(8,128)(2,1)} %get-tuple-element.209), channel_id=1, source_target_pairs={{0,1},{1,0},{2,3},{3,2},{4,5},{5,4},{6,7},{7,6},{8,9},{9,8},{10,11... | collective-permute-start | bytes 6291464 | tf_op jit(solution)/shard_map/ppermute | solution.py:526
  247.6 14.8 %collective-permute-start.22 = (bf16[1024,256]{1,0:T(8,128)(2,1)S(1)}, bf16[1024,256]{1,0:T(8,128)(2,1)S(1)}, u32[]{:S(2)}, u32[]{:S(2)}) collective-permute-start(bf16[1024,256]{1,0:T(8,128)(2,1)S(1)} %add_convert_fusion.4), channel_id=1, source_target_pairs={{0,2},{1,3},{2,0},{3,1},{4,6},{5,7},{6,4},{7,5},{8,10},{9,11},{10,... | collective-permute-start | bytes 1572872 | tf_op jit(solution)/shard_map/ppermute | solution.py:526
  250.5 26.5 %collective-permute-start.25 = (bf16[256,1024]{1,0:T(8,128)(2,1)S(1)}, bf16[256,1024]{1,0:T(8,128)(2,1)S(1)}, u32[]{:S(2)}, u32[]{:S(2)}) collective-permute-start(bf16[256,1024]{1,0:T(8,128)(2,1)S(1)} %add_convert_fusion.5), channel_id=1, source_target_pairs={{0,16},{4,20},{8,24},{12,28},{16,0},{20,4},{24,8},{28,12},{1,17},{... | collective-permute-start | bytes 1572872 | tf_op jit(solution)/shard_map/ppermute | solution.py:526
  252.8 25.1 %collective-permute-start.24 = (bf16[512,512]{1,0:T(8,128)(2,1)S(1)}, bf16[512,512]{1,0:T(8,128)(2,1)S(1)}, u32[]{:S(2)}, u32[]{:S(2)}) collective-permute-start(bf16[512,512]{1,0:T(8,128)(2,1)S(1)} %add_convert_fusion.6), channel_id=1, source_target_pairs={{0,8},{4,12},{8,0},{12,4},{16,24},{20,28},{24,16},{28,20},{1,9},{5... | collective-permute-start | bytes 1572872 | tf_op jit(solution)/shard_map/ppermute | solution.py:526
  254.2 35.0 %collective-permute-start.23 = (bf16[1024,512]{1,0:T(8,128)(2,1)}, bf16[1024,512]{1,0:T(8,128)(2,1)S(1)}, u32[]{:S(2)}, u32[]{:S(2)}) collective-permute-start(bf16[1024,512]{1,0:T(8,128)(2,1)} %fusion.11), channel_id=1, source_target_pairs={{0,2},{1,3},{2,0},{3,1},{4,6},{5,7},{6,4},{7,5},{8,10},{9,11},{10,... | collective-permute-start | bytes 3145736 | tf_op jit(solution)/shard_map/ppermute | solution.py:526
  257.3 44.2 %collective-permute-start.29 = (bf16[256,512]{1,0:T(8,128)(2,1)}, bf16[256,512]{1,0:T(8,128)(2,1)}, u32[]{:S(2)}, u32[]{:S(2)}) collective-permute-start(bf16[256,512]{1,0:T(8,128)(2,1)} %add_convert_fusion.12), channel_id=1, source_target_pairs={{0,16},{4,20},{8,24},{12,28},{16,0},{20,4},{24,8},{28,12},{1,17},{... | collective-permute-start | bytes 786440 | tf_op jit(solution)/shard_map/ppermute | solution.py:526
  264.7 18.2 %copy-start.7 = (f32[1024,128]{1,0:T(8,128)S(1)}, f32[1024,128]{1,0:T(8,128)}, u32[]{:S(2)}) copy-start(f32[1024,128]{1,0:T(8,128)} %get-tuple-element.228.per_head.refs_6_) | copy-start | bytes 1572868
  264.9 19.1 %copy-start.1 = (f32[1032,128]{1,0:T(8,128)S(1)}, f32[1032,128]{1,0:T(8,128)}, u32[]{:S(2)}) copy-start(f32[1032,128]{1,0:T(8,128)} %pad.16.refs_15_.refs_9_.marks.refs_7_) | copy-start | bytes 1585156
  266.7 34.8 %collective-permute-start.31 = (bf16[4,20480]{1,0:T(4,128)(2,1)}, bf16[4,20480]{1,0:T(4,128)(2,1)}, u32[]{:S(2)}, u32[]{:S(2)}) collective-permute-start(bf16[4,20480]{1,0:T(4,128)(2,1)} %bitcast.87), channel_id=1, source_target_pairs={{0,4},{4,0},{8,12},{12,8},{16,20},{20,16},{24,28},{28,24},{1,5},{5... | collective-permute-start | bytes 491528 | tf_op jit(solution)/shard_map/ppermute | solution.py:526
  278.8 22.7 %collective-permute-start.30 = (bf16[256,512]{1,0:T(8,128)(2,1)}, bf16[256,512]{1,0:T(8,128)(2,1)}, u32[]{:S(2)}, u32[]{:S(2)}) collective-permute-start(bf16[256,512]{1,0:T(8,128)(2,1)} %add_convert_fusion.11), channel_id=1, source_target_pairs={{0,16},{4,20},{8,24},{12,28},{16,0},{20,4},{24,8},{28,12},{1,17},{... | collective-permute-start | bytes 786440 | tf_op jit(solution)/shard_map/ppermute | solution.py:526
  278.8 22.7 %collective-permute-start.28 = (bf16[512,256]{1,0:T(8,128)(2,1)}, bf16[512,256]{1,0:T(8,128)(2,1)}, u32[]{:S(2)}, u32[]{:S(2)}) collective-permute-start(bf16[512,256]{1,0:T(8,128)(2,1)} %fusion.14), channel_id=1, source_target_pairs={{0,4},{4,0},{8,12},{12,8},{16,20},{20,16},{24,28},{28,24},{1,5},{5... | collective-permute-start | bytes 786440 | tf_op jit(solution)/shard_map/ppermute | solution.py:526
  289.2 2.4 collective-permute-start.32
  291.6 15.4 %copy-start.3 = (bf16[1024,512]{1,0:T(8,128)(2,1)S(1)}, bf16[1024,512]{1,0:T(8,128)(2,1)}, u32[]{:S(2)}) copy-start(bf16[1024,512]{1,0:T(8,128)(2,1)} %refs_0_.7) | copy-start | bytes 3145732
  291.6 1.4 collective-permute-start.26
  293.0 3.7 %collective-permute-start.33 = (f32[5,256]{1,0:T(8,128)S(1)}, f32[5,256]{1,0:T(8,128)S(1)}, u32[]{:S(2)}, u32[]{:S(2)}) collective-permute-start(f32[5,256]{1,0:T(8,128)S(1)} %slice_add_fusion), channel_id=1, source_target_pairs={{0,2},{1,3},{2,0},{3,1},{4,6},{5,7},{6,4},{7,5},{8,10},{9,11},{10,... | collective-permute-start | bytes 15368 | tf_op jit(solution)/shard_map/ppermute | solution.py:526
  296.6 3.7 %collective-permute-start.27 = (f32[1024]{0:T(1024)S(1)}, f32[1024]{0:T(1024)}, u32[]{:S(2)}, u32[]{:S(2)}) collective-permute-start(f32[1024]{0:T(1024)S(1)} %add.381), channel_id=1, source_target_pairs={{0,2},{1,3},{2,0},{3,1},{4,6},{5,7},{6,4},{7,5},{8,10},{9,11},{10,... | collective-permute-start | bytes 12296 | tf_op jit(solution)/shard_map/ppermute | solution.py:526
  300.3 12.6 %collective-permute-start.34 = (f32[7984]{0:T(1024)}, f32[7984]{0:T(1024)S(1)}, u32[]{:S(2)}, u32[]{:S(2)}) collective-permute-start(f32[7984]{0:T(1024)} %concatenate.55), channel_id=1, source_target_pairs={{0,4},{4,0},{8,12},{12,8},{16,20},{20,16},{24,28},{28,24},{1,5},{5... | collective-permute-start | bytes 95816 | tf_op jit(solution)/shard_map/ppermute | solution.py:526
  303.9 15.8 %collective-permute-start.37 = (bf16[2,20480]{1,0:T(2,128)(2,1)S(1)}, bf16[2,20480]{1,0:T(2,128)(2,1)S(1)}, u32[]{:S(2)}, u32[]{:S(2)}) collective-permute-start(bf16[2,20480]{1,0:T(2,128)(2,1)S(1)} %fusion.16), channel_id=1, source_target_pairs={{0,8},{4,12},{8,0},{12,4},{16,24},{20,28},{24,16},{28,20},{1,9},{5... | collective-permute-start | bytes 245768 | tf_op jit(solution)/shard_map/ppermute | solution.py:526
  313.7 3.9 %collective-permute-start.35 = (f32[7984]{0:T(1024)S(1)}, f32[7984]{0:T(1024)S(1)}, u32[]{:S(2)}, u32[]{:S(2)}) collective-permute-start(f32[7984]{0:T(1024)S(1)} %add.385), channel_id=1, source_target_pairs={{0,8},{4,12},{8,0},{12,4},{16,24},{20,28},{24,16},{28,20},{1,9},{5... | collective-permute-start | bytes 95816 | tf_op jit(solution)/shard_map/ppermute | solution.py:526
  317.6 7.5 %collective-permute-start.36 = (f32[7984]{0:T(1024)S(1)}, f32[7984]{0:T(1024)S(1)}, u32[]{:S(2)}, u32[]{:S(2)}) collective-permute-start(f32[7984]{0:T(1024)S(1)} %add.386), channel_id=1, source_target_pairs={{0,16},{4,20},{8,24},{12,28},{16,0},{20,4},{24,8},{28,12},{1,17},{... | collective-permute-start | bytes 95816 | tf_op jit(solution)/shard_map/ppermute | solution.py:526
  320.9 7.2 %collective-permute-start.38 = (bf16[1,20480]{1,0:T(2,128)(2,1)S(1)}, bf16[1,20480]{1,0:T(2,128)(2,1)S(1)}, u32[]{:S(2)}, u32[]{:S(2)}) collective-permute-start(bf16[1,20480]{1,0:T(2,128)(2,1)S(1)} %fusion.22), channel_id=1, source_target_pairs={{0,16},{4,20},{8,24},{12,28},{16,0},{20,4},{24,8},{28,12},{1,17},{... | collective-permute-start | bytes 122888 | tf_op jit(solution)/shard_map/ppermute | solution.py:526
  (49 other events, 232.8 us)

commit v4 on v3

--- a/solution.py
+++ b/solution.py
@@ -862,29 +862,29 @@
 
     first = gate_part(0, stats, False)
     sum_out = [Sum(first[5], over_x(first[4]), 1, low_bits)]
-    other = gate_part(1, tie(stats, first[5]), True)
+    other = gate_part(1, tie(stats, first[5]), False)
+    sum_out.append(Sum(other[5], over_x(other[4]), 1, low_bits))
     low_mixed, grad_mixer, grad_gate, grad_gain = zip(first[:4], other[:4])
-    gate_send, gate_own = weight_part(tie(grad_gate[0], other[4]), *grad_gate[1:])
+    gate_send, gate_own = weight_part(tie(grad_gate[0], other[5]), *grad_gate[1:])
     sum_gate = Sum(gate_own, over_x(gate_send), 0, low_bits)
     out_far, out_near = output_part(tie(low_gated, gate_own))
 
-    out_far, out_near, stack = meet(sum_out, out_far, out_near, other[4])
+    out_far, out_near = meet(sum_out[:1], out_far, out_near)
     moved = [sum_out[0].advance(), out_far]
     out_far_got = swap(out_far, "tensor", 1)
-    sum_out.append(Sum(stack, None, 2, low_bits))
-    back = backward_part(0, tie(grad_mixer[0], *moved, sum_out[1].sent))
-
-    grad_value, out_far_got = meet(sum_out[:1], back[0], out_far_got)
-    moved = [sum_out[0].advance()]
+    back = backward_part(0, tie(grad_mixer[0], *moved))
+
+    grad_value, out_far_got = meet(sum_out, back[0], out_far_got)
+    moved = [sum_out[1].advance(), sum_out[0].advance()]
     out_sum = add_low(out_near[0], out_far_got[1])
     out_y = swap(out_sum, "tensor", 2)
     value_send, value_own = weight_part(tie(grad_value, *moved, out_sum))
     sum_value = [Sum(value_own, over_x(value_send), 0, low_bits)]
     backs = [back, backward_part(1, tie(grad_mixer[1], value_own))]
 
-    grad_value2, out_y = meet([sum_gate, *sum_out], backs[1][0], out_y)
+    grad_value2, out_y = meet(sum_out, backs[1][0], out_y)
     total_out = [sum_out[0].result()]
-    moved = [sum_gate.advance(), sum_out[1].advance(), total_out[0]]
+    moved = [sum_out[1].advance(), total_out[0]]
     value_send2, value_own2 = weight_part(tie(grad_value2, *moved))
     sum_value.append(Sum(value_own2, over_x(value_send2), 0, low_bits))
     moved = [value_own2]
@@ -913,34 +913,31 @@
         per_head, marks, maps, seg_row, pre_state, conv_state_pad, rate8,
     )
 
-    (grad_state,) = meet(sum_value[:1], grad_state)
+    grad_state, grad_conv_state = meet([sum_gate, sum_out[1]], grad_state, grad_conv_state[:5])
     state_got = swap(grad_state, "tensor", 1)
-    moved = [sum_value[0].advance(), grad_state]
+    grad_conv_state = grad_conv_state + swap(grad_conv_state, "tensor", 1)
+    conv_got = swap(grad_conv_state, "tensor", 2)
+    total_out.append(sum_out[1].result())
+    moved = [sum_gate.advance(), grad_state, total_out[1], grad_conv_state]
     near_far, near = normed_part([tie(grad_gate[0], *moved), *grad_gate[1:]])
 
-    near_far, near, state_got = meet([*sum_value, sum_gate, sum_out[1]], near_far, near, state_got)
+    near_far, near, state_got, conv_got = meet([sum_value[0], sum_gate], near_far, near, state_got, conv_got)
     near_far_got = swap(near_far, "tensor", 1)
     state_sum = add_low(grad_state, state_got)
     state_got = swap(state_sum, "tensor", 2)
-    moved = [sum_value[1].advance(), sum_gate.advance(), state_sum]
+    grad_conv_state = grad_conv_state + conv_got
+    moved = [sum_value[0].advance(), sum_gate.advance(), state_sum]
     near, near_far_got, *_ = lax.optimization_barrier((near, near_far_got, *moved))
     near_sum = add_low(near[0], near_far_got[1])
     over_y = swap(near_sum, "tensor", 2)
-    sum_value[0].got = tie(sum_value[0].got, near_sum)
-    moved = [sum_value[0].advance()]
-    sum_out[1].got = tie(sum_out[1].got, *moved)
-    out_x = sum_out[1].result()
-    out_x_low = out_x[0].astype(BF16)
-    near_sum = tie(near_sum, out_x_low)
     late = (
-        out_x_low, grad_step, norm_gain, grad_conv_state, grad_heads, normed, state_got,
+        grad_step, norm_gain, grad_conv_state, grad_heads, normed, state_got,
         grad_conv, grad_skip, grad_gain, stats, marks, per_head,
     )
     (
-        out_x_low, grad_step, norm_gain, grad_conv_state, grad_heads, normed, state_got,
+        grad_step, norm_gain, grad_conv_state, grad_heads, normed, state_got,
         grad_conv, grad_skip, grad_gain, stats, marks, per_head,
     ) = lax.optimization_barrier((late, near_sum))[0]
-    out_x_got = over_x(out_x_low)
     state_all = add_low(state_sum, state_got)
     own_rows = piece_rows // parts
     grad_w_state = dot(normed, state_all, TN).astype(BF16)
@@ -948,6 +945,13 @@
         grad_w_state.reshape(groups, parts, own_rows, states2), rank, 1, axis=1
     )
     grad_w_step = dot(grad_step[:, :heads], normed, TN).astype(BF16)
+    grad_w_state, grad_w_step, grad_conv, grad_skip, grad_gain, stats, marks = meet(
+        sum_value, grad_w_state, grad_w_step, grad_conv, grad_skip, grad_gain, stats, marks
+    )
+    moved = [sum_value[1].advance(), sum_value[0].advance()]
+    (grad_w_state, grad_w_step, grad_conv, grad_skip, grad_gain, stats, marks), _ = lax.optimization_barrier(
+        ((grad_w_state, grad_w_step, grad_conv, grad_skip, grad_gain, stats, marks), moved)
+    )
     grad_w_step = grad_w_step.reshape(heads, groups, piece_rows).transpose(1, 0, 2)
     small = jnp.concatenate(
         [grad_w_state.reshape(groups, own_rows * states2), grad_w_step.reshape(groups, heads * piece_rows)], axis=1
@@ -956,31 +960,50 @@
     small_own = lax.dynamic_slice_in_dim(small, place[0], 1, 1).reshape(groups // 2, -1)
     small_send = lax.dynamic_slice_in_dim(small, 1 - place[0], 1, 1).reshape(groups // 2, -1)
     small_sum = Sum(small_own, over_x(small_send), 0, low_bits)
-    (small_send,) = meet([sum_value[1], sum_gate], small_send)
-    total_gate = sum_gate.result()
-    moved = [sum_value[1].advance(), total_gate]
-    over_y, *_ = lax.optimization_barrier((over_y, *moved))
+    grad_conv, grad_skip, grad_gate_gain = (
+        jnp.concatenate(array, axis=1) for array in (grad_conv, grad_skip, grad_gain)
+    )
+    skip_sums = jnp.sum(grad_skip.reshape(heads, channels // heads), axis=1)
+    pieces = [
+        grad_conv[:5].reshape(-1), grad_conv_state.reshape(-1), grad_heads[0, :heads], grad_heads[1, :heads],
+        skip_sums, grad_gate_gain[0],
+    ]
+    rest = jnp.concatenate(pieces)
     scale_out = lax.rsqrt(stats[0] / (channels * parts) + EPSILON)
     factor = scale_out * marks[:length, 5]
     branch = out_near[1].astype(F32) + out_far_got[0].astype(F32) + out_y.astype(F32)
     own_tokens = tokens.astype(F32)
     output = (own_tokens + factor[:, None] * branch).astype(BF16)
+
+    over_y, small_send, rest, output = meet([sum_value[1], sum_gate, small_sum], over_y, small_send, rest, output)
+    moved = [sum_value[1].advance(), small_sum.advance()]
+    total_gate = sum_gate.result()
+    over_y = tie(over_y, *moved)
     grad_normed = near[1].astype(F32) + near_far_got[0].astype(F32) + over_y.astype(F32)
     own_gain = lax.dynamic_slice_in_dim(norm_gain, rank * quarter, quarter, 0)
     scale_in = per_head[:, 5 * heads : 5 * heads + 1]
-    row_norm = sum_all(jnp.sum(own_tokens * own_gain * grad_normed, axis=1), "tensor")
-    row_norm, out_x_got = meet([*sum_value, small_sum], row_norm, out_x_got)
+    row_norm = jnp.sum(own_tokens * own_gain * grad_normed, axis=1)
+    grad_norm_gain = jnp.sum(grad_normed * own_tokens * scale_in, axis=0)
+    pack = jnp.concatenate([grad_norm_gain, rest])
+    pieces = [grad_norm_gain, *pieces]
+
+    row_got, pack_got = swap(row_norm, "tensor", 1), swap(pack, "dp", 1)
+    row_norm, row_got, pack, pack_got = meet([*sum_value, small_sum], row_norm, row_got, pack, pack_got)
     moved = [small_sum.advance()]
+    row_norm, pack = row_norm + row_got, pack + pack_got
+    row_got, pack_got = swap(row_norm, "tensor", 2), swap(pack, "dp", 2)
     total_value = [part.result() for part in sum_value]
-    total_out.append(out_x[1] + out_x_got.astype(F32))
+    row_norm, row_got, pack, pack_got, *_ = lax.optimization_barrier((row_norm, row_got, pack, pack_got, *total_value, *moved))
+    row_norm, pack = row_norm + row_got, pack + pack_got
+    bit = 4
+    while bit < groups:
+        pack = pack + swap(pack, "dp", bit)
+        bit *= 2
     grad_tokens = (
         cotangent.astype(F32)
         + scale_in * own_gain * grad_normed
         - own_tokens * scale_in**3 * row_norm[:, None] / width
     ).astype(BF16)
-    grad_norm_gain = jnp.sum(grad_normed * own_tokens * scale_in, axis=0)
-
-    (total_value[0],) = meet([small_sum], tie(total_value[0], *moved))
     small_sum = small_sum.result()[0]
     sum_state = small_sum[: own_rows * states2].reshape(own_rows, states2)
     sum_step = small_sum[own_rows * states2 :].reshape(heads, piece_rows).T
@@ -990,20 +1013,10 @@
     sum_value = jnp.concatenate(total_value, axis=1)
     sum_inner = jnp.stack([sum_gate, sum_value], axis=1)
 
-    grad_conv, grad_skip, grad_gate_gain = (
-        jnp.concatenate(array, axis=1) for array in (grad_conv, grad_skip, grad_gain)
-    )
-    grad_conv_state = sum_all(grad_conv_state[:5], "tensor")
-    skip_sums = jnp.sum(grad_skip.reshape(heads, channels // heads), axis=1)
-    pack = [
-        grad_norm_gain, grad_conv[:5].reshape(-1), grad_conv_state.reshape(-1),
-        grad_heads[0, :heads], grad_heads[1, :heads], skip_sums, grad_gate_gain[0],
-    ]
-    sums_all = sum_all(jnp.concatenate(pack), "dp")
     split = []
     at = 0
-    for piece in pack:
-        split.append(sums_all[at : at + piece.shape[0]])
+    for piece in pieces:
+        split.append(pack[at : at + piece.shape[0]])
         at += piece.shape[0]
     return (
         output,

time: 336 us -> 326 us (0.970)
  starting transfers between devices: 34.7 us -> 40.6 us
  other arithmetic: 49.2 us -> 43.5 us
  waiting for transfers between devices: 48.2 us -> 42.7 us
  local copies, waits for them, and re-layouts: 38 us -> 33.5 us
    ppermute x39, starting transfers between devices: 34.7 us -> 40.6 us  [swap(): return lax.ppermute(array, axis, [(i, i ^ mask) for i in range(count)])]
    ppermute x39, waiting for transfers between devices: 48.2 us -> 42.7 us  [swap(): return lax.ppermute(array, axis, [(i, i ^ mask) for i in range(count)])]
    add x6 -> x5, other arithmetic: 10.6 us -> 6.49 us  [result(): functools.reduce(jnp.add, [term.astype(F32) for term in (*self.terms, sel...]
    convert_element_type x11 -> x12, other arithmetic: 13.9 us -> 14.8 us  [send(): functools.reduce(jnp.add, [term.astype(F32) for term in cut(1 - top)])]
    unnamed x122 -> x107, local copies, waits for them, and re-layouts: 20.2 us -> 20.4 us
  transfers between devices with their start and end apart: 39 -> 39, of which waited for: 12 -> 13; matrix products, arithmetic and copies ran while one was open for 24% -> 21% of each run, Pallas kernels for 41% -> 42%
where the time goes in v4:
time: 326 us; the launch traced here: 321 us
  Pallas kernels  157 us (48%)
  other arithmetic  43.5 us (13%)
  waiting for transfers between devices  42.7 us (13%)
  starting transfers between devices  40.6 us (12%)
  local copies, waits for them, and re-layouts  33.5 us (10%)
    ppermute x39, waiting for transfers between devices, swap(): return lax.ppermute(array, axis, [(i, i ^ mask) for i in range(count)])  42.7 us
    ppermute x39, starting transfers between devices, swap(): return lax.ppermute(array, axis, [(i, i ^ mask) for i in range(count)])  40.6 us
    pallas_call x1, Pallas kernels, shards(): call(functools.partial(front_kernel, parts, heads), (steps,), [held((leng...  37.1 us
    pallas_call x2, Pallas kernels, backward_part(): call(functools.partial(backward_kernel, heads, c * spans), (spans,), [chu...  34.6 us
    unnamed x107, local copies, waits for them, and re-layouts  20.4 us
    pallas_call x3, Pallas kernels, weight_part(): call(weight_kernel, (runs,), [pl.BlockSpec((length, run), lambda j, p: (0...  20.1 us
    pallas_call x2, Pallas kernels, gate_part(): call(functools.partial(gate_kernel, parts, run, channels * parts, stacked...  18.8 us
    pallas_call x1, Pallas kernels, normed_part(): call(functools.partial(normed_kernel, len(grad_gate)), (4,), [held((lengt...  17.3 us
  transfers between devices with their start and end apart: 39, of which 13 were waited for; matrix products, arithmetic and copies ran while one was open for 21% of the time, Pallas kernels for 42%

profile of v4, /device:TPU:0, one launch (start us, length us, event | category | flops | bytes accessed | tf_op | source)
XLA Modules:
  0.0 320.9 jit_solution(3195124596557367489)
XLA Ops:
  0.6 3.0 collective-permute-start.1
  6.9 10.3 %copy.69 = bf16[256,8,2,1024]{3,1,2,0:T(8,128)(2,1)} copy(bf16[256,8,2,1024]{3,2,1,0:T(2,128)(2,1)} %bitcast.89) | data formatting | bytes 16777216
  21.1 6.1 %collective-permute-done.1.refs_2_ = bf16[1024,512]{1,0:T(8,128)(2,1)} collective-permute-done((bf16[1024,512]{1,0:T(8,128)(2,1)}, bf16[1024,512]{1,0:T(8,128)(2,1)}, u32[]{:S(2)}, u32[]{:S(2)}) %collective-permute-start.1) | collective-permute-done | bytes 1048608 | tf_op jit(solution)/shard_map/ppermute | solution.py:526
  27.8 1.7 collective-permute-start.2
  32.5 37.1 %front.1 = (bf16[1024,2048]{1,0:T(8,128)(2,1)}, f32[1024,256]{1,0:T(8,128)}, bf16[1024,256]{1,0:T(8,128)(2,1)}, bf16[256,1024]{1,0:T(8,128)(2,1)}, f32[1024,128]...) custom-call(s32[1]{0:T(128)} %bitcast.rank, ...), custom_call_target="tpu_custom_call" | custom-call | flops 343597376 | bytes 629145 | tf_op jit(solution)/shard_map/front/pallas_call | solution.py:672
  70.0 2.4 collective-permute-done.5.refs_3_
  73.4 11.8 %cotangent.1 = (bf16[1024,1024]{1,0:T(8,128)(2,1)}, f32[8,1024]{1,0:T(8,128)}) custom-call(s32[1]{0:T(128)} %bitcast.rank, bf16[1024,512]{1,0:T(8,128)(2,1)} %refs_0_.7, bf16[1024,512]{1,0:T(8,128)(2,1)} %collective-permute-done.refs_1_, bf16[1024,512]{1,0:T(8,128)(2,1)} %copy-done.5, bf16[1024,512]{1,0:T(8,128)(2,1)} %copy-done.6, ...), custom_call_target="tpu_custom_call" | custom-call | flops 85899344 | bytes 419430 | tf_op jit(solution)/shard_map/cotangent/pallas_call | solution.py:714
  88.3 3.1 collective-permute-done.7
  92.0 9.5 %gate.2 = (bf16[1024,512]{1,0:T(8,128)(2,1)}, bf16[1024,512]{1,0:T(8,128)(2,1)}, bf16[1024,512]{1,0:T(8,128)(2,1)}, f32[1,512]{1,0:T(1,128)}, bf16[512,1024]{1,0:T(8,128)(2,1)}, /*index=5*/bf16[512,1024]{1,0:T(8,128)(2,1)}) custom-call(s32[1]{0:T(128)} %bitcast.1.place, s32[1]{0:T(128)} %bitcast.rank, bf16[1024,512]{1,0:T(8,128)(2,1)} %refs_0_.7, ...), custom_call_target="tpu_custom_call" | custom-call | flops 42949672 | bytes 314572 | tf_op jit(solution)/shard_map/gate/pallas_call | solution.py:744
  101.5 1.6 collective-permute-start.8
  103.0 9.3 %gate.3 = (bf16[1024,512]{1,0:T(8,128)(2,1)}, bf16[1024,512]{1,0:T(8,128)(2,1)}, bf16[1024,512]{1,0:T(8,128)(2,1)}, f32[1,512]{1,0:T(1,128)}, bf16[512,1024]{1,0:T(8,128)(2,1)}, /*index=5*/bf16[512,1024]{1,0:T(8,128)(2,1)}) custom-call(s32[1]{0:T(128)} %bitcast.1.place, s32[1]{0:T(128)} %bitcast.rank, bf16[1024,512]{1,0:T(8,128)(2,1)} %refs_0_.7, ...), custom_call_target="tpu_custom_call" | custom-call | flops 42949672 | bytes 314572 | tf_op jit(solution)/shard_map/gate/pallas_call | solution.py:744
  112.4 8.0 %weights.3 = (bf16[1024,1024]{1,0:T(8,128)(2,1)}, bf16[1024,1024]{1,0:T(8,128)(2,1)}) custom-call(s32[1]{0:T(128)} %bitcast.1.place, bf16[1024,2048]{1,0:T(8,128)(2,1)} %get-tuple-element.250.left_send.left_own, bf16[1024,2048]{1,0:T(8,128)(2,1)} %get-tuple-element.250.left_send.left_own, bf16[1024,512]{1,0:T(8,128)(2,1)} %get-tuple-element.230.refs_0_, ...), custom_call_target="tpu_custom_call" | custom-call | flops 85899344 | bytes 209715 | tf_op jit(solution)/shard_map/weights/pallas_call | solution.py:772
  120.4 9.0 %output.1 = (bf16[2,1024,512]{2,1,0:T(8,128)(2,1)}, bf16[2,1024,512]{2,1,0:T(8,128)(2,1)}) custom-call(s32[1]{0:T(128)} %bitcast.rank, bf16[1024,1024]{1,0:T(8,128)(2,1)} %get-tuple-element.185.refs_5_.gated, bf16[1024,2048]{1,0:T(8,128)(2,1)} %w_out.1), custom_call_target="tpu_custom_call" | custom-call | flops 85899344 | bytes 209715 | tf_op jit(solution)/shard_map/output/pallas_call | solution.py:828
  132.2 1.6 collective-permute-start.10
  133.9 1.5 collective-permute-start.15
  135.4 17.3 %backward.2 = (bf16[1024,512]{1,0:T(8,128)(2,1)}, f32[8,512]{1,0:T(8,128)}, f32[1,512]{1,0:T(1,128)}, f32[1024,128]{1,0:T(8,128)}, f32[1024,128]{1,0:T(8,128)}, /*index=5*/f32[1024,256]{1,0:T(8,128)}) custom-call(f32[1024,1024]{1,0:T(8,128)} %get-tuple-element.183.value, bf16[1024,512]{1,0:T(8,128)(2,1)} %get-tuple-element.191.grad_out, ...), custom_call_target="tpu_custom_call" | custom-call | flops 400000000 | bytes 146800 | tf_op jit(solution)/shard_map/backward/pallas_call | solution.py:792
  152.7 4.0 %collective-permute-done.11 = bf16[512,1024]{1,0:T(8,128)(2,1)S(1)} collective-permute-done((bf16[512,1024]{1,0:T(8,128)(2,1)}, bf16[512,1024]{1,0:T(8,128)(2,1)S(1)}, u32[]{:S(2)}, u32[]{:S(2)}) %collective-permute-start.11) | collective-permute-done | bytes 1048608 | tf_op jit(solution)/shard_map/ppermute | solution.py:526
  160.8 1.6 collective-permute-start.14
  162.4 1.5 add_convert_fusion.14
  163.8 2.6 collective-permute-start.13
  166.5 5.9 %weights.4 = (bf16[1024,512]{1,0:T(8,128)(2,1)}, bf16[1024,512]{1,0:T(8,128)(2,1)}) custom-call(s32[1]{0:T(128)} %bitcast.1.place, bf16[1024,2048]{1,0:T(8,128)(2,1)} %get-tuple-element.250.left_send.left_own, bf16[1024,2048]{1,0:T(8,128)(2,1)} %get-tuple-element.250.left_send.left_own, bf16[1024,512]{1,0:T(8,128)(2,1)} %get-tuple-element.207.refs_0_.refs_2_), custom_call_target="tpu_custom_call" | custom-call | flops 42949672 | bytes 146800 | tf_op jit(solution)/shard_map/weights/pallas_call | solution.py:772
  172.4 17.3 %backward.3 = (bf16[1024,512]{1,0:T(8,128)(2,1)}, f32[8,512]{1,0:T(8,128)}, f32[1,512]{1,0:T(1,128)}, f32[1024,128]{1,0:T(8,128)}, f32[1024,128]{1,0:T(8,128)}, /*index=5*/f32[1024,256]{1,0:T(8,128)}) custom-call(f32[1024,1024]{1,0:T(8,128)} %get-tuple-element.183.value, bf16[1024,512]{1,0:T(8,128)(2,1)} %get-tuple-element.209.grad_out, ...), custom_call_target="tpu_custom_call" | custom-call | flops 400000000 | bytes 146800 | tf_op jit(solution)/shard_map/backward/pallas_call | solution.py:792
  189.8 1.4 add_convert_fusion.13
  192.1 1.4 convert_add_fusion.4
  193.5 6.1 %weights.5 = (bf16[1024,512]{1,0:T(8,128)(2,1)}, bf16[1024,512]{1,0:T(8,128)(2,1)}) custom-call(s32[1]{0:T(128)} %bitcast.1.place, bf16[1024,2048]{1,0:T(8,128)(2,1)} %get-tuple-element.250.left_send.left_own, bf16[1024,2048]{1,0:T(8,128)(2,1)} %get-tuple-element.250.left_send.left_own, bf16[1024,512]{1,0:T(8,128)(2,1)} %get-tuple-element.214.refs_0_.refs_3_), custom_call_target="tpu_custom_call" | custom-call | flops 42949672 | bytes 146800 | tf_op jit(solution)/shard_map/weights/pallas_call | solution.py:772
  199.6 8.0 %finish.1 = (bf16[1024,256]{1,0:T(8,128)(2,1)}, bf16[1024,128]{1,0:T(8,128)(2,1)}, f32[8,256]{1,0:T(8,128)}, f32[8,128]{1,0:T(8,128)}) custom-call(f32[1024,128]{1,0:T(8,128)} %get-tuple-element.216.refs_0_, f32[1024,128]{1,0:T(8,128)} %get-tuple-element.217.refs_1_, f32[1024,256]{1,0:T(8,128)} %get-tuple-element.218.refs_2_, ...), custom_call_target="tpu_custom_call" | custom-call | flops 80000000 | bytes 186286 | tf_op jit(solution)/shard_map/finish/pallas_call | solution.py:892
  207.6 1.6 add_convert_fusion.1
  212.4 17.3 %normed_grad.1 = (bf16[2,1024,512]{2,1,0:T(8,128)(2,1)}, bf16[2,1024,512]{2,1,0:T(8,128)(2,1)}) custom-call(s32[1]{0:T(128)} %bitcast.rank, bf16[1024,512]{1,0:T(8,128)(2,1)} %get-tuple-element.230.refs_0_, bf16[1024,512]{1,0:T(8,128)(2,1)} %get-tuple-element.181.refs_1_, bf16[1024,512]{1,0:T(8,128)(2,1)} %get-tuple-element.207.refs_0_.refs_2_, ...), custom_call_target="tpu_custom_call" | custom-call | flops 204010944 | bytes 335544 | tf_op jit(solution)/shard_map/normed_grad/pallas_call | solution.py:841
  231.6 1.5 collective-permute-start.26
  234.1 1.4 add_convert_fusion.5
  236.6 1.7 collective-permute-start.25
  238.3 2.5 add_convert_fusion.6
  240.8 2.5 collective-permute-start.28
  243.4 1.5 fusion.11
  245.7 4.7 %collective-permute-done.24 = bf16[1024,256]{1,0:T(8,128)(2,1)S(1)} collective-permute-done((bf16[1024,256]{1,0:T(8,128)(2,1)S(1)}, bf16[1024,256]{1,0:T(8,128)(2,1)S(1)}, u32[]{:S(2)}, u32[]{:S(2)}) %collective-permute-start.24) | collective-permute-done | bytes 524320 | tf_op jit(solution)/shard_map/ppermute | solution.py:526
  250.4 1.4 convolution_convert_fusion
  252.5 4.8 %collective-permute-done.26 = bf16[1024,512]{1,0:T(8,128)(2,1)S(1)} collective-permute-done((bf16[1024,512]{1,0:T(8,128)(2,1)}, bf16[1024,512]{1,0:T(8,128)(2,1)S(1)}, u32[]{:S(2)}, u32[]{:S(2)}) %collective-permute-start.26) | collective-permute-done | bytes 1048608 | tf_op jit(solution)/shard_map/ppermute | solution.py:526
  260.7 3.1 collective-permute-start.32
  269.3 3.2 fusion
  274.9 7.5 %collective-permute-done.27 = bf16[512,512]{1,0:T(8,128)(2,1)} collective-permute-done((bf16[512,512]{1,0:T(8,128)(2,1)}, bf16[512,512]{1,0:T(8,128)(2,1)}, u32[]{:S(2)}, u32[]{:S(2)}) %collective-permute-start.27) | collective-permute-done | bytes 524320 | tf_op jit(solution)/shard_map/ppermute | solution.py:526
  284.9 4.1 %collective-permute-start.33 = (bf16[256,512]{1,0:T(8,128)(2,1)S(1)}, bf16[256,512]{1,0:T(8,128)(2,1)S(1)}, u32[]{:S(2)}, u32[]{:S(2)}) collective-permute-start(bf16[256,512]{1,0:T(8,128)(2,1)S(1)} %add_convert_fusion.11), channel_id=1, source_target_pairs={{0,16},{4,20},{8,24},{12,28},{16,0},{20,4},{24,8},{28,12},{1,17},{... | collective-permute-start | bytes 786440 | tf_op jit(solution)/shard_map/ppermute | solution.py:526
  289.1 2.7 fusion.8
  292.4 1.8 add_bitcast_fusion
  294.2 1.5 collective-permute-done.31
  295.8 5.1 %collective-permute-done.33 = bf16[256,512]{1,0:T(8,128)(2,1)S(1)} collective-permute-done((bf16[256,512]{1,0:T(8,128)(2,1)S(1)}, bf16[256,512]{1,0:T(8,128)(2,1)S(1)}, u32[]{:S(2)}, u32[]{:S(2)}) %collective-permute-start.33) | collective-permute-done | bytes 262176 | tf_op jit(solution)/shard_map/ppermute | solution.py:526
  304.8 3.1 collective-permute-start.36
  309.5 3.2 copy.66
  312.8 2.0 fusion.4
  (247 shorter events, 57.6 us)
Async XLA Ops:
  0.6 26.5 %collective-permute-start.1 = (bf16[1024,512]{1,0:T(8,128)(2,1)}, bf16[1024,512]{1,0:T(8,128)(2,1)}, u32[]{:S(2)}, u32[]{:S(2)}) collective-permute-start(bf16[1024,512]{1,0:T(8,128)(2,1)} %refs_0_.4), channel_id=1, source_target_pairs={{0,2},{1,3},{2,0},{3,1},{4,6},{5,7},{6,4},{7,5},{8,10},{9,11},{10,... | collective-permute-start | bytes 3145736 | tf_op jit(solution)/shard_map/ppermute | solution.py:526
  3.7 27.9 %collective-permute-start.3 = (bf16[1024,512]{1,0:T(8,128)(2,1)}, bf16[1024,512]{1,0:T(8,128)(2,1)}, u32[]{:S(2)}, u32[]{:S(2)}) collective-permute-start(bf16[1024,512]{1,0:T(8,128)(2,1)} %refs_0_.4), channel_id=1, source_target_pairs={{0,1},{1,0},{2,3},{3,2},{4,5},{5,4},{6,7},{7,6},{8,9},{9,8},{10,11... | collective-permute-start | bytes 3145736 | tf_op jit(solution)/shard_map/ppermute | solution.py:526
  17.5 12.3 %copy-start.43 = (f32[5,256]{1,0:T(8,128)S(1)}, f32[5,256]{1,0:T(8,128)}, u32[]{:S(2)}) copy-start(f32[5,256]{1,0:T(8,128)} %param.22) | copy-start | bytes 15364
  17.5 12.9 %copy-start.50 = (f32[16]{0:T(128)S(1)}, f32[16]{0:T(128)}, u32[]{:S(2)}) copy-start(f32[16]{0:T(128)} %param.24) | copy-start | bytes 196
  17.5 13.5 %copy-start.49 = (f32[16]{0:T(128)S(1)}, f32[16]{0:T(128)}, u32[]{:S(2)}) copy-start(f32[16]{0:T(128)} %param.23) | copy-start | bytes 196
  27.8 3.8 %collective-permute-start.4 = (bf16[1024,512]{1,0:T(8,128)(2,1)}, bf16[1024,512]{1,0:T(8,128)(2,1)S(1)}, u32[]{:S(2)}, u32[]{:S(2)}) collective-permute-start(bf16[1024,512]{1,0:T(8,128)(2,1)} %collective-permute-done.1.refs_2_), channel_id=1, source_target_pairs={{0,1},{1,0},{2,3},{3,2},{4,5},{5,4},{6,7},{7,6},{8,9},{9,8},{10,11... | collective-permute-start | bytes 3145736 | tf_op jit(solution)/shard_map/ppermute | solution.py:526
  27.8 41.9 %collective-permute-start.2 = (bf16[1024,512]{1,0:T(8,128)(2,1)S(1)}, bf16[1024,512]{1,0:T(8,128)(2,1)S(1)}, u32[]{:S(2)}, u32[]{:S(2)}) collective-permute-start(bf16[1024,512]{1,0:T(8,128)(2,1)S(1)} %copy-done.3), channel_id=1, source_target_pairs={{0,2},{1,3},{2,0},{3,1},{4,6},{5,7},{6,4},{7,5},{8,10},{9,11},{10,... | collective-permute-start | bytes 3145736 | tf_op jit(solution)/shard_map/ppermute | solution.py:526
  29.5 40.5 %collective-permute-start = (bf16[1024,512]{1,0:T(8,128)(2,1)S(1)}, bf16[1024,512]{1,0:T(8,128)(2,1)}, u32[]{:S(2)}, u32[]{:S(2)}) collective-permute-start(bf16[1024,512]{1,0:T(8,128)(2,1)S(1)} %copy-done.3), channel_id=1, source_target_pairs={{0,1},{1,0},{2,3},{3,2},{4,5},{5,4},{6,7},{7,6},{8,9},{9,8},{10,11... | collective-permute-start | bytes 3145736 | tf_op jit(solution)/shard_map/ppermute | solution.py:526
  69.7 2.7 collective-permute-start.5
  85.2 1.5 collective-permute-start.6
  87.4 3.9 %collective-permute-start.7 = (f32[8,1024]{1,0:T(8,128)S(1)}, f32[8,1024]{1,0:T(8,128)S(1)}, u32[]{:S(2)}, u32[]{:S(2)}) collective-permute-start(f32[8,1024]{1,0:T(8,128)S(1)} %add.349), channel_id=1, source_target_pairs={{0,2},{1,3},{2,0},{3,1},{4,6},{5,7},{6,4},{7,5},{8,10},{9,11},{10,... | collective-permute-start | bytes 98312 | tf_op jit(solution)/shard_map/ppermute | solution.py:526
  101.5 27.9 %collective-permute-start.8 = (bf16[512,1024]{1,0:T(8,128)(2,1)}, bf16[512,1024]{1,0:T(8,128)(2,1)S(1)}, u32[]{:S(2)}, u32[]{:S(2)}) collective-permute-start(bf16[512,1024]{1,0:T(8,128)(2,1)} %get-tuple-element.188), channel_id=1, source_target_pairs={{0,4},{4,0},{8,12},{12,8},{16,20},{20,16},{24,28},{28,24},{1,5},{5... | collective-permute-start | bytes 3145736 | tf_op jit(solution)/shard_map/ppermute | solution.py:526
  129.4 27.3 %collective-permute-start.9 = (bf16[2,1024,512]{2,1,0:T(8,128)(2,1)}, bf16[2,1024,512]{2,1,0:T(8,128)(2,1)S(1)}, u32[]{:S(2)}, u32[]{:S(2)}) collective-permute-start(bf16[2,1024,512]{2,1,0:T(8,128)(2,1)} %get-tuple-element.190), channel_id=1, source_target_pairs={{0,1},{1,0},{2,3},{3,2},{4,5},{5,4},{6,7},{7,6},{8,9},{9,8},{10,11... | collective-permute-start | bytes 6291464 | tf_op jit(solution)/shard_map/ppermute | solution.py:526
  130.4 26.3 %collective-permute-start.11 = (bf16[512,1024]{1,0:T(8,128)(2,1)}, bf16[512,1024]{1,0:T(8,128)(2,1)S(1)}, u32[]{:S(2)}, u32[]{:S(2)}) collective-permute-start(bf16[512,1024]{1,0:T(8,128)(2,1)} %get-tuple-element.201), channel_id=1, source_target_pairs={{0,4},{4,0},{8,12},{12,8},{16,20},{20,16},{24,28},{28,24},{1,5},{5... | collective-permute-start | bytes 3145736 | tf_op jit(solution)/shard_map/ppermute | solution.py:526
  132.2 24.4 %collective-permute-start.10 = (bf16[512,512]{1,0:T(8,128)(2,1)S(1)}, bf16[512,512]{1,0:T(8,128)(2,1)S(1)}, u32[]{:S(2)}, u32[]{:S(2)}) collective-permute-start(bf16[512,512]{1,0:T(8,128)(2,1)S(1)} %add_convert_fusion.9), channel_id=1, source_target_pairs={{0,8},{4,12},{8,0},{12,4},{16,24},{20,28},{24,16},{28,20},{1,9},{5... | collective-permute-start | bytes 1572872 | tf_op jit(solution)/shard_map/ppermute | solution.py:526
  133.9 73.7 %collective-permute-start.15 = (bf16[1024,1024]{1,0:T(8,128)(2,1)}, bf16[1024,1024]{1,0:T(8,128)(2,1)}, u32[]{:S(2)}, u32[]{:S(2)}) collective-permute-start(bf16[1024,1024]{1,0:T(8,128)(2,1)} %get-tuple-element.225), channel_id=1, source_target_pairs={{0,4},{4,0},{8,12},{12,8},{16,20},{20,16},{24,28},{28,24},{1,5},{5... | collective-permute-start | bytes 6291464 | tf_op jit(solution)/shard_map/ppermute | solution.py:526
  135.4 22.4 %copy-start.12 = (bf16[2,1024,512]{2,1,0:T(8,128)(2,1)S(1)}, bf16[2,1024,512]{2,1,0:T(8,128)(2,1)}, u32[]{:S(2)}) copy-start(bf16[2,1024,512]{2,1,0:T(8,128)(2,1)} %get-tuple-element.205) | copy-start | bytes 6291460
  158.1 31.7 %collective-permute-start.12 = (bf16[1024,512]{1,0:T(8,128)(2,1)S(1)}, bf16[1024,512]{1,0:T(8,128)(2,1)}, u32[]{:S(2)}, u32[]{:S(2)}) collective-permute-start(bf16[1024,512]{1,0:T(8,128)(2,1)S(1)} %fusion.10), channel_id=1, source_target_pairs={{0,2},{1,3},{2,0},{3,1},{4,6},{5,7},{6,4},{7,5},{8,10},{9,11},{10,... | collective-permute-start | bytes 3145736 | tf_op jit(solution)/shard_map/ppermute | solution.py:526
  160.8 29.0 %collective-permute-start.14 = (bf16[512,512]{1,0:T(8,128)(2,1)}, bf16[512,512]{1,0:T(8,128)(2,1)}, u32[]{:S(2)}, u32[]{:S(2)}) collective-permute-start(bf16[512,512]{1,0:T(8,128)(2,1)} %add_convert_fusion.8), channel_id=1, source_target_pairs={{0,8},{4,12},{8,0},{12,4},{16,24},{20,28},{24,16},{28,20},{1,9},{5... | collective-permute-start | bytes 1572872 | tf_op jit(solution)/shard_map/ppermute | solution.py:526
  163.8 25.9 %collective-permute-start.13 = (bf16[512,256]{1,0:T(8,128)(2,1)S(1)}, bf16[512,256]{1,0:T(8,128)(2,1)S(1)}, u32[]{:S(2)}, u32[]{:S(2)}) collective-permute-start(bf16[512,256]{1,0:T(8,128)(2,1)S(1)} %add_convert_fusion.14), channel_id=1, source_target_pairs={{0,16},{4,20},{8,24},{12,28},{16,0},{20,4},{24,8},{28,12},{1,17},{... | collective-permute-start | bytes 786440 | tf_op jit(solution)/shard_map/ppermute | solution.py:526
  172.4 17.4 %copy-start.24 = (bf16[512,1024]{1,0:T(8,128)(2,1)S(1)}, bf16[512,1024]{1,0:T(8,128)(2,1)}, u32[]{:S(2)}) copy-start(bf16[512,1024]{1,0:T(8,128)(2,1)} %get-tuple-element.179) | copy-start | bytes 3145732
  172.4 19.7 %copy-start.37 = (bf16[512,512]{1,0:T(8,128)(2,1)S(1)}, bf16[512,512]{1,0:T(8,128)(2,1)}, u32[]{:S(2)}) copy-start(bf16[512,512]{1,0:T(8,128)(2,1)} %copy-done.36) | copy-start | bytes 1572868
  191.1 16.4 %collective-permute-start.16 = (bf16[512,256]{1,0:T(8,128)(2,1)S(1)}, bf16[512,256]{1,0:T(8,128)(2,1)S(1)}, u32[]{:S(2)}, u32[]{:S(2)}) collective-permute-start(bf16[512,256]{1,0:T(8,128)(2,1)S(1)} %add_convert_fusion.13), channel_id=1, source_target_pairs={{0,16},{4,20},{8,24},{12,28},{16,0},{20,4},{24,8},{28,12},{1,17},{... | collective-permute-start | bytes 786440 | tf_op jit(solution)/shard_map/ppermute | solution.py:526
  191.6 38.2 %collective-permute-start.20 = (bf16[1024,512]{1,0:T(8,128)(2,1)}, bf16[1024,512]{1,0:T(8,128)(2,1)S(1)}, u32[]{:S(2)}, u32[]{:S(2)}) collective-permute-start(bf16[1024,512]{1,0:T(8,128)(2,1)} %get-tuple-element.234), channel_id=1, source_target_pairs={{0,4},{4,0},{8,12},{12,8},{16,20},{20,16},{24,28},{28,24},{1,5},{5... | collective-permute-start | bytes 3145736 | tf_op jit(solution)/shard_map/ppermute | solution.py:526
  209.2 21.4 %collective-permute-start.21 = (bf16[512,1024]{1,0:T(8,128)(2,1)S(1)}, bf16[512,1024]{1,0:T(8,128)(2,1)S(1)}, u32[]{:S(2)}, u32[]{:S(2)}) collective-permute-start(bf16[512,1024]{1,0:T(8,128)(2,1)S(1)} %add_convert_fusion.1), channel_id=1, source_target_pairs={{0,8},{4,12},{8,0},{12,4},{16,24},{20,28},{24,16},{28,20},{1,9},{5... | collective-permute-start | bytes 3145736 | tf_op jit(solution)/shard_map/ppermute | solution.py:526
  209.7 20.1 %collective-permute-start.18 = (bf16[1024,256]{1,0:T(8,128)(2,1)}, bf16[1024,256]{1,0:T(8,128)(2,1)S(1)}, u32[]{:S(2)}, u32[]{:S(2)}) collective-permute-start(bf16[1024,256]{1,0:T(8,128)(2,1)} %get-tuple-element.227.refs_4_), channel_id=1, source_target_pairs={{0,1},{1,0},{2,3},{3,2},{4,5},{5,4},{6,7},{7,6},{8,9},{9,8},{10,11... | collective-permute-start | bytes 1572872 | tf_op jit(solution)/shard_map/ppermute | solution.py:526
  209.7 1.8 collective-permute-start.17
  211.6 18.2 %collective-permute-start.19 = (f32[5,256]{1,0:T(8,128)S(1)}, f32[5,256]{1,0:T(8,128)S(1)}, u32[]{:S(2)}, u32[]{:S(2)}) collective-permute-start(f32[5,256]{1,0:T(8,128)S(1)} %add.369), channel_id=1, source_target_pairs={{0,2},{1,3},{2,0},{3,1},{4,6},{5,7},{6,4},{7,5},{8,10},{9,11},{10,... | collective-permute-start | bytes 15368 | tf_op jit(solution)/shard_map/ppermute | solution.py:526
  231.6 11.8 %collective-permute-start.22 = (bf16[2,1024,512]{2,1,0:T(8,128)(2,1)}, bf16[2,1024,512]{2,1,0:T(8,128)(2,1)S(1)}, u32[]{:S(2)}, u32[]{:S(2)}) collective-permute-start(bf16[2,1024,512]{2,1,0:T(8,128)(2,1)} %get-tuple-element.236), channel_id=1, source_target_pairs={{0,1},{1,0},{2,3},{3,2},{4,5},{5,4},{6,7},{7,6},{8,9},{9,8},{10,11... | collective-permute-start | bytes 6291464 | tf_op jit(solution)/shard_map/ppermute | solution.py:526
  231.6 25.8 %collective-permute-start.26 = (bf16[1024,512]{1,0:T(8,128)(2,1)}, bf16[1024,512]{1,0:T(8,128)(2,1)S(1)}, u32[]{:S(2)}, u32[]{:S(2)}) collective-permute-start(bf16[1024,512]{1,0:T(8,128)(2,1)} %get-tuple-element.261), channel_id=1, source_target_pairs={{0,4},{4,0},{8,12},{12,8},{16,20},{20,16},{24,28},{28,24},{1,5},{5... | collective-permute-start | bytes 3145736 | tf_op jit(solution)/shard_map/ppermute | solution.py:526
  235.6 14.8 %collective-permute-start.24 = (bf16[1024,256]{1,0:T(8,128)(2,1)S(1)}, bf16[1024,256]{1,0:T(8,128)(2,1)S(1)}, u32[]{:S(2)}, u32[]{:S(2)}) collective-permute-start(bf16[1024,256]{1,0:T(8,128)(2,1)S(1)} %add_convert_fusion.5), channel_id=1, source_target_pairs={{0,2},{1,3},{2,0},{3,1},{4,6},{5,7},{6,4},{7,5},{8,10},{9,11},{10,... | collective-permute-start | bytes 1572872 | tf_op jit(solution)/shard_map/ppermute | solution.py:526
  236.6 22.1 %collective-permute-start.25 = (bf16[512,512]{1,0:T(8,128)(2,1)S(1)}, bf16[512,512]{1,0:T(8,128)(2,1)S(1)}, u32[]{:S(2)}, u32[]{:S(2)}) collective-permute-start(bf16[512,512]{1,0:T(8,128)(2,1)S(1)} %add_convert_fusion.7), channel_id=1, source_target_pairs={{0,8},{4,12},{8,0},{12,4},{16,24},{20,28},{24,16},{28,20},{1,9},{5... | collective-permute-start | bytes 1572872 | tf_op jit(solution)/shard_map/ppermute | solution.py:526
  238.3 12.1 %copy-start = (bf16[1024,2048]{1,0:T(8,128)(2,1)S(1)}, bf16[1024,2048]{1,0:T(8,128)(2,1)}, u32[]{:S(2)}) copy-start(bf16[1024,2048]{1,0:T(8,128)(2,1)} %get-tuple-element.250.left_send.left_own) | copy-start | bytes 12582916
  240.8 34.1 %collective-permute-start.28 = (bf16[256,1024]{1,0:T(8,128)(2,1)}, bf16[256,1024]{1,0:T(8,128)(2,1)}, u32[]{:S(2)}, u32[]{:S(2)}) collective-permute-start(bf16[256,1024]{1,0:T(8,128)(2,1)} %add_convert_fusion.6), channel_id=1, source_target_pairs={{0,16},{4,20},{8,24},{12,28},{16,0},{20,4},{24,8},{28,12},{1,17},{... | collective-permute-start | bytes 1572872 | tf_op jit(solution)/shard_map/ppermute | solution.py:526
  244.8 37.6 %collective-permute-start.23 = (bf16[1024,512]{1,0:T(8,128)(2,1)}, bf16[1024,512]{1,0:T(8,128)(2,1)S(1)}, u32[]{:S(2)}, u32[]{:S(2)}) collective-permute-start(bf16[1024,512]{1,0:T(8,128)(2,1)} %fusion.11), channel_id=1, source_target_pairs={{0,2},{1,3},{2,0},{3,1},{4,6},{5,7},{6,4},{7,5},{8,10},{9,11},{10,... | collective-permute-start | bytes 3145736 | tf_op jit(solution)/shard_map/ppermute | solution.py:526
  260.6 21.9 %collective-permute-start.27 = (bf16[512,512]{1,0:T(8,128)(2,1)}, bf16[512,512]{1,0:T(8,128)(2,1)}, u32[]{:S(2)}, u32[]{:S(2)}) collective-permute-start(bf16[512,512]{1,0:T(8,128)(2,1)} %add_convert_fusion.3), channel_id=1, source_target_pairs={{0,8},{4,12},{8,0},{12,4},{16,24},{20,28},{24,16},{28,20},{1,9},{5... | collective-permute-start | bytes 1572872 | tf_op jit(solution)/shard_map/ppermute | solution.py:526
  260.7 33.5 %collective-permute-start.32 = (bf16[256,512]{1,0:T(8,128)(2,1)}, bf16[256,512]{1,0:T(8,128)(2,1)}, u32[]{:S(2)}, u32[]{:S(2)}) collective-permute-start(bf16[256,512]{1,0:T(8,128)(2,1)} %add_convert_fusion.12), channel_id=1, source_target_pairs={{0,16},{4,20},{8,24},{12,28},{16,0},{20,4},{24,8},{28,12},{1,17},{... | collective-permute-start | bytes 786440 | tf_op jit(solution)/shard_map/ppermute | solution.py:526
  267.1 7.8 %collective-permute-start.29 = (bf16[4,20480]{1,0:T(4,128)(2,1)}, bf16[4,20480]{1,0:T(4,128)(2,1)}, u32[]{:S(2)}, u32[]{:S(2)}) collective-permute-start(bf16[4,20480]{1,0:T(4,128)(2,1)} %bitcast.81), channel_id=1, source_target_pairs={{0,4},{4,0},{8,12},{12,8},{16,20},{20,16},{24,28},{28,24},{1,5},{5... | collective-permute-start | bytes 491528 | tf_op jit(solution)/shard_map/ppermute | solution.py:526
  269.3 14.4 %copy-start.32 = (f32[2,1,1,20480]{3,1,2,0:T(1,128)S(1)}, f32[2,1,1,20480]{3,1,2,0:T(1,128)}, u32[]{:S(2)}) copy-start(f32[2,1,1,20480]{3,1,2,0:T(1,128)} %dynamic-slice_convert_fusion) | copy-start | bytes 491524
  284.9 10.9 %collective-permute-start.34 = (bf16[2,20480]{1,0:T(2,128)(2,1)S(1)}, bf16[2,20480]{1,0:T(2,128)(2,1)S(1)}, u32[]{:S(2)}, u32[]{:S(2)}) collective-permute-start(bf16[2,20480]{1,0:T(2,128)(2,1)S(1)} %fusion.14), channel_id=1, source_target_pairs={{0,8},{4,12},{8,0},{12,4},{16,24},{20,28},{24,16},{28,20},{1,9},{5... | collective-permute-start | bytes 245768 | tf_op jit(solution)/shard_map/ppermute | solution.py:526
  284.9 15.9 %collective-permute-start.33 = (bf16[256,512]{1,0:T(8,128)(2,1)S(1)}, bf16[256,512]{1,0:T(8,128)(2,1)S(1)}, u32[]{:S(2)}, u32[]{:S(2)}) collective-permute-start(bf16[256,512]{1,0:T(8,128)(2,1)S(1)} %add_convert_fusion.11), channel_id=1, source_target_pairs={{0,16},{4,20},{8,24},{12,28},{16,0},{20,4},{24,8},{28,12},{1,17},{... | collective-permute-start | bytes 786440 | tf_op jit(solution)/shard_map/ppermute | solution.py:526
  291.8 4.0 %collective-permute-start.31 = (f32[7984]{0:T(1024)S(1)}, f32[7984]{0:T(1024)S(1)}, u32[]{:S(2)}, u32[]{:S(2)}) collective-permute-start(f32[7984]{0:T(1024)S(1)} %pad_maximum_fusion.6), channel_id=1, source_target_pairs={{0,4},{4,0},{8,12},{12,8},{16,20},{20,16},{24,28},{28,24},{1,5},{5... | collective-permute-start | bytes 95816 | tf_op jit(solution)/shard_map/ppermute | solution.py:526
  292.4 11.1 %copy-start.35 = (bf16[512,512]{1,0:T(8,128)(2,1)S(1)}, bf16[512,512]{1,0:T(8,128)(2,1)}, u32[]{:S(2)}) copy-start(bf16[512,512]{1,0:T(8,128)(2,1)} %copy-done.34) | copy-start | bytes 1572868
  292.4 1.8 collective-permute-start.30
  302.1 12.8 %collective-permute-start.38 = (bf16[1,20480]{1,0:T(2,128)(2,1)S(1)}, bf16[1,20480]{1,0:T(2,128)(2,1)S(1)}, u32[]{:S(2)}, u32[]{:S(2)}) collective-permute-start(bf16[1,20480]{1,0:T(2,128)(2,1)S(1)} %fusion.22), channel_id=1, source_target_pairs={{0,16},{4,20},{8,24},{12,28},{16,0},{20,4},{24,8},{28,12},{1,17},{... | collective-permute-start | bytes 122888 | tf_op jit(solution)/shard_map/ppermute | solution.py:526
  304.8 7.9 %collective-permute-start.36 = (f32[7984]{0:T(1024)S(1)}, f32[7984]{0:T(1024)S(1)}, u32[]{:S(2)}, u32[]{:S(2)}) collective-permute-start(f32[7984]{0:T(1024)S(1)} %add.399), channel_id=1, source_target_pairs={{0,8},{4,12},{8,0},{12,4},{16,24},{20,28},{24,16},{28,20},{1,9},{5... | collective-permute-start | bytes 95816 | tf_op jit(solution)/shard_map/ppermute | solution.py:526
  307.9 4.8 %collective-permute-start.35 = (f32[1024]{0:T(1024)S(1)}, f32[1024]{0:T(1024)S(1)}, u32[]{:S(2)}, u32[]{:S(2)}) collective-permute-start(f32[1024]{0:T(1024)S(1)} %add.398), channel_id=1, source_target_pairs={{0,2},{1,3},{2,0},{3,1},{4,6},{5,7},{6,4},{7,5},{8,10},{9,11},{10,... | collective-permute-start | bytes 12296 | tf_op jit(solution)/shard_map/ppermute | solution.py:526
  312.7 4.9 %collective-permute-start.37 = (f32[7984]{0:T(1024)S(1)}, f32[7984]{0:T(1024)S(1)}, u32[]{:S(2)}, u32[]{:S(2)}) collective-permute-start(f32[7984]{0:T(1024)S(1)} %add.411), channel_id=1, source_target_pairs={{0,16},{4,20},{8,24},{12,28},{16,0},{20,4},{24,8},{28,12},{1,17},{... | collective-permute-start | bytes 95816 | tf_op jit(solution)/shard_map/ppermute | solution.py:526
  (42 other events, 167.5 us)

commit v5 on v4

--- a/solution.py
+++ b/solution.py
@@ -883,8 +883,7 @@
     backs = [back, backward_part(1, tie(grad_mixer[1], value_own))]
 
     grad_value2, out_y = meet(sum_out, backs[1][0], out_y)
-    total_out = [sum_out[0].result()]
-    moved = [sum_out[1].advance(), total_out[0]]
+    moved = [sum_out[1].advance()]
     value_send2, value_own2 = weight_part(tie(grad_value2, *moved))
     sum_value.append(Sum(value_own2, over_x(value_send2), 0, low_bits))
     moved = [value_own2]
@@ -917,8 +916,7 @@
     state_got = swap(grad_state, "tensor", 1)
     grad_conv_state = grad_conv_state + swap(grad_conv_state, "tensor", 1)
     conv_got = swap(grad_conv_state, "tensor", 2)
-    total_out.append(sum_out[1].result())
-    moved = [sum_gate.advance(), grad_state, total_out[1], grad_conv_state]
+    moved = [sum_gate.advance(), grad_state, grad_conv_state]
     near_far, near = normed_part([tie(grad_gate[0], *moved), *grad_gate[1:]])
 
     near_far, near, state_got, conv_got = meet([sum_value[0], sum_gate], near_far, near, state_got, conv_got)
@@ -952,6 +950,7 @@
     (grad_w_state, grad_w_step, grad_conv, grad_skip, grad_gain, stats, marks), _ = lax.optimization_barrier(
         ((grad_w_state, grad_w_step, grad_conv, grad_skip, grad_gain, stats, marks), moved)
     )
+    meet(sum_out, *moved)
     grad_w_step = grad_w_step.reshape(heads, groups, piece_rows).transpose(1, 0, 2)
     small = jnp.concatenate(
         [grad_w_state.reshape(groups, own_rows * states2), grad_w_step.reshape(groups, heads * piece_rows)], axis=1
@@ -968,6 +967,7 @@
         grad_conv[:5].reshape(-1), grad_conv_state.reshape(-1), grad_heads[0, :heads], grad_heads[1, :heads],
         skip_sums, grad_gate_gain[0],
     ]
+    total_out = [part.result() for part in sum_out]
     rest = jnp.concatenate(pieces)
     scale_out = lax.rsqrt(stats[0] / (channels * parts) + EPSILON)
     factor = scale_out * marks[:length, 5]
@@ -975,7 +975,9 @@
     own_tokens = tokens.astype(F32)
     output = (own_tokens + factor[:, None] * branch).astype(BF16)
 
-    over_y, small_send, rest, output = meet([sum_value[1], sum_gate, small_sum], over_y, small_send, rest, output)
+    over_y, small_send, rest, output, *total_out = meet(
+        [sum_value[1], sum_gate, small_sum], over_y, small_send, rest, output, *total_out
+    )
     moved = [sum_value[1].advance(), small_sum.advance()]
     total_gate = sum_gate.result()
     over_y = tie(over_y, *moved)
@@ -988,12 +990,12 @@
     pieces = [grad_norm_gain, *pieces]
 
     row_got, pack_got = swap(row_norm, "tensor", 1), swap(pack, "dp", 1)
-    row_norm, row_got, pack, pack_got = meet([*sum_value, small_sum], row_norm, row_got, pack, pack_got)
-    moved = [small_sum.advance()]
+    row_norm, row_got, pack, pack_got = meet([small_sum], row_norm, row_got, pack, pack_got)
+    small_sum.advance()
     row_norm, pack = row_norm + row_got, pack + pack_got
     row_got, pack_got = swap(row_norm, "tensor", 2), swap(pack, "dp", 2)
+    row_norm, row_got, pack, pack_got = meet([*sum_value, small_sum], row_norm, row_got, pack, pack_got)
     total_value = [part.result() for part in sum_value]
-    row_norm, row_got, pack, pack_got, *_ = lax.optimization_barrier((row_norm, row_got, pack, pack_got, *total_value, *moved))
     row_norm, pack = row_norm + row_got, pack + pack_got
     bit = 4
     while bit < groups:

time: 326 us -> 325 us (level)
  starting transfers between devices: 40.6 us -> 35.4 us
    ppermute x39, starting transfers between devices: 40.6 us -> 35.4 us  [swap(): return lax.ppermute(array, axis, [(i, i ^ mask) for i in range(count)])]
    unnamed x107 -> x117, local copies, waits for them, and re-layouts: 20.4 us -> 19.9 us
  transfers between devices with their start and end apart: 39 -> 39, of which waited for: 13 -> 15; matrix products, arithmetic and copies ran while one was open for 21% -> 21% of each run, Pallas kernels for 42% -> 42%
where the time goes in v5:
time: 325 us; the launch traced here: 320 us
  Pallas kernels  157 us (48%)
  other arithmetic  45.5 us (14%)
  waiting for transfers between devices  44.8 us (14%)
  starting transfers between devices  35.4 us (11%)
  local copies, waits for them, and re-layouts  33 us (10%)
    ppermute x39, waiting for transfers between devices, swap(): return lax.ppermute(array, axis, [(i, i ^ mask) for i in range(count)])  44.8 us
    pallas_call x1, Pallas kernels, shards(): call(functools.partial(front_kernel, parts, heads), (steps,), [held((leng...  37.1 us
    ppermute x39, starting transfers between devices, swap(): return lax.ppermute(array, axis, [(i, i ^ mask) for i in range(count)])  35.4 us
    pallas_call x2, Pallas kernels, backward_part(): call(functools.partial(backward_kernel, heads, c * spans), (spans,), [chu...  34.6 us
    pallas_call x3, Pallas kernels, weight_part(): call(weight_kernel, (runs,), [pl.BlockSpec((length, run), lambda j, p: (0...  20 us
    unnamed x117, local copies, waits for them, and re-layouts  19.9 us
    pallas_call x2, Pallas kernels, gate_part(): call(functools.partial(gate_kernel, parts, run, channels * parts, stacked...  18.9 us
    pallas_call x1, Pallas kernels, normed_part(): call(functools.partial(normed_kernel, len(grad_gate)), (4,), [held((lengt...  17.4 us
  transfers between devices with their start and end apart: 39, of which 15 were waited for; matrix products, arithmetic and copies ran while one was open for 21% of the time, Pallas kernels for 42%

profile of v5, /device:TPU:0, one launch (start us, length us, event | category | flops | bytes accessed | tf_op | source)
XLA Modules:
  0.0 319.5 jit_solution(2055813122622529630)
XLA Ops:
  0.6 3.0 collective-permute-start.1
  6.9 10.3 %copy.69 = bf16[256,8,2,1024]{3,1,2,0:T(8,128)(2,1)} copy(bf16[256,8,2,1024]{3,2,1,0:T(2,128)(2,1)} %bitcast.89) | data formatting | bytes 16777216
  21.1 6.0 %collective-permute-done.1.refs_2_ = bf16[1024,512]{1,0:T(8,128)(2,1)} collective-permute-done((bf16[1024,512]{1,0:T(8,128)(2,1)}, bf16[1024,512]{1,0:T(8,128)(2,1)}, u32[]{:S(2)}, u32[]{:S(2)}) %collective-permute-start.1) | collective-permute-done | bytes 1048608 | tf_op jit(solution)/shard_map/ppermute | solution.py:526
  27.8 1.7 collective-permute-start.2
  31.6 37.1 %front.1 = (bf16[1024,2048]{1,0:T(8,128)(2,1)}, f32[1024,256]{1,0:T(8,128)}, bf16[1024,256]{1,0:T(8,128)(2,1)}, bf16[256,1024]{1,0:T(8,128)(2,1)}, f32[1024,128]...) custom-call(s32[1]{0:T(128)} %bitcast.rank, ...), custom_call_target="tpu_custom_call" | custom-call | flops 343597376 | bytes 629145 | tf_op jit(solution)/shard_map/front/pallas_call | solution.py:672
  69.1 2.4 collective-permute-done.5.refs_3_
  72.4 11.8 %cotangent.1 = (bf16[1024,1024]{1,0:T(8,128)(2,1)}, f32[8,1024]{1,0:T(8,128)}) custom-call(s32[1]{0:T(128)} %bitcast.rank, bf16[1024,512]{1,0:T(8,128)(2,1)} %refs_0_.7, bf16[1024,512]{1,0:T(8,128)(2,1)} %copy-done.6, bf16[1024,512]{1,0:T(8,128)(2,1)} %copy-done.5, bf16[1024,512]{1,0:T(8,128)(2,1)} %copy-done.7, bf16[1024,2048]{1,0:T(8,128)(2,1)} %w_out.1, ...), custom_call_target="tpu_custom_call" | custom-call | flops 85899344 | bytes 419430 | tf_op jit(solution)/shard_map/cotangent/pallas_call | solution.py:714
  87.4 3.0 collective-permute-done.7
  91.0 9.5 %gate.2 = (bf16[1024,512]{1,0:T(8,128)(2,1)}, bf16[1024,512]{1,0:T(8,128)(2,1)}, bf16[1024,512]{1,0:T(8,128)(2,1)}, f32[1,512]{1,0:T(1,128)}, bf16[512,1024]{1,0:T(8,128)(2,1)}, /*index=5*/bf16[512,1024]{1,0:T(8,128)(2,1)}) custom-call(s32[1]{0:T(128)} %bitcast.1.place, s32[1]{0:T(128)} %bitcast.rank, bf16[1024,512]{1,0:T(8,128)(2,1)} %refs_0_.7, ...), custom_call_target="tpu_custom_call" | custom-call | flops 42949672 | bytes 314572 | tf_op jit(solution)/shard_map/gate/pallas_call | solution.py:744
  100.6 1.6 collective-permute-start.8
  102.1 9.3 %gate.3 = (bf16[1024,512]{1,0:T(8,128)(2,1)}, bf16[1024,512]{1,0:T(8,128)(2,1)}, bf16[1024,512]{1,0:T(8,128)(2,1)}, f32[1,512]{1,0:T(1,128)}, bf16[512,1024]{1,0:T(8,128)(2,1)}, /*index=5*/bf16[512,1024]{1,0:T(8,128)(2,1)}) custom-call(s32[1]{0:T(128)} %bitcast.1.place, s32[1]{0:T(128)} %bitcast.rank, bf16[1024,512]{1,0:T(8,128)(2,1)} %refs_0_.7, ...), custom_call_target="tpu_custom_call" | custom-call | flops 42949672 | bytes 314572 | tf_op jit(solution)/shard_map/gate/pallas_call | solution.py:744
  111.5 8.0 %weights.3 = (bf16[1024,1024]{1,0:T(8,128)(2,1)}, bf16[1024,1024]{1,0:T(8,128)(2,1)}) custom-call(s32[1]{0:T(128)} %bitcast.1.place, bf16[1024,2048]{1,0:T(8,128)(2,1)} %get-tuple-element.253.left_send.left_own, bf16[1024,2048]{1,0:T(8,128)(2,1)} %get-tuple-element.253.left_send.left_own, bf16[1024,512]{1,0:T(8,128)(2,1)} %get-tuple-element.233.refs_0_, ...), custom_call_target="tpu_custom_call" | custom-call | flops 85899344 | bytes 209715 | tf_op jit(solution)/shard_map/weights/pallas_call | solution.py:772
  119.5 9.1 %output.1 = (bf16[2,1024,512]{2,1,0:T(8,128)(2,1)}, bf16[2,1024,512]{2,1,0:T(8,128)(2,1)}) custom-call(s32[1]{0:T(128)} %bitcast.rank, bf16[1024,1024]{1,0:T(8,128)(2,1)} %get-tuple-element.190.refs_5_.gated, bf16[1024,2048]{1,0:T(8,128)(2,1)} %w_out.1), custom_call_target="tpu_custom_call" | custom-call | flops 85899344 | bytes 209715 | tf_op jit(solution)/shard_map/output/pallas_call | solution.py:828
  131.3 1.6 collective-permute-start.10
  134.4 17.3 %backward.2 = (bf16[1024,512]{1,0:T(8,128)(2,1)}, f32[8,512]{1,0:T(8,128)}, f32[1,512]{1,0:T(1,128)}, f32[1024,128]{1,0:T(8,128)}, f32[1024,128]{1,0:T(8,128)}, /*index=5*/f32[1024,256]{1,0:T(8,128)}) custom-call(f32[1024,1024]{1,0:T(8,128)} %get-tuple-element.188.value, bf16[1024,512]{1,0:T(8,128)(2,1)} %get-tuple-element.196.grad_out, ...), custom_call_target="tpu_custom_call" | custom-call | flops 400000000 | bytes 146800 | tf_op jit(solution)/shard_map/backward/pallas_call | solution.py:792
  151.8 4.1 %collective-permute-done.11 = bf16[512,1024]{1,0:T(8,128)(2,1)} collective-permute-done((bf16[512,1024]{1,0:T(8,128)(2,1)}, bf16[512,1024]{1,0:T(8,128)(2,1)}, u32[]{:S(2)}, u32[]{:S(2)}) %collective-permute-start.11) | collective-permute-done | bytes 1048608 | tf_op jit(solution)/shard_map/ppermute | solution.py:526
  157.2 2.0 add_convert_fusion.8
  159.2 1.6 collective-permute-start.14
  162.3 2.6 collective-permute-start.13
  164.9 5.9 %weights.4 = (bf16[1024,512]{1,0:T(8,128)(2,1)}, bf16[1024,512]{1,0:T(8,128)(2,1)}) custom-call(s32[1]{0:T(128)} %bitcast.1.place, bf16[1024,2048]{1,0:T(8,128)(2,1)} %get-tuple-element.253.left_send.left_own, bf16[1024,2048]{1,0:T(8,128)(2,1)} %get-tuple-element.253.left_send.left_own, bf16[1024,512]{1,0:T(8,128)(2,1)} %get-tuple-element.212.refs_0_.refs_2_), custom_call_target="tpu_custom_call" | custom-call | flops 42949672 | bytes 146800 | tf_op jit(solution)/shard_map/weights/pallas_call | solution.py:772
  170.8 17.3 %backward.3 = (bf16[1024,512]{1,0:T(8,128)(2,1)}, f32[8,512]{1,0:T(8,128)}, f32[1,512]{1,0:T(1,128)}, f32[1024,128]{1,0:T(8,128)}, f32[1024,128]{1,0:T(8,128)}, /*index=5*/f32[1024,256]{1,0:T(8,128)}) custom-call(f32[1024,1024]{1,0:T(8,128)} %get-tuple-element.188.value, bf16[1024,512]{1,0:T(8,128)(2,1)} %get-tuple-element.214.grad_out, ...), custom_call_target="tpu_custom_call" | custom-call | flops 400000000 | bytes 146800 | tf_op jit(solution)/shard_map/backward/pallas_call | solution.py:792
  188.2 1.6 add_convert_fusion.13
  190.7 6.1 %weights.5 = (bf16[1024,512]{1,0:T(8,128)(2,1)}, bf16[1024,512]{1,0:T(8,128)(2,1)}) custom-call(s32[1]{0:T(128)} %bitcast.1.place, bf16[1024,2048]{1,0:T(8,128)(2,1)} %get-tuple-element.253.left_send.left_own, bf16[1024,2048]{1,0:T(8,128)(2,1)} %get-tuple-element.253.left_send.left_own, bf16[1024,512]{1,0:T(8,128)(2,1)} %get-tuple-element.218.refs_0_.refs_3_), custom_call_target="tpu_custom_call" | custom-call | flops 42949672 | bytes 146800 | tf_op jit(solution)/shard_map/weights/pallas_call | solution.py:772
  196.8 8.0 %finish.1 = (bf16[1024,256]{1,0:T(8,128)(2,1)}, bf16[1024,128]{1,0:T(8,128)(2,1)}, f32[8,256]{1,0:T(8,128)}, f32[8,128]{1,0:T(8,128)}) custom-call(f32[1024,128]{1,0:T(8,128)} %get-tuple-element.220.refs_0_, f32[1024,128]{1,0:T(8,128)} %get-tuple-element.221.refs_1_, f32[1024,256]{1,0:T(8,128)} %get-tuple-element.222.refs_2_, ...), custom_call_target="tpu_custom_call" | custom-call | flops 80000000 | bytes 186286 | tf_op jit(solution)/shard_map/finish/pallas_call | solution.py:891
  205.5 1.6 add_convert_fusion.1
  210.2 17.4 %normed_grad.1 = (bf16[2,1024,512]{2,1,0:T(8,128)(2,1)}, bf16[2,1024,512]{2,1,0:T(8,128)(2,1)}) custom-call(s32[1]{0:T(128)} %bitcast.rank, bf16[1024,512]{1,0:T(8,128)(2,1)} %get-tuple-element.233.refs_0_, bf16[1024,512]{1,0:T(8,128)(2,1)} %get-tuple-element.186.refs_1_, bf16[1024,512]{1,0:T(8,128)(2,1)} %get-tuple-element.212.refs_0_.refs_2_, ...), custom_call_target="tpu_custom_call" | custom-call | flops 204010944 | bytes 335544 | tf_op jit(solution)/shard_map/normed_grad/pallas_call | solution.py:841
  227.6 2.7 collective-permute-done.21
  236.9 2.5 add_convert_fusion.6
  239.4 2.5 collective-permute-start.28
  244.4 4.5 %collective-permute-done.24 = bf16[1024,256]{1,0:T(8,128)(2,1)S(1)} collective-permute-done((bf16[1024,256]{1,0:T(8,128)(2,1)S(1)}, bf16[1024,256]{1,0:T(8,128)(2,1)S(1)}, u32[]{:S(2)}, u32[]{:S(2)}) %collective-permute-start.24) | collective-permute-done | bytes 524320 | tf_op jit(solution)/shard_map/ppermute | solution.py:526
  251.0 6.0 %collective-permute-done.26 = bf16[1024,512]{1,0:T(8,128)(2,1)S(1)} collective-permute-done((bf16[1024,512]{1,0:T(8,128)(2,1)}, bf16[1024,512]{1,0:T(8,128)(2,1)S(1)}, u32[]{:S(2)}, u32[]{:S(2)}) %collective-permute-start.26) | collective-permute-done | bytes 1048608 | tf_op jit(solution)/shard_map/ppermute | solution.py:526
  257.1 2.6 collective-permute-done.25
  259.7 2.1 add_convert_fusion.12
  265.9 1.6 collective-permute-start.29
  268.2 2.3 convert_add_fusion.3
  271.1 2.9 fusion
  274.0 2.2 convert_add_fusion.4
  277.9 4.4 %collective-permute-done.27 = bf16[512,512]{1,0:T(8,128)(2,1)} collective-permute-done((bf16[512,512]{1,0:T(8,128)(2,1)}, bf16[512,512]{1,0:T(8,128)(2,1)}, u32[]{:S(2)}, u32[]{:S(2)}) %collective-permute-start.27) | collective-permute-done | bytes 524320 | tf_op jit(solution)/shard_map/ppermute | solution.py:526
  282.3 1.7 add_convert_fusion.11
  284.2 4.1 %collective-permute-start.36 = (bf16[256,512]{1,0:T(8,128)(2,1)S(1)}, bf16[256,512]{1,0:T(8,128)(2,1)S(1)}, u32[]{:S(2)}, u32[]{:S(2)}) collective-permute-start(bf16[256,512]{1,0:T(8,128)(2,1)S(1)} %add_convert_fusion.11), channel_id=1, source_target_pairs={{0,16},{4,20},{8,24},{12,28},{16,0},{20,4},{24,8},{28,12},{1,17},{... | collective-permute-start | bytes 786440 | tf_op jit(solution)/shard_map/ppermute | solution.py:526
  288.3 2.7 fusion.8
  291.8 1.8 add_bitcast_fusion
  293.5 1.5 collective-permute-done.31
  298.2 1.6 collective-permute-done.33
  299.9 3.8 %collective-permute-done.37 = bf16[1,20480]{1,0:T(2,128)(2,1)S(1)} collective-permute-done((bf16[1,20480]{1,0:T(2,128)(2,1)S(1)}, bf16[1,20480]{1,0:T(2,128)(2,1)S(1)}, u32[]{:S(2)}, u32[]{:S(2)}) %collective-permute-start.37) | collective-permute-done | bytes 40992 | tf_op jit(solution)/shard_map/ppermute | solution.py:526
  305.4 1.6 convert_add_fusion.1
  309.9 2.0 fusion.4
  313.2 2.9 copy.66
  (257 shorter events, 57.7 us)
Async XLA Ops:
  0.6 26.5 %collective-permute-start.1 = (bf16[1024,512]{1,0:T(8,128)(2,1)}, bf16[1024,512]{1,0:T(8,128)(2,1)}, u32[]{:S(2)}, u32[]{:S(2)}) collective-permute-start(bf16[1024,512]{1,0:T(8,128)(2,1)} %refs_0_.4), channel_id=1, source_target_pairs={{0,2},{1,3},{2,0},{3,1},{4,6},{5,7},{6,4},{7,5},{8,10},{9,11},{10,... | collective-permute-start | bytes 3145736 | tf_op jit(solution)/shard_map/ppermute | solution.py:526
  3.7 27.9 %collective-permute-start.3 = (bf16[1024,512]{1,0:T(8,128)(2,1)}, bf16[1024,512]{1,0:T(8,128)(2,1)}, u32[]{:S(2)}, u32[]{:S(2)}) collective-permute-start(bf16[1024,512]{1,0:T(8,128)(2,1)} %refs_0_.4), channel_id=1, source_target_pairs={{0,1},{1,0},{2,3},{3,2},{4,5},{5,4},{6,7},{7,6},{8,9},{9,8},{10,11... | collective-permute-start | bytes 3145736 | tf_op jit(solution)/shard_map/ppermute | solution.py:526
  17.5 12.2 %copy-start.47 = (f32[5,256]{1,0:T(8,128)S(1)}, f32[5,256]{1,0:T(8,128)}, u32[]{:S(2)}) copy-start(f32[5,256]{1,0:T(8,128)} %param.22) | copy-start | bytes 15364
  17.5 12.8 %copy-start.55 = (f32[16]{0:T(128)S(1)}, f32[16]{0:T(128)}, u32[]{:S(2)}) copy-start(f32[16]{0:T(128)} %param.24) | copy-start | bytes 196
  17.5 13.4 %copy-start.53 = (f32[16]{0:T(128)S(1)}, f32[16]{0:T(128)}, u32[]{:S(2)}) copy-start(f32[16]{0:T(128)} %param.23) | copy-start | bytes 196
  27.8 3.8 %collective-permute-start.4 = (bf16[1024,512]{1,0:T(8,128)(2,1)}, bf16[1024,512]{1,0:T(8,128)(2,1)}, u32[]{:S(2)}, u32[]{:S(2)}) collective-permute-start(bf16[1024,512]{1,0:T(8,128)(2,1)} %collective-permute-done.1.refs_2_), channel_id=1, source_target_pairs={{0,1},{1,0},{2,3},{3,2},{4,5},{5,4},{6,7},{7,6},{8,9},{9,8},{10,11... | collective-permute-start | bytes 3145736 | tf_op jit(solution)/shard_map/ppermute | solution.py:526
  27.8 40.9 %collective-permute-start.2 = (bf16[1024,512]{1,0:T(8,128)(2,1)S(1)}, bf16[1024,512]{1,0:T(8,128)(2,1)S(1)}, u32[]{:S(2)}, u32[]{:S(2)}) collective-permute-start(bf16[1024,512]{1,0:T(8,128)(2,1)S(1)} %copy-done.3), channel_id=1, source_target_pairs={{0,2},{1,3},{2,0},{3,1},{4,6},{5,7},{6,4},{7,5},{8,10},{9,11},{10,... | collective-permute-start | bytes 3145736 | tf_op jit(solution)/shard_map/ppermute | solution.py:526
  29.5 39.6 %collective-permute-start = (bf16[1024,512]{1,0:T(8,128)(2,1)S(1)}, bf16[1024,512]{1,0:T(8,128)(2,1)S(1)}, u32[]{:S(2)}, u32[]{:S(2)}) collective-permute-start(bf16[1024,512]{1,0:T(8,128)(2,1)S(1)} %copy-done.3), channel_id=1, source_target_pairs={{0,1},{1,0},{2,3},{3,2},{4,5},{5,4},{6,7},{7,6},{8,9},{9,8},{10,11... | collective-permute-start | bytes 3145736 | tf_op jit(solution)/shard_map/ppermute | solution.py:526
  68.7 2.7 collective-permute-start.5
  84.2 1.5 collective-permute-start.6
  86.5 3.9 %collective-permute-start.7 = (f32[8,1024]{1,0:T(8,128)S(1)}, f32[8,1024]{1,0:T(8,128)S(1)}, u32[]{:S(2)}, u32[]{:S(2)}) collective-permute-start(f32[8,1024]{1,0:T(8,128)S(1)} %add.349), channel_id=1, source_target_pairs={{0,2},{1,3},{2,0},{3,1},{4,6},{5,7},{6,4},{7,5},{8,10},{9,11},{10,... | collective-permute-start | bytes 98312 | tf_op jit(solution)/shard_map/ppermute | solution.py:526
  100.6 28.0 %collective-permute-start.8 = (bf16[512,1024]{1,0:T(8,128)(2,1)}, bf16[512,1024]{1,0:T(8,128)(2,1)S(1)}, u32[]{:S(2)}, u32[]{:S(2)}) collective-permute-start(bf16[512,1024]{1,0:T(8,128)(2,1)} %get-tuple-element.193), channel_id=1, source_target_pairs={{0,4},{4,0},{8,12},{12,8},{16,20},{20,16},{24,28},{28,24},{1,5},{5... | collective-permute-start | bytes 3145736 | tf_op jit(solution)/shard_map/ppermute | solution.py:526
  119.5 10.6 %copy-start.24 = (bf16[512,1024]{1,0:T(8,128)(2,1)S(1)}, bf16[512,1024]{1,0:T(8,128)(2,1)}, u32[]{:S(2)}) copy-start(bf16[512,1024]{1,0:T(8,128)(2,1)} %get-tuple-element.182) | copy-start | bytes 3145732
  129.6 26.3 %collective-permute-start.9 = (bf16[2,1024,512]{2,1,0:T(8,128)(2,1)}, bf16[2,1024,512]{2,1,0:T(8,128)(2,1)S(1)}, u32[]{:S(2)}, u32[]{:S(2)}) collective-permute-start(bf16[2,1024,512]{2,1,0:T(8,128)(2,1)} %get-tuple-element.195), channel_id=1, source_target_pairs={{0,1},{1,0},{2,3},{3,2},{4,5},{5,4},{6,7},{7,6},{8,9},{9,8},{10,11... | collective-permute-start | bytes 6291464 | tf_op jit(solution)/shard_map/ppermute | solution.py:526
  129.6 26.3 %collective-permute-start.11 = (bf16[512,1024]{1,0:T(8,128)(2,1)}, bf16[512,1024]{1,0:T(8,128)(2,1)}, u32[]{:S(2)}, u32[]{:S(2)}) collective-permute-start(bf16[512,1024]{1,0:T(8,128)(2,1)} %get-tuple-element.206), channel_id=1, source_target_pairs={{0,4},{4,0},{8,12},{12,8},{16,20},{20,16},{24,28},{28,24},{1,5},{5... | collective-permute-start | bytes 3145736 | tf_op jit(solution)/shard_map/ppermute | solution.py:526
  131.3 24.5 %collective-permute-start.10 = (bf16[512,512]{1,0:T(8,128)(2,1)S(1)}, bf16[512,512]{1,0:T(8,128)(2,1)S(1)}, u32[]{:S(2)}, u32[]{:S(2)}) collective-permute-start(bf16[512,512]{1,0:T(8,128)(2,1)S(1)} %add_convert_fusion.9), channel_id=1, source_target_pairs={{0,8},{4,12},{8,0},{12,4},{16,24},{20,28},{24,16},{28,20},{1,9},{5... | collective-permute-start | bytes 1572872 | tf_op jit(solution)/shard_map/ppermute | solution.py:526
  132.9 71.8 %collective-permute-start.15 = (bf16[1024,1024]{1,0:T(8,128)(2,1)}, bf16[1024,1024]{1,0:T(8,128)(2,1)}, u32[]{:S(2)}, u32[]{:S(2)}) collective-permute-start(bf16[1024,1024]{1,0:T(8,128)(2,1)} %get-tuple-element.229), channel_id=1, source_target_pairs={{0,4},{4,0},{8,12},{12,8},{16,20},{20,16},{24,28},{28,24},{1,5},{5... | collective-permute-start | bytes 6291464 | tf_op jit(solution)/shard_map/ppermute | solution.py:526
  134.4 21.4 %copy-start.15 = (bf16[2,1024,512]{2,1,0:T(8,128)(2,1)S(1)}, bf16[2,1024,512]{2,1,0:T(8,128)(2,1)}, u32[]{:S(2)}) copy-start(bf16[2,1024,512]{2,1,0:T(8,128)(2,1)} %get-tuple-element.210) | copy-start | bytes 6291460
  156.2 32.0 %collective-permute-start.12 = (bf16[1024,512]{1,0:T(8,128)(2,1)S(1)}, bf16[1024,512]{1,0:T(8,128)(2,1)}, u32[]{:S(2)}, u32[]{:S(2)}) collective-permute-start(bf16[1024,512]{1,0:T(8,128)(2,1)S(1)} %fusion.10), channel_id=1, source_target_pairs={{0,2},{1,3},{2,0},{3,1},{4,6},{5,7},{6,4},{7,5},{8,10},{9,11},{10,... | collective-permute-start | bytes 3145736 | tf_op jit(solution)/shard_map/ppermute | solution.py:526
  159.2 28.9 %collective-permute-start.14 = (bf16[512,512]{1,0:T(8,128)(2,1)}, bf16[512,512]{1,0:T(8,128)(2,1)}, u32[]{:S(2)}, u32[]{:S(2)}) collective-permute-start(bf16[512,512]{1,0:T(8,128)(2,1)} %add_convert_fusion.8), channel_id=1, source_target_pairs={{0,8},{4,12},{8,0},{12,4},{16,24},{20,28},{24,16},{28,20},{1,9},{5... | collective-permute-start | bytes 1572872 | tf_op jit(solution)/shard_map/ppermute | solution.py:526
  162.3 25.9 %collective-permute-start.13 = (bf16[512,256]{1,0:T(8,128)(2,1)S(1)}, bf16[512,256]{1,0:T(8,128)(2,1)S(1)}, u32[]{:S(2)}, u32[]{:S(2)}) collective-permute-start(bf16[512,256]{1,0:T(8,128)(2,1)S(1)} %add_convert_fusion.14), channel_id=1, source_target_pairs={{0,16},{4,20},{8,24},{12,28},{16,0},{20,4},{24,8},{28,12},{1,17},{... | collective-permute-start | bytes 786440 | tf_op jit(solution)/shard_map/ppermute | solution.py:526
  170.8 19.3 %copy-start.54 = (bf16[1024,512]{1,0:T(8,128)(2,1)S(1)}, bf16[1024,512]{1,0:T(8,128)(2,1)}, u32[]{:S(2)}) copy-start(bf16[1024,512]{1,0:T(8,128)(2,1)} %get-tuple-element.237) | copy-start | bytes 3145732
  189.7 15.1 %collective-permute-start.16 = (bf16[512,256]{1,0:T(8,128)(2,1)S(1)}, bf16[512,256]{1,0:T(8,128)(2,1)S(1)}, u32[]{:S(2)}, u32[]{:S(2)}) collective-permute-start(bf16[512,256]{1,0:T(8,128)(2,1)S(1)} %add_convert_fusion.13), channel_id=1, source_target_pairs={{0,16},{4,20},{8,24},{12,28},{16,0},{20,4},{24,8},{28,12},{1,17},{... | collective-permute-start | bytes 786440 | tf_op jit(solution)/shard_map/ppermute | solution.py:526
  190.1 37.5 %collective-permute-start.20 = (bf16[1024,512]{1,0:T(8,128)(2,1)S(1)}, bf16[1024,512]{1,0:T(8,128)(2,1)S(1)}, u32[]{:S(2)}, u32[]{:S(2)}) collective-permute-start(bf16[1024,512]{1,0:T(8,128)(2,1)S(1)} %copy-done.54), channel_id=1, source_target_pairs={{0,4},{4,0},{8,12},{12,8},{16,20},{20,16},{24,28},{28,24},{1,5},{5... | collective-permute-start | bytes 3145736 | tf_op jit(solution)/shard_map/ppermute | solution.py:526
  207.1 23.2 %collective-permute-start.21 = (bf16[512,1024]{1,0:T(8,128)(2,1)S(1)}, bf16[512,1024]{1,0:T(8,128)(2,1)S(1)}, u32[]{:S(2)}, u32[]{:S(2)}) collective-permute-start(bf16[512,1024]{1,0:T(8,128)(2,1)S(1)} %add_convert_fusion.1), channel_id=1, source_target_pairs={{0,8},{4,12},{8,0},{12,4},{16,24},{20,28},{24,16},{28,20},{1,9},{5... | collective-permute-start | bytes 3145736 | tf_op jit(solution)/shard_map/ppermute | solution.py:526
  207.6 20.0 %collective-permute-start.18 = (bf16[1024,256]{1,0:T(8,128)(2,1)}, bf16[1024,256]{1,0:T(8,128)(2,1)S(1)}, u32[]{:S(2)}, u32[]{:S(2)}) collective-permute-start(bf16[1024,256]{1,0:T(8,128)(2,1)} %get-tuple-element.231.refs_4_), channel_id=1, source_target_pairs={{0,1},{1,0},{2,3},{3,2},{4,5},{5,4},{6,7},{7,6},{8,9},{9,8},{10,11... | collective-permute-start | bytes 1572872 | tf_op jit(solution)/shard_map/ppermute | solution.py:526
  207.6 1.5 collective-permute-start.17
  209.1 18.5 %collective-permute-start.19 = (f32[5,256]{1,0:T(8,128)S(1)}, f32[5,256]{1,0:T(8,128)S(1)}, u32[]{:S(2)}, u32[]{:S(2)}) collective-permute-start(f32[5,256]{1,0:T(8,128)S(1)} %add.362), channel_id=1, source_target_pairs={{0,2},{1,3},{2,0},{3,1},{4,6},{5,7},{6,4},{7,5},{8,10},{9,11},{10,... | collective-permute-start | bytes 15368 | tf_op jit(solution)/shard_map/ppermute | solution.py:526
  210.2 25.0 %copy-start.27 = (bf16[1024,512]{1,0:T(8,128)(2,1)S(1)}, bf16[1024,512]{1,0:T(8,128)(2,1)}, u32[]{:S(2)}) copy-start(bf16[1024,512]{1,0:T(8,128)(2,1)} %get-tuple-element.213) | copy-start | bytes 3145732
  231.3 10.6 %collective-permute-start.22 = (bf16[2,1024,512]{2,1,0:T(8,128)(2,1)}, bf16[2,1024,512]{2,1,0:T(8,128)(2,1)S(1)}, u32[]{:S(2)}, u32[]{:S(2)}) collective-permute-start(bf16[2,1024,512]{2,1,0:T(8,128)(2,1)} %get-tuple-element.239), channel_id=1, source_target_pairs={{0,1},{1,0},{2,3},{3,2},{4,5},{5,4},{6,7},{7,6},{8,9},{9,8},{10,11... | collective-permute-start | bytes 6291464 | tf_op jit(solution)/shard_map/ppermute | solution.py:526
  231.3 25.8 %collective-permute-start.26 = (bf16[1024,512]{1,0:T(8,128)(2,1)}, bf16[1024,512]{1,0:T(8,128)(2,1)S(1)}, u32[]{:S(2)}, u32[]{:S(2)}) collective-permute-start(bf16[1024,512]{1,0:T(8,128)(2,1)} %get-tuple-element.264), channel_id=1, source_target_pairs={{0,4},{4,0},{8,12},{12,8},{16,20},{20,16},{24,28},{28,24},{1,5},{5... | collective-permute-start | bytes 3145736 | tf_op jit(solution)/shard_map/ppermute | solution.py:526
  234.1 14.8 %collective-permute-start.24 = (bf16[1024,256]{1,0:T(8,128)(2,1)S(1)}, bf16[1024,256]{1,0:T(8,128)(2,1)S(1)}, u32[]{:S(2)}, u32[]{:S(2)}) collective-permute-start(bf16[1024,256]{1,0:T(8,128)(2,1)S(1)} %add_convert_fusion.5), channel_id=1, source_target_pairs={{0,2},{1,3},{2,0},{3,1},{4,6},{5,7},{6,4},{7,5},{8,10},{9,11},{10,... | collective-permute-start | bytes 1572872 | tf_op jit(solution)/shard_map/ppermute | solution.py:526
  236.4 23.3 %collective-permute-start.25 = (bf16[512,512]{1,0:T(8,128)(2,1)S(1)}, bf16[512,512]{1,0:T(8,128)(2,1)S(1)}, u32[]{:S(2)}, u32[]{:S(2)}) collective-permute-start(bf16[512,512]{1,0:T(8,128)(2,1)S(1)} %add_convert_fusion.7), channel_id=1, source_target_pairs={{0,8},{4,12},{8,0},{12,4},{16,24},{20,28},{24,16},{28,20},{1,9},{5... | collective-permute-start | bytes 1572872 | tf_op jit(solution)/shard_map/ppermute | solution.py:526
  236.9 12.0 %copy-start = (bf16[1024,2048]{1,0:T(8,128)(2,1)S(1)}, bf16[1024,2048]{1,0:T(8,128)(2,1)}, u32[]{:S(2)}) copy-start(bf16[1024,2048]{1,0:T(8,128)(2,1)} %get-tuple-element.253.left_send.left_own) | copy-start | bytes 12582916
  239.4 38.5 %collective-permute-start.28 = (bf16[256,1024]{1,0:T(8,128)(2,1)}, bf16[256,1024]{1,0:T(8,128)(2,1)}, u32[]{:S(2)}, u32[]{:S(2)}) collective-permute-start(bf16[256,1024]{1,0:T(8,128)(2,1)} %add_convert_fusion.6), channel_id=1, source_target_pairs={{0,16},{4,20},{8,24},{12,28},{16,0},{20,4},{24,8},{28,12},{1,17},{... | collective-permute-start | bytes 1572872 | tf_op jit(solution)/shard_map/ppermute | solution.py:526
  243.4 38.8 %collective-permute-start.23 = (bf16[1024,512]{1,0:T(8,128)(2,1)}, bf16[1024,512]{1,0:T(8,128)(2,1)S(1)}, u32[]{:S(2)}, u32[]{:S(2)}) collective-permute-start(bf16[1024,512]{1,0:T(8,128)(2,1)} %fusion.11), channel_id=1, source_target_pairs={{0,2},{1,3},{2,0},{3,1},{4,6},{5,7},{6,4},{7,5},{8,10},{9,11},{10,... | collective-permute-start | bytes 3145736 | tf_op jit(solution)/shard_map/ppermute | solution.py:526
  250.4 11.5 %copy-start.28 = (bf16[1024,512]{1,0:T(8,128)(2,1)S(1)}, bf16[1024,512]{1,0:T(8,128)(2,1)}, u32[]{:S(2)}) copy-start(bf16[1024,512]{1,0:T(8,128)(2,1)} %get-tuple-element.219) | copy-start | bytes 3145732
  262.7 19.5 %collective-permute-start.27 = (bf16[512,512]{1,0:T(8,128)(2,1)}, bf16[512,512]{1,0:T(8,128)(2,1)}, u32[]{:S(2)}, u32[]{:S(2)}) collective-permute-start(bf16[512,512]{1,0:T(8,128)(2,1)} %add_convert_fusion.3), channel_id=1, source_target_pairs={{0,8},{4,12},{8,0},{12,4},{16,24},{20,28},{24,16},{28,20},{1,9},{5... | collective-permute-start | bytes 1572872 | tf_op jit(solution)/shard_map/ppermute | solution.py:526
  262.7 35.5 %collective-permute-start.35 = (bf16[256,512]{1,0:T(8,128)(2,1)}, bf16[256,512]{1,0:T(8,128)(2,1)}, u32[]{:S(2)}, u32[]{:S(2)}) collective-permute-start(bf16[256,512]{1,0:T(8,128)(2,1)} %add_convert_fusion.12), channel_id=1, source_target_pairs={{0,16},{4,20},{8,24},{12,28},{16,0},{20,4},{24,8},{28,12},{1,17},{... | collective-permute-start | bytes 786440 | tf_op jit(solution)/shard_map/ppermute | solution.py:526
  265.9 12.0 %collective-permute-start.29 = (bf16[4,20480]{1,0:T(4,128)(2,1)S(1)}, bf16[4,20480]{1,0:T(4,128)(2,1)S(1)}, u32[]{:S(2)}, u32[]{:S(2)}) collective-permute-start(bf16[4,20480]{1,0:T(4,128)(2,1)S(1)} %bitcast.102), channel_id=1, source_target_pairs={{0,4},{4,0},{8,12},{12,8},{16,20},{20,16},{24,28},{28,24},{1,5},{5... | collective-permute-start | bytes 491528 | tf_op jit(solution)/shard_map/ppermute | solution.py:526
  284.1 11.0 %collective-permute-start.32 = (bf16[2,20480]{1,0:T(2,128)(2,1)S(1)}, bf16[2,20480]{1,0:T(2,128)(2,1)S(1)}, u32[]{:S(2)}, u32[]{:S(2)}) collective-permute-start(bf16[2,20480]{1,0:T(2,128)(2,1)S(1)} %fusion.14), channel_id=1, source_target_pairs={{0,8},{4,12},{8,0},{12,4},{16,24},{20,28},{24,16},{28,20},{1,9},{5... | collective-permute-start | bytes 245768 | tf_op jit(solution)/shard_map/ppermute | solution.py:526
  284.2 19.5 %collective-permute-start.36 = (bf16[256,512]{1,0:T(8,128)(2,1)S(1)}, bf16[256,512]{1,0:T(8,128)(2,1)S(1)}, u32[]{:S(2)}, u32[]{:S(2)}) collective-permute-start(bf16[256,512]{1,0:T(8,128)(2,1)S(1)} %add_convert_fusion.11), channel_id=1, source_target_pairs={{0,16},{4,20},{8,24},{12,28},{16,0},{20,4},{24,8},{28,12},{1,17},{... | collective-permute-start | bytes 786440 | tf_op jit(solution)/shard_map/ppermute | solution.py:526
  291.1 4.0 %collective-permute-start.31 = (f32[7984]{0:T(1024)S(1)}, f32[7984]{0:T(1024)S(1)}, u32[]{:S(2)}, u32[]{:S(2)}) collective-permute-start(f32[7984]{0:T(1024)S(1)} %pad_maximum_fusion.6), channel_id=1, source_target_pairs={{0,4},{4,0},{8,12},{12,8},{16,20},{20,16},{24,28},{28,24},{1,5},{5... | collective-permute-start | bytes 95816 | tf_op jit(solution)/shard_map/ppermute | solution.py:526
  291.8 1.8 collective-permute-start.30
  295.3 8.3 %collective-permute-start.37 = (bf16[1,20480]{1,0:T(2,128)(2,1)S(1)}, bf16[1,20480]{1,0:T(2,128)(2,1)S(1)}, u32[]{:S(2)}, u32[]{:S(2)}) collective-permute-start(bf16[1,20480]{1,0:T(2,128)(2,1)S(1)} %fusion.22), channel_id=1, source_target_pairs={{0,16},{4,20},{8,24},{12,28},{16,0},{20,4},{24,8},{28,12},{1,17},{... | collective-permute-start | bytes 122888 | tf_op jit(solution)/shard_map/ppermute | solution.py:526
  295.4 4.5 %collective-permute-start.34 = (f32[7984]{0:T(1024)S(1)}, f32[7984]{0:T(1024)S(1)}, u32[]{:S(2)}, u32[]{:S(2)}) collective-permute-start(f32[7984]{0:T(1024)S(1)} %add.399), channel_id=1, source_target_pairs={{0,8},{4,12},{8,0},{12,4},{16,24},{20,28},{24,16},{28,20},{1,9},{5... | collective-permute-start | bytes 95816 | tf_op jit(solution)/shard_map/ppermute | solution.py:526
  296.2 3.6 %collective-permute-start.33 = (f32[1024]{0:T(1024)S(1)}, f32[1024]{0:T(1024)S(1)}, u32[]{:S(2)}, u32[]{:S(2)}) collective-permute-start(f32[1024]{0:T(1024)S(1)} %add.398), channel_id=1, source_target_pairs={{0,2},{1,3},{2,0},{3,1},{4,6},{5,7},{6,4},{7,5},{8,10},{9,11},{10,... | collective-permute-start | bytes 12296 | tf_op jit(solution)/shard_map/ppermute | solution.py:526
  307.0 9.1 %collective-permute-start.38 = (f32[7984]{0:T(1024)S(1)}, f32[7984]{0:T(1024)S(1)}, u32[]{:S(2)}, u32[]{:S(2)}) collective-permute-start(f32[7984]{0:T(1024)S(1)} %add.405), channel_id=1, source_target_pairs={{0,16},{4,20},{8,24},{12,28},{16,0},{20,4},{24,8},{28,12},{1,17},{... | collective-permute-start | bytes 95816 | tf_op jit(solution)/shard_map/ppermute | solution.py:526
  (47 other events, 209.6 us)

commit v6 on v5

--- a/solution.py
+++ b/solution.py
@@ -118,8 +118,15 @@
 ):
     pieces, refs = refs[:parts], refs[parts:]
     (gain, w_maps, conv_maps, bias, rate, seg_row, w_gate, w_value, conv, skip, gate_gain, marks,
-     normed, pre_state, maps, maps_t, per_head, rows_out, cross_t, value, gate, mixed, low_gated, memory, squares,
-     proj, cross, state) = refs
+     *outs), (value, gate, mixed, low_gated, memory, squares, proj, cross, state), (
+        normed, pre_state, maps, maps_t, per_head, rows_out, cross_t, sems
+    ) = refs[:-17], refs[-17:-8], refs[-8:]
+    copies = [
+        pltpu.make_async_copy(source, target, sems.at[i])
+        for i, (source, target) in enumerate(
+            zip((normed, pre_state, maps, maps_t, per_head, rows_out, cross_t), outs)
+        )
+    ]
     g = pl.program_id(0)
     length, quarter = pieces[0].shape
     width = quarter * parts
@@ -144,6 +151,7 @@
             return 0
 
         lax.fori_loop(0, blocks, normalise, 0, unroll=2)
+        copies[0].start()
         proj[...] = dot(normed[...], w_maps[...])
 
         def tables(b, _):
@@ -184,6 +192,8 @@
             return 0
 
         lax.fori_loop(0, blocks, tables, 0, unroll=2)
+        for copy in copies[1:]:
+            copy.start()
 
     both = dot(normed[...], jnp.concatenate([w_gate[...], w_value[...]], axis=1))
     gate[...] = both[:, :GROUP].astype(BF16)
@@ -232,6 +242,11 @@
         return 0
 
     lax.fori_loop(0, blocks, block, 0, unroll=UNROLL)
+
+    @pl.when(g == pl.num_programs(0) - 1)
+    def _():
+        for copy in copies:
+            copy.wait()
 
 
 def assemble(pieces, target, sems, where):
@@ -680,8 +695,7 @@
             by_group(8), by_group(1), by_group(1), held((length + 8, LANES)),
         ],
         [
-            held((length, width)), held((length, states2)), held((length, states2)), held((states2, length)),
-            held((length, LANES)), held((steps, blocks * 8, SPAN)), held((length, SPAN)),
+            *[pl.BlockSpec(memory_space=pl.ANY)] * 7,
             by_group(length), by_group(length), by_group(length), by_group(length),
             pl.BlockSpec((blocks, states, GROUP), lambda g, *_: (0, 0, g)), held((length, LANES)),
         ],
@@ -695,6 +709,9 @@
         [
             pltpu.VMEM((length, states2 + LANES), F32), pltpu.VMEM((length, SPAN), F32),
             pltpu.VMEM((states, GROUP), F32),
+            pltpu.VMEM((length, width), BF16), pltpu.VMEM((length, states2), F32), pltpu.VMEM((length, states2), BF16),
+            pltpu.VMEM((states2, length), BF16), pltpu.VMEM((length, LANES), F32),
+            pltpu.VMEM((steps, blocks * 8, SPAN), F32), pltpu.VMEM((length, SPAN), F32), pltpu.SemaphoreType.DMA((7,)),
         ],
         prefetch=1,
         flops=8 * length * width * channels,
@@ -994,8 +1011,7 @@
     small_sum.advance()
     row_norm, pack = row_norm + row_got, pack + pack_got
     row_got, pack_got = swap(row_norm, "tensor", 2), swap(pack, "dp", 2)
-    row_norm, row_got, pack, pack_got = meet([*sum_value, small_sum], row_norm, row_got, pack, pack_got)
-    total_value = [part.result() for part in sum_value]
+    row_norm, row_got, pack, pack_got = lax.optimization_barrier((row_norm, row_got, pack, pack_got))
     row_norm, pack = row_norm + row_got, pack + pack_got
     bit = 4
     while bit < groups:
@@ -1006,6 +1022,8 @@
         + scale_in * own_gain * grad_normed
         - own_tokens * scale_in**3 * row_norm[:, None] / width
     ).astype(BF16)
+    (grad_tokens,) = meet([*sum_value, small_sum], grad_tokens)
+    total_value = [part.result() for part in sum_value]
     small_sum = small_sum.result()[0]
     sum_state = small_sum[: own_rows * states2].reshape(own_rows, states2)
     sum_step = small_sum[own_rows * states2 :].reshape(heads, piece_rows).T

time: 325 us -> 323 us (level)
  other arithmetic: 45.5 us -> 49.2 us
    unnamed x117 -> x113, local copies, waits for them, and re-layouts: 19.9 us -> 18.1 us
  transfers between devices with their start and end apart: 39 -> 39, of which waited for: 15 -> 15; matrix products, arithmetic and copies ran while one was open for 21% -> 22% of each run, Pallas kernels for 42% -> 42%
where the time goes in v6:
time: 323 us; the launch traced here: 318 us
  Pallas kernels  156 us (48%)
  other arithmetic  49.2 us (15%)
  waiting for transfers between devices  41.7 us (13%)
  starting transfers between devices  35.6 us (11%)
  local copies, waits for them, and re-layouts  32 us (10%)
    ppermute x39, waiting for transfers between devices, swap(): return lax.ppermute(array, axis, [(i, i ^ mask) for i in range(count)])  41.7 us
    pallas_call x1, Pallas kernels, shards(): call(functools.partial(front_kernel, parts, heads), (steps,), [held((leng...  36 us
    ppermute x39, starting transfers between devices, swap(): return lax.ppermute(array, axis, [(i, i ^ mask) for i in range(count)])  35.6 us
    pallas_call x2, Pallas kernels, backward_part(): call(functools.partial(backward_kernel, heads, c * spans), (spans,), [chu...  34.6 us
    pallas_call x3, Pallas kernels, weight_part(): call(weight_kernel, (runs,), [pl.BlockSpec((length, run), lambda j, p: (0...  20 us
    pallas_call x2, Pallas kernels, gate_part(): call(functools.partial(gate_kernel, parts, run, channels * parts, stacked...  18.9 us
    convert_element_type x12, other arithmetic, send(): functools.reduce(jnp.add, [term.astype(F32) for term in cut(1 - top)])  18.5 us
    unnamed x113, local copies, waits for them, and re-layouts  18.1 us
  transfers between devices with their start and end apart: 39, of which 15 were waited for; matrix products, arithmetic and copies ran while one was open for 22% of the time, Pallas kernels for 42%

profile of v6, /device:TPU:0, one launch (start us, length us, event | category | flops | bytes accessed | tf_op | source)
XLA Modules:
  0.0 317.9 jit_solution(3151929807756780343)
XLA Ops:
  0.6 3.0 collective-permute-start.1
  6.9 10.3 %copy.69 = bf16[256,8,2,1024]{3,1,2,0:T(8,128)(2,1)} copy(bf16[256,8,2,1024]{3,2,1,0:T(2,128)(2,1)} %bitcast.89) | data formatting | bytes 16777216
  21.1 6.1 %collective-permute-done.1.refs_2_ = bf16[1024,512]{1,0:T(8,128)(2,1)} collective-permute-done((bf16[1024,512]{1,0:T(8,128)(2,1)}, bf16[1024,512]{1,0:T(8,128)(2,1)}, u32[]{:S(2)}, u32[]{:S(2)}) %collective-permute-start.1) | collective-permute-done | bytes 1048608 | tf_op jit(solution)/shard_map/ppermute | solution.py:541
  27.8 1.7 collective-permute-start.2
  31.6 36.0 %front.1 = (bf16[1024,2048]{1,0:T(8,128)(2,1)}, f32[1024,256]{1,0:T(8,128)}, bf16[1024,256]{1,0:T(8,128)(2,1)}, bf16[256,1024]{1,0:T(8,128)(2,1)}, f32[1024,128]...) custom-call(s32[1]{0:T(128)} %bitcast.rank, ...), custom_call_target="tpu_custom_call" | custom-call | flops 343597376 | bytes 629145 | tf_op jit(solution)/shard_map/front/pallas_call | solution.py:687
  67.9 2.4 collective-permute-done.5.refs_3_
  71.3 11.8 %cotangent.1 = (bf16[1024,1024]{1,0:T(8,128)(2,1)}, f32[8,1024]{1,0:T(8,128)}) custom-call(s32[1]{0:T(128)} %bitcast.rank, bf16[1024,512]{1,0:T(8,128)(2,1)} %refs_0_.7, bf16[1024,512]{1,0:T(8,128)(2,1)} %copy-done.6, bf16[1024,512]{1,0:T(8,128)(2,1)} %copy-done.5, bf16[1024,512]{1,0:T(8,128)(2,1)} %copy-done.7, bf16[1024,2048]{1,0:T(8,128)(2,1)} %w_out.1, ...), custom_call_target="tpu_custom_call" | custom-call | flops 85899344 | bytes 419430 | tf_op jit(solution)/shard_map/cotangent/pallas_call | solution.py:731
  86.3 3.0 collective-permute-done.7
  89.9 9.5 %gate.2 = (bf16[1024,512]{1,0:T(8,128)(2,1)}, bf16[1024,512]{1,0:T(8,128)(2,1)}, bf16[1024,512]{1,0:T(8,128)(2,1)}, f32[1,512]{1,0:T(1,128)}, bf16[512,1024]{1,0:T(8,128)(2,1)}, /*index=5*/bf16[512,1024]{1,0:T(8,128)(2,1)}) custom-call(s32[1]{0:T(128)} %bitcast.1.place, s32[1]{0:T(128)} %bitcast.rank, bf16[1024,512]{1,0:T(8,128)(2,1)} %refs_0_.7, ...), custom_call_target="tpu_custom_call" | custom-call | flops 42949672 | bytes 314572 | tf_op jit(solution)/shard_map/gate/pallas_call | solution.py:761
  99.4 1.6 collective-permute-start.8
  101.0 9.3 %gate.3 = (bf16[1024,512]{1,0:T(8,128)(2,1)}, bf16[1024,512]{1,0:T(8,128)(2,1)}, bf16[1024,512]{1,0:T(8,128)(2,1)}, f32[1,512]{1,0:T(1,128)}, bf16[512,1024]{1,0:T(8,128)(2,1)}, /*index=5*/bf16[512,1024]{1,0:T(8,128)(2,1)}) custom-call(s32[1]{0:T(128)} %bitcast.1.place, s32[1]{0:T(128)} %bitcast.rank, bf16[1024,512]{1,0:T(8,128)(2,1)} %refs_0_.7, ...), custom_call_target="tpu_custom_call" | custom-call | flops 42949672 | bytes 314572 | tf_op jit(solution)/shard_map/gate/pallas_call | solution.py:761
  110.3 8.0 %weights.3 = (bf16[1024,1024]{1,0:T(8,128)(2,1)}, bf16[1024,1024]{1,0:T(8,128)(2,1)}) custom-call(s32[1]{0:T(128)} %bitcast.1.place, bf16[1024,2048]{1,0:T(8,128)(2,1)} %get-tuple-element.254.left_send.left_own, bf16[1024,2048]{1,0:T(8,128)(2,1)} %get-tuple-element.254.left_send.left_own, bf16[1024,512]{1,0:T(8,128)(2,1)} %get-tuple-element.234.refs_0_, ...), custom_call_target="tpu_custom_call" | custom-call | flops 85899344 | bytes 209715 | tf_op jit(solution)/shard_map/weights/pallas_call | solution.py:789
  118.3 9.1 %output.1 = (bf16[2,1024,512]{2,1,0:T(8,128)(2,1)}, bf16[2,1024,512]{2,1,0:T(8,128)(2,1)}) custom-call(s32[1]{0:T(128)} %bitcast.rank, bf16[1024,1024]{1,0:T(8,128)(2,1)} %get-tuple-element.191.refs_5_.gated, bf16[1024,2048]{1,0:T(8,128)(2,1)} %w_out.1), custom_call_target="tpu_custom_call" | custom-call | flops 85899344 | bytes 209715 | tf_op jit(solution)/shard_map/output/pallas_call | solution.py:845
  130.2 1.6 collective-permute-start.10
  131.8 1.5 collective-permute-start.15
  133.3 17.3 %backward.2 = (bf16[1024,512]{1,0:T(8,128)(2,1)}, f32[8,512]{1,0:T(8,128)}, f32[1,512]{1,0:T(1,128)}, f32[1024,128]{1,0:T(8,128)}, f32[1024,128]{1,0:T(8,128)}, /*index=5*/f32[1024,256]{1,0:T(8,128)}) custom-call(f32[1024,1024]{1,0:T(8,128)} %get-tuple-element.189.value, bf16[1024,512]{1,0:T(8,128)(2,1)} %get-tuple-element.197.grad_out, ...), custom_call_target="tpu_custom_call" | custom-call | flops 400000000 | bytes 146800 | tf_op jit(solution)/shard_map/backward/pallas_call | solution.py:809
  150.6 4.0 %collective-permute-done.11 = bf16[512,1024]{1,0:T(8,128)(2,1)} collective-permute-done((bf16[512,1024]{1,0:T(8,128)(2,1)}, bf16[512,1024]{1,0:T(8,128)(2,1)}, u32[]{:S(2)}, u32[]{:S(2)}) %collective-permute-start.11) | collective-permute-done | bytes 1048608 | tf_op jit(solution)/shard_map/ppermute | solution.py:541
  156.0 2.0 add_convert_fusion.8
  158.1 1.6 collective-permute-start.14
  161.1 2.7 collective-permute-start.13
  163.8 5.9 %weights.4 = (bf16[1024,512]{1,0:T(8,128)(2,1)}, bf16[1024,512]{1,0:T(8,128)(2,1)}) custom-call(s32[1]{0:T(128)} %bitcast.1.place, bf16[1024,2048]{1,0:T(8,128)(2,1)} %get-tuple-element.254.left_send.left_own, bf16[1024,2048]{1,0:T(8,128)(2,1)} %get-tuple-element.254.left_send.left_own, bf16[1024,512]{1,0:T(8,128)(2,1)} %get-tuple-element.213.refs_0_.refs_2_), custom_call_target="tpu_custom_call" | custom-call | flops 42949672 | bytes 146800 | tf_op jit(solution)/shard_map/weights/pallas_call | solution.py:789
  169.7 17.3 %backward.3 = (bf16[1024,512]{1,0:T(8,128)(2,1)}, f32[8,512]{1,0:T(8,128)}, f32[1,512]{1,0:T(1,128)}, f32[1024,128]{1,0:T(8,128)}, f32[1024,128]{1,0:T(8,128)}, /*index=5*/f32[1024,256]{1,0:T(8,128)}) custom-call(f32[1024,1024]{1,0:T(8,128)} %get-tuple-element.189.value, bf16[1024,512]{1,0:T(8,128)(2,1)} %get-tuple-element.215.grad_out, ...), custom_call_target="tpu_custom_call" | custom-call | flops 400000000 | bytes 146800 | tf_op jit(solution)/shard_map/backward/pallas_call | solution.py:809
  189.5 6.1 %weights.5 = (bf16[1024,512]{1,0:T(8,128)(2,1)}, bf16[1024,512]{1,0:T(8,128)(2,1)}) custom-call(s32[1]{0:T(128)} %bitcast.1.place, bf16[1024,2048]{1,0:T(8,128)(2,1)} %get-tuple-element.254.left_send.left_own, bf16[1024,2048]{1,0:T(8,128)(2,1)} %get-tuple-element.254.left_send.left_own, bf16[1024,512]{1,0:T(8,128)(2,1)} %get-tuple-element.219.refs_0_.refs_3_), custom_call_target="tpu_custom_call" | custom-call | flops 42949672 | bytes 146800 | tf_op jit(solution)/shard_map/weights/pallas_call | solution.py:789
  195.6 8.0 %finish.1 = (bf16[1024,256]{1,0:T(8,128)(2,1)}, bf16[1024,128]{1,0:T(8,128)(2,1)}, f32[8,256]{1,0:T(8,128)}, f32[8,128]{1,0:T(8,128)}) custom-call(f32[1024,128]{1,0:T(8,128)} %get-tuple-element.221.refs_0_, f32[1024,128]{1,0:T(8,128)} %get-tuple-element.222.refs_1_, f32[1024,256]{1,0:T(8,128)} %get-tuple-element.223.refs_2_, ...), custom_call_target="tpu_custom_call" | custom-call | flops 80000000 | bytes 186286 | tf_op jit(solution)/shard_map/finish/pallas_call | solution.py:908
  204.3 1.6 add_convert_fusion.1
  209.0 17.3 %normed_grad.1 = (bf16[2,1024,512]{2,1,0:T(8,128)(2,1)}, bf16[2,1024,512]{2,1,0:T(8,128)(2,1)}) custom-call(s32[1]{0:T(128)} %bitcast.rank, bf16[1024,512]{1,0:T(8,128)(2,1)} %get-tuple-element.234.refs_0_, bf16[1024,512]{1,0:T(8,128)(2,1)} %get-tuple-element.187.refs_1_, bf16[1024,512]{1,0:T(8,128)(2,1)} %get-tuple-element.213.refs_0_.refs_2_, ...), custom_call_target="tpu_custom_call" | custom-call | flops 204010944 | bytes 335544 | tf_op jit(solution)/shard_map/normed_grad/pallas_call | solution.py:858
  226.4 2.7 collective-permute-done.21
  235.6 2.5 add_convert_fusion.6
  238.2 2.5 collective-permute-start.28
  240.7 1.5 fusion.11
  243.1 4.5 %collective-permute-done.24 = bf16[1024,256]{1,0:T(8,128)(2,1)S(1)} collective-permute-done((bf16[1024,256]{1,0:T(8,128)(2,1)S(1)}, bf16[1024,256]{1,0:T(8,128)(2,1)S(1)}, u32[]{:S(2)}, u32[]{:S(2)}) %collective-permute-start.24) | collective-permute-done | bytes 524320 | tf_op jit(solution)/shard_map/ppermute | solution.py:541
  249.8 6.1 %collective-permute-done.26 = bf16[1024,512]{1,0:T(8,128)(2,1)S(1)} collective-permute-done((bf16[1024,512]{1,0:T(8,128)(2,1)}, bf16[1024,512]{1,0:T(8,128)(2,1)S(1)}, u32[]{:S(2)}, u32[]{:S(2)}) %collective-permute-start.26) | collective-permute-done | bytes 1048608 | tf_op jit(solution)/shard_map/ppermute | solution.py:541
  255.9 2.6 collective-permute-done.25
  258.5 2.1 add_convert_fusion.12
  265.3 1.5 collective-permute-start.29
  267.5 2.3 convert_add_fusion.3
  270.5 2.8 fusion
  273.9 2.2 convert_add_fusion.4
  278.5 2.5 collective-permute-done.27
  281.0 2.0 add_convert_fusion.11
  283.3 4.1 %collective-permute-start.36 = (bf16[256,512]{1,0:T(8,128)(2,1)}, bf16[256,512]{1,0:T(8,128)(2,1)}, u32[]{:S(2)}, u32[]{:S(2)}) collective-permute-start(bf16[256,512]{1,0:T(8,128)(2,1)} %add_convert_fusion.11), channel_id=1, source_target_pairs={{0,16},{4,20},{8,24},{12,28},{16,0},{20,4},{24,8},{28,12},{1,17},{... | collective-permute-start | bytes 786440 | tf_op jit(solution)/shard_map/ppermute | solution.py:541
  287.4 2.7 fusion.8
  290.9 1.9 add_bitcast_fusion
  295.3 1.8 fusion.22
  297.9 2.2 collective-permute-done.34
  300.6 2.3 fusion.4
  302.9 2.9 collective-permute-done.38
  314.7 2.9 copy.66
  (253 shorter events, 58.6 us)
Async XLA Ops:
  0.6 26.5 %collective-permute-start.1 = (bf16[1024,512]{1,0:T(8,128)(2,1)}, bf16[1024,512]{1,0:T(8,128)(2,1)}, u32[]{:S(2)}, u32[]{:S(2)}) collective-permute-start(bf16[1024,512]{1,0:T(8,128)(2,1)} %refs_0_.4), channel_id=1, source_target_pairs={{0,2},{1,3},{2,0},{3,1},{4,6},{5,7},{6,4},{7,5},{8,10},{9,11},{10,... | collective-permute-start | bytes 3145736 | tf_op jit(solution)/shard_map/ppermute | solution.py:541
  3.7 27.9 %collective-permute-start.3 = (bf16[1024,512]{1,0:T(8,128)(2,1)}, bf16[1024,512]{1,0:T(8,128)(2,1)}, u32[]{:S(2)}, u32[]{:S(2)}) collective-permute-start(bf16[1024,512]{1,0:T(8,128)(2,1)} %refs_0_.4), channel_id=1, source_target_pairs={{0,1},{1,0},{2,3},{3,2},{4,5},{5,4},{6,7},{7,6},{8,9},{9,8},{10,11... | collective-permute-start | bytes 3145736 | tf_op jit(solution)/shard_map/ppermute | solution.py:541
  17.5 12.2 %copy-start.45 = (f32[5,256]{1,0:T(8,128)S(1)}, f32[5,256]{1,0:T(8,128)}, u32[]{:S(2)}) copy-start(f32[5,256]{1,0:T(8,128)} %param.22) | copy-start | bytes 15364
  17.5 12.8 %copy-start.53 = (f32[16]{0:T(128)S(1)}, f32[16]{0:T(128)}, u32[]{:S(2)}) copy-start(f32[16]{0:T(128)} %param.24) | copy-start | bytes 196
  17.5 13.4 %copy-start.51 = (f32[16]{0:T(128)S(1)}, f32[16]{0:T(128)}, u32[]{:S(2)}) copy-start(f32[16]{0:T(128)} %param.23) | copy-start | bytes 196
  27.8 3.8 %collective-permute-start.4 = (bf16[1024,512]{1,0:T(8,128)(2,1)}, bf16[1024,512]{1,0:T(8,128)(2,1)}, u32[]{:S(2)}, u32[]{:S(2)}) collective-permute-start(bf16[1024,512]{1,0:T(8,128)(2,1)} %collective-permute-done.1.refs_2_), channel_id=1, source_target_pairs={{0,1},{1,0},{2,3},{3,2},{4,5},{5,4},{6,7},{7,6},{8,9},{9,8},{10,11... | collective-permute-start | bytes 3145736 | tf_op jit(solution)/shard_map/ppermute | solution.py:541
  27.8 39.8 %collective-permute-start.2 = (bf16[1024,512]{1,0:T(8,128)(2,1)S(1)}, bf16[1024,512]{1,0:T(8,128)(2,1)S(1)}, u32[]{:S(2)}, u32[]{:S(2)}) collective-permute-start(bf16[1024,512]{1,0:T(8,128)(2,1)S(1)} %copy-done.3), channel_id=1, source_target_pairs={{0,2},{1,3},{2,0},{3,1},{4,6},{5,7},{6,4},{7,5},{8,10},{9,11},{10,... | collective-permute-start | bytes 3145736 | tf_op jit(solution)/shard_map/ppermute | solution.py:541
  29.5 38.4 %collective-permute-start = (bf16[1024,512]{1,0:T(8,128)(2,1)S(1)}, bf16[1024,512]{1,0:T(8,128)(2,1)S(1)}, u32[]{:S(2)}, u32[]{:S(2)}) collective-permute-start(bf16[1024,512]{1,0:T(8,128)(2,1)S(1)} %copy-done.3), channel_id=1, source_target_pairs={{0,1},{1,0},{2,3},{3,2},{4,5},{5,4},{6,7},{7,6},{8,9},{9,8},{10,11... | collective-permute-start | bytes 3145736 | tf_op jit(solution)/shard_map/ppermute | solution.py:541
  67.6 2.7 collective-permute-start.5
  83.1 1.5 collective-permute-start.6
  85.3 3.9 %collective-permute-start.7 = (f32[8,1024]{1,0:T(8,128)S(1)}, f32[8,1024]{1,0:T(8,128)S(1)}, u32[]{:S(2)}, u32[]{:S(2)}) collective-permute-start(f32[8,1024]{1,0:T(8,128)S(1)} %add.349), channel_id=1, source_target_pairs={{0,2},{1,3},{2,0},{3,1},{4,6},{5,7},{6,4},{7,5},{8,10},{9,11},{10,... | collective-permute-start | bytes 98312 | tf_op jit(solution)/shard_map/ppermute | solution.py:541
  99.4 28.0 %collective-permute-start.8 = (bf16[512,1024]{1,0:T(8,128)(2,1)}, bf16[512,1024]{1,0:T(8,128)(2,1)S(1)}, u32[]{:S(2)}, u32[]{:S(2)}) collective-permute-start(bf16[512,1024]{1,0:T(8,128)(2,1)} %get-tuple-element.194), channel_id=1, source_target_pairs={{0,4},{4,0},{8,12},{12,8},{16,20},{20,16},{24,28},{28,24},{1,5},{5... | collective-permute-start | bytes 3145736 | tf_op jit(solution)/shard_map/ppermute | solution.py:541
  128.4 26.3 %collective-permute-start.9 = (bf16[2,1024,512]{2,1,0:T(8,128)(2,1)}, bf16[2,1024,512]{2,1,0:T(8,128)(2,1)S(1)}, u32[]{:S(2)}, u32[]{:S(2)}) collective-permute-start(bf16[2,1024,512]{2,1,0:T(8,128)(2,1)} %get-tuple-element.196), channel_id=1, source_target_pairs={{0,1},{1,0},{2,3},{3,2},{4,5},{5,4},{6,7},{7,6},{8,9},{9,8},{10,11... | collective-permute-start | bytes 6291464 | tf_op jit(solution)/shard_map/ppermute | solution.py:541
  128.4 26.3 %collective-permute-start.11 = (bf16[512,1024]{1,0:T(8,128)(2,1)}, bf16[512,1024]{1,0:T(8,128)(2,1)}, u32[]{:S(2)}, u32[]{:S(2)}) collective-permute-start(bf16[512,1024]{1,0:T(8,128)(2,1)} %get-tuple-element.207), channel_id=1, source_target_pairs={{0,4},{4,0},{8,12},{12,8},{16,20},{20,16},{24,28},{28,24},{1,5},{5... | collective-permute-start | bytes 3145736 | tf_op jit(solution)/shard_map/ppermute | solution.py:541
  130.2 24.5 %collective-permute-start.10 = (bf16[512,512]{1,0:T(8,128)(2,1)S(1)}, bf16[512,512]{1,0:T(8,128)(2,1)S(1)}, u32[]{:S(2)}, u32[]{:S(2)}) collective-permute-start(bf16[512,512]{1,0:T(8,128)(2,1)S(1)} %add_convert_fusion.9), channel_id=1, source_target_pairs={{0,8},{4,12},{8,0},{12,4},{16,24},{20,28},{24,16},{28,20},{1,9},{5... | collective-permute-start | bytes 1572872 | tf_op jit(solution)/shard_map/ppermute | solution.py:541
  131.8 71.8 %collective-permute-start.15 = (bf16[1024,1024]{1,0:T(8,128)(2,1)}, bf16[1024,1024]{1,0:T(8,128)(2,1)}, u32[]{:S(2)}, u32[]{:S(2)}) collective-permute-start(bf16[1024,1024]{1,0:T(8,128)(2,1)} %get-tuple-element.230), channel_id=1, source_target_pairs={{0,4},{4,0},{8,12},{12,8},{16,20},{20,16},{24,28},{28,24},{1,5},{5... | collective-permute-start | bytes 6291464 | tf_op jit(solution)/shard_map/ppermute | solution.py:541
  133.3 21.4 %copy-start.13 = (bf16[2,1024,512]{2,1,0:T(8,128)(2,1)S(1)}, bf16[2,1024,512]{2,1,0:T(8,128)(2,1)}, u32[]{:S(2)}) copy-start(bf16[2,1024,512]{2,1,0:T(8,128)(2,1)} %get-tuple-element.211) | copy-start | bytes 6291460
  155.0 32.0 %collective-permute-start.12 = (bf16[1024,512]{1,0:T(8,128)(2,1)S(1)}, bf16[1024,512]{1,0:T(8,128)(2,1)}, u32[]{:S(2)}, u32[]{:S(2)}) collective-permute-start(bf16[1024,512]{1,0:T(8,128)(2,1)S(1)} %fusion.10), channel_id=1, source_target_pairs={{0,2},{1,3},{2,0},{3,1},{4,6},{5,7},{6,4},{7,5},{8,10},{9,11},{10,... | collective-permute-start | bytes 3145736 | tf_op jit(solution)/shard_map/ppermute | solution.py:541
  158.1 29.0 %collective-permute-start.14 = (bf16[512,512]{1,0:T(8,128)(2,1)}, bf16[512,512]{1,0:T(8,128)(2,1)}, u32[]{:S(2)}, u32[]{:S(2)}) collective-permute-start(bf16[512,512]{1,0:T(8,128)(2,1)} %add_convert_fusion.8), channel_id=1, source_target_pairs={{0,8},{4,12},{8,0},{12,4},{16,24},{20,28},{24,16},{28,20},{1,9},{5... | collective-permute-start | bytes 1572872 | tf_op jit(solution)/shard_map/ppermute | solution.py:541
  161.1 25.9 %collective-permute-start.13 = (bf16[512,256]{1,0:T(8,128)(2,1)S(1)}, bf16[512,256]{1,0:T(8,128)(2,1)S(1)}, u32[]{:S(2)}, u32[]{:S(2)}) collective-permute-start(bf16[512,256]{1,0:T(8,128)(2,1)S(1)} %add_convert_fusion.14), channel_id=1, source_target_pairs={{0,16},{4,20},{8,24},{12,28},{16,0},{20,4},{24,8},{28,12},{1,17},{... | collective-permute-start | bytes 786440 | tf_op jit(solution)/shard_map/ppermute | solution.py:541
  169.7 19.2 %copy-start.52 = (bf16[1024,512]{1,0:T(8,128)(2,1)S(1)}, bf16[1024,512]{1,0:T(8,128)(2,1)}, u32[]{:S(2)}) copy-start(bf16[1024,512]{1,0:T(8,128)(2,1)} %get-tuple-element.238) | copy-start | bytes 3145732
  188.5 15.0 %collective-permute-start.16 = (bf16[512,256]{1,0:T(8,128)(2,1)S(1)}, bf16[512,256]{1,0:T(8,128)(2,1)S(1)}, u32[]{:S(2)}, u32[]{:S(2)}) collective-permute-start(bf16[512,256]{1,0:T(8,128)(2,1)S(1)} %add_convert_fusion.13), channel_id=1, source_target_pairs={{0,16},{4,20},{8,24},{12,28},{16,0},{20,4},{24,8},{28,12},{1,17},{... | collective-permute-start | bytes 786440 | tf_op jit(solution)/shard_map/ppermute | solution.py:541
  188.9 37.4 %collective-permute-start.20 = (bf16[1024,512]{1,0:T(8,128)(2,1)S(1)}, bf16[1024,512]{1,0:T(8,128)(2,1)S(1)}, u32[]{:S(2)}, u32[]{:S(2)}) collective-permute-start(bf16[1024,512]{1,0:T(8,128)(2,1)S(1)} %copy-done.52), channel_id=1, source_target_pairs={{0,4},{4,0},{8,12},{12,8},{16,20},{20,16},{24,28},{28,24},{1,5},{5... | collective-permute-start | bytes 3145736 | tf_op jit(solution)/shard_map/ppermute | solution.py:541
  205.9 23.2 %collective-permute-start.21 = (bf16[512,1024]{1,0:T(8,128)(2,1)S(1)}, bf16[512,1024]{1,0:T(8,128)(2,1)S(1)}, u32[]{:S(2)}, u32[]{:S(2)}) collective-permute-start(bf16[512,1024]{1,0:T(8,128)(2,1)S(1)} %add_convert_fusion.1), channel_id=1, source_target_pairs={{0,8},{4,12},{8,0},{12,4},{16,24},{20,28},{24,16},{28,20},{1,9},{5... | collective-permute-start | bytes 3145736 | tf_op jit(solution)/shard_map/ppermute | solution.py:541
  206.3 20.0 %collective-permute-start.18 = (bf16[1024,256]{1,0:T(8,128)(2,1)}, bf16[1024,256]{1,0:T(8,128)(2,1)S(1)}, u32[]{:S(2)}, u32[]{:S(2)}) collective-permute-start(bf16[1024,256]{1,0:T(8,128)(2,1)} %get-tuple-element.232.refs_4_), channel_id=1, source_target_pairs={{0,1},{1,0},{2,3},{3,2},{4,5},{5,4},{6,7},{7,6},{8,9},{9,8},{10,11... | collective-permute-start | bytes 1572872 | tf_op jit(solution)/shard_map/ppermute | solution.py:541
  206.3 1.5 collective-permute-start.17
  207.9 18.5 %collective-permute-start.19 = (f32[5,256]{1,0:T(8,128)S(1)}, f32[5,256]{1,0:T(8,128)S(1)}, u32[]{:S(2)}, u32[]{:S(2)}) collective-permute-start(f32[5,256]{1,0:T(8,128)S(1)} %add.362), channel_id=1, source_target_pairs={{0,2},{1,3},{2,0},{3,1},{4,6},{5,7},{6,4},{7,5},{8,10},{9,11},{10,... | collective-permute-start | bytes 15368 | tf_op jit(solution)/shard_map/ppermute | solution.py:541
  209.0 25.0 %copy-start.22 = (bf16[1024,512]{1,0:T(8,128)(2,1)S(1)}, bf16[1024,512]{1,0:T(8,128)(2,1)}, u32[]{:S(2)}) copy-start(bf16[1024,512]{1,0:T(8,128)(2,1)} %get-tuple-element.214) | copy-start | bytes 3145732
  230.1 10.6 %collective-permute-start.22 = (bf16[2,1024,512]{2,1,0:T(8,128)(2,1)}, bf16[2,1024,512]{2,1,0:T(8,128)(2,1)S(1)}, u32[]{:S(2)}, u32[]{:S(2)}) collective-permute-start(bf16[2,1024,512]{2,1,0:T(8,128)(2,1)} %get-tuple-element.240), channel_id=1, source_target_pairs={{0,1},{1,0},{2,3},{3,2},{4,5},{5,4},{6,7},{7,6},{8,9},{9,8},{10,11... | collective-permute-start | bytes 6291464 | tf_op jit(solution)/shard_map/ppermute | solution.py:541
  230.1 25.8 %collective-permute-start.26 = (bf16[1024,512]{1,0:T(8,128)(2,1)}, bf16[1024,512]{1,0:T(8,128)(2,1)S(1)}, u32[]{:S(2)}, u32[]{:S(2)}) collective-permute-start(bf16[1024,512]{1,0:T(8,128)(2,1)} %get-tuple-element.265), channel_id=1, source_target_pairs={{0,4},{4,0},{8,12},{12,8},{16,20},{20,16},{24,28},{28,24},{1,5},{5... | collective-permute-start | bytes 3145736 | tf_op jit(solution)/shard_map/ppermute | solution.py:541
  232.8 14.8 %collective-permute-start.24 = (bf16[1024,256]{1,0:T(8,128)(2,1)S(1)}, bf16[1024,256]{1,0:T(8,128)(2,1)S(1)}, u32[]{:S(2)}, u32[]{:S(2)}) collective-permute-start(bf16[1024,256]{1,0:T(8,128)(2,1)S(1)} %add_convert_fusion.5), channel_id=1, source_target_pairs={{0,2},{1,3},{2,0},{3,1},{4,6},{5,7},{6,4},{7,5},{8,10},{9,11},{10,... | collective-permute-start | bytes 1572872 | tf_op jit(solution)/shard_map/ppermute | solution.py:541
  235.1 23.4 %collective-permute-start.25 = (bf16[512,512]{1,0:T(8,128)(2,1)S(1)}, bf16[512,512]{1,0:T(8,128)(2,1)S(1)}, u32[]{:S(2)}, u32[]{:S(2)}) collective-permute-start(bf16[512,512]{1,0:T(8,128)(2,1)S(1)} %add_convert_fusion.7), channel_id=1, source_target_pairs={{0,8},{4,12},{8,0},{12,4},{16,24},{20,28},{24,16},{28,20},{1,9},{5... | collective-permute-start | bytes 1572872 | tf_op jit(solution)/shard_map/ppermute | solution.py:541
  235.6 12.0 %copy-start = (bf16[1024,2048]{1,0:T(8,128)(2,1)S(1)}, bf16[1024,2048]{1,0:T(8,128)(2,1)}, u32[]{:S(2)}) copy-start(bf16[1024,2048]{1,0:T(8,128)(2,1)} %get-tuple-element.254.left_send.left_own) | copy-start | bytes 12582916
  238.2 40.3 %collective-permute-start.28 = (bf16[256,1024]{1,0:T(8,128)(2,1)}, bf16[256,1024]{1,0:T(8,128)(2,1)}, u32[]{:S(2)}, u32[]{:S(2)}) collective-permute-start(bf16[256,1024]{1,0:T(8,128)(2,1)} %add_convert_fusion.6), channel_id=1, source_target_pairs={{0,16},{4,20},{8,24},{12,28},{16,0},{20,4},{24,8},{28,12},{1,17},{... | collective-permute-start | bytes 1572872 | tf_op jit(solution)/shard_map/ppermute | solution.py:541
  242.2 38.8 %collective-permute-start.23 = (bf16[1024,512]{1,0:T(8,128)(2,1)}, bf16[1024,512]{1,0:T(8,128)(2,1)S(1)}, u32[]{:S(2)}, u32[]{:S(2)}) collective-permute-start(bf16[1024,512]{1,0:T(8,128)(2,1)} %fusion.11), channel_id=1, source_target_pairs={{0,2},{1,3},{2,0},{3,1},{4,6},{5,7},{6,4},{7,5},{8,10},{9,11},{10,... | collective-permute-start | bytes 3145736 | tf_op jit(solution)/shard_map/ppermute | solution.py:541
  261.5 19.5 %collective-permute-start.27 = (bf16[512,512]{1,0:T(8,128)(2,1)}, bf16[512,512]{1,0:T(8,128)(2,1)}, u32[]{:S(2)}, u32[]{:S(2)}) collective-permute-start(bf16[512,512]{1,0:T(8,128)(2,1)} %add_convert_fusion.3), channel_id=1, source_target_pairs={{0,8},{4,12},{8,0},{12,4},{16,24},{20,28},{24,16},{28,20},{1,9},{5... | collective-permute-start | bytes 1572872 | tf_op jit(solution)/shard_map/ppermute | solution.py:541
  261.5 47.4 %collective-permute-start.35 = (bf16[256,512]{1,0:T(8,128)(2,1)}, bf16[256,512]{1,0:T(8,128)(2,1)}, u32[]{:S(2)}, u32[]{:S(2)}) collective-permute-start(bf16[256,512]{1,0:T(8,128)(2,1)} %add_convert_fusion.12), channel_id=1, source_target_pairs={{0,16},{4,20},{8,24},{12,28},{16,0},{20,4},{24,8},{28,12},{1,17},{... | collective-permute-start | bytes 786440 | tf_op jit(solution)/shard_map/ppermute | solution.py:541
  265.3 13.2 %collective-permute-start.29 = (bf16[4,20480]{1,0:T(4,128)(2,1)}, bf16[4,20480]{1,0:T(4,128)(2,1)S(1)}, u32[]{:S(2)}, u32[]{:S(2)}) collective-permute-start(bf16[4,20480]{1,0:T(4,128)(2,1)} %bitcast.81), channel_id=1, source_target_pairs={{0,4},{4,0},{8,12},{12,8},{16,20},{20,16},{24,28},{28,24},{1,5},{5... | collective-permute-start | bytes 491528 | tf_op jit(solution)/shard_map/ppermute | solution.py:541
  277.9 12.3 %copy-start.40 = (f32[512]{0:T(512)}, f32[512]{0:T(512)S(1)}, u32[]{:S(2)}) copy-start(f32[512]{0:T(512)S(1)} %dynamic_slice.228) | copy-start | bytes 6148
  278.5 11.7 %copy-start.36 = (bf16[4,20480]{1,0:T(4,128)(2,1)}, bf16[4,20480]{1,0:T(4,128)(2,1)S(1)}, u32[]{:S(2)}) copy-start(bf16[4,20480]{1,0:T(4,128)(2,1)S(1)} %collective-permute-done.29) | copy-start | bytes 491524
  283.2 11.0 %collective-permute-start.32 = (bf16[2,20480]{1,0:T(2,128)(2,1)S(1)}, bf16[2,20480]{1,0:T(2,128)(2,1)S(1)}, u32[]{:S(2)}, u32[]{:S(2)}) collective-permute-start(bf16[2,20480]{1,0:T(2,128)(2,1)S(1)} %fusion.14), channel_id=1, source_target_pairs={{0,8},{4,12},{8,0},{12,4},{16,24},{20,28},{24,16},{28,20},{1,9},{5... | collective-permute-start | bytes 245768 | tf_op jit(solution)/shard_map/ppermute | solution.py:541
  283.3 25.6 %collective-permute-start.36 = (bf16[256,512]{1,0:T(8,128)(2,1)}, bf16[256,512]{1,0:T(8,128)(2,1)}, u32[]{:S(2)}, u32[]{:S(2)}) collective-permute-start(bf16[256,512]{1,0:T(8,128)(2,1)} %add_convert_fusion.11), channel_id=1, source_target_pairs={{0,16},{4,20},{8,24},{12,28},{16,0},{20,4},{24,8},{28,12},{1,17},{... | collective-permute-start | bytes 786440 | tf_op jit(solution)/shard_map/ppermute | solution.py:541
  290.2 4.0 %collective-permute-start.31 = (f32[7984]{0:T(1024)S(1)}, f32[7984]{0:T(1024)S(1)}, u32[]{:S(2)}, u32[]{:S(2)}) collective-permute-start(f32[7984]{0:T(1024)S(1)} %pad_maximum_fusion.6), channel_id=1, source_target_pairs={{0,4},{4,0},{8,12},{12,8},{16,20},{20,16},{24,28},{28,24},{1,5},{5... | collective-permute-start | bytes 95816 | tf_op jit(solution)/shard_map/ppermute | solution.py:541
  290.8 3.0 collective-permute-start.30
  294.2 6.0 %collective-permute-start.34 = (f32[7984]{0:T(1024)S(1)}, f32[7984]{0:T(1024)S(1)}, u32[]{:S(2)}, u32[]{:S(2)}) collective-permute-start(f32[7984]{0:T(1024)S(1)} %add.399), channel_id=1, source_target_pairs={{0,8},{4,12},{8,0},{12,4},{16,24},{20,28},{24,16},{28,20},{1,9},{5... | collective-permute-start | bytes 95816 | tf_op jit(solution)/shard_map/ppermute | solution.py:541
  294.3 3.6 %collective-permute-start.33 = (f32[1024]{0:T(1024)S(1)}, f32[1024]{0:T(1024)S(1)}, u32[]{:S(2)}, u32[]{:S(2)}) collective-permute-start(f32[1024]{0:T(1024)S(1)} %add.398), channel_id=1, source_target_pairs={{0,2},{1,3},{2,0},{3,1},{4,6},{5,7},{6,4},{7,5},{8,10},{9,11},{10,... | collective-permute-start | bytes 12296 | tf_op jit(solution)/shard_map/ppermute | solution.py:541
  297.1 11.8 %collective-permute-start.37 = (bf16[1,20480]{1,0:T(2,128)(2,1)}, bf16[1,20480]{1,0:T(2,128)(2,1)}, u32[]{:S(2)}, u32[]{:S(2)}) collective-permute-start(bf16[1,20480]{1,0:T(2,128)(2,1)} %fusion.22), channel_id=1, source_target_pairs={{0,16},{4,20},{8,24},{12,28},{16,0},{20,4},{24,8},{28,12},{1,17},{... | collective-permute-start | bytes 122888 | tf_op jit(solution)/shard_map/ppermute | solution.py:541
  300.1 5.7 %collective-permute-start.38 = (f32[7984]{0:T(1024)S(1)}, f32[7984]{0:T(1024)S(1)}, u32[]{:S(2)}, u32[]{:S(2)}) collective-permute-start(f32[7984]{0:T(1024)S(1)} %add.405), channel_id=1, source_target_pairs={{0,16},{4,20},{8,24},{12,28},{16,0},{20,4},{24,8},{28,12},{1,17},{... | collective-permute-start | bytes 95816 | tf_op jit(solution)/shard_map/ppermute | solution.py:541
  (45 other events, 229.2 us)

commit v7 on v6

--- a/solution.py
+++ b/solution.py
@@ -922,7 +922,7 @@
         flops=4e9,
         moved=length * 2048 * CHUNKS + length * 5000,
         name="finish",
-        vmem=56,
+        vmem=32,
     )(
         tie(cross_parts[0], *moved), folded_parts[0], maps_parts[0],
         *[part for three in zip(cross_parts[1:], folded_parts[1:], maps_parts[1:]) for part in three],

time: 323 us -> 322 us (level)
  waiting for transfers between devices: 41.7 us -> 46.4 us
  Pallas kernels: 156 us -> 152 us
    ppermute x39, waiting for transfers between devices: 41.7 us -> 46.4 us  [swap(): return lax.ppermute(array, axis, [(i, i ^ mask) for i in range(count)])]
    pallas_call x1, Pallas kernels: 7.98 us -> 4.13 us  [shards(): call(functools.partial(finish_kernel, heads, CHUNKS), (1,), [held((length...]
    unnamed x113 -> x131, local copies, waits for them, and re-layouts: 18.1 us -> 17.5 us
  transfers between devices with their start and end apart: 39 -> 39, of which waited for: 15 -> 14; matrix products, arithmetic and copies ran while one was open for 22% -> 22% of each run, Pallas kernels for 42% -> 41%
where the time goes in v7:
time: 322 us; the launch traced here: 317 us
  Pallas kernels  152 us (47%)
  other arithmetic  49.7 us (15%)
  waiting for transfers between devices  46.4 us (14%)
  starting transfers between devices  34.7 us (11%)
  local copies, waits for them, and re-layouts  29.9 us (9%)
    ppermute x39, waiting for transfers between devices, swap(): return lax.ppermute(array, axis, [(i, i ^ mask) for i in range(count)])  46.4 us
    pallas_call x1, Pallas kernels, shards(): call(functools.partial(front_kernel, parts, heads), (steps,), [held((leng...  36 us
    ppermute x39, starting transfers between devices, swap(): return lax.ppermute(array, axis, [(i, i ^ mask) for i in range(count)])  34.7 us
    pallas_call x2, Pallas kernels, backward_part(): call(functools.partial(backward_kernel, heads, c * spans), (spans,), [chu...  34.7 us
    pallas_call x3, Pallas kernels, weight_part(): call(weight_kernel, (runs,), [pl.BlockSpec((length, run), lambda j, p: (0...  20.4 us
    convert_element_type x12, other arithmetic, send(): functools.reduce(jnp.add, [term.astype(F32) for term in cut(1 - top)])  19.2 us
    pallas_call x2, Pallas kernels, gate_part(): call(functools.partial(gate_kernel, parts, run, channels * parts, stacked...  18.8 us
    unnamed x131, local copies, waits for them, and re-layouts  17.5 us
  transfers between devices with their start and end apart: 39, of which 14 were waited for; matrix products, arithmetic and copies ran while one was open for 22% of the time, Pallas kernels for 41%

profile of v7, /device:TPU:0, one launch (start us, length us, event | category | flops | bytes accessed | tf_op | source)
XLA Modules:
  0.0 316.7 jit_solution(16907464458526316047)
XLA Ops:
  0.6 3.0 collective-permute-start.1
  6.9 10.3 %copy.69 = bf16[256,8,2,1024]{3,1,2,0:T(8,128)(2,1)} copy(bf16[256,8,2,1024]{3,2,1,0:T(2,128)(2,1)} %bitcast.91) | data formatting | bytes 16777216
  21.1 6.1 %collective-permute-done.1.refs_2_ = bf16[1024,512]{1,0:T(8,128)(2,1)} collective-permute-done((bf16[1024,512]{1,0:T(8,128)(2,1)}, bf16[1024,512]{1,0:T(8,128)(2,1)}, u32[]{:S(2)}, u32[]{:S(2)}) %collective-permute-start.1) | collective-permute-done | bytes 1048608 | tf_op jit(solution)/shard_map/ppermute | solution.py:541
  27.8 1.7 collective-permute-start.2
  31.6 36.0 %front.1 = (bf16[1024,2048]{1,0:T(8,128)(2,1)}, f32[1024,256]{1,0:T(8,128)}, bf16[1024,256]{1,0:T(8,128)(2,1)}, bf16[256,1024]{1,0:T(8,128)(2,1)}, f32[1024,128]...) custom-call(s32[1]{0:T(128)} %bitcast.rank, ...), custom_call_target="tpu_custom_call" | custom-call | flops 343597376 | bytes 629145 | tf_op jit(solution)/shard_map/front/pallas_call | solution.py:687
  68.0 2.4 collective-permute-done.5.refs_3_
  71.3 11.8 %cotangent.1 = (bf16[1024,1024]{1,0:T(8,128)(2,1)}, f32[8,1024]{1,0:T(8,128)}) custom-call(s32[1]{0:T(128)} %bitcast.rank, bf16[1024,512]{1,0:T(8,128)(2,1)} %refs_0_.7, bf16[1024,512]{1,0:T(8,128)(2,1)} %copy-done.21, bf16[1024,512]{1,0:T(8,128)(2,1)} %copy-done.20, bf16[1024,512]{1,0:T(8,128)(2,1)} %copy-done.22, bf16[1024,2048]{1,0:T(8,128)(2,1)} %w_out.1, ...), custom_call_target="tpu_custom_call" | custom-call | flops 85899344 | bytes 419430 | tf_op jit(solution)/shard_map/cotangent/pallas_call | solution.py:731
  86.3 3.0 collective-permute-done.7
  89.9 9.5 %gate.2 = (bf16[1024,512]{1,0:T(8,128)(2,1)}, bf16[1024,512]{1,0:T(8,128)(2,1)}, bf16[1024,512]{1,0:T(8,128)(2,1)}, f32[1,512]{1,0:T(1,128)}, bf16[512,1024]{1,0:T(8,128)(2,1)}, /*index=5*/bf16[512,1024]{1,0:T(8,128)(2,1)}) custom-call(s32[1]{0:T(128)} %bitcast.1.place, s32[1]{0:T(128)} %bitcast.rank, bf16[1024,512]{1,0:T(8,128)(2,1)} %refs_0_.7, ...), custom_call_target="tpu_custom_call" | custom-call | flops 42949672 | bytes 314572 | tf_op jit(solution)/shard_map/gate/pallas_call | solution.py:761
  99.4 1.6 collective-permute-start.8
  101.0 9.3 %gate.3 = (bf16[1024,512]{1,0:T(8,128)(2,1)}, bf16[1024,512]{1,0:T(8,128)(2,1)}, bf16[1024,512]{1,0:T(8,128)(2,1)}, f32[1,512]{1,0:T(1,128)}, bf16[512,1024]{1,0:T(8,128)(2,1)}, /*index=5*/bf16[512,1024]{1,0:T(8,128)(2,1)}) custom-call(s32[1]{0:T(128)} %bitcast.1.place, s32[1]{0:T(128)} %bitcast.rank, bf16[1024,512]{1,0:T(8,128)(2,1)} %refs_0_.7, ...), custom_call_target="tpu_custom_call" | custom-call | flops 42949672 | bytes 314572 | tf_op jit(solution)/shard_map/gate/pallas_call | solution.py:761
  110.3 8.0 %weights.3 = (bf16[1024,1024]{1,0:T(8,128)(2,1)}, bf16[1024,1024]{1,0:T(8,128)(2,1)}) custom-call(s32[1]{0:T(128)} %bitcast.1.place, bf16[1024,2048]{1,0:T(8,128)(2,1)} %get-tuple-element.254.left_send.left_own, bf16[1024,2048]{1,0:T(8,128)(2,1)} %get-tuple-element.254.left_send.left_own, bf16[1024,512]{1,0:T(8,128)(2,1)} %get-tuple-element.234.refs_0_, ...), custom_call_target="tpu_custom_call" | custom-call | flops 85899344 | bytes 209715 | tf_op jit(solution)/shard_map/weights/pallas_call | solution.py:789
  118.3 9.1 %output.1 = (bf16[2,1024,512]{2,1,0:T(8,128)(2,1)}, bf16[2,1024,512]{2,1,0:T(8,128)(2,1)}) custom-call(s32[1]{0:T(128)} %bitcast.rank, bf16[1024,1024]{1,0:T(8,128)(2,1)} %get-tuple-element.191.refs_5_.gated, bf16[1024,2048]{1,0:T(8,128)(2,1)} %w_out.1), custom_call_target="tpu_custom_call" | custom-call | flops 85899344 | bytes 209715 | tf_op jit(solution)/shard_map/output/pallas_call | solution.py:845
  130.1 1.6 collective-permute-start.10
  131.7 1.5 collective-permute-start.15
  133.2 17.3 %backward.2 = (bf16[1024,512]{1,0:T(8,128)(2,1)}, f32[8,512]{1,0:T(8,128)}, f32[1,512]{1,0:T(1,128)}, f32[1024,128]{1,0:T(8,128)}, f32[1024,128]{1,0:T(8,128)}, /*index=5*/f32[1024,256]{1,0:T(8,128)}) custom-call(f32[1024,1024]{1,0:T(8,128)} %get-tuple-element.189.value, bf16[1024,512]{1,0:T(8,128)(2,1)} %get-tuple-element.197.grad_out, ...), custom_call_target="tpu_custom_call" | custom-call | flops 400000000 | bytes 146800 | tf_op jit(solution)/shard_map/backward/pallas_call | solution.py:809
  150.6 4.1 %collective-permute-done.11 = bf16[512,1024]{1,0:T(8,128)(2,1)} collective-permute-done((bf16[512,1024]{1,0:T(8,128)(2,1)}, bf16[512,1024]{1,0:T(8,128)(2,1)}, u32[]{:S(2)}, u32[]{:S(2)}) %collective-permute-start.11) | collective-permute-done | bytes 1048608 | tf_op jit(solution)/shard_map/ppermute | solution.py:541
  156.0 2.0 add_convert_fusion.8
  158.0 1.6 collective-permute-start.14
  159.6 1.5 add_convert_fusion.14
  161.0 2.7 collective-permute-start.13
  163.7 5.9 %weights.4 = (bf16[1024,512]{1,0:T(8,128)(2,1)}, bf16[1024,512]{1,0:T(8,128)(2,1)}) custom-call(s32[1]{0:T(128)} %bitcast.1.place, bf16[1024,2048]{1,0:T(8,128)(2,1)} %get-tuple-element.254.left_send.left_own, bf16[1024,2048]{1,0:T(8,128)(2,1)} %get-tuple-element.254.left_send.left_own, bf16[1024,512]{1,0:T(8,128)(2,1)} %get-tuple-element.213.refs_0_.refs_2_), custom_call_target="tpu_custom_call" | custom-call | flops 42949672 | bytes 146800 | tf_op jit(solution)/shard_map/weights/pallas_call | solution.py:789
  169.6 17.4 %backward.3 = (bf16[1024,512]{1,0:T(8,128)(2,1)}, f32[8,512]{1,0:T(8,128)}, f32[1,512]{1,0:T(1,128)}, f32[1024,128]{1,0:T(8,128)}, f32[1024,128]{1,0:T(8,128)}, /*index=5*/f32[1024,256]{1,0:T(8,128)}) custom-call(f32[1024,1024]{1,0:T(8,128)} %get-tuple-element.189.value, bf16[1024,512]{1,0:T(8,128)(2,1)} %get-tuple-element.215.grad_out, ...), custom_call_target="tpu_custom_call" | custom-call | flops 400000000 | bytes 146800 | tf_op jit(solution)/shard_map/backward/pallas_call | solution.py:809
  187.0 1.6 add_convert_fusion.13
  189.7 6.4 %weights.5 = (bf16[1024,512]{1,0:T(8,128)(2,1)}, bf16[1024,512]{1,0:T(8,128)(2,1)}) custom-call(s32[1]{0:T(128)} %bitcast.1.place, bf16[1024,2048]{1,0:T(8,128)(2,1)} %get-tuple-element.254.left_send.left_own, bf16[1024,2048]{1,0:T(8,128)(2,1)} %get-tuple-element.254.left_send.left_own, bf16[1024,512]{1,0:T(8,128)(2,1)} %get-tuple-element.219.refs_0_.refs_3_), custom_call_target="tpu_custom_call" | custom-call | flops 42949672 | bytes 146800 | tf_op jit(solution)/shard_map/weights/pallas_call | solution.py:789
  196.3 4.1 %finish.1 = (bf16[1024,256]{1,0:T(8,128)(2,1)S(1)}, bf16[1024,128]{1,0:T(8,128)(2,1)S(1)}, f32[8,256]{1,0:T(8,128)S(1)}, f32[8,128]{1,0:T(8,128)S(1)}) custom-call(f32[1024,128]{1,0:T(8,128)S(1)} %copy-done.9, f32[1024,128]{1,0:T(8,128)S(1)} %copy-done.10, f32[1024,256]{1,0:T(8,128)S(1)} %copy-done.7, f32[1024,128]{1,0:T(8,128)S(1)} %copy-done.11, ...), custom_call_target="tpu_custom_call" | custom-call | flops 80000000 | bytes 186286 | tf_op jit(solution)/shard_map/finish/pallas_call | solution.py:908
  201.7 1.7 add_convert_fusion.1
  206.6 17.3 %normed_grad.1 = (bf16[2,1024,512]{2,1,0:T(8,128)(2,1)}, bf16[2,1024,512]{2,1,0:T(8,128)(2,1)}) custom-call(s32[1]{0:T(128)} %bitcast.rank, bf16[1024,512]{1,0:T(8,128)(2,1)} %get-tuple-element.234.refs_0_, bf16[1024,512]{1,0:T(8,128)(2,1)} %get-tuple-element.187.refs_1_, bf16[1024,512]{1,0:T(8,128)(2,1)} %get-tuple-element.213.refs_0_.refs_2_, ...), custom_call_target="tpu_custom_call" | custom-call | flops 204010944 | bytes 335544 | tf_op jit(solution)/shard_map/normed_grad/pallas_call | solution.py:858
  223.9 4.7 %collective-permute-done.21 = bf16[512,1024]{1,0:T(8,128)(2,1)S(1)} collective-permute-done((bf16[512,1024]{1,0:T(8,128)(2,1)S(1)}, bf16[512,1024]{1,0:T(8,128)(2,1)S(1)}, u32[]{:S(2)}, u32[]{:S(2)}) %collective-permute-start.21) | collective-permute-done | bytes 1048608 | tf_op jit(solution)/shard_map/ppermute | solution.py:541
  234.3 2.5 add_convert_fusion.6
  237.8 1.5 fusion.11
  240.4 5.9 %collective-permute-done.24 = bf16[1024,256]{1,0:T(8,128)(2,1)S(1)} collective-permute-done((bf16[1024,256]{1,0:T(8,128)(2,1)S(1)}, bf16[1024,256]{1,0:T(8,128)(2,1)S(1)}, u32[]{:S(2)}, u32[]{:S(2)}) %collective-permute-start.24) | collective-permute-done | bytes 524320 | tf_op jit(solution)/shard_map/ppermute | solution.py:541
  248.5 6.9 %collective-permute-done.26 = bf16[1024,512]{1,0:T(8,128)(2,1)S(1)} collective-permute-done((bf16[1024,512]{1,0:T(8,128)(2,1)}, bf16[1024,512]{1,0:T(8,128)(2,1)S(1)}, u32[]{:S(2)}, u32[]{:S(2)}) %collective-permute-start.26) | collective-permute-done | bytes 1048608 | tf_op jit(solution)/shard_map/ppermute | solution.py:541
  255.6 2.2 add_convert_fusion.12
  263.4 1.7 collective-permute-start.29
  265.1 1.5 convert_add_fusion.3
  267.9 2.9 fusion
  270.8 1.4 convert_add_fusion.4
  273.9 5.8 %collective-permute-done.27 = bf16[512,512]{1,0:T(8,128)(2,1)} collective-permute-done((bf16[512,512]{1,0:T(8,128)(2,1)}, bf16[512,512]{1,0:T(8,128)(2,1)}, u32[]{:S(2)}, u32[]{:S(2)}) %collective-permute-start.27) | collective-permute-done | bytes 524320 | tf_op jit(solution)/shard_map/ppermute | solution.py:541
  279.7 2.0 add_convert_fusion.11
  282.9 2.4 collective-permute-start.36
  285.3 3.0 fusion.8
  289.4 1.9 add_bitcast_fusion
  294.7 2.9 collective-permute-start.37
  297.6 2.2 collective-permute-done.34
  299.9 3.3 %fusion.4 = bf16[1024,512]{1,0:T(8,128)(2,1)} fusion(bf16[1024,512]{1,0:T(8,128)(2,1)S(1)} %copy-done.17, bf16[1024,512]{1,0:T(8,128)(2,1)S(1)} %copy-done.19, f32[1024]{0:T(1024)S(1)} %add.400, f32[1024]{0:T(1024)S(1)} %get-tuple-element.386, f32[512]{0:T(512)S(1)} %dynamic_slice.228, f32[1024]{0:T(1024)S(1)} %get-tuple-element.387, ...), kind=kLoop, calls=%fused_computation.10 | loop fusion | flops 7864320 | bytes 6305792 | tf_op jit(solution)/shard_map/convert_element_type | solution.py:1024
  303.2 1.4 collective-permute-done.38
  313.5 2.9 copy.66
  (271 shorter events, 57.3 us)
Async XLA Ops:
  0.6 26.5 %collective-permute-start.1 = (bf16[1024,512]{1,0:T(8,128)(2,1)}, bf16[1024,512]{1,0:T(8,128)(2,1)}, u32[]{:S(2)}, u32[]{:S(2)}) collective-permute-start(bf16[1024,512]{1,0:T(8,128)(2,1)} %refs_0_.4), channel_id=1, source_target_pairs={{0,2},{1,3},{2,0},{3,1},{4,6},{5,7},{6,4},{7,5},{8,10},{9,11},{10,... | collective-permute-start | bytes 3145736 | tf_op jit(solution)/shard_map/ppermute | solution.py:541
  3.7 27.9 %collective-permute-start.3 = (bf16[1024,512]{1,0:T(8,128)(2,1)}, bf16[1024,512]{1,0:T(8,128)(2,1)}, u32[]{:S(2)}, u32[]{:S(2)}) collective-permute-start(bf16[1024,512]{1,0:T(8,128)(2,1)} %refs_0_.4), channel_id=1, source_target_pairs={{0,1},{1,0},{2,3},{3,2},{4,5},{5,4},{6,7},{7,6},{8,9},{9,8},{10,11... | collective-permute-start | bytes 3145736 | tf_op jit(solution)/shard_map/ppermute | solution.py:541
  17.5 12.2 %copy-start.55 = (f32[5,256]{1,0:T(8,128)S(1)}, f32[5,256]{1,0:T(8,128)}, u32[]{:S(2)}) copy-start(f32[5,256]{1,0:T(8,128)} %param.22) | copy-start | bytes 15364
  17.5 12.8 %copy-start.62 = (f32[16]{0:T(128)S(1)}, f32[16]{0:T(128)}, u32[]{:S(2)}) copy-start(f32[16]{0:T(128)} %param.24) | copy-start | bytes 196
  17.6 13.4 %copy-start.61 = (f32[16]{0:T(128)S(1)}, f32[16]{0:T(128)}, u32[]{:S(2)}) copy-start(f32[16]{0:T(128)} %param.23) | copy-start | bytes 196
  27.8 3.8 %collective-permute-start.4 = (bf16[1024,512]{1,0:T(8,128)(2,1)}, bf16[1024,512]{1,0:T(8,128)(2,1)}, u32[]{:S(2)}, u32[]{:S(2)}) collective-permute-start(bf16[1024,512]{1,0:T(8,128)(2,1)} %collective-permute-done.1.refs_2_), channel_id=1, source_target_pairs={{0,1},{1,0},{2,3},{3,2},{4,5},{5,4},{6,7},{7,6},{8,9},{9,8},{10,11... | collective-permute-start | bytes 3145736 | tf_op jit(solution)/shard_map/ppermute | solution.py:541
  27.8 39.8 %collective-permute-start.2 = (bf16[1024,512]{1,0:T(8,128)(2,1)S(1)}, bf16[1024,512]{1,0:T(8,128)(2,1)S(1)}, u32[]{:S(2)}, u32[]{:S(2)}) collective-permute-start(bf16[1024,512]{1,0:T(8,128)(2,1)S(1)} %copy-done.18), channel_id=1, source_target_pairs={{0,2},{1,3},{2,0},{3,1},{4,6},{5,7},{6,4},{7,5},{8,10},{9,11},{10,... | collective-permute-start | bytes 3145736 | tf_op jit(solution)/shard_map/ppermute | solution.py:541
  29.5 38.4 %collective-permute-start = (bf16[1024,512]{1,0:T(8,128)(2,1)S(1)}, bf16[1024,512]{1,0:T(8,128)(2,1)S(1)}, u32[]{:S(2)}, u32[]{:S(2)}) collective-permute-start(bf16[1024,512]{1,0:T(8,128)(2,1)S(1)} %copy-done.18), channel_id=1, source_target_pairs={{0,1},{1,0},{2,3},{3,2},{4,5},{5,4},{6,7},{7,6},{8,9},{9,8},{10,11... | collective-permute-start | bytes 3145736 | tf_op jit(solution)/shard_map/ppermute | solution.py:541
  67.6 2.7 collective-permute-start.5
  83.1 1.5 collective-permute-start.6
  85.4 3.9 %collective-permute-start.7 = (f32[8,1024]{1,0:T(8,128)S(1)}, f32[8,1024]{1,0:T(8,128)S(1)}, u32[]{:S(2)}, u32[]{:S(2)}) collective-permute-start(f32[8,1024]{1,0:T(8,128)S(1)} %add.349), channel_id=1, source_target_pairs={{0,2},{1,3},{2,0},{3,1},{4,6},{5,7},{6,4},{7,5},{8,10},{9,11},{10,... | collective-permute-start | bytes 98312 | tf_op jit(solution)/shard_map/ppermute | solution.py:541
  99.4 28.0 %collective-permute-start.8 = (bf16[512,1024]{1,0:T(8,128)(2,1)}, bf16[512,1024]{1,0:T(8,128)(2,1)S(1)}, u32[]{:S(2)}, u32[]{:S(2)}) collective-permute-start(bf16[512,1024]{1,0:T(8,128)(2,1)} %get-tuple-element.194), channel_id=1, source_target_pairs={{0,4},{4,0},{8,12},{12,8},{16,20},{20,16},{24,28},{28,24},{1,5},{5... | collective-permute-start | bytes 3145736 | tf_op jit(solution)/shard_map/ppermute | solution.py:541
  118.3 10.6 %copy-start.33 = (bf16[512,1024]{1,0:T(8,128)(2,1)S(1)}, bf16[512,1024]{1,0:T(8,128)(2,1)}, u32[]{:S(2)}) copy-start(bf16[512,1024]{1,0:T(8,128)(2,1)} %get-tuple-element.183) | copy-start | bytes 3145732
  128.3 26.3 %collective-permute-start.9 = (bf16[2,1024,512]{2,1,0:T(8,128)(2,1)}, bf16[2,1024,512]{2,1,0:T(8,128)(2,1)S(1)}, u32[]{:S(2)}, u32[]{:S(2)}) collective-permute-start(bf16[2,1024,512]{2,1,0:T(8,128)(2,1)} %get-tuple-element.196), channel_id=1, source_target_pairs={{0,1},{1,0},{2,3},{3,2},{4,5},{5,4},{6,7},{7,6},{8,9},{9,8},{10,11... | collective-permute-start | bytes 6291464 | tf_op jit(solution)/shard_map/ppermute | solution.py:541
  128.4 26.3 %collective-permute-start.11 = (bf16[512,1024]{1,0:T(8,128)(2,1)}, bf16[512,1024]{1,0:T(8,128)(2,1)}, u32[]{:S(2)}, u32[]{:S(2)}) collective-permute-start(bf16[512,1024]{1,0:T(8,128)(2,1)} %get-tuple-element.207), channel_id=1, source_target_pairs={{0,4},{4,0},{8,12},{12,8},{16,20},{20,16},{24,28},{28,24},{1,5},{5... | collective-permute-start | bytes 3145736 | tf_op jit(solution)/shard_map/ppermute | solution.py:541
  130.1 24.5 %collective-permute-start.10 = (bf16[512,512]{1,0:T(8,128)(2,1)S(1)}, bf16[512,512]{1,0:T(8,128)(2,1)S(1)}, u32[]{:S(2)}, u32[]{:S(2)}) collective-permute-start(bf16[512,512]{1,0:T(8,128)(2,1)S(1)} %add_convert_fusion.9), channel_id=1, source_target_pairs={{0,8},{4,12},{8,0},{12,4},{16,24},{20,28},{24,16},{28,20},{1,9},{5... | collective-permute-start | bytes 1572872 | tf_op jit(solution)/shard_map/ppermute | solution.py:541
  131.7 68.7 %collective-permute-start.15 = (bf16[1024,1024]{1,0:T(8,128)(2,1)}, bf16[1024,1024]{1,0:T(8,128)(2,1)}, u32[]{:S(2)}, u32[]{:S(2)}) collective-permute-start(bf16[1024,1024]{1,0:T(8,128)(2,1)} %get-tuple-element.230), channel_id=1, source_target_pairs={{0,4},{4,0},{8,12},{12,8},{16,20},{20,16},{24,28},{28,24},{1,5},{5... | collective-permute-start | bytes 6291464 | tf_op jit(solution)/shard_map/ppermute | solution.py:541
  133.2 21.4 %copy-start.27 = (bf16[2,1024,512]{2,1,0:T(8,128)(2,1)S(1)}, bf16[2,1024,512]{2,1,0:T(8,128)(2,1)}, u32[]{:S(2)}) copy-start(bf16[2,1024,512]{2,1,0:T(8,128)(2,1)} %get-tuple-element.211) | copy-start | bytes 6291460
  154.9 32.1 %collective-permute-start.12 = (bf16[1024,512]{1,0:T(8,128)(2,1)S(1)}, bf16[1024,512]{1,0:T(8,128)(2,1)}, u32[]{:S(2)}, u32[]{:S(2)}) collective-permute-start(bf16[1024,512]{1,0:T(8,128)(2,1)S(1)} %fusion.10), channel_id=1, source_target_pairs={{0,2},{1,3},{2,0},{3,1},{4,6},{5,7},{6,4},{7,5},{8,10},{9,11},{10,... | collective-permute-start | bytes 3145736 | tf_op jit(solution)/shard_map/ppermute | solution.py:541
  158.0 29.0 %collective-permute-start.14 = (bf16[512,512]{1,0:T(8,128)(2,1)}, bf16[512,512]{1,0:T(8,128)(2,1)}, u32[]{:S(2)}, u32[]{:S(2)}) collective-permute-start(bf16[512,512]{1,0:T(8,128)(2,1)} %add_convert_fusion.8), channel_id=1, source_target_pairs={{0,8},{4,12},{8,0},{12,4},{16,24},{20,28},{24,16},{28,20},{1,9},{5... | collective-permute-start | bytes 1572872 | tf_op jit(solution)/shard_map/ppermute | solution.py:541
  161.0 25.9 %collective-permute-start.13 = (bf16[512,256]{1,0:T(8,128)(2,1)S(1)}, bf16[512,256]{1,0:T(8,128)(2,1)S(1)}, u32[]{:S(2)}, u32[]{:S(2)}) collective-permute-start(bf16[512,256]{1,0:T(8,128)(2,1)S(1)} %add_convert_fusion.14), channel_id=1, source_target_pairs={{0,16},{4,20},{8,24},{12,28},{16,0},{20,4},{24,8},{28,12},{1,17},{... | collective-permute-start | bytes 786440 | tf_op jit(solution)/shard_map/ppermute | solution.py:541
  188.6 13.1 %collective-permute-start.16 = (bf16[512,256]{1,0:T(8,128)(2,1)S(1)}, bf16[512,256]{1,0:T(8,128)(2,1)S(1)}, u32[]{:S(2)}, u32[]{:S(2)}) collective-permute-start(bf16[512,256]{1,0:T(8,128)(2,1)S(1)} %add_convert_fusion.13), channel_id=1, source_target_pairs={{0,16},{4,20},{8,24},{12,28},{16,0},{20,4},{24,8},{28,12},{1,17},{... | collective-permute-start | bytes 786440 | tf_op jit(solution)/shard_map/ppermute | solution.py:541
  189.1 34.8 %collective-permute-start.20 = (bf16[1024,512]{1,0:T(8,128)(2,1)}, bf16[1024,512]{1,0:T(8,128)(2,1)}, u32[]{:S(2)}, u32[]{:S(2)}) collective-permute-start(bf16[1024,512]{1,0:T(8,128)(2,1)} %get-tuple-element.238), channel_id=1, source_target_pairs={{0,4},{4,0},{8,12},{12,8},{16,20},{20,16},{24,28},{28,24},{1,5},{5... | collective-permute-start | bytes 3145736 | tf_op jit(solution)/shard_map/ppermute | solution.py:541
  201.7 22.2 %copy-start.50 = (bf16[512,256]{1,0:T(8,128)(2,1)}, bf16[512,256]{1,0:T(8,128)(2,1)S(1)}, u32[]{:S(2)}) copy-start(bf16[512,256]{1,0:T(8,128)(2,1)S(1)} %collective-permute-done.16) | copy-start | bytes 786436
  203.4 25.1 %collective-permute-start.21 = (bf16[512,1024]{1,0:T(8,128)(2,1)S(1)}, bf16[512,1024]{1,0:T(8,128)(2,1)S(1)}, u32[]{:S(2)}, u32[]{:S(2)}) collective-permute-start(bf16[512,1024]{1,0:T(8,128)(2,1)S(1)} %add_convert_fusion.1), channel_id=1, source_target_pairs={{0,8},{4,12},{8,0},{12,4},{16,24},{20,28},{24,16},{28,20},{1,9},{5... | collective-permute-start | bytes 3145736 | tf_op jit(solution)/shard_map/ppermute | solution.py:541
  203.5 20.4 %collective-permute-start.18 = (bf16[1024,256]{1,0:T(8,128)(2,1)S(1)}, bf16[1024,256]{1,0:T(8,128)(2,1)S(1)}, u32[]{:S(2)}, u32[]{:S(2)}) collective-permute-start(bf16[1024,256]{1,0:T(8,128)(2,1)S(1)} %get-tuple-element.232.refs_4_), channel_id=1, source_target_pairs={{0,1},{1,0},{2,3},{3,2},{4,5},{5,4},{6,7},{7,6},{8,9},{9,8},{10,11... | collective-permute-start | bytes 1572872 | tf_op jit(solution)/shard_map/ppermute | solution.py:541
  203.6 1.9 collective-permute-start.17
  205.5 18.4 %collective-permute-start.19 = (f32[5,256]{1,0:T(8,128)S(1)}, f32[5,256]{1,0:T(8,128)S(1)}, u32[]{:S(2)}, u32[]{:S(2)}) collective-permute-start(f32[5,256]{1,0:T(8,128)S(1)} %add.362), channel_id=1, source_target_pairs={{0,2},{1,3},{2,0},{3,1},{4,6},{5,7},{6,4},{7,5},{8,10},{9,11},{10,... | collective-permute-start | bytes 15368 | tf_op jit(solution)/shard_map/ppermute | solution.py:541
  229.5 8.3 %collective-permute-start.22 = (bf16[2,1024,512]{2,1,0:T(8,128)(2,1)}, bf16[2,1024,512]{2,1,0:T(8,128)(2,1)S(1)}, u32[]{:S(2)}, u32[]{:S(2)}) collective-permute-start(bf16[2,1024,512]{2,1,0:T(8,128)(2,1)} %get-tuple-element.240), channel_id=1, source_target_pairs={{0,1},{1,0},{2,3},{3,2},{4,5},{5,4},{6,7},{7,6},{8,9},{9,8},{10,11... | collective-permute-start | bytes 6291464 | tf_op jit(solution)/shard_map/ppermute | solution.py:541
  229.5 25.8 %collective-permute-start.26 = (bf16[1024,512]{1,0:T(8,128)(2,1)}, bf16[1024,512]{1,0:T(8,128)(2,1)S(1)}, u32[]{:S(2)}, u32[]{:S(2)}) collective-permute-start(bf16[1024,512]{1,0:T(8,128)(2,1)} %get-tuple-element.265), channel_id=1, source_target_pairs={{0,4},{4,0},{8,12},{12,8},{16,20},{20,16},{24,28},{28,24},{1,5},{5... | collective-permute-start | bytes 3145736 | tf_op jit(solution)/shard_map/ppermute | solution.py:541
  231.5 14.8 %collective-permute-start.24 = (bf16[1024,256]{1,0:T(8,128)(2,1)S(1)}, bf16[1024,256]{1,0:T(8,128)(2,1)S(1)}, u32[]{:S(2)}, u32[]{:S(2)}) collective-permute-start(bf16[1024,256]{1,0:T(8,128)(2,1)S(1)} %add_convert_fusion.5), channel_id=1, source_target_pairs={{0,2},{1,3},{2,0},{3,1},{4,6},{5,7},{6,4},{7,5},{8,10},{9,11},{10,... | collective-permute-start | bytes 1572872 | tf_op jit(solution)/shard_map/ppermute | solution.py:541
  234.0 21.6 %collective-permute-start.25 = (bf16[512,512]{1,0:T(8,128)(2,1)S(1)}, bf16[512,512]{1,0:T(8,128)(2,1)S(1)}, u32[]{:S(2)}, u32[]{:S(2)}) collective-permute-start(bf16[512,512]{1,0:T(8,128)(2,1)S(1)} %add_convert_fusion.7), channel_id=1, source_target_pairs={{0,8},{4,12},{8,0},{12,4},{16,24},{20,28},{24,16},{28,20},{1,9},{5... | collective-permute-start | bytes 1572872 | tf_op jit(solution)/shard_map/ppermute | solution.py:541
  234.3 12.0 %copy-start.16 = (bf16[1024,2048]{1,0:T(8,128)(2,1)S(1)}, bf16[1024,2048]{1,0:T(8,128)(2,1)}, u32[]{:S(2)}) copy-start(bf16[1024,2048]{1,0:T(8,128)(2,1)} %get-tuple-element.254.left_send.left_own) | copy-start | bytes 12582916
  236.8 37.1 %collective-permute-start.28 = (bf16[256,1024]{1,0:T(8,128)(2,1)}, bf16[256,1024]{1,0:T(8,128)(2,1)}, u32[]{:S(2)}, u32[]{:S(2)}) collective-permute-start(bf16[256,1024]{1,0:T(8,128)(2,1)} %add_convert_fusion.6), channel_id=1, source_target_pairs={{0,16},{4,20},{8,24},{12,28},{16,0},{20,4},{24,8},{28,12},{1,17},{... | collective-permute-start | bytes 1572872 | tf_op jit(solution)/shard_map/ppermute | solution.py:541
  239.3 40.4 %collective-permute-start.23 = (bf16[1024,512]{1,0:T(8,128)(2,1)}, bf16[1024,512]{1,0:T(8,128)(2,1)}, u32[]{:S(2)}, u32[]{:S(2)}) collective-permute-start(bf16[1024,512]{1,0:T(8,128)(2,1)} %fusion.11), channel_id=1, source_target_pairs={{0,2},{1,3},{2,0},{3,1},{4,6},{5,7},{6,4},{7,5},{8,10},{9,11},{10,... | collective-permute-start | bytes 3145736 | tf_op jit(solution)/shard_map/ppermute | solution.py:541
  258.7 21.0 %collective-permute-start.27 = (bf16[512,512]{1,0:T(8,128)(2,1)}, bf16[512,512]{1,0:T(8,128)(2,1)}, u32[]{:S(2)}, u32[]{:S(2)}) collective-permute-start(bf16[512,512]{1,0:T(8,128)(2,1)} %add_convert_fusion.3), channel_id=1, source_target_pairs={{0,8},{4,12},{8,0},{12,4},{16,24},{20,28},{24,16},{28,20},{1,9},{5... | collective-permute-start | bytes 1572872 | tf_op jit(solution)/shard_map/ppermute | solution.py:541
  258.8 48.9 %collective-permute-start.35 = (bf16[256,512]{1,0:T(8,128)(2,1)}, bf16[256,512]{1,0:T(8,128)(2,1)}, u32[]{:S(2)}, u32[]{:S(2)}) collective-permute-start(bf16[256,512]{1,0:T(8,128)(2,1)} %add_convert_fusion.12), channel_id=1, source_target_pairs={{0,16},{4,20},{8,24},{12,28},{16,0},{20,4},{24,8},{28,12},{1,17},{... | collective-permute-start | bytes 786440 | tf_op jit(solution)/shard_map/ppermute | solution.py:541
  263.4 10.5 %collective-permute-start.29 = (bf16[4,20480]{1,0:T(4,128)(2,1)}, bf16[4,20480]{1,0:T(4,128)(2,1)}, u32[]{:S(2)}, u32[]{:S(2)}) collective-permute-start(bf16[4,20480]{1,0:T(4,128)(2,1)} %bitcast.81), channel_id=1, source_target_pairs={{0,4},{4,0},{8,12},{12,8},{16,20},{20,16},{24,28},{28,24},{1,5},{5... | collective-permute-start | bytes 491528 | tf_op jit(solution)/shard_map/ppermute | solution.py:541
  270.8 10.9 %copy-start.41 = (f32[2,1,1,20480]{3,1,2,0:T(1,128)S(1)}, f32[2,1,1,20480]{3,1,2,0:T(1,128)}, u32[]{:S(2)}) copy-start(f32[2,1,1,20480]{3,1,2,0:T(1,128)} %dynamic-slice_convert_fusion) | copy-start | bytes 491524
  282.8 9.6 %collective-permute-start.32 = (bf16[2,20480]{1,0:T(2,128)(2,1)S(1)}, bf16[2,20480]{1,0:T(2,128)(2,1)S(1)}, u32[]{:S(2)}, u32[]{:S(2)}) collective-permute-start(bf16[2,20480]{1,0:T(2,128)(2,1)S(1)} %fusion.14), channel_id=1, source_target_pairs={{0,8},{4,12},{8,0},{12,4},{16,24},{20,28},{24,16},{28,20},{1,9},{5... | collective-permute-start | bytes 245768 | tf_op jit(solution)/shard_map/ppermute | solution.py:541
  282.9 24.9 %collective-permute-start.36 = (bf16[256,512]{1,0:T(8,128)(2,1)}, bf16[256,512]{1,0:T(8,128)(2,1)}, u32[]{:S(2)}, u32[]{:S(2)}) collective-permute-start(bf16[256,512]{1,0:T(8,128)(2,1)} %add_convert_fusion.11), channel_id=1, source_target_pairs={{0,16},{4,20},{8,24},{12,28},{16,0},{20,4},{24,8},{28,12},{1,17},{... | collective-permute-start | bytes 786440 | tf_op jit(solution)/shard_map/ppermute | solution.py:541
  288.3 4.0 %collective-permute-start.31 = (f32[7984]{0:T(1024)S(1)}, f32[7984]{0:T(1024)S(1)}, u32[]{:S(2)}, u32[]{:S(2)}) collective-permute-start(f32[7984]{0:T(1024)S(1)} %pad_maximum_fusion.6), channel_id=1, source_target_pairs={{0,4},{4,0},{8,12},{12,8},{16,20},{20,16},{24,28},{28,24},{1,5},{5... | collective-permute-start | bytes 95816 | tf_op jit(solution)/shard_map/ppermute | solution.py:541
  289.4 3.0 collective-permute-start.30
  292.4 10.8 %copy-start.47 = (bf16[2,20480]{1,0:T(2,128)(2,1)}, bf16[2,20480]{1,0:T(2,128)(2,1)S(1)}, u32[]{:S(2)}) copy-start(bf16[2,20480]{1,0:T(2,128)(2,1)S(1)} %collective-permute-done.32) | copy-start | bytes 245764
  292.4 7.4 %collective-permute-start.34 = (f32[7984]{0:T(1024)S(1)}, f32[7984]{0:T(1024)S(1)}, u32[]{:S(2)}, u32[]{:S(2)}) collective-permute-start(f32[7984]{0:T(1024)S(1)} %add.399), channel_id=1, source_target_pairs={{0,8},{4,12},{8,0},{12,4},{16,24},{20,28},{24,16},{28,20},{1,9},{5... | collective-permute-start | bytes 95816 | tf_op jit(solution)/shard_map/ppermute | solution.py:541
  292.6 5.1 %collective-permute-start.33 = (f32[1024]{0:T(1024)S(1)}, f32[1024]{0:T(1024)S(1)}, u32[]{:S(2)}, u32[]{:S(2)}) collective-permute-start(f32[1024]{0:T(1024)S(1)} %add.398), channel_id=1, source_target_pairs={{0,2},{1,3},{2,0},{3,1},{4,6},{5,7},{6,4},{7,5},{8,10},{9,11},{10,... | collective-permute-start | bytes 12296 | tf_op jit(solution)/shard_map/ppermute | solution.py:541
  294.7 13.0 %collective-permute-start.37 = (bf16[1,20480]{1,0:T(2,128)(2,1)S(1)}, bf16[1,20480]{1,0:T(2,128)(2,1)S(1)}, u32[]{:S(2)}, u32[]{:S(2)}) collective-permute-start(bf16[1,20480]{1,0:T(2,128)(2,1)S(1)} %fusion.22), channel_id=1, source_target_pairs={{0,16},{4,20},{8,24},{12,28},{16,0},{20,4},{24,8},{28,12},{1,17},{... | collective-permute-start | bytes 122888 | tf_op jit(solution)/shard_map/ppermute | solution.py:541
  299.8 4.8 %collective-permute-start.38 = (f32[7984]{0:T(1024)S(1)}, f32[7984]{0:T(1024)S(1)}, u32[]{:S(2)}, u32[]{:S(2)}) collective-permute-start(f32[7984]{0:T(1024)S(1)} %add.405), channel_id=1, source_target_pairs={{0,16},{4,20},{8,24},{12,28},{16,0},{20,4},{24,8},{28,12},{1,17},{... | collective-permute-start | bytes 95816 | tf_op jit(solution)/shard_map/ppermute | solution.py:541
  (54 other events, 302.5 us)
